TPU v7x, 32 devices: a whole 2x2x4 slice. The times are simulated.
32 devices in a mesh: kpt: 4 (over y, x), occ: 8 (over z, core).
Axes of the slice: x: 2, y: 2, z: 4, core: 2. Of those that a mesh axis runs over, the one named last changes fastest.
Arguments:
- factor: bfloat16 [2, 8, 8, 2, 256, 512], P(None, 'kpt', 'occ'), may hold values from -1.0546875 to 1.0546875
- partner: int32 [2, 8], replicated, may hold values from 0 to 7, as said below
- occ_energy: float32 [8, 8], replicated, may hold values from -3 to -0.5
- vir_sorted: float32 [8, 256], replicated, may hold values from 0.3 to 4.3, as said below
- vir_order: int32 [8, 256], replicated, may hold values from 0 to 255, each once within a row
Outputs:
- gradient_factor: bfloat16 [2, 8, 8, 2, 256, 512], P(None, 'kpt', 'occ')
Inputs may be any that keep to these rules, and one draw needn't show every extreme that they name: With group g holding k-points g * 2 to (g + 1) * 2 - 1, partner[0, k] lies in group (k // 2) XOR 1 and partner[1, k] in group (k // 2) XOR 2; which k-point of that group is arbitrary, and several k-points may share one. `vir_sorted`: each row is ascending and begins with 0.3.
All inputs are finite; a program needn't handle non-finite values.
Results may differ from a plain program's by a relative error of at most 0.0037.
Values may be sent and summed in bfloat16 or wider, within the bound.
No kernel may reach another device: no remote copies, remote signals or barrier semaphores. Data moves between devices by JAX's collectives and lax.ppermute only.
A program may use at most 64 MiB of HBM per device.

v0:
```python
import jax
import jax.numpy as jnp
from jax import lax
from jax.sharding import PartitionSpec as P

REACH = 1


def swapped_2(block, axis, distance):
    count = lax.axis_size(axis)
    route = []
    for low in range(count):
        high = low | 1 << distance
        if high != low and high < count:
            route += [(low, high), (high, low)]
    return lax.ppermute(block, axis, route)


def padded(cells, sides, width):
    for axis, dim in sides:
        count = lax.axis_size(axis)
        head = lax.slice_in_dim(cells, 0, width, axis=dim)
        tail = lax.slice_in_dim(cells, cells.shape[dim] - width, cells.shape[dim], axis=dim)
        cells = jnp.concatenate(
            [
                lax.ppermute(tail, axis, [(i, (i + 1) % count) for i in range(count)]),
                cells,
                lax.ppermute(head, axis, [((i + 1) % count, i) for i in range(count)]),
            ],
            axis=dim,
        )
    return cells


def pick_rows(table, indices):
    matches = indices[:, None] == jnp.arange(table.shape[0], dtype=jnp.int32)[None, :]
    return jnp.sum(jnp.where(matches[:, :, None], table[None, :, :], 0), axis=1)


def pick_columns(rows, indices):
    matches = indices[:, None] == jnp.arange(rows.shape[1], dtype=jnp.int32)[None, :]
    return jnp.sum(jnp.where(matches[None, :, :], rows[:, None, :], 0), axis=2)


def virtual_rows(vir_sorted, vir_order, indices):
    levels = pick_rows(vir_sorted, indices)
    ranks = pick_rows(vir_order, indices)
    matches = ranks[:, :, None] == jnp.arange(vir_sorted.shape[1], dtype=jnp.int32)[None, None, :]
    return jnp.sum(jnp.where(matches, levels[:, None, :], 0.0), axis=2)


def body(factor, partner, occ_energy, vir_sorted, vir_order):
    transfers = factor.shape[0]
    kpt_count = factor.shape[1]
    occ_count = factor.shape[2]
    orbital_total = occ_energy.shape[1]
    group_id = lax.axis_index("kpt")
    orbit_id = lax.axis_index("occ")
    kpt_ids = group_id * kpt_count + jnp.arange(kpt_count, dtype=jnp.int32)
    occ_ids = orbit_id * occ_count + jnp.arange(occ_count, dtype=jnp.int32)
    top_bit = lax.axis_size("kpt").bit_length() - 2
    flip_bits = [0, top_bit]
    own_virtual = virtual_rows(vir_sorted, vir_order, kpt_ids)
    own_occupied = pick_columns(pick_rows(occ_energy, kpt_ids), occ_ids)

    def fetch_window(transfer):
        flip_bit = flip_bits[transfer]
        partner_group = jnp.bitwise_xor(group_id, 1 << flip_bit)
        partner_ids = pick_rows(partner[transfer][:, None], kpt_ids)[:, 0]
        slot_ids = partner_ids - partner_group * kpt_count
        own_block = factor[transfer]
        swapped = swapped_2(own_block, "kpt", flip_bit)
        swapped = jnp.take(swapped, slot_ids, axis=0)
        extended = padded(swapped, (("occ", 1),), REACH)
        return (extended, partner_ids)

    def contract_window(transfer, fetched):
        extended, partner_ids = fetched
        own_block = factor[transfer]
        rotated = jnp.stack([own_block[:, :, 1], -own_block[:, :, 0]], axis=2)
        stacked = jnp.stack([own_block, rotated], axis=2)
        partner_virtual = virtual_rows(vir_sorted, vir_order, partner_ids)
        partner_rows = pick_rows(occ_energy, partner_ids)
        gradient = jnp.zeros(own_block.shape, jnp.float32)
        for offset in range(-REACH, REACH + 1):
            window = extended[:, REACH + offset : REACH + offset + occ_count]
            pair_ints = jnp.einsum(
                "kircaq,kicbq->kirab", stacked, window, preferred_element_type=jnp.float32
            )
            columns = jnp.remainder(occ_ids + offset, orbital_total)
            partner_occ = pick_columns(partner_rows, columns)
            denominator = (
                own_occupied[:, :, None, None]
                + partner_occ[:, :, None, None]
                - partner_virtual[:, None, :, None]
                - own_virtual[:, None, None, :]
            )
            amplitude = (pair_ints / denominator[:, :, None]).astype(jnp.bfloat16)
            real_part = amplitude[:, :, 0]
            imag_part = amplitude[:, :, 1]
            combined = jnp.stack(
                [
                    jnp.stack([real_part, -imag_part], axis=2),
                    jnp.stack([imag_part, real_part], axis=2),
                ],
                axis=2,
            )
            gradient = gradient + jnp.einsum(
                "kixcab,kicbq->kixaq", combined, window, preferred_element_type=jnp.float32
            )
        return gradient.astype(jnp.bfloat16)

    results = [contract_window(transfer, fetch_window(transfer)) for transfer in range(transfers)]
    return jnp.stack(results, axis=0)


def solution(mesh):
    in_specs = (P(None, "kpt", "occ", None, None, None), P(), P(), P(), P())
    out_specs = P(None, "kpt", "occ", None, None, None)
    return jax.shard_map(body, mesh=mesh, in_specs=in_specs, out_specs=out_specs, check_vma=False)
```

profile of v0, /device:TPU:0, one launch (start us, length us, event | category | flops | bytes accessed | tf_op | source)
XLA Modules:
  0.0 88.7 jit_solution(13167632134473912505)
XLA Ops:
  0.0 3.3 %slice_bitcast_fusion.3 = (bf16[2,1,1,2,256,512]{5,4,3,2,0,1:T(8,128)(2,1)}, bf16[2,1,2,256,512]{4,3,2,0,1:T(8,128)(2,1)S(1)}, bf16[2,1,2,256,512]{4,3,2,0,1:T(8,128)(2,1)S(1)}, bf16[2,1,1,2,256,512]{5,4,3,2,0,1:T(8,128)(2,1)}) fusion(bf16[2,2,1,2,256,512]{5,4,3,1,2,0:T(8,128)(2,1)} %bitcast.272), kind=kLoop, calls=%fused_computation.72 | loop fusion | bytes 6291456 | tf_op jit(solution)/shard_map/stack;squeeze | solution.py:81
  3.3 2.9 %collective-permute-start = (bf16[2,1,2,256,512]{4,3,2,0,1:T(8,128)(2,1)S(1)}, bf16[2,1,2,256,512]{4,3,2,0,1:T(8,128)(2,1)}, u32[]{:S(2)}, u32[]{:S(2)}) collective-permute-start(bf16[2,1,2,256,512]{4,3,2,0,1:T(8,128)(2,1)S(1)} %get-tuple-element.31), channel_id=1, source_target_pairs={{0,8},{8,0},{16,24},{24,16},{1,9},{9,1},{17,25},{25,17},{2,10},{10... | collective-permute-start | bytes 3145736 | tf_op jit(solution)/shard_map/ppermute | solution.py:16
  6.2 1.5 %collective-permute-start.3 = (bf16[2,1,2,256,512]{4,3,2,0,1:T(8,128)(2,1)S(1)}, bf16[2,1,2,256,512]{4,3,2,0,1:T(8,128)(2,1)}, u32[]{:S(2)}, u32[]{:S(2)}) collective-permute-start(bf16[2,1,2,256,512]{4,3,2,0,1:T(8,128)(2,1)S(1)} %get-tuple-element.32), channel_id=1, source_target_pairs={{0,16},{16,0},{8,24},{24,8},{1,17},{17,1},{9,25},{25,9},{2,18},{18... | collective-permute-start | bytes 3145736 | tf_op jit(solution)/shard_map/ppermute | solution.py:16
  7.8 1.1 %fusion.57 = (bf16[2,1,1,256,512]{4,3,2,0,1:T(8,128)(2,1)}, bf16[2,1,1,256,512]{4,3,2,0,1:T(8,128)(2,1)}, bf16[2,1,1,256,512]{4,3,2,0,1:T(8,128)(2,1)S(1)}, bf16[2,1,1,256,512]{4,3,2,0,1:T(8,128)(2,1)S(1)}) fusion(bf16[2,1,2,256,512]{4,3,2,0,1:T(8,128)(2,1)S(1)} %get-tuple-element.31, bf16[2,1,2,256,512]{4,3,2,0,1:T(8,128)(2,1)S(1)} %get-tuple-element.32), kind=kLoop, calls=%fused_computation.159 | loop fusion | flops 524288 | bytes 4194304 | tf_op jit(solution)/shard_map/slice | solution.py:80
  9.0 0.2 select_reduce_fusion.13
  9.2 0.1 iota_compare_fusion.3
  9.3 0.1 select_reduce_fusion.10
  9.4 0.1 select_reduce_fusion.8
  9.5 0.1 select_reduce_fusion.7
  9.7 0.1 fusion.50
  9.8 0.3 select_reduce_fusion.2
  10.0 0.3 select_reduce_fusion
  10.3 0.3 select_reduce_fusion.1
  10.5 2.3 %maximum_bitcast_fusion.3 = bf16[2,1,1,2,256,512]{5,4,3,2,0,1:T(8,128)(2,1)} fusion(bf16[2,1,1,256,512]{4,3,2,0,1:T(8,128)(2,1)} %get-tuple-element.35, bf16[2,1,1,256,512]{4,3,2,0,1:T(8,128)(2,1)} %get-tuple-element.34), kind=kLoop, calls=%fused_computation.37 | loop fusion | flops 524288 | bytes 2097152 | tf_op jit(solution)/shard_map/stack | solution.py:81
  12.8 1.1 %maximum_bitcast_fusion.7 = bf16[2,1,1,2,256,512]{5,4,3,2,0,1:T(8,128)(2,1)} fusion(bf16[2,1,1,256,512]{4,3,2,0,1:T(8,128)(2,1)S(1)} %get-tuple-element.92, bf16[2,1,1,256,512]{4,3,2,0,1:T(8,128)(2,1)S(1)} %get-tuple-element.93), kind=kLoop, calls=%fused_computation.41 | loop fusion | flops 524288 | bytes 2097152 | tf_op jit(solution)/shard_map/stack | solution.py:81
  13.9 0.2 fusion.46
  14.1 0.1 broadcast_subtract_fusion.9
  14.3 2.1 %broadcast_subtract_fusion.3 = (f32[2,256,256]{2,1,0:T(8,128)}, f32[2,256,256]{2,1,0:T(8,128)}, f32[2,256,256]{2,1,0:T(8,128)}, f32[2,256,256]{2,1,0:T(8,128)}, ...) fusion(f32[2,256]{1,0:T(2,128)S(1)} %get-tuple-element.74, f32[2,256]{1,0:T(2,128)S(1)} %select_reduce_fusion.1, ...), kind=kLoop, calls=%fused_computation.96 | loop fusion | flops 786432 | bytes 3160064 | tf_op jit(solution)/shard_map/sub | solution.py:93
  16.4 13.1 %collective-permute-done = bf16[2,1,2,256,512]{4,3,2,0,1:T(8,128)(2,1)} collective-permute-done((bf16[2,1,2,256,512]{4,3,2,0,1:T(8,128)(2,1)S(1)}, bf16[2,1,2,256,512]{4,3,2,0,1:T(8,128)(2,1)}, u32[]{:S(2)}, u32[]{:S(2)}) %collective-permute-start) | collective-permute-done | bytes 1048608 | tf_op jit(solution)/shard_map/ppermute | solution.py:16
  29.5 1.8 %gather_fusion = bf16[2,2,256,512]{3,2,1,0:T(8,128)(2,1)S(1)} fusion(bf16[2,2,256,512]{3,2,1,0:T(8,128)(2,1)} %bitcast.7, s32[1024]{0:T(1024)S(1)} %pad_clamp_fusion.1), kind=kCustom, calls=%fused_computation.clone | custom fusion | bytes 2097160 | tf_op jit(solution)/shard_map/jit(_take)/gather | solution.py:73
  31.4 0.2 bitcast_select_fusion.1
  31.5 2.5 %collective-permute-start.2 = (bf16[2,1,2,256,512]{4,3,2,0,1:T(8,128)(2,1)S(1)}, bf16[2,1,2,256,512]{4,3,2,0,1:T(8,128)(2,1)S(1)}, u32[]{:S(2)}, u32[]{:S(2)}) collective-permute-start(bf16[2,1,2,256,512]{4,3,2,0,1:T(8,128)(2,1)S(1)} %bitcast_select_fusion.1), channel_id=1, source_target_pairs={{1,0},{2,1},{3,2},{4,3},{5,4},{6,5},{7,6},{0,7},{9,8},{10,9},{11,1... | collective-permute-start | bytes 3145736 | tf_op jit(solution)/shard_map/ppermute | solution.py:28
  34.0 1.8 %gather_fusion.1 = bf16[2,2,256,512]{3,2,1,0:T(8,128)(2,1)S(1)} fusion(bf16[2,2,256,512]{3,2,1,0:T(8,128)(2,1)} %bitcast.56, s32[1024]{0:T(1024)S(1)} %pad_clamp_fusion), kind=kCustom, calls=%fused_computation.1.clone | custom fusion | bytes 2097160 | tf_op jit(solution)/shard_map/jit(_take)/gather | solution.py:73
  35.9 0.2 bitcast_select_fusion
  36.0 3.6 %collective-permute-start.5 = (bf16[2,1,2,256,512]{4,3,2,0,1:T(8,128)(2,1)S(1)}, bf16[2,1,2,256,512]{4,3,2,0,1:T(8,128)(2,1)S(1)}, u32[]{:S(2)}, u32[]{:S(2)}) collective-permute-start(bf16[2,1,2,256,512]{4,3,2,0,1:T(8,128)(2,1)S(1)} %bitcast_select_fusion), channel_id=1, source_target_pairs={{1,0},{2,1},{3,2},{4,3},{5,4},{6,5},{7,6},{0,7},{9,8},{10,9},{11,1... | collective-permute-start | bytes 3145736 | tf_op jit(solution)/shard_map/ppermute | solution.py:28
  39.7 1.9 %fusion.9 = bf16[2,1,2,256,256]{4,3,2,0,1:T(8,128)(2,1)S(1)} fusion(bf16[2,1,2,256,512]{4,3,2,0,1:T(8,128)(2,1)S(1)} %bitcast_select_fusion.1, bf16[2,1,1,2,256,512]{5,4,3,2,0,1:T(8,128)(2,1)S(1)} %copy-done.1, bf16[2,1,1,2,256,512]{5,4,3,2,0,1:T(8,128)(2,1)S(1)} %copy-done.3, f32[2,256,256]{2,1,0:T(8,128)} %get-tuple-element.69), kind=kOutput, calls=%fused_computation.24 | convolution fusion | flops 538443776 | bytes 4194304 | tf_op jit(solution)/shard_map/kircaq,kicbq->kirab/dot_general | solution.py:87
  41.7 0.7 fusion.18
  42.5 0.1 maximum_bitcast_fusion.19
  42.6 0.1 maximum_bitcast_fusion.25
  42.7 0.7 fusion.32
  43.4 0.7 fusion.24
  44.1 13.4 %collective-permute-done.2 = bf16[2,1,2,256,512]{4,3,2,0,1:T(8,128)(2,1)S(1)} collective-permute-done((bf16[2,1,2,256,512]{4,3,2,0,1:T(8,128)(2,1)S(1)}, bf16[2,1,2,256,512]{4,3,2,0,1:T(8,128)(2,1)S(1)}, u32[]{:S(2)}, u32[]{:S(2)}) %collective-permute-start.2) | collective-permute-done | bytes 1048608 | tf_op jit(solution)/shard_map/ppermute | solution.py:28
  57.6 0.7 fusion.12
  58.3 3.1 %collective-permute-done.1 = bf16[2,1,2,256,512]{4,3,2,0,1:T(8,128)(2,1)} collective-permute-done((bf16[2,1,2,256,512]{4,3,2,0,1:T(8,128)(2,1)S(1)}, bf16[2,1,2,256,512]{4,3,2,0,1:T(8,128)(2,1)}, u32[]{:S(2)}, u32[]{:S(2)}) %collective-permute-start.1) | collective-permute-done | bytes 1048608 | tf_op jit(solution)/shard_map/ppermute | solution.py:26
  61.4 2.0 %fusion.6 = bf16[2,1,2,256,256]{4,3,2,0,1:T(8,128)(2,1)S(1)} fusion(bf16[2,1,2,256,512]{4,3,2,0,1:T(8,128)(2,1)} %collective-permute-done.1, bf16[2,1,1,2,256,512]{5,4,3,2,0,1:T(8,128)(2,1)S(1)} %copy-done.1, bf16[2,1,1,2,256,512]{5,4,3,2,0,1:T(8,128)(2,1)S(1)} %copy-done.3, f32[2,256,256]{2,1,0:T(8,128)S(1)} %copy-done.6), kind=kOutput, calls=%fused_computation.21 | convolution fusion | flops 538443776 | bytes 4194304 | tf_op jit(solution)/shard_map/kircaq,kicbq->kirab/dot_general | solution.py:87
  63.5 15.4 %collective-permute-done.5 = bf16[2,1,2,256,512]{4,3,2,0,1:T(8,128)(2,1)S(1)} collective-permute-done((bf16[2,1,2,256,512]{4,3,2,0,1:T(8,128)(2,1)S(1)}, bf16[2,1,2,256,512]{4,3,2,0,1:T(8,128)(2,1)S(1)}, u32[]{:S(2)}, u32[]{:S(2)}) %collective-permute-start.5) | collective-permute-done | bytes 1048608 | tf_op jit(solution)/shard_map/ppermute | solution.py:28
  79.0 0.7 fusion.21
  79.8 2.1 %collective-permute-done.4 = bf16[2,1,2,256,512]{4,3,2,0,1:T(8,128)(2,1)S(1)} collective-permute-done((bf16[2,1,2,256,512]{4,3,2,0,1:T(8,128)(2,1)S(1)}, bf16[2,1,2,256,512]{4,3,2,0,1:T(8,128)(2,1)S(1)}, u32[]{:S(2)}, u32[]{:S(2)}) %collective-permute-start.4) | collective-permute-done | bytes 1048608 | tf_op jit(solution)/shard_map/ppermute | solution.py:26
  81.9 0.7 fusion.15
  82.7 0.1 maximum_bitcast_fusion.21
  82.8 0.1 maximum_bitcast_fusion.17
  82.9 0.1 maximum_bitcast_fusion.27
  83.0 0.1 maximum_bitcast_fusion.23
  83.1 1.9 %fusion.35 = f32[2,2,256,512,1]{3,2,4,1,0:T(8,128)S(1)} fusion(bf16[2,1,2,256,512]{4,3,2,0,1:T(8,128)(2,1)} %collective-permute-done.1, bf16[2,1,1,2,256,256]{5,4,3,0,2,1:T(8,128)(2,1)S(1)} %get-tuple-element.59, bf16[2,1,1,2,256,256]{5,4,3,0,2,1:T(8,128)(2,1)S(1)} %get-tuple-element.58), kind=kOutput, calls=%fused_computation.58 | convolution fusion | flops 537395200 | bytes 4194304 | tf_op jit(solution)/shard_map/kixcab,kicbq->kixaq/dot_general | solution.py:108
  85.0 0.7 fusion.27
  85.7 0.7 fusion.2
  86.4 0.7 fusion.3
  87.2 1.5 %maximum_bitcast_fusion.2 = bf16[2,2,1,2,256,512]{5,4,3,2,1,0:T(8,128)(2,1)} fusion(bf16[1,2,1,2,256,512]{5,4,3,1,2,0:T(8,128)(2,1)S(1)} %fusion.3, bf16[1,2,1,2,256,512]{5,4,3,1,2,0:T(8,128)(2,1)S(1)} %fusion.2), kind=kLoop, calls=%fused_computation.4 | loop fusion | flops 1048576 | bytes 4194304 | tf_op jit(solution)/shard_map/stack | solution.py:114
  (47 shorter events, 0.6 us)
Async XLA Ops:
  3.3 26.2 %collective-permute-start = (bf16[2,1,2,256,512]{4,3,2,0,1:T(8,128)(2,1)S(1)}, bf16[2,1,2,256,512]{4,3,2,0,1:T(8,128)(2,1)}, u32[]{:S(2)}, u32[]{:S(2)}) collective-permute-start(bf16[2,1,2,256,512]{4,3,2,0,1:T(8,128)(2,1)S(1)} %get-tuple-element.31), channel_id=1, source_target_pairs={{0,8},{8,0},{16,24},{24,16},{1,9},{9,1},{17,25},{25,17},{2,10},{10... | collective-permute-start | bytes 3145736 | tf_op jit(solution)/shard_map/ppermute | solution.py:16
  6.2 27.8 %collective-permute-start.3 = (bf16[2,1,2,256,512]{4,3,2,0,1:T(8,128)(2,1)S(1)}, bf16[2,1,2,256,512]{4,3,2,0,1:T(8,128)(2,1)}, u32[]{:S(2)}, u32[]{:S(2)}) collective-permute-start(bf16[2,1,2,256,512]{4,3,2,0,1:T(8,128)(2,1)S(1)} %get-tuple-element.32), channel_id=1, source_target_pairs={{0,16},{16,0},{8,24},{24,8},{1,17},{17,1},{9,25},{25,9},{2,18},{18... | collective-permute-start | bytes 3145736 | tf_op jit(solution)/shard_map/ppermute | solution.py:16
  7.8 1.2 %copy-start.12 = (s32[2,8]{1,0:T(2,128)S(1)}, s32[2,8]{1,0:T(2,128)}, u32[]{:S(2)}) copy-start(s32[2,8]{1,0:T(2,128)} %param.8) | copy-start | bytes 196
  7.8 1.5 %copy-start.11 = (f32[8,8]{1,0:T(8,128)S(1)}, f32[8,8]{1,0:T(8,128)}, u32[]{:S(2)}) copy-start(f32[8,8]{1,0:T(8,128)} %param.9) | copy-start | bytes 772
  7.8 1.6 %copy-start.9 = (s32[8,256]{1,0:T(8,128)S(1)}, s32[8,256]{1,0:T(8,128)}, u32[]{:S(2)}) copy-start(s32[8,256]{1,0:T(8,128)} %param.11) | copy-start | bytes 24580
  7.8 1.7 %copy-start.10 = (f32[8,256]{1,0:T(8,128)S(1)}, f32[8,256]{1,0:T(8,128)}, u32[]{:S(2)}) copy-start(f32[8,256]{1,0:T(8,128)} %param.10) | copy-start | bytes 24580
  31.5 26.0 %collective-permute-start.2 = (bf16[2,1,2,256,512]{4,3,2,0,1:T(8,128)(2,1)S(1)}, bf16[2,1,2,256,512]{4,3,2,0,1:T(8,128)(2,1)S(1)}, u32[]{:S(2)}, u32[]{:S(2)}) collective-permute-start(bf16[2,1,2,256,512]{4,3,2,0,1:T(8,128)(2,1)S(1)} %bitcast_select_fusion.1), channel_id=1, source_target_pairs={{1,0},{2,1},{3,2},{4,3},{5,4},{6,5},{7,6},{0,7},{9,8},{10,9},{11,1... | collective-permute-start | bytes 3145736 | tf_op jit(solution)/shard_map/ppermute | solution.py:28
  34.0 27.4 %collective-permute-start.1 = (bf16[2,1,2,256,512]{4,3,2,0,1:T(8,128)(2,1)S(1)}, bf16[2,1,2,256,512]{4,3,2,0,1:T(8,128)(2,1)}, u32[]{:S(2)}, u32[]{:S(2)}) collective-permute-start(bf16[2,1,2,256,512]{4,3,2,0,1:T(8,128)(2,1)S(1)} %bitcast_select_fusion.1), channel_id=1, source_target_pairs={{0,1},{1,2},{2,3},{3,4},{4,5},{5,6},{6,7},{7,0},{8,9},{9,10},{10,1... | collective-permute-start | bytes 3145736 | tf_op jit(solution)/shard_map/ppermute | solution.py:26
  35.9 3.8 %copy-start.1 = (bf16[2,1,1,2,256,512]{5,4,3,2,0,1:T(8,128)(2,1)S(1)}, bf16[2,1,1,2,256,512]{5,4,3,2,0,1:T(8,128)(2,1)}, u32[]{:S(2)}) copy-start(bf16[2,1,1,2,256,512]{5,4,3,2,0,1:T(8,128)(2,1)} %maximum_bitcast_fusion.3) | copy-start | bytes 3145732
  35.9 3.8 %copy-start.3 = (bf16[2,1,1,2,256,512]{5,4,3,2,0,1:T(8,128)(2,1)S(1)}, bf16[2,1,1,2,256,512]{5,4,3,2,0,1:T(8,128)(2,1)}, u32[]{:S(2)}) copy-start(bf16[2,1,1,2,256,512]{5,4,3,2,0,1:T(8,128)(2,1)} %get-tuple-element.30) | copy-start | bytes 3145732
  36.0 42.9 %collective-permute-start.5 = (bf16[2,1,2,256,512]{4,3,2,0,1:T(8,128)(2,1)S(1)}, bf16[2,1,2,256,512]{4,3,2,0,1:T(8,128)(2,1)S(1)}, u32[]{:S(2)}, u32[]{:S(2)}) collective-permute-start(bf16[2,1,2,256,512]{4,3,2,0,1:T(8,128)(2,1)S(1)} %bitcast_select_fusion), channel_id=1, source_target_pairs={{1,0},{2,1},{3,2},{4,3},{5,4},{6,5},{7,6},{0,7},{9,8},{10,9},{11,1... | collective-permute-start | bytes 3145736 | tf_op jit(solution)/shard_map/ppermute | solution.py:28
  39.6 42.3 %collective-permute-start.4 = (bf16[2,1,2,256,512]{4,3,2,0,1:T(8,128)(2,1)S(1)}, bf16[2,1,2,256,512]{4,3,2,0,1:T(8,128)(2,1)S(1)}, u32[]{:S(2)}, u32[]{:S(2)}) collective-permute-start(bf16[2,1,2,256,512]{4,3,2,0,1:T(8,128)(2,1)S(1)} %bitcast_select_fusion), channel_id=1, source_target_pairs={{0,1},{1,2},{2,3},{3,4},{4,5},{5,6},{6,7},{7,0},{8,9},{9,10},{10,1... | collective-permute-start | bytes 3145736 | tf_op jit(solution)/shard_map/ppermute | solution.py:26
  39.6 2.0 %copy-start = (bf16[2,1,1,2,256,512]{5,4,3,2,0,1:T(8,128)(2,1)S(1)}, bf16[2,1,1,2,256,512]{5,4,3,2,0,1:T(8,128)(2,1)}, u32[]{:S(2)}) copy-start(bf16[2,1,1,2,256,512]{5,4,3,2,0,1:T(8,128)(2,1)} %maximum_bitcast_fusion.7) | copy-start | bytes 3145732
  39.7 2.0 %copy-start.2 = (bf16[2,1,1,2,256,512]{5,4,3,2,0,1:T(8,128)(2,1)S(1)}, bf16[2,1,1,2,256,512]{5,4,3,2,0,1:T(8,128)(2,1)}, u32[]{:S(2)}) copy-start(bf16[2,1,1,2,256,512]{5,4,3,2,0,1:T(8,128)(2,1)} %get-tuple-element.33) | copy-start | bytes 3145732
  39.7 2.0 %copy-start.8 = (f32[2,256,256]{2,1,0:T(8,128)S(1)}, f32[2,256,256]{2,1,0:T(8,128)}, u32[]{:S(2)}) copy-start(f32[2,256,256]{2,1,0:T(8,128)} %get-tuple-element.71) | copy-start | bytes 1572868
  43.4 14.2 %copy-start.7 = (f32[2,256,256]{2,1,0:T(8,128)S(1)}, f32[2,256,256]{2,1,0:T(8,128)}, u32[]{:S(2)}) copy-start(f32[2,256,256]{2,1,0:T(8,128)} %get-tuple-element.68) | copy-start | bytes 1572868
  57.6 3.9 %copy-start.6 = (f32[2,256,256]{2,1,0:T(8,128)S(1)}, f32[2,256,256]{2,1,0:T(8,128)}, u32[]{:S(2)}) copy-start(f32[2,256,256]{2,1,0:T(8,128)} %get-tuple-element.73) | copy-start | bytes 1572868
  63.4 15.6 %copy-start.5 = (f32[2,256,256]{2,1,0:T(8,128)S(1)}, f32[2,256,256]{2,1,0:T(8,128)}, u32[]{:S(2)}) copy-start(f32[2,256,256]{2,1,0:T(8,128)} %get-tuple-element.72) | copy-start | bytes 1572868
  79.0 2.9 %copy-start.4 = (f32[2,256,256]{2,1,0:T(8,128)S(1)}, f32[2,256,256]{2,1,0:T(8,128)}, u32[]{:S(2)}) copy-start(f32[2,256,256]{2,1,0:T(8,128)} %get-tuple-element.70) | copy-start | bytes 1572868
where the time goes:
time: 89 us; the launch traced here: 88.7 us
  waiting for transfers between devices  47.3 us (53%)
  matrix products  12.3 us (14%)
  other arithmetic  11.1 us (12%)
  starting transfers between devices  10.5 us (12%)
  local copies, waits for them, and re-layouts  7.05 us (8%)
    ppermute x2, waiting for transfers between devices, padded(): lax.ppermute(head, axis, [((i + 1) % count, i) for i in range(count)])  28.9 us
    ppermute x2, waiting for transfers between devices, swapped_2(): return lax.ppermute(block, axis, route)  13.1 us
    dot_general x6, matrix products, contract_window(): jnp.einsum('kircaq,kicbq->kirab', stacked, window, preferred_element_type...  6.85 us
    ppermute x2, starting transfers between devices, padded(): lax.ppermute(head, axis, [((i + 1) % count, i) for i in range(count)])  6.07 us
    dot_general x6, matrix products, contract_window(): jnp.einsum('kixcab,kicbq->kixaq', combined, window, preferred_element_typ...  5.48 us
    ppermute x2, waiting for transfers between devices, padded(): lax.ppermute(tail, axis, [(i, (i + 1) % count) for i in range(count)])  5.25 us
    ppermute x2, starting transfers between devices, swapped_2(): return lax.ppermute(block, axis, route)  4.46 us
    gather x2, local copies, waits for them, and re-layouts, fetch_window(): swapped = jnp.take(swapped, slot_ids, axis=0)  3.67 us
  transfers between devices with their start and end apart: 6, of which 5 were waited for; matrix products, arithmetic and copies ran while one was open for 23% of the time, Pallas kernels for 0%

commit v1 on v0

v1 whole, which is shorter than its diff:
```python
import functools

import jax
import jax.numpy as jnp
from jax import lax
from jax.experimental import pallas as pl
from jax.experimental.pallas import tpu as pltpu
from jax.sharding import PartitionSpec as P

F32 = jnp.float32
BF16 = jnp.bfloat16


def group_swap(block, bit):
    count = lax.axis_size("kpt")
    return lax.ppermute(block, "kpt", [(g, g ^ (1 << bit)) for g in range(count)])


def near_swap(block):
    count = lax.axis_size("occ")
    return lax.ppermute(block, "occ", [(i, i ^ 1) for i in range(count)])


def far_swap(block):
    count = lax.axis_size("occ")
    return lax.ppermute(
        block, "occ", [(i, (i + (1 if i % 2 else count - 1)) % count) for i in range(count)]
    )


def virtual_energies(vir_sorted, vir_order):
    ranks = jnp.arange(vir_sorted.shape[1], dtype=jnp.int32)
    matches = vir_order[:, :, None] == ranks[None, None, :]
    return jnp.sum(jnp.where(matches, vir_sorted[:, None, :], 0.0), axis=2)


def nt_dot(left, right):
    return lax.dot_general(left, right, (((1,), (1,)), ((), ())), preferred_element_type=F32)


def kernel(transfer, bit, kc, places, first, ids, partner, occ, *refs):
    row_ref, col_ref, own_ref = refs[:3]
    windows = refs[3 : 3 + len(places)]
    rest = refs[3 + len(places) :]
    out_ref = rest[-1]
    nv, naux = own_ref.shape[-2:]
    point = ids[0] * kc + pl.program_id(0)
    far_point = partner[transfer, point]
    orbit, total = ids[1], occ.shape[1]
    parity = lax.rem(orbit, 2)
    columns = {
        "own": orbit,
        "near": orbit + 1 - 2 * parity,
        "far": lax.rem(orbit + total - 1 + 2 * parity, total),
    }
    own = own_ref[...].reshape(2, nv, naux)
    real, imag = own[0], own[1]
    left = jnp.concatenate([real, imag], axis=0)
    right = jnp.concatenate([imag, -real], axis=0)
    gradient = None if first else rest[0][...].reshape(2 * nv, naux)
    for place, window_ref in zip(places, windows):
        window = window_ref[...].reshape(2, nv, naux)
        pair = nt_dot(left, window[0]) + nt_dot(right, window[1])
        level = occ[point, orbit] + occ[far_point, columns[place]]
        denominator = (level - col_ref[0]) - row_ref[0]
        real_part = (pair[:nv] / denominator).astype(BF16)
        imag_part = (pair[nv:] / denominator).astype(BF16)
        combined = jnp.concatenate(
            [
                jnp.concatenate([real_part, -imag_part], axis=1),
                jnp.concatenate([imag_part, real_part], axis=1),
            ],
            axis=0,
        )
        term = jnp.dot(combined, window.reshape(2 * nv, naux), preferred_element_type=F32)
        gradient = term if gradient is None else gradient + term
    out_ref[...] = gradient.reshape(out_ref.shape).astype(out_ref.dtype)


def contract(transfer, bit, scalars, rows, cols, factor, windows, base=None, result=None):
    _, kc, _, _, nv, naux = factor.shape
    final = base is not None
    places = [place for place, _ in windows]

    def own_at(k, *_):
        return (transfer, k, 0, 0, 0, 0)

    def slot_at(k, ids, partner, occ):
        far_group = jnp.bitwise_xor(ids[0], 1 << bit)
        return (partner[transfer, ids[0] * kc + k] - far_group * kc, 0, 0, 0, 0)

    own_block = (1, 1, 1, 2, nv, naux)
    term_block = (1, 2, nv, naux)
    term_spec = pl.BlockSpec(term_block, lambda k, *_: (k, 0, 0, 0))
    in_specs = [
        pl.BlockSpec((1, 1, nv), lambda k, ids, *_: (ids[0] * kc + k, 0, 0)),
        pl.BlockSpec((1, nv, 1), lambda k, ids, partner, _: (partner[transfer, ids[0] * kc + k], 0, 0)),
        pl.BlockSpec(own_block, own_at),
    ] + [pl.BlockSpec((1, 1, 2, nv, naux), slot_at)] * len(windows)
    operands = [rows, cols, factor] + [window for _, window in windows]
    aliases = {}
    if final:
        in_specs.append(term_spec)
        operands.append(base)
        out_shape = jax.ShapeDtypeStruct(factor.shape, BF16)
        out_spec = pl.BlockSpec(own_block, own_at)
        if result is not None:
            in_specs.append(pl.BlockSpec(memory_space=pl.ANY))
            aliases = {len(scalars) + len(operands): 0}
            operands.append(result)
    else:
        out_shape = jax.ShapeDtypeStruct((kc, 2, nv, naux), F32)
        out_spec = term_spec
    flops = kc * len(windows) * 16 * nv * nv * naux
    moved = kc * nv * naux * (4 * (1 + len(windows)) + (12 if final else 8))
    return pl.pallas_call(
        functools.partial(kernel, transfer, bit, kc, places, not final),
        out_shape=out_shape,
        grid_spec=pltpu.PrefetchScalarGridSpec(
            num_scalar_prefetch=len(scalars), grid=(kc,), in_specs=in_specs, out_specs=out_spec
        ),
        input_output_aliases=aliases,
        cost_estimate=pl.CostEstimate(flops=flops, bytes_accessed=moved, transcendentals=0),
        compiler_params=pltpu.CompilerParams(vmem_limit_bytes=24 * 1024 * 1024),
    )(*scalars, *operands)


def body(factor, partner, occ_energy, vir_sorted, vir_order):
    top_bit = lax.axis_size("kpt").bit_length() - 2
    ids = jnp.stack([lax.axis_index("kpt"), lax.axis_index("occ")]).astype(jnp.int32)
    scalars = (ids, partner, occ_energy)

    one, two = factor[0], factor[1]
    one_far_own = far_swap(one)
    one_swapped = group_swap(one, 0)
    two_swapped = group_swap(two, top_bit)
    one_far = group_swap(one_far_own, 0)
    two_far = far_swap(two_swapped)
    one_near = near_swap(one_swapped)
    two_near = near_swap(two_swapped)

    virtual = virtual_energies(vir_sorted, vir_order)
    rows, cols = virtual[:, None, :], virtual[:, :, None]
    call = functools.partial(contract, scalars=scalars, rows=rows, cols=cols, factor=factor)
    base_one = call(0, 0, windows=[("own", one_swapped), ("near", one_near)])
    base_two = call(1, top_bit, windows=[("own", two_swapped), ("near", two_near)])
    result = call(0, 0, windows=[("far", one_far)], base=base_one)
    return call(1, top_bit, windows=[("far", two_far)], base=base_two, result=result)


def solution(mesh):
    spec = P(None, "kpt", "occ", None, None, None)
    in_specs = (spec, P(), P(), P(), P())
    return jax.shard_map(body, mesh=mesh, in_specs=in_specs, out_specs=spec, check_vma=False)
```

time: 89 us -> 69.5 us (0.78)
  Pallas kernels: 0 us -> 19 us
  matrix products: 12.3 us -> 0 us
  waiting for transfers between devices: 47.3 us -> 37 us
  other arithmetic: 11.1 us -> 0.84 us
  local copies, waits for them, and re-layouts: 7.05 us -> 2.3 us
    pallas_call x0 -> x4, Pallas kernels: none -> 19 us  [contract(): pl.pallas_call(functools.partial(kernel, transfer, bit, kc, places, not f...]
    dot_general x12 -> x0, matrix products: 12.3 us -> none  [the longest x6 6.85 us: contract_window(): jnp.einsum('kircaq,kicbq->kirab', stacked, window, preferred_element_type...]
    ppermute x6 -> x7, waiting for transfers between devices: 47.3 us -> 37 us  [the longest x3 33.2 us: group_swap(): return lax.ppermute(block, 'kpt', [(g, g ^ 1 << bit) for g in range(count)])]
    another operation x9 -> x1, other arithmetic: 5.31 us -> 0.08 us  [body(): jnp.stack([lax.axis_index('kpt'), lax.axis_index('occ')]).astype(jnp.int32)]
    gather x2 -> x0, local copies, waits for them, and re-layouts: 3.67 us -> none  [fetch_window(): swapped = jnp.take(swapped, slot_ids, axis=0)]
    another operation x1 -> x0, local copies, waits for them, and re-layouts: 3.31 us -> none  [contract_window(): stacked = jnp.stack([own_block, rotated], axis=2)]
    sub x3 -> x0, other arithmetic: 2.24 us -> none  [contract_window(): own_occupied[:, :, None, None] + partner_occ[:, :, None, None]]
    squeeze x0 -> x1, local copies, waits for them, and re-layouts: none -> 1.91 us  [body(): one, two = (factor[0], factor[1])]
  transfers between devices with their start and end apart: 6 -> 7, of which waited for: 5 -> 3; matrix products, arithmetic and copies ran while one was open for 23% -> 2% of each run, Pallas kernels for 0% -> 20%
where the time goes in v1:
time: 69.5 us; the launch traced here: 69.2 us
  waiting for transfers between devices  37 us (53%)
  Pallas kernels  19 us (27%)
  starting transfers between devices  10 us (14%)
  local copies, waits for them, and re-layouts  2.3 us (3%)
  other arithmetic  0.84 us (1%)
    ppermute x3, waiting for transfers between devices, group_swap(): return lax.ppermute(block, 'kpt', [(g, g ^ 1 << bit) for g in range(count)])  33.2 us
    pallas_call x4, Pallas kernels, contract(): pl.pallas_call(functools.partial(kernel, transfer, bit, kc, places, not f...  19 us
    ppermute x2, starting transfers between devices, far_swap(): lax.ppermute(block, 'occ', [(i, (i + (1 if i % 2 else count - 1)) % count...  5.47 us
    ppermute x3, starting transfers between devices, group_swap(): return lax.ppermute(block, 'kpt', [(g, g ^ 1 << bit) for g in range(count)])  4.54 us
    ppermute x2, waiting for transfers between devices, far_swap(): lax.ppermute(block, 'occ', [(i, (i + (1 if i % 2 else count - 1)) % count...  3.83 us
    squeeze x1, local copies, waits for them, and re-layouts, body(): one, two = (factor[0], factor[1])  1.91 us
  transfers between devices with their start and end apart: 7, of which 3 were waited for; matrix products, arithmetic and copies ran while one was open for 2% of the time, Pallas kernels for 20%

profile of v1, /device:TPU:0, one launch (start us, length us, event | category | flops | bytes accessed | tf_op | source)
XLA Modules:
  0.0 69.2 jit_solution(3312332096782387393)
XLA Ops:
  0.0 0.0 copy-start.3
  0.0 0.0 copy-start.4
  0.0 0.0 copy-start
  0.0 0.0 copy-start.1
  0.0 0.0 copy-start.2
  0.0 1.9 %slice_bitcast_fusion = (bf16[2,1,2,256,512]{4,3,2,1,0:T(8,128)(2,1)S(1)}, bf16[2,1,2,256,512]{4,3,2,1,0:T(8,128)(2,1)S(1)}) fusion(bf16[2,2,1,2,256,512]{5,4,3,1,2,0:T(8,128)(2,1)} %bitcast.8), kind=kLoop, calls=%fused_computation.2 | loop fusion | bytes 4194304 | tf_op jit(solution)/shard_map/squeeze | solution.py:133
  1.9 3.0 %collective-permute-start.5 = (bf16[2,1,2,256,512]{4,3,2,1,0:T(8,128)(2,1)S(1)}, bf16[2,1,2,256,512]{4,3,2,1,0:T(8,128)(2,1)}, u32[]{:S(2)}, u32[]{:S(2)}) collective-permute-start(bf16[2,1,2,256,512]{4,3,2,1,0:T(8,128)(2,1)S(1)} %get-tuple-element.5), channel_id=1, source_target_pairs={{0,8},{8,0},{16,24},{24,16},{1,9},{9,1},{17,25},{25,17},{2,10},{10... | collective-permute-start | bytes 3145736 | tf_op jit(solution)/shard_map/ppermute | solution.py:16
  5.0 2.8 %collective-permute-start.3 = (bf16[2,1,2,256,512]{4,3,2,1,0:T(8,128)(2,1)S(1)}, bf16[2,1,2,256,512]{4,3,2,1,0:T(8,128)(2,1)}, u32[]{:S(2)}, u32[]{:S(2)}) collective-permute-start(bf16[2,1,2,256,512]{4,3,2,1,0:T(8,128)(2,1)S(1)} %get-tuple-element.5), channel_id=1, source_target_pairs={{0,7},{1,2},{2,1},{3,4},{4,3},{5,6},{6,5},{7,0},{8,15},{9,10},{10,... | collective-permute-start | bytes 3145736 | tf_op jit(solution)/shard_map/ppermute | solution.py:26
  7.7 1.5 %collective-permute-start = (bf16[2,1,2,256,512]{4,3,2,1,0:T(8,128)(2,1)S(1)}, bf16[2,1,2,256,512]{4,3,2,1,0:T(8,128)(2,1)}, u32[]{:S(2)}, u32[]{:S(2)}) collective-permute-start(bf16[2,1,2,256,512]{4,3,2,1,0:T(8,128)(2,1)S(1)} %get-tuple-element.6), channel_id=1, source_target_pairs={{0,16},{8,24},{16,0},{24,8},{1,17},{9,25},{17,1},{25,9},{2,18},{10... | collective-permute-start | bytes 3145736 | tf_op jit(solution)/shard_map/ppermute | solution.py:16
  9.2 19.0 %collective-permute-done.5.refs_3_ = bf16[2,1,2,256,512]{4,3,2,1,0:T(8,128)(2,1)} collective-permute-done((bf16[2,1,2,256,512]{4,3,2,1,0:T(8,128)(2,1)S(1)}, bf16[2,1,2,256,512]{4,3,2,1,0:T(8,128)(2,1)}, u32[]{:S(2)}, u32[]{:S(2)}) %collective-permute-start.5) | collective-permute-done | bytes 1048608 | tf_op jit(solution)/shard_map/ppermute | solution.py:16
  28.2 0.0 collective-permute-start.6
  28.2 3.8 %collective-permute-done.3 = bf16[2,1,2,256,512]{4,3,2,1,0:T(8,128)(2,1)} collective-permute-done((bf16[2,1,2,256,512]{4,3,2,1,0:T(8,128)(2,1)S(1)}, bf16[2,1,2,256,512]{4,3,2,1,0:T(8,128)(2,1)}, u32[]{:S(2)}, u32[]{:S(2)}) %collective-permute-start.3) | collective-permute-done | bytes 1048608 | tf_op jit(solution)/shard_map/ppermute | solution.py:26
  32.1 0.0 collective-permute-start.4
  32.1 0.0 collective-permute-done.refs_3_
  32.1 0.0 collective-permute-start.2
  32.1 2.7 %collective-permute-start.1 = (bf16[2,1,2,256,512]{4,3,2,1,0:T(8,128)(2,1)}, bf16[2,1,2,256,512]{4,3,2,1,0:T(8,128)(2,1)}, u32[]{:S(2)}, u32[]{:S(2)}) collective-permute-start(bf16[2,1,2,256,512]{4,3,2,1,0:T(8,128)(2,1)} %collective-permute-done.refs_3_), channel_id=1, source_target_pairs={{0,7},{1,2},{2,1},{3,4},{4,3},{5,6},{6,5},{7,0},{8,15},{9,10},{10,... | collective-permute-start | bytes 3145736 | tf_op jit(solution)/shard_map/ppermute | solution.py:26
  34.8 0.0 copy-done.3
  34.8 0.0 copy-done.4
  34.8 0.8 %select_reduce_fusion = f32[8,256]{1,0:T(8,128)S(1)} fusion(f32[8,256]{1,0:T(8,128)S(1)} %copy-done.3, s32[8,256]{1,0:T(8,128)S(1)} %copy-done.4), kind=kLoop, calls=%fused_computation | loop fusion | flops 1570816 | bytes 24576 | tf_op jit(solution)/shard_map/reduce_sum | solution.py:34
  35.6 0.4 copy.24.refs_1_
  35.9 0.1 pad_add_fusion.ids
  36.0 0.0 collective-permute-done.6.refs_4_
  36.0 0.0 copy-done
  36.0 0.0 copy-done.1
  36.0 0.0 copy-done.2
  36.0 4.5 %shard_map.56.refs_4_ = f32[2,2,256,512]{3,2,1,0:T(8,128)S(1)} custom-call(s32[2]{0:T(128)S(1)} %pad_add_fusion.ids, s32[2,8]{1,0:T(2,128)S(1)} %copy-done.2, f32[8,8]{1,0:T(8,128)S(1)} %copy-done.1, f32[8,1,256]{2,1,0:T(1,128)S(1)} %broadcast_in_dim.23.refs_0_, f32[8,256,1]{2,1,0:T(8,128)S(1)} %copy.24.refs_1_, ...), custom_call_target="tpu_custom_call" | custom-call | flops 2147483648 | bytes 5242880 | tf_op jit(solution)/shard_map/pallas_call | solution.py:116
  40.5 14.2 %collective-permute-done.4.refs_3_ = bf16[2,1,2,256,512]{4,3,2,1,0:T(8,128)(2,1)} collective-permute-done((bf16[2,1,2,256,512]{4,3,2,1,0:T(8,128)(2,1)}, bf16[2,1,2,256,512]{4,3,2,1,0:T(8,128)(2,1)}, u32[]{:S(2)}, u32[]{:S(2)}) %collective-permute-start.4) | collective-permute-done | bytes 1048608 | tf_op jit(solution)/shard_map/ppermute | solution.py:16
  54.7 5.0 %shard_map.57.refs_5_ = bf16[2,2,1,2,256,512]{5,4,3,2,1,0:T(8,128)(2,1)} custom-call(s32[2]{0:T(128)S(1)} %pad_add_fusion.ids, s32[2,8]{1,0:T(2,128)S(1)} %copy-done.2, f32[8,8]{1,0:T(8,128)S(1)} %copy-done.1, f32[8,1,256]{2,1,0:T(1,128)S(1)} %broadcast_in_dim.23.refs_0_, f32[8,256,1]{2,1,0:T(8,128)S(1)} %copy.24.refs_1_, ...), custom_call_target="tpu_custom_call" | custom-call | flops 1073741824 | bytes 5242880 | tf_op jit(solution)/shard_map/pallas_call | solution.py:116
  59.7 0.0 collective-permute-done.2.refs_4_
  59.7 4.5 %shard_map.55.refs_4_ = f32[2,2,256,512]{3,2,1,0:T(8,128)S(1)} custom-call(s32[2]{0:T(128)S(1)} %pad_add_fusion.ids, s32[2,8]{1,0:T(2,128)S(1)} %copy-done.2, f32[8,8]{1,0:T(8,128)S(1)} %copy-done.1, f32[8,1,256]{2,1,0:T(1,128)S(1)} %broadcast_in_dim.23.refs_0_, f32[8,256,1]{2,1,0:T(8,128)S(1)} %copy.24.refs_1_, ...), custom_call_target="tpu_custom_call" | custom-call | flops 2147483648 | bytes 5242880 | tf_op jit(solution)/shard_map/pallas_call | solution.py:116
  64.2 0.0 collective-permute-done.1.refs_3_
  64.2 5.0 %shard_map.58 = bf16[2,2,1,2,256,512]{5,4,3,2,1,0:T(8,128)(2,1)} custom-call(s32[2]{0:T(128)S(1)} %pad_add_fusion.ids, s32[2,8]{1,0:T(2,128)S(1)} %copy-done.2, f32[8,8]{1,0:T(8,128)S(1)} %copy-done.1, f32[8,1,256]{2,1,0:T(1,128)S(1)} %broadcast_in_dim.23.refs_0_, f32[8,256,1]{2,1,0:T(8,128)S(1)} %copy.24.refs_1_, ...), custom_call_target="tpu_custom_call", output_to_operand_aliasing={{}: (8, {})} | custom-call | flops 1073741824 | bytes 5242880 | tf_op jit(solution)/shard_map/pallas_call | solution.py:116
  (1 shorter events, 0.0 us)
Async XLA Ops:
  0.0 34.8 %copy-start.3 = (f32[8,256]{1,0:T(8,128)S(1)}, f32[8,256]{1,0:T(8,128)}, u32[]{:S(2)}) copy-start(f32[8,256]{1,0:T(8,128)} %param.8) | copy-start | bytes 24580
  0.0 34.8 %copy-start.4 = (s32[8,256]{1,0:T(8,128)S(1)}, s32[8,256]{1,0:T(8,128)}, u32[]{:S(2)}) copy-start(s32[8,256]{1,0:T(8,128)} %param.9) | copy-start | bytes 24580
  0.0 36.0 %copy-start = (bf16[2,2,1,2,256,512]{5,4,3,2,1,0:T(8,128)(2,1)S(1)}, bf16[2,2,1,2,256,512]{5,4,3,2,1,0:T(8,128)(2,1)}, u32[]{:S(2)}) copy-start(bf16[2,2,1,2,256,512]{5,4,3,2,1,0:T(8,128)(2,1)} %refs_2_.7) | copy-start | bytes 6291460
  0.0 36.0 %copy-start.1 = (f32[8,8]{1,0:T(8,128)S(1)}, f32[8,8]{1,0:T(8,128)}, u32[]{:S(2)}) copy-start(f32[8,8]{1,0:T(8,128)} %occ.7) | copy-start | bytes 772
  0.0 36.0 %copy-start.2 = (s32[2,8]{1,0:T(2,128)S(1)}, s32[2,8]{1,0:T(2,128)}, u32[]{:S(2)}) copy-start(s32[2,8]{1,0:T(2,128)} %partner.7) | copy-start | bytes 196
  1.9 26.3 %collective-permute-start.5 = (bf16[2,1,2,256,512]{4,3,2,1,0:T(8,128)(2,1)S(1)}, bf16[2,1,2,256,512]{4,3,2,1,0:T(8,128)(2,1)}, u32[]{:S(2)}, u32[]{:S(2)}) collective-permute-start(bf16[2,1,2,256,512]{4,3,2,1,0:T(8,128)(2,1)S(1)} %get-tuple-element.5), channel_id=1, source_target_pairs={{0,8},{8,0},{16,24},{24,16},{1,9},{9,1},{17,25},{25,17},{2,10},{10... | collective-permute-start | bytes 3145736 | tf_op jit(solution)/shard_map/ppermute | solution.py:16
  5.0 27.1 %collective-permute-start.3 = (bf16[2,1,2,256,512]{4,3,2,1,0:T(8,128)(2,1)S(1)}, bf16[2,1,2,256,512]{4,3,2,1,0:T(8,128)(2,1)}, u32[]{:S(2)}, u32[]{:S(2)}) collective-permute-start(bf16[2,1,2,256,512]{4,3,2,1,0:T(8,128)(2,1)S(1)} %get-tuple-element.5), channel_id=1, source_target_pairs={{0,7},{1,2},{2,1},{3,4},{4,3},{5,6},{6,5},{7,0},{8,15},{9,10},{10,... | collective-permute-start | bytes 3145736 | tf_op jit(solution)/shard_map/ppermute | solution.py:26
  7.7 24.3 %collective-permute-start = (bf16[2,1,2,256,512]{4,3,2,1,0:T(8,128)(2,1)S(1)}, bf16[2,1,2,256,512]{4,3,2,1,0:T(8,128)(2,1)}, u32[]{:S(2)}, u32[]{:S(2)}) collective-permute-start(bf16[2,1,2,256,512]{4,3,2,1,0:T(8,128)(2,1)S(1)} %get-tuple-element.6), channel_id=1, source_target_pairs={{0,16},{8,24},{16,0},{24,8},{1,17},{9,25},{17,1},{25,9},{2,18},{10... | collective-permute-start | bytes 3145736 | tf_op jit(solution)/shard_map/ppermute | solution.py:16
  28.2 7.8 %collective-permute-start.6 = (bf16[2,1,2,256,512]{4,3,2,1,0:T(8,128)(2,1)}, bf16[2,1,2,256,512]{4,3,2,1,0:T(8,128)(2,1)}, u32[]{:S(2)}, u32[]{:S(2)}) collective-permute-start(bf16[2,1,2,256,512]{4,3,2,1,0:T(8,128)(2,1)} %collective-permute-done.5.refs_3_), channel_id=1, source_target_pairs={{0,1},{1,0},{2,3},{3,2},{4,5},{5,4},{6,7},{7,6},{8,9},{9,8},{10,11... | collective-permute-start | bytes 3145736 | tf_op jit(solution)/shard_map/ppermute | solution.py:21
  32.1 22.7 %collective-permute-start.4 = (bf16[2,1,2,256,512]{4,3,2,1,0:T(8,128)(2,1)}, bf16[2,1,2,256,512]{4,3,2,1,0:T(8,128)(2,1)}, u32[]{:S(2)}, u32[]{:S(2)}) collective-permute-start(bf16[2,1,2,256,512]{4,3,2,1,0:T(8,128)(2,1)} %collective-permute-done.3), channel_id=1, source_target_pairs={{0,8},{8,0},{16,24},{24,16},{1,9},{9,1},{17,25},{25,17},{2,10},{10... | collective-permute-start | bytes 3145736 | tf_op jit(solution)/shard_map/ppermute | solution.py:16
  32.1 27.7 %collective-permute-start.2 = (bf16[2,1,2,256,512]{4,3,2,1,0:T(8,128)(2,1)}, bf16[2,1,2,256,512]{4,3,2,1,0:T(8,128)(2,1)}, u32[]{:S(2)}, u32[]{:S(2)}) collective-permute-start(bf16[2,1,2,256,512]{4,3,2,1,0:T(8,128)(2,1)} %collective-permute-done.refs_3_), channel_id=1, source_target_pairs={{0,1},{1,0},{2,3},{3,2},{4,5},{5,4},{6,7},{7,6},{8,9},{9,8},{10,11... | collective-permute-start | bytes 3145736 | tf_op jit(solution)/shard_map/ppermute | solution.py:21
  32.1 32.2 %collective-permute-start.1 = (bf16[2,1,2,256,512]{4,3,2,1,0:T(8,128)(2,1)}, bf16[2,1,2,256,512]{4,3,2,1,0:T(8,128)(2,1)}, u32[]{:S(2)}, u32[]{:S(2)}) collective-permute-start(bf16[2,1,2,256,512]{4,3,2,1,0:T(8,128)(2,1)} %collective-permute-done.refs_3_), channel_id=1, source_target_pairs={{0,7},{1,2},{2,1},{3,4},{4,3},{5,6},{6,5},{7,0},{8,15},{9,10},{10,... | collective-permute-start | bytes 3145736 | tf_op jit(solution)/shard_map/ppermute | solution.py:26

commit v2 on v1

v2 whole, which is shorter than its diff:
```python
import functools

import jax
import jax.numpy as jnp
from jax import lax
from jax.experimental import pallas as pl
from jax.experimental.pallas import tpu as pltpu
from jax.sharding import PartitionSpec as P

F32 = jnp.float32
BF16 = jnp.bfloat16


def group_swap(block, bit):
    count = lax.axis_size("kpt")
    return lax.ppermute(block, "kpt", [(g, g ^ (1 << bit)) for g in range(count)])


def near_swap(block):
    count = lax.axis_size("occ")
    return lax.ppermute(block, "occ", [(i, i ^ 1) for i in range(count)])


def far_swap(block):
    count = lax.axis_size("occ")
    return lax.ppermute(
        block, "occ", [(i, (i + (1 if i % 2 else count - 1)) % count) for i in range(count)]
    )


def virtual_energies(vir_sorted, vir_order):
    ranks = jnp.arange(vir_sorted.shape[1], dtype=jnp.int32)
    matches = vir_order[:, :, None] == ranks[None, None, :]
    return jnp.sum(jnp.where(matches, vir_sorted[:, None, :], 0.0), axis=2)


def nt_dot(left, right):
    return lax.dot_general(left, right, (((1,), (1,)), ((), ())), preferred_element_type=F32)


def column_of(row):
    return jnp.transpose(jnp.broadcast_to(row, (8, row.shape[1])))[:, :1]


def kernel(transfer, bit, places, final, has_base, ids, partner, occ, virtual, factor, *refs):
    windows, rest = refs[: len(places)], refs[len(places) :]
    base = rest[0] if has_base else None
    _, kc, _, _, nv, naux = factor.shape
    total = occ.shape[1]
    group, orbit = ids[0], ids[1]
    far_group = jnp.bitwise_xor(group, 1 << bit)
    parity = lax.rem(orbit, 2)
    columns = {
        "own": orbit,
        "near": orbit + 1 - 2 * parity,
        "far": lax.rem(orbit + total - 1 + 2 * parity, total),
    }
    copies = []
    for k in range(kc):
        point = group * kc + k
        far_point = partner[transfer, point]
        slot = far_point - far_group * kc
        row = virtual[pl.ds(point, 1), :]
        column = column_of(virtual[pl.ds(far_point, 1), :])
        real, imag = factor[transfer, k, 0, 0], factor[transfer, k, 0, 1]
        left = jnp.concatenate([real, imag], axis=0)
        right = jnp.concatenate([imag, -real], axis=0)
        gradient = base[k].reshape(2 * nv, naux) if has_base else None
        for place, window_ref in zip(places, windows):
            window = window_ref[slot, 0]
            pair = nt_dot(left, window[0]) + nt_dot(right, window[1])
            level = occ[point, orbit] + occ[far_point, columns[place]]
            denominator = (level - column) - row
            real_part = (pair[:nv] / denominator).astype(BF16)
            imag_part = (pair[nv:] / denominator).astype(BF16)
            combined = jnp.concatenate(
                [
                    jnp.concatenate([real_part, -imag_part], axis=1),
                    jnp.concatenate([imag_part, real_part], axis=1),
                ],
                axis=0,
            )
            term = jnp.dot(combined, window.reshape(2 * nv, naux), preferred_element_type=F32)
            gradient = term if gradient is None else gradient + term
        gradient = gradient.reshape(2, nv, naux)
        if final:
            out, staged, sems = rest[-3:]
            staged[k] = gradient.astype(BF16)
            copy = pltpu.make_async_copy(staged.at[k], out.at[transfer, k, 0], sems.at[k])
            copy.start()
            copies.append(copy)
        else:
            rest[-1][k] = gradient
    for copy in copies:
        copy.wait()


def contract(transfer, bit, scalars, virtual, factor, windows, base=None, result=None, final=False):
    _, kc, _, _, nv, naux = factor.shape
    places = [place for place, _ in windows]
    vmem, smem = pl.BlockSpec(memory_space=pltpu.VMEM), pl.BlockSpec(memory_space=pltpu.SMEM)
    operands = [*scalars, virtual, factor] + [window for _, window in windows]
    in_specs = [smem] * len(scalars) + [vmem] * (2 + len(windows))
    aliases, scratch = {}, []
    if base is not None:
        in_specs.append(vmem)
        operands.append(base)
    if final:
        out_shape = jax.ShapeDtypeStruct(factor.shape, BF16)
        out_spec = pl.BlockSpec(memory_space=pl.ANY)
        scratch = [pltpu.VMEM((kc, 2, nv, naux), BF16), pltpu.SemaphoreType.DMA((kc,))]
        if result is not None:
            aliases = {len(operands): 0}
            in_specs.append(pl.BlockSpec(memory_space=pl.ANY))
            operands.append(result)
    else:
        out_shape = jax.ShapeDtypeStruct((kc, 2, nv, naux), F32)
        out_spec = vmem
        if base is not None:
            aliases = {len(operands) - 1: 0}
    flops = kc * len(windows) * 16 * nv * nv * naux
    moved = kc * nv * naux * (4 * (1 + len(windows)) + 8)
    return pl.pallas_call(
        functools.partial(kernel, transfer, bit, places, final, base is not None),
        out_shape=out_shape,
        in_specs=in_specs,
        out_specs=out_spec,
        scratch_shapes=scratch,
        input_output_aliases=aliases,
        cost_estimate=pl.CostEstimate(flops=flops, bytes_accessed=moved, transcendentals=0),
        compiler_params=pltpu.CompilerParams(vmem_limit_bytes=24 * 1024 * 1024),
    )(*operands)


def body(factor, partner, occ_energy, vir_sorted, vir_order):
    top_bit = lax.axis_size("kpt").bit_length() - 2
    ids = jnp.stack([lax.axis_index("kpt"), lax.axis_index("occ")]).astype(jnp.int32)
    scalars = (ids, partner, occ_energy)

    one, two = factor[0], factor[1]
    one_far_own = far_swap(one)
    one_swapped = group_swap(one, 0)
    two_swapped = group_swap(two, top_bit)
    one_far = group_swap(one_far_own, 0)
    two_far = far_swap(two_swapped)
    one_near = near_swap(one_swapped)
    two_near = near_swap(two_swapped)

    virtual = virtual_energies(vir_sorted, vir_order)
    call = functools.partial(contract, scalars=scalars, virtual=virtual, factor=factor)
    base_one = call(0, 0, windows=[("own", one_swapped), ("near", one_near)])
    base_two = call(1, top_bit, windows=[("own", two_swapped), ("near", two_near)])
    result = call(0, 0, windows=[("far", one_far)], base=base_one, final=True)
    return call(1, top_bit, windows=[("far", two_far)], base=base_two, result=result, final=True)


def solution(mesh):
    spec = P(None, "kpt", "occ", None, None, None)
    in_specs = (spec, P(), P(), P(), P())
    return jax.shard_map(body, mesh=mesh, in_specs=in_specs, out_specs=spec, check_vma=False)
```

time: 69.5 us -> 67 us (0.964)
  Pallas kernels: 19 us -> 16.1 us
  waiting for transfers between devices: 37 us -> 37.8 us
    pallas_call x4, Pallas kernels: 19 us -> 16.1 us  [contract(): pl.pallas_call(functools.partial(kernel, transfer, bit, places, final, ba...]
    ppermute x3, waiting for transfers between devices: 33.2 us -> 34 us  [group_swap(): return lax.ppermute(block, 'kpt', [(g, g ^ 1 << bit) for g in range(count)])]
  transfers between devices with their start and end apart: 7 -> 7, of which waited for: 3 -> 3; matrix products, arithmetic and copies ran while one was open for 2% -> 1% of each run, Pallas kernels for 20% -> 18%
where the time goes in v2:
time: 67 us; the launch traced here: 66.8 us
  waiting for transfers between devices  37.8 us (56%)
  Pallas kernels  16.1 us (24%)
  starting transfers between devices  10 us (15%)
  local copies, waits for them, and re-layouts  1.92 us (3%)
  other arithmetic  0.83 us (1%)
    ppermute x3, waiting for transfers between devices, group_swap(): return lax.ppermute(block, 'kpt', [(g, g ^ 1 << bit) for g in range(count)])  34 us
    pallas_call x4, Pallas kernels, contract(): pl.pallas_call(functools.partial(kernel, transfer, bit, places, final, ba...  16.1 us
    ppermute x2, starting transfers between devices, far_swap(): lax.ppermute(block, 'occ', [(i, (i + (1 if i % 2 else count - 1)) % count...  5.47 us
    ppermute x3, starting transfers between devices, group_swap(): return lax.ppermute(block, 'kpt', [(g, g ^ 1 << bit) for g in range(count)])  4.54 us
    ppermute x2, waiting for transfers between devices, far_swap(): lax.ppermute(block, 'occ', [(i, (i + (1 if i % 2 else count - 1)) % count...  3.83 us
    squeeze x1, local copies, waits for them, and re-layouts, body(): one, two = (factor[0], factor[1])  1.9 us
  transfers between devices with their start and end apart: 7, of which 3 were waited for; matrix products, arithmetic and copies ran while one was open for 1% of the time, Pallas kernels for 18%

profile of v2, /device:TPU:0, one launch (start us, length us, event | category | flops | bytes accessed | tf_op | source)
XLA Modules:
  0.0 66.8 jit_solution(8762387208096479297)
XLA Ops:
  0.0 0.0 copy-start.3
  0.0 0.0 copy-start.4
  0.0 0.0 copy-start
  0.0 0.0 copy-start.1
  0.0 0.0 copy-start.2
  0.0 1.9 %slice_bitcast_fusion = (bf16[2,1,2,256,512]{4,3,2,1,0:T(8,128)(2,1)S(1)}, bf16[2,1,2,256,512]{4,3,2,1,0:T(8,128)(2,1)S(1)}) fusion(bf16[2,2,1,2,256,512]{5,4,3,1,2,0:T(8,128)(2,1)} %bitcast.7), kind=kLoop, calls=%fused_computation.2 | loop fusion | bytes 4194304 | tf_op jit(solution)/shard_map/squeeze | solution.py:140
  1.9 3.0 %collective-permute-start.5 = (bf16[2,1,2,256,512]{4,3,2,1,0:T(8,128)(2,1)S(1)}, bf16[2,1,2,256,512]{4,3,2,1,0:T(8,128)(2,1)}, u32[]{:S(2)}, u32[]{:S(2)}) collective-permute-start(bf16[2,1,2,256,512]{4,3,2,1,0:T(8,128)(2,1)S(1)} %get-tuple-element.5), channel_id=1, source_target_pairs={{0,8},{8,0},{16,24},{24,16},{1,9},{9,1},{17,25},{25,17},{2,10},{10... | collective-permute-start | bytes 3145736 | tf_op jit(solution)/shard_map/ppermute | solution.py:16
  4.9 2.8 %collective-permute-start.3 = (bf16[2,1,2,256,512]{4,3,2,1,0:T(8,128)(2,1)S(1)}, bf16[2,1,2,256,512]{4,3,2,1,0:T(8,128)(2,1)}, u32[]{:S(2)}, u32[]{:S(2)}) collective-permute-start(bf16[2,1,2,256,512]{4,3,2,1,0:T(8,128)(2,1)S(1)} %get-tuple-element.5), channel_id=1, source_target_pairs={{0,7},{1,2},{2,1},{3,4},{4,3},{5,6},{6,5},{7,0},{8,15},{9,10},{10,... | collective-permute-start | bytes 3145736 | tf_op jit(solution)/shard_map/ppermute | solution.py:26
  7.7 1.5 %collective-permute-start = (bf16[2,1,2,256,512]{4,3,2,1,0:T(8,128)(2,1)S(1)}, bf16[2,1,2,256,512]{4,3,2,1,0:T(8,128)(2,1)}, u32[]{:S(2)}, u32[]{:S(2)}) collective-permute-start(bf16[2,1,2,256,512]{4,3,2,1,0:T(8,128)(2,1)S(1)} %get-tuple-element.6), channel_id=1, source_target_pairs={{0,16},{8,24},{16,0},{24,8},{1,17},{9,25},{17,1},{25,9},{2,18},{10... | collective-permute-start | bytes 3145736 | tf_op jit(solution)/shard_map/ppermute | solution.py:16
  9.2 19.0 %collective-permute-done.5.refs_0_ = bf16[2,1,2,256,512]{4,3,2,1,0:T(8,128)(2,1)} collective-permute-done((bf16[2,1,2,256,512]{4,3,2,1,0:T(8,128)(2,1)S(1)}, bf16[2,1,2,256,512]{4,3,2,1,0:T(8,128)(2,1)}, u32[]{:S(2)}, u32[]{:S(2)}) %collective-permute-start.5) | collective-permute-done | bytes 1048608 | tf_op jit(solution)/shard_map/ppermute | solution.py:16
  28.2 0.0 collective-permute-start.6
  28.2 3.8 %collective-permute-done.3 = bf16[2,1,2,256,512]{4,3,2,1,0:T(8,128)(2,1)} collective-permute-done((bf16[2,1,2,256,512]{4,3,2,1,0:T(8,128)(2,1)S(1)}, bf16[2,1,2,256,512]{4,3,2,1,0:T(8,128)(2,1)}, u32[]{:S(2)}, u32[]{:S(2)}) %collective-permute-start.3) | collective-permute-done | bytes 1048608 | tf_op jit(solution)/shard_map/ppermute | solution.py:26
  32.0 0.0 collective-permute-start.4
  32.0 0.0 collective-permute-done.refs_0_
  32.0 0.0 collective-permute-start.2
  32.1 2.7 %collective-permute-start.1 = (bf16[2,1,2,256,512]{4,3,2,1,0:T(8,128)(2,1)}, bf16[2,1,2,256,512]{4,3,2,1,0:T(8,128)(2,1)}, u32[]{:S(2)}, u32[]{:S(2)}) collective-permute-start(bf16[2,1,2,256,512]{4,3,2,1,0:T(8,128)(2,1)} %collective-permute-done.refs_0_), channel_id=1, source_target_pairs={{0,7},{1,2},{2,1},{3,4},{4,3},{5,6},{6,5},{7,0},{8,15},{9,10},{10,... | collective-permute-start | bytes 3145736 | tf_op jit(solution)/shard_map/ppermute | solution.py:26
  34.8 0.1 pad_add_fusion.ids
  34.8 0.0 copy-done.3
  34.8 0.0 copy-done.4
  34.8 0.8 %select_reduce_fusion.virtual = f32[8,256]{1,0:T(8,128)S(1)} fusion(f32[8,256]{1,0:T(8,128)S(1)} %copy-done.3, s32[8,256]{1,0:T(8,128)S(1)} %copy-done.4), kind=kLoop, calls=%fused_computation | loop fusion | flops 1570816 | bytes 24576 | tf_op jit(solution)/shard_map/reduce_sum | solution.py:34
  35.6 0.0 collective-permute-done.6.refs_1_
  35.6 0.0 copy-done
  35.6 0.0 copy-done.1
  35.6 0.0 copy-done.2
  35.6 4.0 %shard_map.56.refs_1_ = f32[2,2,256,512]{3,2,1,0:T(8,128)S(1)} custom-call(s32[2]{0:T(128)S(1)} %pad_add_fusion.ids, s32[2,8]{1,0:T(2,128)S(1)} %copy-done.2, f32[8,8]{1,0:T(8,128)S(1)} %copy-done.1, f32[8,256]{1,0:T(8,128)S(1)} %select_reduce_fusion.virtual, bf16[2,2,1,2,256,512]{5,4,3,2,1,0:T(8,128)(2,1)S(1)} %copy-done, ...), custom_call_target="tpu_custom_call" | custom-call | flops 2147483648 | bytes 5242880 | tf_op jit(solution)/shard_map/pallas_call | solution.py:123
  39.6 15.0 %collective-permute-done.4.refs_0_ = bf16[2,1,2,256,512]{4,3,2,1,0:T(8,128)(2,1)S(1)} collective-permute-done((bf16[2,1,2,256,512]{4,3,2,1,0:T(8,128)(2,1)}, bf16[2,1,2,256,512]{4,3,2,1,0:T(8,128)(2,1)S(1)}, u32[]{:S(2)}, u32[]{:S(2)}) %collective-permute-start.4) | collective-permute-done | bytes 1048608 | tf_op jit(solution)/shard_map/ppermute | solution.py:16
  54.6 3.8 %shard_map.57.refs_2_ = bf16[2,2,1,2,256,512]{5,4,3,2,1,0:T(8,128)(2,1)} custom-call(s32[2]{0:T(128)S(1)} %pad_add_fusion.ids, s32[2,8]{1,0:T(2,128)S(1)} %copy-done.2, f32[8,8]{1,0:T(8,128)S(1)} %copy-done.1, f32[8,256]{1,0:T(8,128)S(1)} %select_reduce_fusion.virtual, bf16[2,2,1,2,256,512]{5,4,3,2,1,0:T(8,128)(2,1)S(1)} %copy-done, ...), custom_call_target="tpu_custom_call" | custom-call | flops 1073741824 | bytes 4194304 | tf_op jit(solution)/shard_map/pallas_call | solution.py:123
  58.4 0.0 collective-permute-done.2.refs_1_
  58.4 4.0 %shard_map.55.refs_1_ = f32[2,2,256,512]{3,2,1,0:T(8,128)S(1)} custom-call(s32[2]{0:T(128)S(1)} %pad_add_fusion.ids, s32[2,8]{1,0:T(2,128)S(1)} %copy-done.2, f32[8,8]{1,0:T(8,128)S(1)} %copy-done.1, f32[8,256]{1,0:T(8,128)S(1)} %select_reduce_fusion.virtual, bf16[2,2,1,2,256,512]{5,4,3,2,1,0:T(8,128)(2,1)S(1)} %copy-done, ...), custom_call_target="tpu_custom_call" | custom-call | flops 2147483648 | bytes 5242880 | tf_op jit(solution)/shard_map/pallas_call | solution.py:123
  62.4 0.0 collective-permute-done.1.refs_0_
  62.4 4.4 %shard_map.58 = bf16[2,2,1,2,256,512]{5,4,3,2,1,0:T(8,128)(2,1)} custom-call(s32[2]{0:T(128)S(1)} %pad_add_fusion.ids, s32[2,8]{1,0:T(2,128)S(1)} %copy-done.2, f32[8,8]{1,0:T(8,128)S(1)} %copy-done.1, f32[8,256]{1,0:T(8,128)S(1)} %select_reduce_fusion.virtual, bf16[2,2,1,2,256,512]{5,4,3,2,1,0:T(8,128)(2,1)S(1)} %copy-done, ...), custom_call_target="tpu_custom_call", output_to_operand_aliasing={{}: (7, {})} | custom-call | flops 1073741824 | bytes 4194304 | tf_op jit(solution)/shard_map/pallas_call | solution.py:123
Async XLA Ops:
  0.0 34.8 %copy-start.3 = (f32[8,256]{1,0:T(8,128)S(1)}, f32[8,256]{1,0:T(8,128)}, u32[]{:S(2)}) copy-start(f32[8,256]{1,0:T(8,128)} %param.8) | copy-start | bytes 24580
  0.0 34.8 %copy-start.4 = (s32[8,256]{1,0:T(8,128)S(1)}, s32[8,256]{1,0:T(8,128)}, u32[]{:S(2)}) copy-start(s32[8,256]{1,0:T(8,128)} %param.9) | copy-start | bytes 24580
  0.0 35.6 %copy-start = (bf16[2,2,1,2,256,512]{5,4,3,2,1,0:T(8,128)(2,1)S(1)}, bf16[2,2,1,2,256,512]{5,4,3,2,1,0:T(8,128)(2,1)}, u32[]{:S(2)}) copy-start(bf16[2,2,1,2,256,512]{5,4,3,2,1,0:T(8,128)(2,1)} %factor.7) | copy-start | bytes 6291460
  0.0 35.6 %copy-start.1 = (f32[8,8]{1,0:T(8,128)S(1)}, f32[8,8]{1,0:T(8,128)}, u32[]{:S(2)}) copy-start(f32[8,8]{1,0:T(8,128)} %occ.7) | copy-start | bytes 772
  0.0 35.6 %copy-start.2 = (s32[2,8]{1,0:T(2,128)S(1)}, s32[2,8]{1,0:T(2,128)}, u32[]{:S(2)}) copy-start(s32[2,8]{1,0:T(2,128)} %partner.7) | copy-start | bytes 196
  1.9 26.3 %collective-permute-start.5 = (bf16[2,1,2,256,512]{4,3,2,1,0:T(8,128)(2,1)S(1)}, bf16[2,1,2,256,512]{4,3,2,1,0:T(8,128)(2,1)}, u32[]{:S(2)}, u32[]{:S(2)}) collective-permute-start(bf16[2,1,2,256,512]{4,3,2,1,0:T(8,128)(2,1)S(1)} %get-tuple-element.5), channel_id=1, source_target_pairs={{0,8},{8,0},{16,24},{24,16},{1,9},{9,1},{17,25},{25,17},{2,10},{10... | collective-permute-start | bytes 3145736 | tf_op jit(solution)/shard_map/ppermute | solution.py:16
  4.9 27.1 %collective-permute-start.3 = (bf16[2,1,2,256,512]{4,3,2,1,0:T(8,128)(2,1)S(1)}, bf16[2,1,2,256,512]{4,3,2,1,0:T(8,128)(2,1)}, u32[]{:S(2)}, u32[]{:S(2)}) collective-permute-start(bf16[2,1,2,256,512]{4,3,2,1,0:T(8,128)(2,1)S(1)} %get-tuple-element.5), channel_id=1, source_target_pairs={{0,7},{1,2},{2,1},{3,4},{4,3},{5,6},{6,5},{7,0},{8,15},{9,10},{10,... | collective-permute-start | bytes 3145736 | tf_op jit(solution)/shard_map/ppermute | solution.py:26
  7.7 24.3 %collective-permute-start = (bf16[2,1,2,256,512]{4,3,2,1,0:T(8,128)(2,1)S(1)}, bf16[2,1,2,256,512]{4,3,2,1,0:T(8,128)(2,1)}, u32[]{:S(2)}, u32[]{:S(2)}) collective-permute-start(bf16[2,1,2,256,512]{4,3,2,1,0:T(8,128)(2,1)S(1)} %get-tuple-element.6), channel_id=1, source_target_pairs={{0,16},{8,24},{16,0},{24,8},{1,17},{9,25},{17,1},{25,9},{2,18},{10... | collective-permute-start | bytes 3145736 | tf_op jit(solution)/shard_map/ppermute | solution.py:16
  28.2 7.4 %collective-permute-start.6 = (bf16[2,1,2,256,512]{4,3,2,1,0:T(8,128)(2,1)}, bf16[2,1,2,256,512]{4,3,2,1,0:T(8,128)(2,1)}, u32[]{:S(2)}, u32[]{:S(2)}) collective-permute-start(bf16[2,1,2,256,512]{4,3,2,1,0:T(8,128)(2,1)} %collective-permute-done.5.refs_0_), channel_id=1, source_target_pairs={{0,1},{1,0},{2,3},{3,2},{4,5},{5,4},{6,7},{7,6},{8,9},{9,8},{10,11... | collective-permute-start | bytes 3145736 | tf_op jit(solution)/shard_map/ppermute | solution.py:21
  32.0 22.6 %collective-permute-start.4 = (bf16[2,1,2,256,512]{4,3,2,1,0:T(8,128)(2,1)}, bf16[2,1,2,256,512]{4,3,2,1,0:T(8,128)(2,1)S(1)}, u32[]{:S(2)}, u32[]{:S(2)}) collective-permute-start(bf16[2,1,2,256,512]{4,3,2,1,0:T(8,128)(2,1)} %collective-permute-done.3), channel_id=1, source_target_pairs={{0,8},{8,0},{16,24},{24,16},{1,9},{9,1},{17,25},{25,17},{2,10},{10... | collective-permute-start | bytes 3145736 | tf_op jit(solution)/shard_map/ppermute | solution.py:16
  32.0 26.4 %collective-permute-start.2 = (bf16[2,1,2,256,512]{4,3,2,1,0:T(8,128)(2,1)}, bf16[2,1,2,256,512]{4,3,2,1,0:T(8,128)(2,1)}, u32[]{:S(2)}, u32[]{:S(2)}) collective-permute-start(bf16[2,1,2,256,512]{4,3,2,1,0:T(8,128)(2,1)} %collective-permute-done.refs_0_), channel_id=1, source_target_pairs={{0,1},{1,0},{2,3},{3,2},{4,5},{5,4},{6,7},{7,6},{8,9},{9,8},{10,11... | collective-permute-start | bytes 3145736 | tf_op jit(solution)/shard_map/ppermute | solution.py:21
  32.1 30.3 %collective-permute-start.1 = (bf16[2,1,2,256,512]{4,3,2,1,0:T(8,128)(2,1)}, bf16[2,1,2,256,512]{4,3,2,1,0:T(8,128)(2,1)}, u32[]{:S(2)}, u32[]{:S(2)}) collective-permute-start(bf16[2,1,2,256,512]{4,3,2,1,0:T(8,128)(2,1)} %collective-permute-done.refs_0_), channel_id=1, source_target_pairs={{0,7},{1,2},{2,1},{3,4},{4,3},{5,6},{6,5},{7,0},{8,15},{9,10},{10,... | collective-permute-start | bytes 3145736 | tf_op jit(solution)/shard_map/ppermute | solution.py:26

commit v3 on v2

v3 whole, which is shorter than its diff:
```python
import functools

import jax
import jax.numpy as jnp
from jax import lax
from jax.experimental import pallas as pl
from jax.experimental.pallas import tpu as pltpu
from jax.sharding import PartitionSpec as P

F32 = jnp.float32
BF16 = jnp.bfloat16


def group_swap(block, bit):
    count = lax.axis_size("kpt")
    return lax.ppermute(block, "kpt", [(g, g ^ (1 << bit)) for g in range(count)])


def near_swap(block):
    count = lax.axis_size("occ")
    return lax.ppermute(block, "occ", [(i, i ^ 1) for i in range(count)])


def far_swap(block):
    count = lax.axis_size("occ")
    return lax.ppermute(
        block, "occ", [(i, (i + (1 if i % 2 else count - 1)) % count) for i in range(count)]
    )


def after(block, *others):
    return lax.optimization_barrier((block, *others))[0]


def virtual_energies(vir_sorted, vir_order):
    ranks = jnp.arange(vir_sorted.shape[1], dtype=jnp.int32)
    matches = vir_order[:, :, None] == ranks[None, None, :]
    return jnp.sum(jnp.where(matches, vir_sorted[:, None, :], 0.0), axis=2)


def column_of(row):
    return jnp.transpose(jnp.broadcast_to(row, (8, row.shape[1])))[:, :1]


def kernel(bits, units, final, has_base, ids, partner, occ, virtual, factor, *refs):
    windows, rest = refs[: len(units)], refs[len(units) :]
    base = rest[0] if has_base else None
    _, kc, _, _, nv, naux = factor.shape
    total = occ.shape[1]
    group, orbit = ids[0], ids[1]
    parity = lax.rem(orbit, 2)
    columns = {
        "own": orbit,
        "near": orbit + 1 - 2 * parity,
        "far": lax.rem(orbit + total - 1 + 2 * parity, total),
    }
    transfers = sorted({unit[0] for unit in units})

    def point_step(k, carry):
        point = group * kc + k
        for transfer in transfers:
            far_point = partner[transfer, point]
            slot = far_point - jnp.bitwise_xor(group, 1 << bits[transfer]) * kc
            row = virtual[pl.ds(point, 1), :]
            column = column_of(virtual[pl.ds(far_point, 1), :])
            left = factor[transfer, k, 0].reshape(2 * nv, naux)
            amplitudes, blocks = [], []
            for (at, place, start), window_ref in zip(units, windows):
                if at != transfer:
                    continue
                size = window_ref.shape[2]
                window = window_ref[slot].reshape(2 * size, naux)
                products = lax.dot_general(
                    left, window, (((1,), (1,)), ((), ())), preferred_element_type=F32
                )
                level = occ[point, orbit] + occ[far_point, columns[place]]
                inverse = 1.0 / ((level - column) - row[:, start : start + size])
                real_part = ((products[:nv, :size] + products[nv:, size:]) * inverse).astype(BF16)
                imag_part = ((products[nv:, :size] - products[:nv, size:]) * inverse).astype(BF16)
                amplitudes.append(
                    jnp.concatenate(
                        [
                            jnp.concatenate([real_part, -imag_part], axis=1),
                            jnp.concatenate([imag_part, real_part], axis=1),
                        ],
                        axis=0,
                    )
                )
                blocks.append(window)
            gradient = jnp.dot(
                jnp.concatenate(amplitudes, axis=1),
                jnp.concatenate(blocks, axis=0),
                preferred_element_type=F32,
            )
            gradient = gradient.reshape(2, nv, naux)
            if has_base:
                gradient = gradient + base[transfer, k]
            if final:
                out, staged, sems = rest[-3:]
                staged[k] = gradient.astype(BF16)
                pltpu.make_async_copy(staged.at[k], out.at[transfer, k, 0], sems.at[k]).start()
            else:
                rest[-1][transfer, k] = gradient
        return carry

    lax.fori_loop(0, kc, point_step, 0)
    if final:
        out, staged, sems = rest[-3:]
        for k in range(kc):
            pltpu.make_async_copy(staged.at[k], out.at[transfers[0], k, 0], sems.at[k]).wait()


def contract(bits, scalars, virtual, factor, terms, base=None, result=None, final=False):
    transfer_count, kc, _, _, nv, naux = factor.shape
    units = [term[:3] for term in terms]
    windows = [term[3] for term in terms]
    vmem, smem = pl.BlockSpec(memory_space=pltpu.VMEM), pl.BlockSpec(memory_space=pltpu.SMEM)
    operands = [*scalars, virtual, factor, *windows]
    in_specs = [smem] * len(scalars) + [vmem] * (2 + len(windows))
    aliases, scratch = {}, []
    if base is not None:
        in_specs.append(vmem)
        operands.append(base)
    if final:
        out_shape = jax.ShapeDtypeStruct(factor.shape, BF16)
        out_spec = pl.BlockSpec(memory_space=pl.ANY)
        scratch = [pltpu.VMEM((kc, 2, nv, naux), BF16), pltpu.SemaphoreType.DMA((kc,))]
        if result is not None:
            aliases = {len(operands): 0}
            in_specs.append(pl.BlockSpec(memory_space=pl.ANY))
            operands.append(result)
    else:
        out_shape = jax.ShapeDtypeStruct((transfer_count, kc, 2, nv, naux), F32)
        out_spec = vmem
        if base is not None:
            aliases = {len(operands) - 1: 0}
    size = sum(window.size for window in windows)
    return pl.pallas_call(
        functools.partial(kernel, bits, units, final, base is not None),
        out_shape=out_shape,
        in_specs=in_specs,
        out_specs=out_spec,
        scratch_shapes=scratch,
        input_output_aliases=aliases,
        cost_estimate=pl.CostEstimate(
            flops=8 * size * nv, bytes_accessed=2 * size + 4 * factor.size, transcendentals=0
        ),
        compiler_params=pltpu.CompilerParams(vmem_limit_bytes=24 * 1024 * 1024),
    )(*operands)


def body(factor, partner, occ_energy, vir_sorted, vir_order):
    bits = (0, lax.axis_size("kpt").bit_length() - 2)
    half = factor.shape[4] // 2
    ids = jnp.stack([lax.axis_index("kpt"), lax.axis_index("occ")]).astype(jnp.int32)
    scalars = (ids, partner, occ_energy)

    a = [factor[t, :, 0, :, :half] for t in range(2)]
    b = [factor[t, :, 0, :, half:] for t in range(2)]
    a_beside = [far_swap(a[t]) for t in range(2)]
    b_own = [group_swap(b[t], bits[t]) for t in range(2)]
    b_far = [far_swap(b_own[t]) for t in range(2)]
    a_own = [group_swap(after(a[t], b_own[t]), bits[t]) for t in range(2)]
    b_near = [near_swap(b_own[t]) for t in range(2)]
    a_near = [near_swap(a_own[t]) for t in range(2)]
    a_far = [group_swap(after(a_beside[t], a_own[t]), bits[t]) for t in range(2)]

    virtual = virtual_energies(vir_sorted, vir_order)
    call = functools.partial(contract, bits, scalars, virtual, factor)

    def terms(place, start, windows):
        return [(t, place, start, windows[t]) for t in range(2)]

    total = call(terms("own", half, b_own) + terms("near", half, b_near))
    total = call(terms("own", 0, a_own) + terms("near", 0, a_near), base=total)
    total = call(terms("far", 0, a_far), base=total)
    last = terms("far", half, b_far)
    result = call(last[:1], base=total, final=True)
    return call(last[1:], base=total, result=result, final=True)


def solution(mesh):
    spec = P(None, "kpt", "occ", None, None, None)
    in_specs = (spec, P(), P(), P(), P())
    return jax.shard_map(body, mesh=mesh, in_specs=in_specs, out_specs=spec, check_vma=False)
```

time: 67 us -> 68 us (1.015)
  waiting for transfers between devices: 37.8 us -> 28.1 us
  starting transfers between devices: 10 us -> 16.2 us
  Pallas kernels: 16.1 us -> 18.8 us
  local copies, waits for them, and re-layouts: 1.92 us -> 3.66 us
    ppermute x3 -> x6, waiting for transfers between devices: 34 us -> 16.9 us  [group_swap(): return lax.ppermute(block, 'kpt', [(g, g ^ 1 << bit) for g in range(count)])]
    ppermute x2 -> x4, waiting for transfers between devices: 3.83 us -> 11.2 us  [far_swap(): lax.ppermute(block, 'occ', [(i, (i + (1 if i % 2 else count - 1)) % count...]
    ppermute x3 -> x6, starting transfers between devices: 4.54 us -> 8.34 us  [group_swap(): return lax.ppermute(block, 'kpt', [(g, g ^ 1 << bit) for g in range(count)])]
    pallas_call x4 -> x5, Pallas kernels: 16.1 us -> 18.8 us  [contract(): pl.pallas_call(functools.partial(kernel, bits, units, final, base is not...]
    ppermute x2 -> x4, starting transfers between devices: 5.47 us -> 7.81 us  [far_swap(): lax.ppermute(block, 'occ', [(i, (i + (1 if i % 2 else count - 1)) % count...]
    unnamed x10 -> x14, local copies, waits for them, and re-layouts: 0.02 us -> 1.85 us
  transfers between devices with their start and end apart: 7 -> 14, of which waited for: 3 -> 6; matrix products, arithmetic and copies ran while one was open for 1% -> 1% of each run, Pallas kernels for 18% -> 23%
where the time goes in v3:
time: 68 us; the launch traced here: 67.7 us
  waiting for transfers between devices  28.1 us (41%)
  Pallas kernels  18.8 us (28%)
  starting transfers between devices  16.2 us (24%)
  local copies, waits for them, and re-layouts  3.66 us (5%)
  other arithmetic  0.83 us (1%)
    pallas_call x5, Pallas kernels, contract(): pl.pallas_call(functools.partial(kernel, bits, units, final, base is not...  18.8 us
    ppermute x6, waiting for transfers between devices, group_swap(): return lax.ppermute(block, 'kpt', [(g, g ^ 1 << bit) for g in range(count)])  16.9 us
    ppermute x4, waiting for transfers between devices, far_swap(): lax.ppermute(block, 'occ', [(i, (i + (1 if i % 2 else count - 1)) % count...  11.2 us
    ppermute x6, starting transfers between devices, group_swap(): return lax.ppermute(block, 'kpt', [(g, g ^ 1 << bit) for g in range(count)])  8.34 us
    ppermute x4, starting transfers between devices, far_swap(): lax.ppermute(block, 'occ', [(i, (i + (1 if i % 2 else count - 1)) % count...  7.81 us
    unnamed x14, local copies, waits for them, and re-layouts  1.85 us
    squeeze x1, local copies, waits for them, and re-layouts, body(): a = [factor[t, :, 0, :, :half] for t in range(2)]  1.81 us
  transfers between devices with their start and end apart: 14, of which 6 were waited for; matrix products, arithmetic and copies ran while one was open for 1% of the time, Pallas kernels for 23%

profile of v3, /device:TPU:0, one launch (start us, length us, event | category | flops | bytes accessed | tf_op | source)
XLA Modules:
  0.0 67.7 jit_solution(17003053783896151179)
XLA Ops:
  0.0 0.0 copy-start.5
  0.0 0.0 copy-start
  0.0 0.0 copy-start.3
  0.0 0.0 copy-start.4
  0.0 1.8 %slice_bitcast_fusion = (bf16[2,2,128,512]{3,2,1,0:T(8,128)(2,1)S(1)}, bf16[2,2,128,512]{3,2,1,0:T(8,128)(2,1)S(1)}, bf16[2,2,128,512]{3,2,1,0:T(8,128)(2,1)S(1)}, bf16[2,2,128,512]{3,2,1,0:T(8,128)(2,1)S(1)}) fusion(bf16[2,2,1,2,256,512]{5,4,3,1,2,0:T(8,128)(2,1)} %bitcast.11), kind=kLoop, calls=%fused_computation.2 | loop fusion | bytes 4194304 | tf_op jit(solution)/shard_map/squeeze | solution.py:158
  1.8 3.0 %collective-permute-start.3 = (bf16[2,2,128,512]{3,2,1,0:T(8,128)(2,1)S(1)}, bf16[2,2,128,512]{3,2,1,0:T(8,128)(2,1)S(1)}, u32[]{:S(2)}, u32[]{:S(2)}) collective-permute-start(bf16[2,2,128,512]{3,2,1,0:T(8,128)(2,1)S(1)} %get-tuple-element.14), channel_id=1, source_target_pairs={{0,8},{8,0},{16,24},{24,16},{1,9},{9,1},{17,25},{25,17},{2,10},{10... | collective-permute-start | bytes 1572872 | tf_op jit(solution)/shard_map/ppermute | solution.py:16
  4.8 1.5 %collective-permute-start = (bf16[2,2,128,512]{3,2,1,0:T(8,128)(2,1)S(1)}, bf16[2,2,128,512]{3,2,1,0:T(8,128)(2,1)S(1)}, u32[]{:S(2)}, u32[]{:S(2)}) collective-permute-start(bf16[2,2,128,512]{3,2,1,0:T(8,128)(2,1)S(1)} %get-tuple-element.16), channel_id=1, source_target_pairs={{0,16},{8,24},{16,0},{24,8},{1,17},{9,25},{17,1},{25,9},{2,18},{10... | collective-permute-start | bytes 1572872 | tf_op jit(solution)/shard_map/ppermute | solution.py:16
  6.4 2.5 %collective-permute-start.6 = (bf16[2,2,128,512]{3,2,1,0:T(8,128)(2,1)S(1)}, bf16[2,2,128,512]{3,2,1,0:T(8,128)(2,1)}, u32[]{:S(2)}, u32[]{:S(2)}) collective-permute-start(bf16[2,2,128,512]{3,2,1,0:T(8,128)(2,1)S(1)} %get-tuple-element.11), channel_id=1, source_target_pairs={{0,7},{1,2},{2,1},{3,4},{4,3},{5,6},{6,5},{7,0},{8,15},{9,10},{10,... | collective-permute-start | bytes 1572872 | tf_op jit(solution)/shard_map/ppermute | solution.py:26
  8.8 7.9 %collective-permute-done.3.refs_0_ = bf16[2,2,128,512]{3,2,1,0:T(8,128)(2,1)S(1)} collective-permute-done((bf16[2,2,128,512]{3,2,1,0:T(8,128)(2,1)S(1)}, bf16[2,2,128,512]{3,2,1,0:T(8,128)(2,1)S(1)}, u32[]{:S(2)}, u32[]{:S(2)}) %collective-permute-start.3) | collective-permute-done | bytes 524320 | tf_op jit(solution)/shard_map/ppermute | solution.py:16
  16.8 1.7 %collective-permute-start.4 = (bf16[2,2,128,512]{3,2,1,0:T(8,128)(2,1)S(1)}, bf16[2,2,128,512]{3,2,1,0:T(8,128)(2,1)}, u32[]{:S(2)}, u32[]{:S(2)}) collective-permute-start(bf16[2,2,128,512]{3,2,1,0:T(8,128)(2,1)S(1)} %get-tuple-element.9), channel_id=1, source_target_pairs={{0,8},{8,0},{16,24},{24,16},{1,9},{9,1},{17,25},{25,17},{2,10},{10... | collective-permute-start | bytes 1572872 | tf_op jit(solution)/shard_map/ppermute | solution.py:16
  18.5 0.0 collective-permute-done.refs_1_
  18.5 1.5 %collective-permute-start.7 = (bf16[2,2,128,512]{3,2,1,0:T(8,128)(2,1)S(1)}, bf16[2,2,128,512]{3,2,1,0:T(8,128)(2,1)}, u32[]{:S(2)}, u32[]{:S(2)}) collective-permute-start(bf16[2,2,128,512]{3,2,1,0:T(8,128)(2,1)S(1)} %get-tuple-element.11), channel_id=1, source_target_pairs={{0,16},{8,24},{16,0},{24,8},{1,17},{9,25},{17,1},{25,9},{2,18},{10... | collective-permute-start | bytes 1572872 | tf_op jit(solution)/shard_map/ppermute | solution.py:16
  20.0 1.7 %collective-permute-start.2 = (bf16[2,2,128,512]{3,2,1,0:T(8,128)(2,1)S(1)}, bf16[2,2,128,512]{3,2,1,0:T(8,128)(2,1)}, u32[]{:S(2)}, u32[]{:S(2)}) collective-permute-start(bf16[2,2,128,512]{3,2,1,0:T(8,128)(2,1)S(1)} %get-tuple-element.9), channel_id=1, source_target_pairs={{0,7},{1,2},{2,1},{3,4},{4,3},{5,6},{6,5},{7,0},{8,15},{9,10},{10,... | collective-permute-start | bytes 1572872 | tf_op jit(solution)/shard_map/ppermute | solution.py:26
  21.7 0.0 collective-permute-start.11
  21.8 0.5 collective-permute-done.6
  22.2 0.0 collective-permute-start.12
  22.3 7.8 %collective-permute-done.4.refs_0_ = bf16[2,2,128,512]{3,2,1,0:T(8,128)(2,1)} collective-permute-done((bf16[2,2,128,512]{3,2,1,0:T(8,128)(2,1)S(1)}, bf16[2,2,128,512]{3,2,1,0:T(8,128)(2,1)}, u32[]{:S(2)}, u32[]{:S(2)}) %collective-permute-start.4) | collective-permute-done | bytes 524320 | tf_op jit(solution)/shard_map/ppermute | solution.py:16
  30.1 0.0 collective-permute-start.9
  30.1 1.1 %collective-permute-done.7.refs_1_ = bf16[2,2,128,512]{3,2,1,0:T(8,128)(2,1)} collective-permute-done((bf16[2,2,128,512]{3,2,1,0:T(8,128)(2,1)S(1)}, bf16[2,2,128,512]{3,2,1,0:T(8,128)(2,1)}, u32[]{:S(2)}, u32[]{:S(2)}) %collective-permute-start.7) | collective-permute-done | bytes 524320 | tf_op jit(solution)/shard_map/ppermute | solution.py:16
  31.2 0.0 collective-permute-start.10
  31.2 4.7 %collective-permute-done.2 = bf16[2,2,128,512]{3,2,1,0:T(8,128)(2,1)} collective-permute-done((bf16[2,2,128,512]{3,2,1,0:T(8,128)(2,1)S(1)}, bf16[2,2,128,512]{3,2,1,0:T(8,128)(2,1)}, u32[]{:S(2)}, u32[]{:S(2)}) %collective-permute-start.2) | collective-permute-done | bytes 524320 | tf_op jit(solution)/shard_map/ppermute | solution.py:26
  35.9 0.5 collective-permute-start.8
  36.4 0.0 collective-permute-done.11.refs_2_
  36.4 0.0 copy-start.1
  36.4 0.8 %copy-done.1 = bf16[2,2,128,512]{3,2,1,0:T(8,128)(2,1)} copy-done((bf16[2,2,128,512]{3,2,1,0:T(8,128)(2,1)}, bf16[2,2,128,512]{3,2,1,0:T(8,128)(2,1)S(1)}, u32[]{:S(2)}) %copy-start.1) | copy-done | bytes 524312
  37.2 0.0 collective-permute-start.5
  37.2 0.0 copy-done.5
  37.2 0.0 copy-done.6
  37.2 0.8 %select_reduce_fusion.virtual = f32[8,256]{1,0:T(8,128)S(1)} fusion(f32[8,256]{1,0:T(8,128)S(1)} %copy-done.5, s32[8,256]{1,0:T(8,128)S(1)} %copy-done.6), kind=kLoop, calls=%fused_computation | loop fusion | flops 1570816 | bytes 24576 | tf_op jit(solution)/shard_map/reduce_sum | solution.py:38
  38.0 0.0 collective-permute-done.12.refs_3_
  38.0 1.4 %collective-permute-start.13 = (bf16[2,2,128,512]{3,2,1,0:T(8,128)(2,1)S(1)}, bf16[2,2,128,512]{3,2,1,0:T(8,128)(2,1)S(1)}, u32[]{:S(2)}, u32[]{:S(2)}) collective-permute-start(bf16[2,2,128,512]{3,2,1,0:T(8,128)(2,1)S(1)} %collective-permute-done.3.refs_0_), channel_id=1, source_target_pairs={{0,7},{1,2},{2,1},{3,4},{4,3},{5,6},{6,5},{7,0},{8,15},{9,10},{10,... | collective-permute-start | bytes 1572872 | tf_op jit(solution)/shard_map/ppermute | solution.py:26
  39.4 0.1 pad_add_fusion.ids
  39.4 0.0 collective-permute-done.9.refs_2_
  39.4 2.3 %collective-permute-start.1 = (bf16[2,2,128,512]{3,2,1,0:T(8,128)(2,1)S(1)}, bf16[2,2,128,512]{3,2,1,0:T(8,128)(2,1)S(1)}, u32[]{:S(2)}, u32[]{:S(2)}) collective-permute-start(bf16[2,2,128,512]{3,2,1,0:T(8,128)(2,1)S(1)} %collective-permute-done.refs_1_), channel_id=1, source_target_pairs={{0,7},{1,2},{2,1},{3,4},{4,3},{5,6},{6,5},{7,0},{8,15},{9,10},{10,... | collective-permute-start | bytes 1572872 | tf_op jit(solution)/shard_map/ppermute | solution.py:26
  41.7 0.0 copy-done
  41.7 0.0 copy-done.3
  41.7 0.0 copy-done.4
  41.7 1.0 %copy-done.2 = bf16[2,2,128,512]{3,2,1,0:T(8,128)(2,1)S(1)} copy-done((bf16[2,2,128,512]{3,2,1,0:T(8,128)(2,1)S(1)}, bf16[2,2,128,512]{3,2,1,0:T(8,128)(2,1)}, u32[]{:S(2)}) %copy-start.2) | copy-done | bytes 524312
  42.8 4.0 %shard_map.55.refs_4_ = f32[2,2,2,256,512]{4,3,2,1,0:T(8,128)S(1)} custom-call(s32[2]{0:T(128)S(1)} %pad_add_fusion.ids, s32[2,8]{1,0:T(2,128)S(1)} %copy-done.4, f32[8,8]{1,0:T(8,128)S(1)} %copy-done.3, f32[8,256]{1,0:T(8,128)S(1)} %select_reduce_fusion.virtual, bf16[2,2,1,2,256,512]{5,4,3,2,1,0:T(8,128)(2,1)S(1)} %copy-done, ...), custom_call_target="tpu_custom_call" | custom-call | flops 2147483648 | bytes 6291456 | tf_op jit(solution)/shard_map/pallas_call | solution.py:138
  46.8 0.0 collective-permute-done.10.refs_3_
  46.8 4.6 %shard_map.56.refs_2_ = f32[2,2,2,256,512]{4,3,2,1,0:T(8,128)S(1)} custom-call(s32[2]{0:T(128)S(1)} %pad_add_fusion.ids, s32[2,8]{1,0:T(2,128)S(1)} %copy-done.4, f32[8,8]{1,0:T(8,128)S(1)} %copy-done.3, f32[8,256]{1,0:T(8,128)S(1)} %select_reduce_fusion.virtual, bf16[2,2,1,2,256,512]{5,4,3,2,1,0:T(8,128)(2,1)S(1)} %copy-done, ...), custom_call_target="tpu_custom_call", output_to_operand_aliasing={{}: (9, {})} | custom-call | flops 2147483648 | bytes 6291456 | tf_op jit(solution)/shard_map/pallas_call | solution.py:138
  51.4 0.0 collective-permute-done.8.refs_1_
  51.4 0.0 collective-permute-done.5.refs_0_
  51.4 4.1 %shard_map.57.refs_1_ = f32[2,2,2,256,512]{4,3,2,1,0:T(8,128)S(1)} custom-call(s32[2]{0:T(128)S(1)} %pad_add_fusion.ids, s32[2,8]{1,0:T(2,128)S(1)} %copy-done.4, f32[8,8]{1,0:T(8,128)S(1)} %copy-done.3, f32[8,256]{1,0:T(8,128)S(1)} %select_reduce_fusion.virtual, bf16[2,2,1,2,256,512]{5,4,3,2,1,0:T(8,128)(2,1)S(1)} %copy-done, ...), custom_call_target="tpu_custom_call", output_to_operand_aliasing={{}: (7, {})} | custom-call | flops 1073741824 | bytes 5242880 | tf_op jit(solution)/shard_map/pallas_call | solution.py:138
  55.5 0.0 collective-permute-done.13.refs_0_
  55.5 3.1 %shard_map.58.refs_2_ = bf16[2,2,1,2,256,512]{5,4,3,2,1,0:T(8,128)(2,1)} custom-call(s32[2]{0:T(128)S(1)} %pad_add_fusion.ids, s32[2,8]{1,0:T(2,128)S(1)} %copy-done.4, f32[8,8]{1,0:T(8,128)S(1)} %copy-done.3, f32[8,256]{1,0:T(8,128)S(1)} %select_reduce_fusion.virtual, bf16[2,2,1,2,256,512]{5,4,3,2,1,0:T(8,128)(2,1)S(1)} %copy-done, ...), custom_call_target="tpu_custom_call" | custom-call | flops 536870912 | bytes 4718592 | tf_op jit(solution)/shard_map/pallas_call | solution.py:138
  58.6 6.1 %collective-permute-done.1.refs_0_ = bf16[2,2,128,512]{3,2,1,0:T(8,128)(2,1)S(1)} collective-permute-done((bf16[2,2,128,512]{3,2,1,0:T(8,128)(2,1)S(1)}, bf16[2,2,128,512]{3,2,1,0:T(8,128)(2,1)S(1)}, u32[]{:S(2)}, u32[]{:S(2)}) %collective-permute-start.1) | collective-permute-done | bytes 524320 | tf_op jit(solution)/shard_map/ppermute | solution.py:26
  64.7 3.1 %shard_map.59 = bf16[2,2,1,2,256,512]{5,4,3,2,1,0:T(8,128)(2,1)} custom-call(s32[2]{0:T(128)S(1)} %pad_add_fusion.ids, s32[2,8]{1,0:T(2,128)S(1)} %copy-done.4, f32[8,8]{1,0:T(8,128)S(1)} %copy-done.3, f32[8,256]{1,0:T(8,128)S(1)} %select_reduce_fusion.virtual, bf16[2,2,1,2,256,512]{5,4,3,2,1,0:T(8,128)(2,1)S(1)} %copy-done, ...), custom_call_target="tpu_custom_call", output_to_operand_aliasing={{}: (7, {})} | custom-call | flops 536870912 | bytes 4718592 | tf_op jit(solution)/shard_map/pallas_call | solution.py:138
  (2 shorter events, 0.0 us)
Async XLA Ops:
  0.0 37.2 %copy-start.5 = (f32[8,256]{1,0:T(8,128)S(1)}, f32[8,256]{1,0:T(8,128)}, u32[]{:S(2)}) copy-start(f32[8,256]{1,0:T(8,128)} %param.8) | copy-start | bytes 24580
  0.0 37.2 %copy-start.6 = (s32[8,256]{1,0:T(8,128)S(1)}, s32[8,256]{1,0:T(8,128)}, u32[]{:S(2)}) copy-start(s32[8,256]{1,0:T(8,128)} %param.9) | copy-start | bytes 24580
  0.0 41.7 %copy-start = (bf16[2,2,1,2,256,512]{5,4,3,2,1,0:T(8,128)(2,1)S(1)}, bf16[2,2,1,2,256,512]{5,4,3,2,1,0:T(8,128)(2,1)}, u32[]{:S(2)}) copy-start(bf16[2,2,1,2,256,512]{5,4,3,2,1,0:T(8,128)(2,1)} %factor.9) | copy-start | bytes 6291460
  0.0 41.7 %copy-start.3 = (f32[8,8]{1,0:T(8,128)S(1)}, f32[8,8]{1,0:T(8,128)}, u32[]{:S(2)}) copy-start(f32[8,8]{1,0:T(8,128)} %occ.9) | copy-start | bytes 772
  0.0 41.7 %copy-start.4 = (s32[2,8]{1,0:T(2,128)S(1)}, s32[2,8]{1,0:T(2,128)}, u32[]{:S(2)}) copy-start(s32[2,8]{1,0:T(2,128)} %partner.9) | copy-start | bytes 196
  1.8 14.9 %collective-permute-start.3 = (bf16[2,2,128,512]{3,2,1,0:T(8,128)(2,1)S(1)}, bf16[2,2,128,512]{3,2,1,0:T(8,128)(2,1)S(1)}, u32[]{:S(2)}, u32[]{:S(2)}) collective-permute-start(bf16[2,2,128,512]{3,2,1,0:T(8,128)(2,1)S(1)} %get-tuple-element.14), channel_id=1, source_target_pairs={{0,8},{8,0},{16,24},{24,16},{1,9},{9,1},{17,25},{25,17},{2,10},{10... | collective-permute-start | bytes 1572872 | tf_op jit(solution)/shard_map/ppermute | solution.py:16
  4.8 13.7 %collective-permute-start = (bf16[2,2,128,512]{3,2,1,0:T(8,128)(2,1)S(1)}, bf16[2,2,128,512]{3,2,1,0:T(8,128)(2,1)S(1)}, u32[]{:S(2)}, u32[]{:S(2)}) collective-permute-start(bf16[2,2,128,512]{3,2,1,0:T(8,128)(2,1)S(1)} %get-tuple-element.16), channel_id=1, source_target_pairs={{0,16},{8,24},{16,0},{24,8},{1,17},{9,25},{17,1},{25,9},{2,18},{10... | collective-permute-start | bytes 1572872 | tf_op jit(solution)/shard_map/ppermute | solution.py:16
  6.4 15.9 %collective-permute-start.6 = (bf16[2,2,128,512]{3,2,1,0:T(8,128)(2,1)S(1)}, bf16[2,2,128,512]{3,2,1,0:T(8,128)(2,1)}, u32[]{:S(2)}, u32[]{:S(2)}) collective-permute-start(bf16[2,2,128,512]{3,2,1,0:T(8,128)(2,1)S(1)} %get-tuple-element.11), channel_id=1, source_target_pairs={{0,7},{1,2},{2,1},{3,4},{4,3},{5,6},{6,5},{7,0},{8,15},{9,10},{10,... | collective-permute-start | bytes 1572872 | tf_op jit(solution)/shard_map/ppermute | solution.py:26
  16.8 13.3 %collective-permute-start.4 = (bf16[2,2,128,512]{3,2,1,0:T(8,128)(2,1)S(1)}, bf16[2,2,128,512]{3,2,1,0:T(8,128)(2,1)}, u32[]{:S(2)}, u32[]{:S(2)}) collective-permute-start(bf16[2,2,128,512]{3,2,1,0:T(8,128)(2,1)S(1)} %get-tuple-element.9), channel_id=1, source_target_pairs={{0,8},{8,0},{16,24},{24,16},{1,9},{9,1},{17,25},{25,17},{2,10},{10... | collective-permute-start | bytes 1572872 | tf_op jit(solution)/shard_map/ppermute | solution.py:16
  18.5 12.7 %collective-permute-start.7 = (bf16[2,2,128,512]{3,2,1,0:T(8,128)(2,1)S(1)}, bf16[2,2,128,512]{3,2,1,0:T(8,128)(2,1)}, u32[]{:S(2)}, u32[]{:S(2)}) collective-permute-start(bf16[2,2,128,512]{3,2,1,0:T(8,128)(2,1)S(1)} %get-tuple-element.11), channel_id=1, source_target_pairs={{0,16},{8,24},{16,0},{24,8},{1,17},{9,25},{17,1},{25,9},{2,18},{10... | collective-permute-start | bytes 1572872 | tf_op jit(solution)/shard_map/ppermute | solution.py:16
  20.0 15.9 %collective-permute-start.2 = (bf16[2,2,128,512]{3,2,1,0:T(8,128)(2,1)S(1)}, bf16[2,2,128,512]{3,2,1,0:T(8,128)(2,1)}, u32[]{:S(2)}, u32[]{:S(2)}) collective-permute-start(bf16[2,2,128,512]{3,2,1,0:T(8,128)(2,1)S(1)} %get-tuple-element.9), channel_id=1, source_target_pairs={{0,7},{1,2},{2,1},{3,4},{4,3},{5,6},{6,5},{7,0},{8,15},{9,10},{10,... | collective-permute-start | bytes 1572872 | tf_op jit(solution)/shard_map/ppermute | solution.py:26
  21.7 14.7 %collective-permute-start.11 = (bf16[2,2,128,512]{3,2,1,0:T(8,128)(2,1)S(1)}, bf16[2,2,128,512]{3,2,1,0:T(8,128)(2,1)S(1)}, u32[]{:S(2)}, u32[]{:S(2)}) collective-permute-start(bf16[2,2,128,512]{3,2,1,0:T(8,128)(2,1)S(1)} %collective-permute-done.3.refs_0_), channel_id=1, source_target_pairs={{0,1},{1,0},{2,3},{3,2},{4,5},{5,4},{6,7},{7,6},{8,9},{9,8},{10,11... | collective-permute-start | bytes 1572872 | tf_op jit(solution)/shard_map/ppermute | solution.py:21
  22.2 15.8 %collective-permute-start.12 = (bf16[2,2,128,512]{3,2,1,0:T(8,128)(2,1)S(1)}, bf16[2,2,128,512]{3,2,1,0:T(8,128)(2,1)}, u32[]{:S(2)}, u32[]{:S(2)}) collective-permute-start(bf16[2,2,128,512]{3,2,1,0:T(8,128)(2,1)S(1)} %collective-permute-done.refs_1_), channel_id=1, source_target_pairs={{0,1},{1,0},{2,3},{3,2},{4,5},{5,4},{6,7},{7,6},{8,9},{9,8},{10,11... | collective-permute-start | bytes 1572872 | tf_op jit(solution)/shard_map/ppermute | solution.py:21
  30.1 9.4 %collective-permute-start.9 = (bf16[2,2,128,512]{3,2,1,0:T(8,128)(2,1)}, bf16[2,2,128,512]{3,2,1,0:T(8,128)(2,1)}, u32[]{:S(2)}, u32[]{:S(2)}) collective-permute-start(bf16[2,2,128,512]{3,2,1,0:T(8,128)(2,1)} %collective-permute-done.4.refs_0_), channel_id=1, source_target_pairs={{0,1},{1,0},{2,3},{3,2},{4,5},{5,4},{6,7},{7,6},{8,9},{9,8},{10,11... | collective-permute-start | bytes 1572872 | tf_op jit(solution)/shard_map/ppermute | solution.py:21
  31.2 15.6 %collective-permute-start.10 = (bf16[2,2,128,512]{3,2,1,0:T(8,128)(2,1)}, bf16[2,2,128,512]{3,2,1,0:T(8,128)(2,1)}, u32[]{:S(2)}, u32[]{:S(2)}) collective-permute-start(bf16[2,2,128,512]{3,2,1,0:T(8,128)(2,1)} %collective-permute-done.7.refs_1_), channel_id=1, source_target_pairs={{0,1},{1,0},{2,3},{3,2},{4,5},{5,4},{6,7},{7,6},{8,9},{9,8},{10,11... | collective-permute-start | bytes 1572872 | tf_op jit(solution)/shard_map/ppermute | solution.py:21
  35.9 15.5 %collective-permute-start.8 = (bf16[2,2,128,512]{3,2,1,0:T(8,128)(2,1)}, bf16[2,2,128,512]{3,2,1,0:T(8,128)(2,1)}, u32[]{:S(2)}, u32[]{:S(2)}) collective-permute-start(bf16[2,2,128,512]{3,2,1,0:T(8,128)(2,1)} %collective-permute-done.6), channel_id=1, source_target_pairs={{0,16},{8,24},{16,0},{24,8},{1,17},{9,25},{17,1},{25,9},{2,18},{10... | collective-permute-start | bytes 1572872 | tf_op jit(solution)/shard_map/ppermute | solution.py:16
  36.4 0.8 %copy-start.1 = (bf16[2,2,128,512]{3,2,1,0:T(8,128)(2,1)}, bf16[2,2,128,512]{3,2,1,0:T(8,128)(2,1)S(1)}, u32[]{:S(2)}) copy-start(bf16[2,2,128,512]{3,2,1,0:T(8,128)(2,1)S(1)} %collective-permute-done.11.refs_2_) | copy-start | bytes 1572868
  37.2 14.2 %collective-permute-start.5 = (bf16[2,2,128,512]{3,2,1,0:T(8,128)(2,1)}, bf16[2,2,128,512]{3,2,1,0:T(8,128)(2,1)}, u32[]{:S(2)}, u32[]{:S(2)}) collective-permute-start(bf16[2,2,128,512]{3,2,1,0:T(8,128)(2,1)} %collective-permute-done.2), channel_id=1, source_target_pairs={{0,8},{8,0},{16,24},{24,16},{1,9},{9,1},{17,25},{25,17},{2,10},{10... | collective-permute-start | bytes 1572872 | tf_op jit(solution)/shard_map/ppermute | solution.py:16
  38.0 17.5 %collective-permute-start.13 = (bf16[2,2,128,512]{3,2,1,0:T(8,128)(2,1)S(1)}, bf16[2,2,128,512]{3,2,1,0:T(8,128)(2,1)S(1)}, u32[]{:S(2)}, u32[]{:S(2)}) collective-permute-start(bf16[2,2,128,512]{3,2,1,0:T(8,128)(2,1)S(1)} %collective-permute-done.3.refs_0_), channel_id=1, source_target_pairs={{0,7},{1,2},{2,1},{3,4},{4,3},{5,6},{6,5},{7,0},{8,15},{9,10},{10,... | collective-permute-start | bytes 1572872 | tf_op jit(solution)/shard_map/ppermute | solution.py:26
  39.4 25.2 %collective-permute-start.1 = (bf16[2,2,128,512]{3,2,1,0:T(8,128)(2,1)S(1)}, bf16[2,2,128,512]{3,2,1,0:T(8,128)(2,1)S(1)}, u32[]{:S(2)}, u32[]{:S(2)}) collective-permute-start(bf16[2,2,128,512]{3,2,1,0:T(8,128)(2,1)S(1)} %collective-permute-done.refs_1_), channel_id=1, source_target_pairs={{0,7},{1,2},{2,1},{3,4},{4,3},{5,6},{6,5},{7,0},{8,15},{9,10},{10,... | collective-permute-start | bytes 1572872 | tf_op jit(solution)/shard_map/ppermute | solution.py:26
  41.7 1.0 %copy-start.2 = (bf16[2,2,128,512]{3,2,1,0:T(8,128)(2,1)S(1)}, bf16[2,2,128,512]{3,2,1,0:T(8,128)(2,1)}, u32[]{:S(2)}) copy-start(bf16[2,2,128,512]{3,2,1,0:T(8,128)(2,1)} %copy-done.1) | copy-start | bytes 1572868

commit v4 on v2

v4 whole, which is shorter than its diff:
```python
import functools

import jax
import jax.numpy as jnp
from jax import lax
from jax.experimental import pallas as pl
from jax.experimental.pallas import tpu as pltpu
from jax.sharding import PartitionSpec as P

F32 = jnp.float32
BF16 = jnp.bfloat16
ANY = pl.BlockSpec(memory_space=pl.ANY)
VMEM = pl.BlockSpec(memory_space=pltpu.VMEM)
SMEM = pl.BlockSpec(memory_space=pltpu.SMEM)
PARAMS = pltpu.CompilerParams(vmem_limit_bytes=20 * 1024 * 1024)
COST = pl.CostEstimate(flops=0, bytes_accessed=0, transcendentals=0)


def group_swap(block, bit):
    count = lax.axis_size("kpt")
    return lax.ppermute(block, "kpt", [(g, g ^ (1 << bit)) for g in range(count)])


def near_swap(block):
    count = lax.axis_size("occ")
    return lax.ppermute(block, "occ", [(i, i ^ 1) for i in range(count)])


def far_swap(block):
    count = lax.axis_size("occ")
    return lax.ppermute(
        block, "occ", [(i, (i + (1 if i % 2 else count - 1)) % count) for i in range(count)]
    )


def virtual_energies(vir_sorted, vir_order):
    ranks = jnp.arange(vir_sorted.shape[1], dtype=jnp.int32)
    matches = vir_order[:, :, None] == ranks[None, None, :]
    return jnp.sum(jnp.where(matches, vir_sorted[:, None, :], 0.0), axis=2)


def column_of(row):
    return jnp.transpose(jnp.broadcast_to(row, (8, row.shape[1])))[:, :1]


def pack_kernel(bits, early, partner, factor, *refs):
    *wholes, part, sems = refs
    half = part.shape[2]
    kc = factor.shape[1]
    group = lax.axis_index("kpt")
    copies = []
    for transfer, bit in enumerate(bits):
        far_group = jnp.bitwise_xor(group, 1 << bit)
        slots = [partner[transfer, far_group * kc + k] - group * kc for k in range(kc)]
        for at, (t, k, h) in enumerate(early):
            if t == transfer:
                source = factor.at[transfer, slots[k], 0, :, pl.ds(h * half, half), :]
                copies.append((source, part.at[at]))
        for k in range(kc):
            copies.append((factor.at[transfer, slots[k], 0], wholes[transfer].at[k]))
    copies = [
        pltpu.make_async_copy(source, target, sems.at[at])
        for at, (source, target) in enumerate(copies)
    ]
    for copy in copies:
        copy.start()
    for copy in copies:
        copy.wait()


def pack(bits, early, partner, factor):
    _, kc, _, parts, nv, naux = factor.shape
    shapes = [(kc, parts, nv, naux)] * len(bits)
    shapes.append((len(early), parts, nv // 2, naux))
    copies = len(early) + kc * len(bits)
    return pl.pallas_call(
        functools.partial(pack_kernel, bits, early),
        out_shape=[jax.ShapeDtypeStruct(shape, BF16) for shape in shapes],
        in_specs=[SMEM, ANY],
        out_specs=[VMEM] * len(shapes),
        scratch_shapes=[pltpu.SemaphoreType.DMA((copies,))],
        cost_estimate=COST,
        compiler_params=PARAMS,
    )(partner, factor)


def inverse_kernel(bits, partner, occ, virtual, out):
    _, _, kc, nv, _ = out.shape
    total = occ.shape[1]
    group, orbit = lax.axis_index("kpt"), lax.axis_index("occ")
    parity = lax.rem(orbit, 2)
    columns = (orbit, orbit + 1 - 2 * parity, lax.rem(orbit + total - 1 + 2 * parity, total))

    def point_step(k, carry):
        point = group * kc + k
        row = virtual[pl.ds(point, 1), :]
        for transfer in range(len(bits)):
            far_point = partner[transfer, point]
            column = column_of(virtual[pl.ds(far_point, 1), :])
            for place, index in enumerate(columns):
                level = occ[point, orbit] + occ[far_point, index]
                out[transfer, place, k] = 1.0 / ((level - column) - row)
        return carry

    lax.fori_loop(0, kc, point_step, 0)


def inverses(bits, partner, occ_energy, virtual, kc):
    nv = virtual.shape[1]
    return pl.pallas_call(
        functools.partial(inverse_kernel, bits),
        out_shape=jax.ShapeDtypeStruct((len(bits), 3, kc, nv, nv), F32),
        in_specs=[SMEM, SMEM, VMEM],
        out_specs=VMEM,
        cost_estimate=COST,
        compiler_params=PARAMS,
    )(partner, occ_energy, virtual)


def gradient_sum(own, terms, base):
    _, nv, naux = own.shape
    left = own.reshape(2 * nv, naux)
    amplitudes, blocks = [], []
    for window, inverse in terms:
        size = window.shape[1]
        window = window.reshape(2 * size, naux)
        products = lax.dot_general(
            left, window, (((1,), (1,)), ((), ())), preferred_element_type=F32
        )
        real_part = ((products[:nv, :size] + products[nv:, size:]) * inverse).astype(BF16)
        imag_part = ((products[nv:, :size] - products[:nv, size:]) * inverse).astype(BF16)
        upper = jnp.concatenate([real_part, -imag_part], axis=1)
        lower = jnp.concatenate([imag_part, real_part], axis=1)
        amplitudes.append(jnp.concatenate([upper, lower], axis=0))
        blocks.append(window)
    gradient = jnp.dot(
        jnp.concatenate(amplitudes, axis=1),
        jnp.concatenate(blocks, axis=0),
        preferred_element_type=F32,
    ).reshape(2, nv, naux)
    return gradient if base is None else gradient + base


def first_kernel(transfers, factor, inverse, *refs):
    owns, nears, out = refs[:transfers], refs[transfers:-1], refs[-1]

    def point_step(k, carry):
        for t in range(transfers):
            terms = [(owns[t][k], inverse[t, 0, k]), (nears[t][k], inverse[t, 1, k])]
            out[t, k] = gradient_sum(factor[t, k, 0], terms, None)
        return carry

    lax.fori_loop(0, factor.shape[1], point_step, 0)


def first_terms(factor, inverse, owns, nears):
    transfers, kc, _, parts, nv, naux = factor.shape
    operands = [factor, inverse, *owns, *nears]
    return pl.pallas_call(
        functools.partial(first_kernel, transfers),
        out_shape=jax.ShapeDtypeStruct((transfers, kc, parts, nv, naux), F32),
        in_specs=[VMEM] * len(operands),
        out_specs=VMEM,
        cost_estimate=COST,
        compiler_params=PARAMS,
    )(*operands)


def far_kernel(sources, ends, keep, has_result, factor, inverse, *refs):
    count = len(sources)
    windows, total = refs[:count], refs[count]
    kept = refs[count + 1 + has_result] if keep else None
    half = windows[0].shape[2]
    out, staged, sems = refs[-3:]
    copies = []
    for t in range(factor.shape[0]):
        for k in range(factor.shape[1]):
            terms = [
                (window[at], inverse[t, 2, k, :, unit[2] * half : (unit[2] + 1) * half])
                for window, units in zip(windows, sources)
                for at, unit in enumerate(units)
                if unit[:2] == (t, k)
            ]
            if not terms:
                continue
            gradient = gradient_sum(factor[t, k, 0], terms, total[t, k])
            if (t, k) in ends:
                at = len(copies)
                staged[at] = gradient.astype(BF16)
                copy = pltpu.make_async_copy(staged.at[at], out.at[t, k, 0], sems.at[at])
                copy.start()
                copies.append(copy)
            else:
                kept[t, k] = gradient
    for copy in copies:
        copy.wait()


def far_terms(sources, ends, keep, factor, inverse, windows, total, result=None):
    _, _, _, parts, nv, naux = factor.shape
    operands = [factor, inverse, *windows, total]
    in_specs = [VMEM] * len(operands)
    aliases = {}
    if keep:
        aliases[len(operands) - 1] = 0
    if result is not None:
        aliases[len(operands)] = int(keep)
        operands.append(result)
        in_specs.append(ANY)
    out_shape = [jax.ShapeDtypeStruct(factor.shape, BF16)]
    out_specs = [ANY]
    if keep:
        out_shape.insert(0, jax.ShapeDtypeStruct(total.shape, F32))
        out_specs.insert(0, VMEM)
    return pl.pallas_call(
        functools.partial(far_kernel, sources, ends, keep, result is not None),
        out_shape=out_shape,
        in_specs=in_specs,
        out_specs=out_specs,
        scratch_shapes=[
            pltpu.VMEM((len(ends), parts, nv, naux), BF16),
            pltpu.SemaphoreType.DMA((len(ends),)),
        ],
        input_output_aliases=aliases,
        cost_estimate=COST,
        compiler_params=PARAMS,
    )(*operands)


def body(factor, partner, occ_energy, vir_sorted, vir_order):
    transfers, kc = factor.shape[:2]
    half = factor.shape[4] // 2
    bits = (0, lax.axis_size("kpt").bit_length() - 2)
    order = [[(t, k, h) for h in range(2) for k in range(kc)] for t in range(transfers)]
    cuts = [kc + kc // 2, kc]
    early = [order[t][: cuts[t]] for t in range(transfers)]
    late = order[0][cuts[0] :] + order[1][cuts[1] :]
    late_ends = {unit[:2] for unit in late}
    early_ends = {unit[:2] for unit in order[0] + order[1]} - late_ends

    *wholes, part = pack(bits, early[0] + early[1], partner, factor)
    beside = far_swap(part)
    owns = [group_swap(wholes[t], bits[t]) for t in range(transfers)]
    late_block = jnp.concatenate(
        [owns[0][cuts[0] - kc :, :, half:], owns[1][cuts[1] - kc :, :, half:]]
    )
    late_window = far_swap(late_block)
    beside, _ = lax.optimization_barrier((beside, late_block))
    nears = [near_swap(owns[t]) for t in range(transfers)]
    early_windows = [
        group_swap(beside[: cuts[0]], bits[0]),
        group_swap(beside[cuts[0] :], bits[1]),
    ]

    virtual = virtual_energies(vir_sorted, vir_order)
    inverse = inverses(bits, partner, occ_energy, virtual, kc)
    total = first_terms(factor, inverse, owns, nears)
    total, result = far_terms(early, early_ends, True, factor, inverse, early_windows, total)
    (result,) = far_terms([late], late_ends, False, factor, inverse, [late_window], total, result)
    return result


def solution(mesh):
    spec = P(None, "kpt", "occ", None, None, None)
    in_specs = (spec, P(), P(), P(), P())
    return jax.shard_map(body, mesh=mesh, in_specs=in_specs, out_specs=spec, check_vma=False)
```

time: 67 us -> 62.6 us (0.934)
  Pallas kernels: 16.1 us -> 12.1 us
  waiting for transfers between devices: 37.8 us -> 36.3 us
    ppermute x3 -> x4, waiting for transfers between devices: 34 us -> 28.5 us  [group_swap(): return lax.ppermute(block, 'kpt', [(g, g ^ 1 << bit) for g in range(count)])]
    pallas_call x4 -> x5, Pallas kernels: 16.1 us -> 12.1 us  [the longest x1 5.03 us: first_terms(): pl.pallas_call(functools.partial(first_kernel, transfers), out_shape=jax....]
    ppermute x2, waiting for transfers between devices: 3.83 us -> 7.81 us  [far_swap(): lax.ppermute(block, 'occ', [(i, (i + (1 if i % 2 else count - 1)) % count...]
    unnamed x10 -> x12, local copies, waits for them, and re-layouts: 0.02 us -> 2.29 us
    squeeze x1 -> x0, local copies, waits for them, and re-layouts: 1.9 us -> none  [body(): one, two = (factor[0], factor[1])]
    ppermute x3 -> x4, starting transfers between devices: 4.54 us -> 6.18 us  [group_swap(): return lax.ppermute(block, 'kpt', [(g, g ^ 1 << bit) for g in range(count)])]
    ppermute x2, starting transfers between devices: 5.47 us -> 4.43 us  [far_swap(): lax.ppermute(block, 'occ', [(i, (i + (1 if i % 2 else count - 1)) % count...]
  transfers between devices with their start and end apart: 7 -> 8, of which waited for: 3 -> 6; matrix products, arithmetic and copies ran while one was open for 1% -> 2% of each run, Pallas kernels for 18% -> 14%
where the time goes in v4:
time: 62.6 us; the launch traced here: 62.4 us
  waiting for transfers between devices  36.3 us (58%)
  Pallas kernels  12.1 us (19%)
  starting transfers between devices  10.6 us (17%)
  local copies, waits for them, and re-layouts  2.46 us (4%)
  other arithmetic  0.83 us (1%)
    ppermute x4, waiting for transfers between devices, group_swap(): return lax.ppermute(block, 'kpt', [(g, g ^ 1 << bit) for g in range(count)])  28.5 us
    ppermute x2, waiting for transfers between devices, far_swap(): lax.ppermute(block, 'occ', [(i, (i + (1 if i % 2 else count - 1)) % count...  7.81 us
    ppermute x4, starting transfers between devices, group_swap(): return lax.ppermute(block, 'kpt', [(g, g ^ 1 << bit) for g in range(count)])  6.18 us
    pallas_call x1, Pallas kernels, first_terms(): pl.pallas_call(functools.partial(first_kernel, transfers), out_shape=jax....  5.03 us
    pallas_call x2, Pallas kernels, far_terms(): pl.pallas_call(functools.partial(far_kernel, sources, ends, keep, result...  4.56 us
    ppermute x2, starting transfers between devices, far_swap(): lax.ppermute(block, 'occ', [(i, (i + (1 if i % 2 else count - 1)) % count...  4.43 us
    unnamed x12, local copies, waits for them, and re-layouts  2.29 us
    pallas_call x1, Pallas kernels, inverses(): pl.pallas_call(functools.partial(inverse_kernel, bits), out_shape=jax.Sha...  1.59 us
  transfers between devices with their start and end apart: 8, of which 6 were waited for; matrix products, arithmetic and copies ran while one was open for 2% of the time, Pallas kernels for 14%

profile of v4, /device:TPU:0, one launch (start us, length us, event | category | flops | bytes accessed | tf_op | source)
XLA Modules:
  0.0 62.4 jit_solution(13897620713358616833)
XLA Ops:
  0.0 0.0 copy-start
  0.0 1.6 %copy-done = bf16[2,2,1,2,256,512]{5,4,3,2,1,0:T(8,128)(2,1)S(1)} copy-done((bf16[2,2,1,2,256,512]{5,4,3,2,1,0:T(8,128)(2,1)S(1)}, bf16[2,2,1,2,256,512]{5,4,3,2,1,0:T(8,128)(2,1)}, u32[]{:S(2)}) %copy-start) | copy-done | bytes 2097176
  1.6 0.0 copy-start.3
  1.6 0.7 %copy-done.3 = s32[2,8]{1,0:T(2,128)S(1)} copy-done((s32[2,8]{1,0:T(2,128)S(1)}, s32[2,8]{1,0:T(2,128)}, u32[]{:S(2)}) %copy-start.3) | copy-done | bytes 88
  2.3 0.9 %shard_map.56 = (bf16[2,2,256,512]{3,2,1,0:T(8,128)(2,1)S(1)}, bf16[2,2,256,512]{3,2,1,0:T(8,128)(2,1)S(1)}, bf16[5,2,128,512]{3,2,1,0:T(8,128)(2,1)S(1)}) custom-call(s32[2,8]{1,0:T(2,128)S(1)} %copy-done.3, bf16[2,2,1,2,256,512]{5,4,3,2,1,0:T(8,128)(2,1)S(1)} %copy-done), custom_call_target="tpu_custom_call" | custom-call | tf_op jit(solution)/shard_map/pallas_call | solution.py:76
  3.2 3.0 %collective-permute-start = (bf16[2,2,256,512]{3,2,1,0:T(8,128)(2,1)S(1)}, bf16[2,2,256,512]{3,2,1,0:T(8,128)(2,1)S(1)}, u32[]{:S(2)}, u32[]{:S(2)}) collective-permute-start(bf16[2,2,256,512]{3,2,1,0:T(8,128)(2,1)S(1)} %get-tuple-element.11), channel_id=1, source_target_pairs={{0,8},{8,0},{16,24},{24,16},{1,9},{9,1},{17,25},{25,17},{2,10},{10... | collective-permute-start | bytes 3145736 | tf_op jit(solution)/shard_map/ppermute | solution.py:21
  6.2 2.8 %collective-permute-start.3 = (bf16[5,2,128,512]{3,2,1,0:T(8,128)(2,1)S(1)}, bf16[5,2,128,512]{3,2,1,0:T(8,128)(2,1)S(1)}, u32[]{:S(2)}, u32[]{:S(2)}) collective-permute-start(bf16[5,2,128,512]{3,2,1,0:T(8,128)(2,1)S(1)} %get-tuple-element.13), channel_id=1, source_target_pairs={{0,7},{1,2},{2,1},{3,4},{4,3},{5,6},{6,5},{7,0},{8,15},{9,10},{10,... | collective-permute-start | bytes 3932168 | tf_op jit(solution)/shard_map/ppermute | solution.py:31
  8.9 1.5 %collective-permute-start.1 = (bf16[2,2,256,512]{3,2,1,0:T(8,128)(2,1)S(1)}, bf16[2,2,256,512]{3,2,1,0:T(8,128)(2,1)S(1)}, u32[]{:S(2)}, u32[]{:S(2)}) collective-permute-start(bf16[2,2,256,512]{3,2,1,0:T(8,128)(2,1)S(1)} %get-tuple-element.12), channel_id=1, source_target_pairs={{0,16},{8,24},{16,0},{24,8},{1,17},{9,25},{17,1},{25,9},{2,18},{10... | collective-permute-start | bytes 3145736 | tf_op jit(solution)/shard_map/ppermute | solution.py:21
  10.5 18.9 %collective-permute-done.refs_0_ = bf16[2,2,256,512]{3,2,1,0:T(8,128)(2,1)S(1)} collective-permute-done((bf16[2,2,256,512]{3,2,1,0:T(8,128)(2,1)S(1)}, bf16[2,2,256,512]{3,2,1,0:T(8,128)(2,1)S(1)}, u32[]{:S(2)}, u32[]{:S(2)}) %collective-permute-start) | collective-permute-done | bytes 1048608 | tf_op jit(solution)/shard_map/ppermute | solution.py:21
  29.3 0.0 collective-permute-start.6
  29.3 3.6 %collective-permute-done.1.refs_1_ = bf16[2,2,256,512]{3,2,1,0:T(8,128)(2,1)S(1)} collective-permute-done((bf16[2,2,256,512]{3,2,1,0:T(8,128)(2,1)S(1)}, bf16[2,2,256,512]{3,2,1,0:T(8,128)(2,1)S(1)}, u32[]{:S(2)}, u32[]{:S(2)}) %collective-permute-start.1) | collective-permute-done | bytes 1048608 | tf_op jit(solution)/shard_map/ppermute | solution.py:21
  32.9 0.0 collective-permute-start.7
  33.0 0.0 copy-start.4
  33.0 0.0 copy-start.5
  33.0 0.0 copy-start.2
  33.0 0.1 pad_maximum_fusion
  33.1 5.7 %collective-permute-done.3 = bf16[5,2,128,512]{3,2,1,0:T(8,128)(2,1)S(1)} collective-permute-done((bf16[5,2,128,512]{3,2,1,0:T(8,128)(2,1)S(1)}, bf16[5,2,128,512]{3,2,1,0:T(8,128)(2,1)S(1)}, u32[]{:S(2)}, u32[]{:S(2)}) %collective-permute-start.3) | collective-permute-done | bytes 1310752 | tf_op jit(solution)/shard_map/ppermute | solution.py:31
  38.8 0.1 slice.14
  38.9 0.0 copy-start.1
  38.9 0.1 collective-permute-start.4
  39.0 1.7 %collective-permute-start.2 = (bf16[3,2,128,512]{3,2,1,0:T(8,128)(2,1)S(1)}, bf16[3,2,128,512]{3,2,1,0:T(8,128)(2,1)S(1)}, u32[]{:S(2)}, u32[]{:S(2)}) collective-permute-start(bf16[3,2,128,512]{3,2,1,0:T(8,128)(2,1)S(1)} %pad_maximum_fusion), channel_id=1, source_target_pairs={{0,7},{1,2},{2,1},{3,4},{4,3},{5,6},{6,5},{7,0},{8,15},{9,10},{10,... | collective-permute-start | bytes 2359304 | tf_op jit(solution)/shard_map/ppermute | solution.py:31
  40.7 1.6 %collective-permute-start.5 = (bf16[2,2,128,512]{3,2,1,0:T(8,128)(2,1)S(1)}, bf16[2,2,128,512]{3,2,1,0:T(8,128)(2,1)S(1)}, u32[]{:S(2)}, u32[]{:S(2)}) collective-permute-start(bf16[2,2,128,512]{3,2,1,0:T(8,128)(2,1)S(1)} %slice.15), channel_id=1, source_target_pairs={{0,16},{8,24},{16,0},{24,8},{1,17},{9,25},{17,1},{25,9},{2,18},{10... | collective-permute-start | bytes 1572872 | tf_op jit(solution)/shard_map/ppermute | solution.py:21
  42.3 0.0 copy-done.4
  42.3 0.0 copy-done.5
  42.3 0.8 %select_reduce_fusion.virtual = f32[8,256]{1,0:T(8,128)S(1)} fusion(f32[8,256]{1,0:T(8,128)S(1)} %copy-done.4, s32[8,256]{1,0:T(8,128)S(1)} %copy-done.5), kind=kLoop, calls=%fused_computation | loop fusion | flops 1570816 | bytes 24576 | tf_op jit(solution)/shard_map/reduce_sum | solution.py:39
  43.0 0.0 copy-done.2
  43.0 1.6 %shard_map.55.inverse = f32[2,3,2,256,256]{4,3,2,1,0:T(8,128)S(1)} custom-call(s32[2,8]{1,0:T(2,128)S(1)} %copy-done.3, f32[8,8]{1,0:T(8,128)S(1)} %copy-done.2, f32[8,256]{1,0:T(8,128)S(1)} %select_reduce_fusion.virtual), custom_call_target="tpu_custom_call" | custom-call | tf_op jit(solution)/shard_map/pallas_call | solution.py:110
  44.6 0.0 collective-permute-done.6.refs_2_
  44.6 0.0 collective-permute-done.7.refs_3_
  44.7 0.0 copy-done.1
  44.7 5.0 %shard_map.57.refs_2_ = f32[2,2,2,256,512]{4,3,2,1,0:T(8,128)S(1)} custom-call(bf16[2,2,1,2,256,512]{5,4,3,2,1,0:T(8,128)(2,1)S(1)} %copy-done.1, f32[2,3,2,256,256]{4,3,2,1,0:T(8,128)S(1)} %shard_map.55.inverse, bf16[2,2,256,512]{3,2,1,0:T(8,128)(2,1)S(1)} %collective-permute-done.refs_0_, bf16[2,2,256,512]{3,2,1,0:T(8,128)(2,1)S(1)} %collective-permute-done.1.refs_1_, ...), custom_call_target="tpu_custom_call" | custom-call | tf_op jit(solution)/shard_map/pallas_call | solution.py:159
  49.7 2.0 %collective-permute-done.5.refs_1_ = bf16[2,2,128,512]{3,2,1,0:T(8,128)(2,1)S(1)} collective-permute-done((bf16[2,2,128,512]{3,2,1,0:T(8,128)(2,1)S(1)}, bf16[2,2,128,512]{3,2,1,0:T(8,128)(2,1)S(1)}, u32[]{:S(2)}, u32[]{:S(2)}) %collective-permute-start.5) | collective-permute-done | bytes 524320 | tf_op jit(solution)/shard_map/ppermute | solution.py:21
  51.8 3.9 %collective-permute-done.4.refs_0_ = bf16[3,2,128,512]{3,2,1,0:T(8,128)(2,1)S(1)} collective-permute-done((bf16[3,2,128,512]{3,2,1,0:T(8,128)(2,1)S(1)}, bf16[3,2,128,512]{3,2,1,0:T(8,128)(2,1)S(1)}, u32[]{:S(2)}, u32[]{:S(2)}) %collective-permute-start.4) | collective-permute-done | bytes 786464 | tf_op jit(solution)/shard_map/ppermute | solution.py:21
  55.7 2.1 %shard_map.58 = (f32[2,2,2,256,512]{4,3,2,1,0:T(8,128)S(1)}, bf16[2,2,1,2,256,512]{5,4,3,2,1,0:T(8,128)(2,1)}) custom-call(bf16[2,2,1,2,256,512]{5,4,3,2,1,0:T(8,128)(2,1)S(1)} %copy-done.1, f32[2,3,2,256,256]{4,3,2,1,0:T(8,128)S(1)} %shard_map.55.inverse, ...), custom_call_target="tpu_custom_call", output_to_operand_aliasing={{0}: (4, {})} | custom-call | tf_op jit(solution)/shard_map/pallas_call | solution.py:215
  57.8 2.1 %collective-permute-done.2.refs_0_ = bf16[3,2,128,512]{3,2,1,0:T(8,128)(2,1)S(1)} collective-permute-done((bf16[3,2,128,512]{3,2,1,0:T(8,128)(2,1)S(1)}, bf16[3,2,128,512]{3,2,1,0:T(8,128)(2,1)S(1)}, u32[]{:S(2)}, u32[]{:S(2)}) %collective-permute-start.2) | collective-permute-done | bytes 786464 | tf_op jit(solution)/shard_map/ppermute | solution.py:31
  60.0 2.5 %shard_map.59 = bf16[2,2,1,2,256,512]{5,4,3,2,1,0:T(8,128)(2,1)} custom-call(bf16[2,2,1,2,256,512]{5,4,3,2,1,0:T(8,128)(2,1)S(1)} %copy-done.1, f32[2,3,2,256,256]{4,3,2,1,0:T(8,128)S(1)} %shard_map.55.inverse, bf16[3,2,128,512]{3,2,1,0:T(8,128)(2,1)S(1)} %collective-permute-done.2.refs_0_, ...), custom_call_target="tpu_custom_call", output_to_operand_aliasing={{}: (4, {})} | custom-call | tf_op jit(solution)/shard_map/pallas_call | solution.py:215
  (3 shorter events, 0.1 us)
Async XLA Ops:
  0.0 1.6 %copy-start = (bf16[2,2,1,2,256,512]{5,4,3,2,1,0:T(8,128)(2,1)S(1)}, bf16[2,2,1,2,256,512]{5,4,3,2,1,0:T(8,128)(2,1)}, u32[]{:S(2)}) copy-start(bf16[2,2,1,2,256,512]{5,4,3,2,1,0:T(8,128)(2,1)} %factor.7) | copy-start | bytes 6291460
  1.6 0.7 %copy-start.3 = (s32[2,8]{1,0:T(2,128)S(1)}, s32[2,8]{1,0:T(2,128)}, u32[]{:S(2)}) copy-start(s32[2,8]{1,0:T(2,128)} %partner.3) | copy-start | bytes 196
  3.2 26.2 %collective-permute-start = (bf16[2,2,256,512]{3,2,1,0:T(8,128)(2,1)S(1)}, bf16[2,2,256,512]{3,2,1,0:T(8,128)(2,1)S(1)}, u32[]{:S(2)}, u32[]{:S(2)}) collective-permute-start(bf16[2,2,256,512]{3,2,1,0:T(8,128)(2,1)S(1)} %get-tuple-element.11), channel_id=1, source_target_pairs={{0,8},{8,0},{16,24},{24,16},{1,9},{9,1},{17,25},{25,17},{2,10},{10... | collective-permute-start | bytes 3145736 | tf_op jit(solution)/shard_map/ppermute | solution.py:21
  6.2 32.6 %collective-permute-start.3 = (bf16[5,2,128,512]{3,2,1,0:T(8,128)(2,1)S(1)}, bf16[5,2,128,512]{3,2,1,0:T(8,128)(2,1)S(1)}, u32[]{:S(2)}, u32[]{:S(2)}) collective-permute-start(bf16[5,2,128,512]{3,2,1,0:T(8,128)(2,1)S(1)} %get-tuple-element.13), channel_id=1, source_target_pairs={{0,7},{1,2},{2,1},{3,4},{4,3},{5,6},{6,5},{7,0},{8,15},{9,10},{10,... | collective-permute-start | bytes 3932168 | tf_op jit(solution)/shard_map/ppermute | solution.py:31
  8.9 24.0 %collective-permute-start.1 = (bf16[2,2,256,512]{3,2,1,0:T(8,128)(2,1)S(1)}, bf16[2,2,256,512]{3,2,1,0:T(8,128)(2,1)S(1)}, u32[]{:S(2)}, u32[]{:S(2)}) collective-permute-start(bf16[2,2,256,512]{3,2,1,0:T(8,128)(2,1)S(1)} %get-tuple-element.12), channel_id=1, source_target_pairs={{0,16},{8,24},{16,0},{24,8},{1,17},{9,25},{17,1},{25,9},{2,18},{10... | collective-permute-start | bytes 3145736 | tf_op jit(solution)/shard_map/ppermute | solution.py:21
  29.3 15.3 %collective-permute-start.6 = (bf16[2,2,256,512]{3,2,1,0:T(8,128)(2,1)S(1)}, bf16[2,2,256,512]{3,2,1,0:T(8,128)(2,1)S(1)}, u32[]{:S(2)}, u32[]{:S(2)}) collective-permute-start(bf16[2,2,256,512]{3,2,1,0:T(8,128)(2,1)S(1)} %collective-permute-done.refs_0_), channel_id=1, source_target_pairs={{0,1},{1,0},{2,3},{3,2},{4,5},{5,4},{6,7},{7,6},{8,9},{9,8},{10,11... | collective-permute-start | bytes 3145736 | tf_op jit(solution)/shard_map/ppermute | solution.py:26
  32.9 11.7 %collective-permute-start.7 = (bf16[2,2,256,512]{3,2,1,0:T(8,128)(2,1)S(1)}, bf16[2,2,256,512]{3,2,1,0:T(8,128)(2,1)S(1)}, u32[]{:S(2)}, u32[]{:S(2)}) collective-permute-start(bf16[2,2,256,512]{3,2,1,0:T(8,128)(2,1)S(1)} %collective-permute-done.1.refs_1_), channel_id=1, source_target_pairs={{0,1},{1,0},{2,3},{3,2},{4,5},{5,4},{6,7},{7,6},{8,9},{9,8},{10,11... | collective-permute-start | bytes 3145736 | tf_op jit(solution)/shard_map/ppermute | solution.py:26
  33.0 9.3 %copy-start.4 = (f32[8,256]{1,0:T(8,128)S(1)}, f32[8,256]{1,0:T(8,128)}, u32[]{:S(2)}) copy-start(f32[8,256]{1,0:T(8,128)} %param.8) | copy-start | bytes 24580
  33.0 9.2 %copy-start.5 = (s32[8,256]{1,0:T(8,128)S(1)}, s32[8,256]{1,0:T(8,128)}, u32[]{:S(2)}) copy-start(s32[8,256]{1,0:T(8,128)} %param.9) | copy-start | bytes 24580
  33.0 10.0 %copy-start.2 = (f32[8,8]{1,0:T(8,128)S(1)}, f32[8,8]{1,0:T(8,128)}, u32[]{:S(2)}) copy-start(f32[8,8]{1,0:T(8,128)} %occ.1) | copy-start | bytes 772
  38.9 5.8 %copy-start.1 = (bf16[2,2,1,2,256,512]{5,4,3,2,1,0:T(8,128)(2,1)S(1)}, bf16[2,2,1,2,256,512]{5,4,3,2,1,0:T(8,128)(2,1)}, u32[]{:S(2)}) copy-start(bf16[2,2,1,2,256,512]{5,4,3,2,1,0:T(8,128)(2,1)} %factor.7) | copy-start | bytes 6291460
  38.9 16.8 %collective-permute-start.4 = (bf16[3,2,128,512]{3,2,1,0:T(8,128)(2,1)S(1)}, bf16[3,2,128,512]{3,2,1,0:T(8,128)(2,1)S(1)}, u32[]{:S(2)}, u32[]{:S(2)}) collective-permute-start(bf16[3,2,128,512]{3,2,1,0:T(8,128)(2,1)S(1)} %slice.14), channel_id=1, source_target_pairs={{0,8},{8,0},{16,24},{24,16},{1,9},{9,1},{17,25},{25,17},{2,10},{10... | collective-permute-start | bytes 2359304 | tf_op jit(solution)/shard_map/ppermute | solution.py:21
  39.0 21.0 %collective-permute-start.2 = (bf16[3,2,128,512]{3,2,1,0:T(8,128)(2,1)S(1)}, bf16[3,2,128,512]{3,2,1,0:T(8,128)(2,1)S(1)}, u32[]{:S(2)}, u32[]{:S(2)}) collective-permute-start(bf16[3,2,128,512]{3,2,1,0:T(8,128)(2,1)S(1)} %pad_maximum_fusion), channel_id=1, source_target_pairs={{0,7},{1,2},{2,1},{3,4},{4,3},{5,6},{6,5},{7,0},{8,15},{9,10},{10,... | collective-permute-start | bytes 2359304 | tf_op jit(solution)/shard_map/ppermute | solution.py:31
  40.7 11.1 %collective-permute-start.5 = (bf16[2,2,128,512]{3,2,1,0:T(8,128)(2,1)S(1)}, bf16[2,2,128,512]{3,2,1,0:T(8,128)(2,1)S(1)}, u32[]{:S(2)}, u32[]{:S(2)}) collective-permute-start(bf16[2,2,128,512]{3,2,1,0:T(8,128)(2,1)S(1)} %slice.15), channel_id=1, source_target_pairs={{0,16},{8,24},{16,0},{24,8},{1,17},{9,25},{17,1},{25,9},{2,18},{10... | collective-permute-start | bytes 1572872 | tf_op jit(solution)/shard_map/ppermute | solution.py:21

commit v5 on v4

v5 whole, which is shorter than its diff:
```python
import functools

import jax
import jax.numpy as jnp
from jax import lax
from jax.experimental import pallas as pl
from jax.experimental.pallas import tpu as pltpu
from jax.sharding import PartitionSpec as P

F32 = jnp.float32
BF16 = jnp.bfloat16
ANY = pl.BlockSpec(memory_space=pl.ANY)
VMEM = pl.BlockSpec(memory_space=pltpu.VMEM)
SMEM = pl.BlockSpec(memory_space=pltpu.SMEM)
PARAMS = pltpu.CompilerParams(vmem_limit_bytes=20 * 1024 * 1024)
COST = pl.CostEstimate(flops=0, bytes_accessed=0, transcendentals=0)


def group_swap(block, bit):
    count = lax.axis_size("kpt")
    return lax.ppermute(block, "kpt", [(g, g ^ (1 << bit)) for g in range(count)])


def near_swap(block):
    count = lax.axis_size("occ")
    return lax.ppermute(block, "occ", [(i, i ^ 1) for i in range(count)])


def far_swap(block):
    count = lax.axis_size("occ")
    return lax.ppermute(
        block, "occ", [(i, (i + (1 if i % 2 else count - 1)) % count) for i in range(count)]
    )


def virtual_energies(vir_sorted, vir_order):
    ranks = jnp.arange(vir_sorted.shape[1], dtype=jnp.int32)
    matches = vir_order[:, :, None] == ranks[None, None, :]
    return jnp.sum(jnp.where(matches, vir_sorted[:, None, :], 0.0), axis=2)


def column_of(row):
    return jnp.transpose(jnp.broadcast_to(row, (8, row.shape[1])))[:, :1]


def pack_kernel(bits, partner, factor, early, *refs):
    lates, sems = refs[:-1], refs[-1]
    kc, half = factor.shape[1], early.shape[2]
    group = lax.axis_index("kpt")
    copies = []
    for transfer, bit in enumerate(bits):
        far_group = jnp.bitwise_xor(group, 1 << bit)
        for k in range(kc):
            slot = partner[transfer, far_group * kc + k] - group * kc
            block = factor.at[transfer, slot, 0]
            targets = (early.at[transfer * kc + k], lates[transfer].at[k])
            for h, target in enumerate(targets):
                source = block.at[:, pl.ds(h * half, half), :]
                copies.append(pltpu.make_async_copy(source, target, sems.at[len(copies)]))
                copies[-1].start()
    for copy in copies:
        copy.wait()


def pack(bits, partner, factor):
    transfers, kc, _, parts, nv, naux = factor.shape
    counts = [transfers * kc] + [kc] * transfers
    return pl.pallas_call(
        functools.partial(pack_kernel, bits),
        out_shape=[jax.ShapeDtypeStruct((n, parts, nv // 2, naux), BF16) for n in counts],
        in_specs=[SMEM, ANY],
        out_specs=[VMEM] * len(counts),
        scratch_shapes=[pltpu.SemaphoreType.DMA((2 * transfers * kc,))],
        cost_estimate=COST,
        compiler_params=PARAMS,
    )(
        pltpu.with_memory_space_constraint(partner, pltpu.HBM),
        pltpu.with_memory_space_constraint(factor, pltpu.HBM),
    )


def inverse_kernel(bits, partner, occ, virtual, out):
    _, _, kc, nv, _ = out.shape
    total = occ.shape[1]
    group, orbit = lax.axis_index("kpt"), lax.axis_index("occ")
    parity = lax.rem(orbit, 2)
    columns = (orbit, orbit + 1 - 2 * parity, lax.rem(orbit + total - 1 + 2 * parity, total))

    def point_step(k, carry):
        point = group * kc + k
        row = virtual[pl.ds(point, 1), :]
        for transfer in range(len(bits)):
            far_point = partner[transfer, point]
            column = column_of(virtual[pl.ds(far_point, 1), :])
            for place, index in enumerate(columns):
                level = occ[point, orbit] + occ[far_point, index]
                out[transfer, place, k] = 1.0 / ((level - column) - row)
        return carry

    lax.fori_loop(0, kc, point_step, 0)


def inverses(bits, partner, occ_energy, virtual, kc):
    nv = virtual.shape[1]
    return pl.pallas_call(
        functools.partial(inverse_kernel, bits),
        out_shape=jax.ShapeDtypeStruct((len(bits), 3, kc, nv, nv), F32),
        in_specs=[SMEM, SMEM, VMEM],
        out_specs=VMEM,
        cost_estimate=COST,
        compiler_params=PARAMS,
    )(partner, occ_energy, virtual)


def gradient_sum(own, terms, base):
    _, nv, naux = own.shape
    left = own.reshape(2 * nv, naux)
    amplitudes, blocks = [], []
    for window, inverse in terms:
        size = window.shape[1]
        window = window.reshape(2 * size, naux)
        products = lax.dot_general(
            left, window, (((1,), (1,)), ((), ())), preferred_element_type=F32
        )
        real_part = ((products[:nv, :size] + products[nv:, size:]) * inverse).astype(BF16)
        imag_part = ((products[nv:, :size] - products[:nv, size:]) * inverse).astype(BF16)
        upper = jnp.concatenate([real_part, -imag_part], axis=1)
        lower = jnp.concatenate([imag_part, real_part], axis=1)
        amplitudes.append(jnp.concatenate([upper, lower], axis=0))
        blocks.append(window)
    gradient = jnp.dot(
        jnp.concatenate(amplitudes, axis=1),
        jnp.concatenate(blocks, axis=0),
        preferred_element_type=F32,
    ).reshape(2, nv, naux)
    return gradient if base is None else gradient + base


def half_of(h, half):
    return slice(h * half, (h + 1) * half)


def first_kernel(factor, inverse, *refs):
    transfers, kc = factor.shape[:2]
    owns, nears, out = refs[: 2 * transfers], refs[2 * transfers : -1], refs[-1]
    half = nears[0].shape[2]

    def point_step(k, carry):
        for t in range(transfers):
            terms = []
            for h in range(2):
                rows = half_of(h, half)
                terms.append((owns[h * transfers + t][k], inverse[t, 0, k, :, rows]))
                terms.append((nears[h][t * kc + k], inverse[t, 1, k, :, rows]))
            out[t, k] = gradient_sum(factor[t, k, 0], terms, None)
        return carry

    lax.fori_loop(0, kc, point_step, 0)


def first_terms(factor, inverse, owns, nears):
    transfers, kc, _, parts, nv, naux = factor.shape
    operands = [factor, inverse, *owns, *nears]
    return pl.pallas_call(
        first_kernel,
        out_shape=jax.ShapeDtypeStruct((transfers, kc, parts, nv, naux), F32),
        in_specs=[VMEM] * len(operands),
        out_specs=VMEM,
        cost_estimate=COST,
        compiler_params=PARAMS,
    )(*operands)


def early_kernel(factor, inverse, *refs):
    windows, total, out = refs[:-2], refs[-2], refs[-1]
    half = windows[0].shape[2]

    def point_step(k, carry):
        for t, window in enumerate(windows):
            terms = [(window[k], inverse[t, 2, k, :, half_of(0, half)])]
            out[t, k] = gradient_sum(factor[t, k, 0], terms, total[t, k])
        return carry

    lax.fori_loop(0, factor.shape[1], point_step, 0)


def early_terms(factor, inverse, windows, total):
    operands = [factor, inverse, *windows, total]
    return pl.pallas_call(
        early_kernel,
        out_shape=jax.ShapeDtypeStruct(total.shape, F32),
        in_specs=[VMEM] * len(operands),
        out_specs=VMEM,
        input_output_aliases={len(operands) - 1: 0},
        cost_estimate=COST,
        compiler_params=PARAMS,
    )(*operands)


def last_kernel(factor, inverse, window, total, out, staged, sems):
    transfers, kc = factor.shape[:2]
    half = window.shape[2]
    copies = []
    for t in range(transfers):
        for k in range(kc):
            at = t * kc + k
            terms = [(window[at], inverse[t, 2, k, :, half_of(1, half)])]
            staged[at] = gradient_sum(factor[t, k, 0], terms, total[t, k]).astype(BF16)
            copies.append(pltpu.make_async_copy(staged.at[at], out.at[t, k, 0], sems.at[at]))
            copies[-1].start()
    for copy in copies:
        copy.wait()


def last_terms(factor, inverse, window, total):
    count = window.shape[0]
    _, _, _, parts, nv, naux = factor.shape
    return pl.pallas_call(
        last_kernel,
        out_shape=jax.ShapeDtypeStruct(factor.shape, BF16),
        in_specs=[VMEM] * 4,
        out_specs=ANY,
        scratch_shapes=[
            pltpu.VMEM((count, parts, nv, naux), BF16),
            pltpu.SemaphoreType.DMA((count,)),
        ],
        cost_estimate=COST,
        compiler_params=PARAMS,
    )(factor, inverse, window, total)


def body(factor, partner, occ_energy, vir_sorted, vir_order):
    transfers, kc = factor.shape[:2]
    bits = (0, lax.axis_size("kpt").bit_length() - 2)

    part, *lates = pack(bits, partner, factor)
    beside = far_swap(part)
    late_own = [group_swap(lates[t], bits[t]) for t in range(transfers)]
    early_own = [group_swap(part[t * kc : (t + 1) * kc], bits[t]) for t in range(transfers)]
    late_block = jnp.concatenate(late_own)
    late_far = far_swap(late_block)
    late_near = near_swap(late_block)
    early_near = near_swap(jnp.concatenate(lax.optimization_barrier((*early_own, late_block))[:-1]))
    early_far = [group_swap(beside[t * kc : (t + 1) * kc], bits[t]) for t in range(transfers)]

    virtual = virtual_energies(vir_sorted, vir_order)
    inverse = inverses(bits, partner, occ_energy, virtual, kc)
    total = first_terms(factor, inverse, early_own + late_own, [early_near, late_near])
    total = early_terms(factor, inverse, early_far, total)
    return last_terms(factor, inverse, late_far, total)


def solution(mesh):
    spec = P(None, "kpt", "occ", None, None, None)
    in_specs = (spec, P(), P(), P(), P())
    return jax.shard_map(body, mesh=mesh, in_specs=in_specs, out_specs=spec, check_vma=False)
```

time: 62.6 us -> 60.3 us (0.963)
  waiting for transfers between devices: 36.3 us -> 30.7 us
  starting transfers between devices: 10.6 us -> 14.1 us
  local copies, waits for them, and re-layouts: 2.46 us -> 0.27 us
  Pallas kernels: 12.1 us -> 14.1 us
    ppermute x4 -> x6, waiting for transfers between devices: 28.5 us -> 23.6 us  [group_swap(): return lax.ppermute(block, 'kpt', [(g, g ^ 1 << bit) for g in range(count)])]
    unnamed x12 -> x11, local copies, waits for them, and re-layouts: 2.29 us -> 0.07 us
    pallas_call x4, Pallas kernels: 10.5 us -> 12.5 us  [the longest x1 4.74 us: first_terms(): pl.pallas_call(first_kernel, out_shape=jax.ShapeDtypeStruct((transfers, k...]
    ppermute x4 -> x6, starting transfers between devices: 6.18 us -> 7.75 us  [group_swap(): return lax.ppermute(block, 'kpt', [(g, g ^ 1 << bit) for g in range(count)])]
    ppermute x2, starting transfers between devices: 4.43 us -> 5.77 us  [far_swap(): lax.ppermute(block, 'occ', [(i, (i + (1 if i % 2 else count - 1)) % count...]
    ppermute x2, waiting for transfers between devices: 7.81 us -> 7.11 us  [far_swap(): lax.ppermute(block, 'occ', [(i, (i + (1 if i % 2 else count - 1)) % count...]
  transfers between devices with their start and end apart: 8 -> 10, of which waited for: 6 -> 6; matrix products, arithmetic and copies ran while one was open for 2% -> 2% of each run, Pallas kernels for 14% -> 15%
where the time goes in v5:
time: 60.3 us; the launch traced here: 60.2 us
  waiting for transfers between devices  30.7 us (51%)
  Pallas kernels  14.1 us (23%)
  starting transfers between devices  14.1 us (23%)
  other arithmetic  0.85 us (1%)
    ppermute x6, waiting for transfers between devices, group_swap(): return lax.ppermute(block, 'kpt', [(g, g ^ 1 << bit) for g in range(count)])  23.6 us
    ppermute x6, starting transfers between devices, group_swap(): return lax.ppermute(block, 'kpt', [(g, g ^ 1 << bit) for g in range(count)])  7.75 us
    ppermute x2, waiting for transfers between devices, far_swap(): lax.ppermute(block, 'occ', [(i, (i + (1 if i % 2 else count - 1)) % count...  7.11 us
    ppermute x2, starting transfers between devices, far_swap(): lax.ppermute(block, 'occ', [(i, (i + (1 if i % 2 else count - 1)) % count...  5.77 us
    pallas_call x1, Pallas kernels, first_terms(): pl.pallas_call(first_kernel, out_shape=jax.ShapeDtypeStruct((transfers, k...  4.74 us
    pallas_call x1, Pallas kernels, early_terms(): pl.pallas_call(early_kernel, out_shape=jax.ShapeDtypeStruct(total.shape,...  2.75 us
    pallas_call x1, Pallas kernels, last_terms(): pl.pallas_call(last_kernel, out_shape=jax.ShapeDtypeStruct(factor.shape,...  2.74 us
    pallas_call x1, Pallas kernels, pack(): pl.pallas_call(functools.partial(pack_kernel, bits), out_shape=[jax.Shape...  2.27 us
  transfers between devices with their start and end apart: 10, of which 6 were waited for; matrix products, arithmetic and copies ran while one was open for 2% of the time, Pallas kernels for 15%

profile of v5, /device:TPU:0, one launch (start us, length us, event | category | flops | bytes accessed | tf_op | source)
XLA Modules:
  0.0 60.2 jit_solution(6527990307729277847)
XLA Ops:
  0.0 2.3 %shard_map.56 = (bf16[4,2,128,512]{3,2,1,0:T(8,128)(2,1)S(1)}, bf16[2,2,128,512]{3,2,1,0:T(8,128)(2,1)S(1)}, bf16[2,2,128,512]{3,2,1,0:T(8,128)(2,1)S(1)}) custom-call(s32[2,8]{1,0:T(2,128)} %partner.3, bf16[2,2,1,2,256,512]{5,4,3,2,1,0:T(8,128)(2,1)} %factor.7), custom_call_target="tpu_custom_call" | custom-call | tf_op jit(solution)/shard_map/pallas_call | solution.py:68
  2.3 3.0 %collective-permute-start = (bf16[2,2,128,512]{3,2,1,0:T(8,128)(2,1)S(1)}, bf16[2,2,128,512]{3,2,1,0:T(8,128)(2,1)S(1)}, u32[]{:S(2)}, u32[]{:S(2)}) collective-permute-start(bf16[2,2,128,512]{3,2,1,0:T(8,128)(2,1)S(1)} %get-tuple-element.10), channel_id=1, source_target_pairs={{0,8},{8,0},{16,24},{24,16},{1,9},{9,1},{17,25},{25,17},{2,10},{10... | collective-permute-start | bytes 1572872 | tf_op jit(solution)/shard_map/ppermute | solution.py:21
  5.3 1.6 %collective-permute-start.1 = (bf16[2,2,128,512]{3,2,1,0:T(8,128)(2,1)S(1)}, bf16[2,2,128,512]{3,2,1,0:T(8,128)(2,1)S(1)}, u32[]{:S(2)}, u32[]{:S(2)}) collective-permute-start(bf16[2,2,128,512]{3,2,1,0:T(8,128)(2,1)S(1)} %get-tuple-element.11), channel_id=1, source_target_pairs={{0,16},{8,24},{16,0},{24,8},{1,17},{9,25},{17,1},{25,9},{2,18},{10... | collective-permute-start | bytes 1572872 | tf_op jit(solution)/shard_map/ppermute | solution.py:21
  6.9 2.5 %collective-permute-start.3 = (bf16[4,2,128,512]{3,2,1,0:T(8,128)(2,1)S(1)}, bf16[4,2,128,512]{3,2,1,0:T(8,128)(2,1)S(1)}, u32[]{:S(2)}, u32[]{:S(2)}) collective-permute-start(bf16[4,2,128,512]{3,2,1,0:T(8,128)(2,1)S(1)} %get-tuple-element.12), channel_id=1, source_target_pairs={{0,7},{1,2},{2,1},{3,4},{4,3},{5,6},{6,5},{7,0},{8,15},{9,10},{10,... | collective-permute-start | bytes 3145736 | tf_op jit(solution)/shard_map/ppermute | solution.py:31
  9.4 0.1 fusion
  9.5 0.5 collective-permute-start.7
  10.0 0.5 collective-permute-start.6
  10.5 7.5 %collective-permute-done.refs_2_ = bf16[2,2,128,512]{3,2,1,0:T(8,128)(2,1)S(1)} collective-permute-done((bf16[2,2,128,512]{3,2,1,0:T(8,128)(2,1)S(1)}, bf16[2,2,128,512]{3,2,1,0:T(8,128)(2,1)S(1)}, u32[]{:S(2)}, u32[]{:S(2)}) %collective-permute-start) | collective-permute-done | bytes 524320 | tf_op jit(solution)/shard_map/ppermute | solution.py:21
  18.1 2.1 %collective-permute-done.1.refs_3_ = bf16[2,2,128,512]{3,2,1,0:T(8,128)(2,1)S(1)} collective-permute-done((bf16[2,2,128,512]{3,2,1,0:T(8,128)(2,1)S(1)}, bf16[2,2,128,512]{3,2,1,0:T(8,128)(2,1)S(1)}, u32[]{:S(2)}, u32[]{:S(2)}) %collective-permute-start.1) | collective-permute-done | bytes 524320 | tf_op jit(solution)/shard_map/ppermute | solution.py:21
  20.2 0.0 copy-start.3
  20.2 0.0 copy-start.4
  20.2 0.0 copy-start.1
  20.2 0.0 copy-start.2
  20.2 9.7 %collective-permute-done.7.refs_1_ = bf16[2,2,128,512]{3,2,1,0:T(8,128)(2,1)S(1)} collective-permute-done((bf16[2,2,128,512]{3,2,1,0:T(8,128)(2,1)S(1)}, bf16[2,2,128,512]{3,2,1,0:T(8,128)(2,1)S(1)}, u32[]{:S(2)}, u32[]{:S(2)}) %collective-permute-start.7) | collective-permute-done | bytes 524320 | tf_op jit(solution)/shard_map/ppermute | solution.py:21
  29.9 0.0 collective-permute-done.6.refs_0_
  29.9 0.1 pad_maximum_fusion
  30.0 0.1 collective-permute-start.8
  30.1 0.5 collective-permute-start.9
  30.6 3.3 %collective-permute-start.2 = (bf16[4,2,128,512]{3,2,1,0:T(8,128)(2,1)S(1)}, bf16[4,2,128,512]{3,2,1,0:T(8,128)(2,1)S(1)}, u32[]{:S(2)}, u32[]{:S(2)}) collective-permute-start(bf16[4,2,128,512]{3,2,1,0:T(8,128)(2,1)S(1)} %constant_dynamic-update-slice_fusion), channel_id=1, source_target_pairs={{0,7},{1,2},{2,1},{3,4},{4,3},{5,6},{6,5},{7,0},{8,15},{9,10},{10,... | collective-permute-start | bytes 3145736 | tf_op jit(solution)/shard_map/ppermute | solution.py:31
  33.9 0.0 collective-permute-done.3
  33.9 0.1 fusion.1
  33.9 0.0 copy-start
  34.0 1.7 %collective-permute-start.5 = (bf16[2,2,128,512]{3,2,1,0:T(8,128)(2,1)S(1)}, bf16[2,2,128,512]{3,2,1,0:T(8,128)(2,1)S(1)}, u32[]{:S(2)}, u32[]{:S(2)}) collective-permute-start(bf16[2,2,128,512]{3,2,1,0:T(8,128)(2,1)S(1)} %get-tuple-element.17), channel_id=1, source_target_pairs={{0,16},{8,24},{16,0},{24,8},{1,17},{9,25},{17,1},{25,9},{2,18},{10... | collective-permute-start | bytes 1572872 | tf_op jit(solution)/shard_map/ppermute | solution.py:21
  35.6 0.5 collective-permute-start.4
  36.1 0.0 copy-done.3
  36.1 0.0 copy-done.4
  36.1 0.8 %select_reduce_fusion.virtual = f32[8,256]{1,0:T(8,128)S(1)} fusion(f32[8,256]{1,0:T(8,128)S(1)} %copy-done.3, s32[8,256]{1,0:T(8,128)S(1)} %copy-done.4), kind=kLoop, calls=%fused_computation | loop fusion | flops 1570816 | bytes 24576 | tf_op jit(solution)/shard_map/reduce_sum | solution.py:39
  36.8 0.0 copy-done.1
  36.9 0.0 copy-done.2
  36.9 1.6 %shard_map.55.inverse = f32[2,3,2,256,256]{4,3,2,1,0:T(8,128)S(1)} custom-call(s32[2,8]{1,0:T(2,128)S(1)} %copy-done.2, f32[8,8]{1,0:T(8,128)S(1)} %copy-done.1, f32[8,256]{1,0:T(8,128)S(1)} %select_reduce_fusion.virtual), custom_call_target="tpu_custom_call" | custom-call | tf_op jit(solution)/shard_map/pallas_call | solution.py:105
  38.5 0.0 collective-permute-done.8.refs_4_
  38.5 0.0 collective-permute-done.9.refs_5_
  38.5 0.0 copy-done
  38.5 4.7 %shard_map.57.refs_2_ = f32[2,2,2,256,512]{4,3,2,1,0:T(8,128)S(1)} custom-call(bf16[2,2,1,2,256,512]{5,4,3,2,1,0:T(8,128)(2,1)S(1)} %copy-done, f32[2,3,2,256,256]{4,3,2,1,0:T(8,128)S(1)} %shard_map.55.inverse, bf16[2,2,128,512]{3,2,1,0:T(8,128)(2,1)S(1)} %collective-permute-done.6.refs_0_, bf16[2,2,128,512]{3,2,1,0:T(8,128)(2,1)S(1)} %collective-permute-done.7.refs_1_, ...), custom_call_target="tpu_custom_call" | custom-call | tf_op jit(solution)/shard_map/pallas_call | solution.py:164
  43.2 3.0 %collective-permute-done.5.refs_1_ = bf16[2,2,128,512]{3,2,1,0:T(8,128)(2,1)S(1)} collective-permute-done((bf16[2,2,128,512]{3,2,1,0:T(8,128)(2,1)S(1)}, bf16[2,2,128,512]{3,2,1,0:T(8,128)(2,1)S(1)}, u32[]{:S(2)}, u32[]{:S(2)}) %collective-permute-start.5) | collective-permute-done | bytes 524320 | tf_op jit(solution)/shard_map/ppermute | solution.py:21
  46.3 1.3 %collective-permute-done.4.refs_0_ = bf16[2,2,128,512]{3,2,1,0:T(8,128)(2,1)S(1)} collective-permute-done((bf16[2,2,128,512]{3,2,1,0:T(8,128)(2,1)S(1)}, bf16[2,2,128,512]{3,2,1,0:T(8,128)(2,1)S(1)}, u32[]{:S(2)}, u32[]{:S(2)}) %collective-permute-start.4) | collective-permute-done | bytes 524320 | tf_op jit(solution)/shard_map/ppermute | solution.py:21
  47.6 2.7 %shard_map.58.total = f32[2,2,2,256,512]{4,3,2,1,0:T(8,128)S(1)} custom-call(bf16[2,2,1,2,256,512]{5,4,3,2,1,0:T(8,128)(2,1)S(1)} %copy-done, f32[2,3,2,256,256]{4,3,2,1,0:T(8,128)S(1)} %shard_map.55.inverse, bf16[2,2,128,512]{3,2,1,0:T(8,128)(2,1)S(1)} %collective-permute-done.4.refs_0_, ...), custom_call_target="tpu_custom_call", output_to_operand_aliasing={{}: (4, {})} | custom-call | tf_op jit(solution)/shard_map/pallas_call | solution.py:189
  50.3 7.1 %collective-permute-done.2.window = bf16[4,2,128,512]{3,2,1,0:T(8,128)(2,1)S(1)} collective-permute-done((bf16[4,2,128,512]{3,2,1,0:T(8,128)(2,1)S(1)}, bf16[4,2,128,512]{3,2,1,0:T(8,128)(2,1)S(1)}, u32[]{:S(2)}, u32[]{:S(2)}) %collective-permute-start.2) | collective-permute-done | bytes 1048608 | tf_op jit(solution)/shard_map/ppermute | solution.py:31
  57.4 2.7 %shard_map.59 = bf16[2,2,1,2,256,512]{5,4,3,2,1,0:T(8,128)(2,1)} custom-call(bf16[2,2,1,2,256,512]{5,4,3,2,1,0:T(8,128)(2,1)S(1)} %copy-done, f32[2,3,2,256,256]{4,3,2,1,0:T(8,128)S(1)} %shard_map.55.inverse, bf16[4,2,128,512]{3,2,1,0:T(8,128)(2,1)S(1)} %collective-permute-done.2.window, f32[2,2,2,256,512]{4,3,2,1,0:T(8,128)S(1)} %shard_map.58.total), custom_call_target="tpu_custom_call" | custom-call | tf_op jit(solution)/shard_map/pallas_call | solution.py:218
  (2 shorter events, 0.1 us)
Async XLA Ops:
  2.3 15.8 %collective-permute-start = (bf16[2,2,128,512]{3,2,1,0:T(8,128)(2,1)S(1)}, bf16[2,2,128,512]{3,2,1,0:T(8,128)(2,1)S(1)}, u32[]{:S(2)}, u32[]{:S(2)}) collective-permute-start(bf16[2,2,128,512]{3,2,1,0:T(8,128)(2,1)S(1)} %get-tuple-element.10), channel_id=1, source_target_pairs={{0,8},{8,0},{16,24},{24,16},{1,9},{9,1},{17,25},{25,17},{2,10},{10... | collective-permute-start | bytes 1572872 | tf_op jit(solution)/shard_map/ppermute | solution.py:21
  5.3 14.8 %collective-permute-start.1 = (bf16[2,2,128,512]{3,2,1,0:T(8,128)(2,1)S(1)}, bf16[2,2,128,512]{3,2,1,0:T(8,128)(2,1)S(1)}, u32[]{:S(2)}, u32[]{:S(2)}) collective-permute-start(bf16[2,2,128,512]{3,2,1,0:T(8,128)(2,1)S(1)} %get-tuple-element.11), channel_id=1, source_target_pairs={{0,16},{8,24},{16,0},{24,8},{1,17},{9,25},{17,1},{25,9},{2,18},{10... | collective-permute-start | bytes 1572872 | tf_op jit(solution)/shard_map/ppermute | solution.py:21
  6.9 27.0 %collective-permute-start.3 = (bf16[4,2,128,512]{3,2,1,0:T(8,128)(2,1)S(1)}, bf16[4,2,128,512]{3,2,1,0:T(8,128)(2,1)S(1)}, u32[]{:S(2)}, u32[]{:S(2)}) collective-permute-start(bf16[4,2,128,512]{3,2,1,0:T(8,128)(2,1)S(1)} %get-tuple-element.12), channel_id=1, source_target_pairs={{0,7},{1,2},{2,1},{3,4},{4,3},{5,6},{6,5},{7,0},{8,15},{9,10},{10,... | collective-permute-start | bytes 3145736 | tf_op jit(solution)/shard_map/ppermute | solution.py:31
  9.5 20.4 %collective-permute-start.7 = (bf16[2,2,128,512]{3,2,1,0:T(8,128)(2,1)S(1)}, bf16[2,2,128,512]{3,2,1,0:T(8,128)(2,1)S(1)}, u32[]{:S(2)}, u32[]{:S(2)}) collective-permute-start(bf16[2,2,128,512]{3,2,1,0:T(8,128)(2,1)S(1)} %get-tuple-element.15), channel_id=1, source_target_pairs={{0,16},{8,24},{16,0},{24,8},{1,17},{9,25},{17,1},{25,9},{2,18},{10... | collective-permute-start | bytes 1572872 | tf_op jit(solution)/shard_map/ppermute | solution.py:21
  10.0 19.9 %collective-permute-start.6 = (bf16[2,2,128,512]{3,2,1,0:T(8,128)(2,1)S(1)}, bf16[2,2,128,512]{3,2,1,0:T(8,128)(2,1)S(1)}, u32[]{:S(2)}, u32[]{:S(2)}) collective-permute-start(bf16[2,2,128,512]{3,2,1,0:T(8,128)(2,1)S(1)} %get-tuple-element.16), channel_id=1, source_target_pairs={{0,8},{8,0},{16,24},{24,16},{1,9},{9,1},{17,25},{25,17},{2,10},{10... | collective-permute-start | bytes 1572872 | tf_op jit(solution)/shard_map/ppermute | solution.py:21
  20.2 15.9 %copy-start.3 = (f32[8,256]{1,0:T(8,128)S(1)}, f32[8,256]{1,0:T(8,128)}, u32[]{:S(2)}) copy-start(f32[8,256]{1,0:T(8,128)} %param.8) | copy-start | bytes 24580
  20.2 15.9 %copy-start.4 = (s32[8,256]{1,0:T(8,128)S(1)}, s32[8,256]{1,0:T(8,128)}, u32[]{:S(2)}) copy-start(s32[8,256]{1,0:T(8,128)} %param.9) | copy-start | bytes 24580
  20.2 16.6 %copy-start.1 = (f32[8,8]{1,0:T(8,128)S(1)}, f32[8,8]{1,0:T(8,128)}, u32[]{:S(2)}) copy-start(f32[8,8]{1,0:T(8,128)} %occ.1) | copy-start | bytes 772
  20.2 16.6 %copy-start.2 = (s32[2,8]{1,0:T(2,128)S(1)}, s32[2,8]{1,0:T(2,128)}, u32[]{:S(2)}) copy-start(s32[2,8]{1,0:T(2,128)} %partner.3) | copy-start | bytes 196
  30.0 8.5 %collective-permute-start.8 = (bf16[4,2,128,512]{3,2,1,0:T(8,128)(2,1)S(1)}, bf16[4,2,128,512]{3,2,1,0:T(8,128)(2,1)S(1)}, u32[]{:S(2)}, u32[]{:S(2)}) collective-permute-start(bf16[4,2,128,512]{3,2,1,0:T(8,128)(2,1)S(1)} %pad_maximum_fusion), channel_id=1, source_target_pairs={{0,1},{1,0},{2,3},{3,2},{4,5},{5,4},{6,7},{7,6},{8,9},{9,8},{10,11... | collective-permute-start | bytes 3145736 | tf_op jit(solution)/shard_map/ppermute | solution.py:26
  30.1 8.4 %collective-permute-start.9 = (bf16[4,2,128,512]{3,2,1,0:T(8,128)(2,1)S(1)}, bf16[4,2,128,512]{3,2,1,0:T(8,128)(2,1)S(1)}, u32[]{:S(2)}, u32[]{:S(2)}) collective-permute-start(bf16[4,2,128,512]{3,2,1,0:T(8,128)(2,1)S(1)} %constant_dynamic-update-slice_fusion), channel_id=1, source_target_pairs={{0,1},{1,0},{2,3},{3,2},{4,5},{5,4},{6,7},{7,6},{8,9},{9,8},{10,11... | collective-permute-start | bytes 3145736 | tf_op jit(solution)/shard_map/ppermute | solution.py:26
  30.6 26.8 %collective-permute-start.2 = (bf16[4,2,128,512]{3,2,1,0:T(8,128)(2,1)S(1)}, bf16[4,2,128,512]{3,2,1,0:T(8,128)(2,1)S(1)}, u32[]{:S(2)}, u32[]{:S(2)}) collective-permute-start(bf16[4,2,128,512]{3,2,1,0:T(8,128)(2,1)S(1)} %constant_dynamic-update-slice_fusion), channel_id=1, source_target_pairs={{0,7},{1,2},{2,1},{3,4},{4,3},{5,6},{6,5},{7,0},{8,15},{9,10},{10,... | collective-permute-start | bytes 3145736 | tf_op jit(solution)/shard_map/ppermute | solution.py:31
  33.9 4.5 %copy-start = (bf16[2,2,1,2,256,512]{5,4,3,2,1,0:T(8,128)(2,1)S(1)}, bf16[2,2,1,2,256,512]{5,4,3,2,1,0:T(8,128)(2,1)}, u32[]{:S(2)}) copy-start(bf16[2,2,1,2,256,512]{5,4,3,2,1,0:T(8,128)(2,1)} %factor.7) | copy-start | bytes 6291460
  34.0 12.3 %collective-permute-start.5 = (bf16[2,2,128,512]{3,2,1,0:T(8,128)(2,1)S(1)}, bf16[2,2,128,512]{3,2,1,0:T(8,128)(2,1)S(1)}, u32[]{:S(2)}, u32[]{:S(2)}) collective-permute-start(bf16[2,2,128,512]{3,2,1,0:T(8,128)(2,1)S(1)} %get-tuple-element.17), channel_id=1, source_target_pairs={{0,16},{8,24},{16,0},{24,8},{1,17},{9,25},{17,1},{25,9},{2,18},{10... | collective-permute-start | bytes 1572872 | tf_op jit(solution)/shard_map/ppermute | solution.py:21
  35.6 12.0 %collective-permute-start.4 = (bf16[2,2,128,512]{3,2,1,0:T(8,128)(2,1)S(1)}, bf16[2,2,128,512]{3,2,1,0:T(8,128)(2,1)S(1)}, u32[]{:S(2)}, u32[]{:S(2)}) collective-permute-start(bf16[2,2,128,512]{3,2,1,0:T(8,128)(2,1)S(1)} %get-tuple-element.18), channel_id=1, source_target_pairs={{0,8},{8,0},{16,24},{24,16},{1,9},{9,1},{17,25},{25,17},{2,10},{10... | collective-permute-start | bytes 1572872 | tf_op jit(solution)/shard_map/ppermute | solution.py:21

commit v6 on v5

--- a/solution.py
+++ b/solution.py
@@ -13,6 +13,7 @@
 VMEM = pl.BlockSpec(memory_space=pltpu.VMEM)
 SMEM = pl.BlockSpec(memory_space=pltpu.SMEM)
 PARAMS = pltpu.CompilerParams(vmem_limit_bytes=20 * 1024 * 1024)
+WORK = 16
 COST = pl.CostEstimate(flops=0, bytes_accessed=0, transcendentals=0)
 
 
@@ -33,6 +34,10 @@
     )
 
 
+def after(block, *others):
+    return lax.optimization_barrier((block, *others))[0]
+
+
 def virtual_energies(vir_sorted, vir_order):
     ranks = jnp.arange(vir_sorted.shape[1], dtype=jnp.int32)
     matches = vir_order[:, :, None] == ranks[None, None, :]
@@ -43,35 +48,33 @@
     return jnp.transpose(jnp.broadcast_to(row, (8, row.shape[1])))[:, :1]
 
 
-def pack_kernel(bits, partner, factor, early, *refs):
-    lates, sems = refs[:-1], refs[-1]
-    kc, half = factor.shape[1], early.shape[2]
+def pack_kernel(bits, h, partner, factor, *refs):
+    outs, sems = refs[:-1], refs[-1]
+    kc, half = factor.shape[1], outs[0].shape[2]
+    targets = [out.at[n] for out in outs for n in range(out.shape[0])]
     group = lax.axis_index("kpt")
     copies = []
     for transfer, bit in enumerate(bits):
         far_group = jnp.bitwise_xor(group, 1 << bit)
         for k in range(kc):
             slot = partner[transfer, far_group * kc + k] - group * kc
-            block = factor.at[transfer, slot, 0]
-            targets = (early.at[transfer * kc + k], lates[transfer].at[k])
-            for h, target in enumerate(targets):
-                source = block.at[:, pl.ds(h * half, half), :]
-                copies.append(pltpu.make_async_copy(source, target, sems.at[len(copies)]))
-                copies[-1].start()
+            source = factor.at[transfer, slot, 0, :, pl.ds(h * half, half), :]
+            at = transfer * kc + k
+            copies.append(pltpu.make_async_copy(source, targets[at], sems.at[at]))
+            copies[-1].start()
     for copy in copies:
         copy.wait()
 
 
-def pack(bits, partner, factor):
-    transfers, kc, _, parts, nv, naux = factor.shape
-    counts = [transfers * kc] + [kc] * transfers
-    return pl.pallas_call(
-        functools.partial(pack_kernel, bits),
+def pack(bits, h, counts, partner, factor, work):
+    _, _, _, parts, nv, naux = factor.shape
+    return pl.pallas_call(
+        functools.partial(pack_kernel, bits, h),
         out_shape=[jax.ShapeDtypeStruct((n, parts, nv // 2, naux), BF16) for n in counts],
         in_specs=[SMEM, ANY],
         out_specs=[VMEM] * len(counts),
-        scratch_shapes=[pltpu.SemaphoreType.DMA((2 * transfers * kc,))],
-        cost_estimate=COST,
+        scratch_shapes=[pltpu.SemaphoreType.DMA((sum(counts),))],
+        cost_estimate=pl.CostEstimate(flops=0, bytes_accessed=work, transcendentals=0),
         compiler_params=PARAMS,
     )(
         pltpu.with_memory_space_constraint(partner, pltpu.HBM),
@@ -142,25 +145,26 @@
 
 def first_kernel(factor, inverse, *refs):
     transfers, kc = factor.shape[:2]
-    owns, nears, out = refs[: 2 * transfers], refs[2 * transfers : -1], refs[-1]
-    half = nears[0].shape[2]
+    owns, near, out = refs[: 2 * transfers], refs[-2], refs[-1]
+    half = near.shape[2]
 
     def point_step(k, carry):
         for t in range(transfers):
-            terms = []
-            for h in range(2):
-                rows = half_of(h, half)
-                terms.append((owns[h * transfers + t][k], inverse[t, 0, k, :, rows]))
-                terms.append((nears[h][t * kc + k], inverse[t, 1, k, :, rows]))
+            first, second = half_of(0, half), half_of(1, half)
+            terms = [
+                (owns[t][k], inverse[t, 0, k, :, first]),
+                (owns[transfers + t][k], inverse[t, 0, k, :, second]),
+                (near[t * kc + k], inverse[t, 1, k, :, first]),
+            ]
             out[t, k] = gradient_sum(factor[t, k, 0], terms, None)
         return carry
 
     lax.fori_loop(0, kc, point_step, 0)
 
 
-def first_terms(factor, inverse, owns, nears):
+def first_terms(factor, inverse, owns, near):
     transfers, kc, _, parts, nv, naux = factor.shape
-    operands = [factor, inverse, *owns, *nears]
+    operands = [factor, inverse, *owns, near]
     return pl.pallas_call(
         first_kernel,
         out_shape=jax.ShapeDtypeStruct((transfers, kc, parts, nv, naux), F32),
@@ -171,23 +175,26 @@
     )(*operands)
 
 
-def early_kernel(factor, inverse, *refs):
-    windows, total, out = refs[:-2], refs[-2], refs[-1]
-    half = windows[0].shape[2]
+def second_kernel(factor, inverse, near, *refs):
+    fars, total, out = refs[:-2], refs[-2], refs[-1]
+    kc, half = factor.shape[1], near.shape[2]
 
     def point_step(k, carry):
-        for t, window in enumerate(windows):
-            terms = [(window[k], inverse[t, 2, k, :, half_of(0, half)])]
+        for t, far in enumerate(fars):
+            terms = [
+                (near[t * kc + k], inverse[t, 1, k, :, half_of(1, half)]),
+                (far[k], inverse[t, 2, k, :, half_of(0, half)]),
+            ]
             out[t, k] = gradient_sum(factor[t, k, 0], terms, total[t, k])
         return carry
 
-    lax.fori_loop(0, factor.shape[1], point_step, 0)
-
-
-def early_terms(factor, inverse, windows, total):
-    operands = [factor, inverse, *windows, total]
-    return pl.pallas_call(
-        early_kernel,
+    lax.fori_loop(0, kc, point_step, 0)
+
+
+def second_terms(factor, inverse, near, fars, total):
+    operands = [factor, inverse, near, *fars, total]
+    return pl.pallas_call(
+        second_kernel,
         out_shape=jax.ShapeDtypeStruct(total.shape, F32),
         in_specs=[VMEM] * len(operands),
         out_specs=VMEM,
@@ -233,20 +240,24 @@
     transfers, kc = factor.shape[:2]
     bits = (0, lax.axis_size("kpt").bit_length() - 2)
 
-    part, *lates = pack(bits, partner, factor)
+    (part,) = pack(bits, 0, [transfers * kc], partner, factor, 0)
     beside = far_swap(part)
+    lates = pack(bits, 1, [kc] * transfers, after(partner, part), factor, WORK * factor.size)
     late_own = [group_swap(lates[t], bits[t]) for t in range(transfers)]
     early_own = [group_swap(part[t * kc : (t + 1) * kc], bits[t]) for t in range(transfers)]
     late_block = jnp.concatenate(late_own)
     late_far = far_swap(late_block)
     late_near = near_swap(late_block)
-    early_near = near_swap(jnp.concatenate(lax.optimization_barrier((*early_own, late_block))[:-1]))
+    early_block = jnp.concatenate(early_own)
+    early_near = jnp.concatenate(
+        [near_swap(after(early_block[:-1], beside)), near_swap(early_block[-1:])]
+    )
     early_far = [group_swap(beside[t * kc : (t + 1) * kc], bits[t]) for t in range(transfers)]
 
     virtual = virtual_energies(vir_sorted, vir_order)
     inverse = inverses(bits, partner, occ_energy, virtual, kc)
-    total = first_terms(factor, inverse, early_own + late_own, [early_near, late_near])
-    total = early_terms(factor, inverse, early_far, total)
+    total = first_terms(factor, inverse, early_own + late_own, early_near)
+    total = second_terms(factor, inverse, late_near, early_far, total)
     return last_terms(factor, inverse, late_far, total)
 
 

time: 60.3 us -> 56.1 us (0.930)
  waiting for transfers between devices: 30.7 us -> 27.5 us
  starting transfers between devices: 14.1 us -> 12.2 us
  Pallas kernels: 14.1 us -> 14.9 us
    ppermute x2, waiting for transfers between devices: 7.11 us -> 0.01 us  [far_swap(): lax.ppermute(block, 'occ', [(i, (i + (1 if i % 2 else count - 1)) % count...]
    ppermute x6, waiting for transfers between devices: 23.6 us -> 27.1 us  [group_swap(): return lax.ppermute(block, 'kpt', [(g, g ^ 1 << bit) for g in range(count)])]
    pallas_call x2 -> x3, Pallas kernels: 5.02 us -> 6.77 us  [the longest x2 3.85 us: pack(): pl.pallas_call(functools.partial(pack_kernel, bits, h), out_shape=[jax.Sh...]
    ppermute x6, starting transfers between devices: 7.75 us -> 6.3 us  [group_swap(): return lax.ppermute(block, 'kpt', [(g, g ^ 1 << bit) for g in range(count)])]
    pallas_call x1, Pallas kernels: 4.74 us -> 3.76 us  [first_terms(): pl.pallas_call(first_kernel, out_shape=jax.ShapeDtypeStruct((transfers, k...]
    ppermute x2, starting transfers between devices: 5.77 us -> 5.16 us  [far_swap(): lax.ppermute(block, 'occ', [(i, (i + (1 if i % 2 else count - 1)) % count...]
  transfers between devices with their start and end apart: 10 -> 11, of which waited for: 6 -> 6; matrix products, arithmetic and copies ran while one was open for 2% -> 2% of each run, Pallas kernels for 15% -> 18%
where the time goes in v6:
time: 56.1 us; the launch traced here: 55.9 us
  waiting for transfers between devices  27.5 us (49%)
  Pallas kernels  14.9 us (27%)
  starting transfers between devices  12.2 us (22%)
  other arithmetic  0.92 us (2%)
    ppermute x6, waiting for transfers between devices, group_swap(): return lax.ppermute(block, 'kpt', [(g, g ^ 1 << bit) for g in range(count)])  27.1 us
    ppermute x6, starting transfers between devices, group_swap(): return lax.ppermute(block, 'kpt', [(g, g ^ 1 << bit) for g in range(count)])  6.3 us
    ppermute x2, starting transfers between devices, far_swap(): lax.ppermute(block, 'occ', [(i, (i + (1 if i % 2 else count - 1)) % count...  5.16 us
    pallas_call x2, Pallas kernels, pack(): pl.pallas_call(functools.partial(pack_kernel, bits, h), out_shape=[jax.Sh...  3.85 us
    pallas_call x1, Pallas kernels, first_terms(): pl.pallas_call(first_kernel, out_shape=jax.ShapeDtypeStruct((transfers, k...  3.76 us
    pallas_call x1, Pallas kernels, second_terms(): pl.pallas_call(second_kernel, out_shape=jax.ShapeDtypeStruct(total.shape,...  2.93 us
    pallas_call x1, Pallas kernels, last_terms(): pl.pallas_call(last_kernel, out_shape=jax.ShapeDtypeStruct(factor.shape,...  2.74 us
    pallas_call x1, Pallas kernels, inverses(): pl.pallas_call(functools.partial(inverse_kernel, bits), out_shape=jax.Sha...  1.59 us
  transfers between devices with their start and end apart: 11, of which 6 were waited for; matrix products, arithmetic and copies ran while one was open for 2% of the time, Pallas kernels for 18%

profile of v6, /device:TPU:0, one launch (start us, length us, event | category | flops | bytes accessed | tf_op | source)
XLA Modules:
  0.0 55.9 jit_solution(12778088108561480430)
XLA Ops:
  0.0 1.9 %shard_map.56 = bf16[4,2,128,512]{3,2,1,0:T(8,128)(2,1)S(1)} custom-call(s32[2,8]{1,0:T(2,128)} %partner.4, bf16[2,2,1,2,256,512]{5,4,3,2,1,0:T(8,128)(2,1)} %factor.9), custom_call_target="tpu_custom_call" | custom-call | tf_op jit(solution)/shard_map/pallas_call | solution.py:71
  1.9 4.6 %collective-permute-start.4 = (bf16[4,2,128,512]{3,2,1,0:T(8,128)(2,1)S(1)}, bf16[4,2,128,512]{3,2,1,0:T(8,128)(2,1)S(1)}, u32[]{:S(2)}, u32[]{:S(2)}) collective-permute-start(bf16[4,2,128,512]{3,2,1,0:T(8,128)(2,1)S(1)} %shard_map.56), channel_id=1, source_target_pairs={{0,7},{1,2},{2,1},{3,4},{4,3},{5,6},{6,5},{7,0},{8,15},{9,10},{10,... | collective-permute-start | bytes 3145736 | tf_op jit(solution)/shard_map/ppermute | solution.py:32
  6.5 1.9 %shard_map.57 = (bf16[2,2,128,512]{3,2,1,0:T(8,128)(2,1)S(1)}, bf16[2,2,128,512]{3,2,1,0:T(8,128)(2,1)S(1)}) custom-call(s32[2,8]{1,0:T(2,128)} %partner.4, bf16[2,2,1,2,256,512]{5,4,3,2,1,0:T(8,128)(2,1)} %factor.9), custom_call_target="tpu_custom_call" | custom-call | bytes 16777216 | tf_op jit(solution)/shard_map/pallas_call | solution.py:71
  8.4 1.6 %collective-permute-start = (bf16[2,2,128,512]{3,2,1,0:T(8,128)(2,1)S(1)}, bf16[2,2,128,512]{3,2,1,0:T(8,128)(2,1)S(1)}, u32[]{:S(2)}, u32[]{:S(2)}) collective-permute-start(bf16[2,2,128,512]{3,2,1,0:T(8,128)(2,1)S(1)} %get-tuple-element.10), channel_id=1, source_target_pairs={{0,8},{8,0},{16,24},{24,16},{1,9},{9,1},{17,25},{25,17},{2,10},{10... | collective-permute-start | bytes 1572872 | tf_op jit(solution)/shard_map/ppermute | solution.py:22
  10.0 1.5 %collective-permute-start.1 = (bf16[2,2,128,512]{3,2,1,0:T(8,128)(2,1)S(1)}, bf16[2,2,128,512]{3,2,1,0:T(8,128)(2,1)S(1)}, u32[]{:S(2)}, u32[]{:S(2)}) collective-permute-start(bf16[2,2,128,512]{3,2,1,0:T(8,128)(2,1)S(1)} %get-tuple-element.11), channel_id=1, source_target_pairs={{0,16},{8,24},{16,0},{24,8},{1,17},{9,25},{17,1},{25,9},{2,18},{10... | collective-permute-start | bytes 1572872 | tf_op jit(solution)/shard_map/ppermute | solution.py:22
  11.5 0.1 fusion
  11.6 0.6 %collective-permute-start.8 = (bf16[2,2,128,512]{3,2,1,0:T(8,128)(2,1)S(1)}, bf16[2,2,128,512]{3,2,1,0:T(8,128)(2,1)S(1)}, u32[]{:S(2)}, u32[]{:S(2)}) collective-permute-start(bf16[2,2,128,512]{3,2,1,0:T(8,128)(2,1)S(1)} %get-tuple-element.13), channel_id=1, source_target_pairs={{0,16},{8,24},{16,0},{24,8},{1,17},{9,25},{17,1},{25,9},{2,18},{10... | collective-permute-start | bytes 1572872 | tf_op jit(solution)/shard_map/ppermute | solution.py:22
  12.1 0.5 collective-permute-start.7
  12.7 10.7 %collective-permute-done.refs_2_ = bf16[2,2,128,512]{3,2,1,0:T(8,128)(2,1)S(1)} collective-permute-done((bf16[2,2,128,512]{3,2,1,0:T(8,128)(2,1)S(1)}, bf16[2,2,128,512]{3,2,1,0:T(8,128)(2,1)S(1)}, u32[]{:S(2)}, u32[]{:S(2)}) %collective-permute-start) | collective-permute-done | bytes 524320 | tf_op jit(solution)/shard_map/ppermute | solution.py:22
  23.4 1.5 %collective-permute-done.1.refs_3_ = bf16[2,2,128,512]{3,2,1,0:T(8,128)(2,1)S(1)} collective-permute-done((bf16[2,2,128,512]{3,2,1,0:T(8,128)(2,1)S(1)}, bf16[2,2,128,512]{3,2,1,0:T(8,128)(2,1)S(1)}, u32[]{:S(2)}, u32[]{:S(2)}) %collective-permute-start.1) | collective-permute-done | bytes 524320 | tf_op jit(solution)/shard_map/ppermute | solution.py:22
  24.9 0.0 copy-start.3
  24.9 0.0 copy-start.4
  24.9 0.0 copy-start.1
  24.9 0.0 copy-start.2
  24.9 0.1 collective-permute-start.3
  25.0 0.6 %collective-permute-start.2 = (bf16[4,2,128,512]{3,2,1,0:T(8,128)(2,1)S(1)}, bf16[4,2,128,512]{3,2,1,0:T(8,128)(2,1)S(1)}, u32[]{:S(2)}, u32[]{:S(2)}) collective-permute-start(bf16[4,2,128,512]{3,2,1,0:T(8,128)(2,1)S(1)} %constant_dynamic-update-slice_fusion), channel_id=1, source_target_pairs={{0,7},{1,2},{2,1},{3,4},{4,3},{5,6},{6,5},{7,0},{8,15},{9,10},{10,... | collective-permute-start | bytes 3145736 | tf_op jit(solution)/shard_map/ppermute | solution.py:32
  25.6 7.8 %collective-permute-done.8.refs_1_ = bf16[2,2,128,512]{3,2,1,0:T(8,128)(2,1)S(1)} collective-permute-done((bf16[2,2,128,512]{3,2,1,0:T(8,128)(2,1)S(1)}, bf16[2,2,128,512]{3,2,1,0:T(8,128)(2,1)S(1)}, u32[]{:S(2)}, u32[]{:S(2)}) %collective-permute-start.8) | collective-permute-done | bytes 524320 | tf_op jit(solution)/shard_map/ppermute | solution.py:22
  33.4 0.0 collective-permute-done.7.refs_0_
  33.4 0.1 pad_maximum_fusion.1
  33.5 0.0 collective-permute-done.4
  33.5 0.1 collective-permute-start.9
  33.6 0.6 collective-permute-start.10
  34.2 0.1 fusion.1
  34.2 1.6 %collective-permute-start.6 = (bf16[2,2,128,512]{3,2,1,0:T(8,128)(2,1)S(1)}, bf16[2,2,128,512]{3,2,1,0:T(8,128)(2,1)S(1)}, u32[]{:S(2)}, u32[]{:S(2)}) collective-permute-start(bf16[2,2,128,512]{3,2,1,0:T(8,128)(2,1)S(1)} %get-tuple-element.15), channel_id=1, source_target_pairs={{0,16},{8,24},{16,0},{24,8},{1,17},{9,25},{17,1},{25,9},{2,18},{10... | collective-permute-start | bytes 1572872 | tf_op jit(solution)/shard_map/ppermute | solution.py:22
  35.8 0.4 collective-permute-done.10
  36.2 0.5 collective-permute-start.5
  36.8 0.0 copy-done.3
  36.8 0.0 copy-done.4
  36.8 0.8 %select_reduce_fusion.virtual = f32[8,256]{1,0:T(8,128)S(1)} fusion(f32[8,256]{1,0:T(8,128)S(1)} %copy-done.3, s32[8,256]{1,0:T(8,128)S(1)} %copy-done.4), kind=kLoop, calls=%fused_computation | loop fusion | flops 1570816 | bytes 24576 | tf_op jit(solution)/shard_map/reduce_sum | solution.py:44
  37.5 0.0 copy-done.1
  37.5 0.0 copy-done.2
  37.5 0.0 copy-start
  37.6 1.6 %shard_map.55.inverse = f32[2,3,2,256,256]{4,3,2,1,0:T(8,128)S(1)} custom-call(s32[2,8]{1,0:T(2,128)S(1)} %copy-done.1, f32[8,8]{1,0:T(8,128)S(1)} %copy-done.2, f32[8,256]{1,0:T(8,128)S(1)} %select_reduce_fusion.virtual), custom_call_target="tpu_custom_call" | custom-call | tf_op jit(solution)/shard_map/pallas_call | solution.py:108
  39.2 0.0 collective-permute-done.9
  39.2 0.1 pad_maximum_fusion.refs_4_
  39.3 0.0 copy-done
  39.3 3.8 %shard_map.58.refs_2_ = f32[2,2,2,256,512]{4,3,2,1,0:T(8,128)S(1)} custom-call(bf16[2,2,1,2,256,512]{5,4,3,2,1,0:T(8,128)(2,1)S(1)} %copy-done, f32[2,3,2,256,256]{4,3,2,1,0:T(8,128)S(1)} %shard_map.55.inverse, bf16[2,2,128,512]{3,2,1,0:T(8,128)(2,1)S(1)} %collective-permute-done.7.refs_0_, bf16[2,2,128,512]{3,2,1,0:T(8,128)(2,1)S(1)} %collective-permute-done.8.refs_1_, ...), custom_call_target="tpu_custom_call" | custom-call | tf_op jit(solution)/shard_map/pallas_call | solution.py:168
  43.0 0.0 collective-permute-done.3.near
  43.1 5.1 %collective-permute-done.6.refs_1_ = bf16[2,2,128,512]{3,2,1,0:T(8,128)(2,1)S(1)} collective-permute-done((bf16[2,2,128,512]{3,2,1,0:T(8,128)(2,1)S(1)}, bf16[2,2,128,512]{3,2,1,0:T(8,128)(2,1)S(1)}, u32[]{:S(2)}, u32[]{:S(2)}) %collective-permute-start.6) | collective-permute-done | bytes 524320 | tf_op jit(solution)/shard_map/ppermute | solution.py:22
  48.1 2.0 %collective-permute-done.5.refs_0_ = bf16[2,2,128,512]{3,2,1,0:T(8,128)(2,1)S(1)} collective-permute-done((bf16[2,2,128,512]{3,2,1,0:T(8,128)(2,1)S(1)}, bf16[2,2,128,512]{3,2,1,0:T(8,128)(2,1)S(1)}, u32[]{:S(2)}, u32[]{:S(2)}) %collective-permute-start.5) | collective-permute-done | bytes 524320 | tf_op jit(solution)/shard_map/ppermute | solution.py:22
  50.2 2.9 %shard_map.59.total = f32[2,2,2,256,512]{4,3,2,1,0:T(8,128)S(1)} custom-call(bf16[2,2,1,2,256,512]{5,4,3,2,1,0:T(8,128)(2,1)S(1)} %copy-done, f32[2,3,2,256,256]{4,3,2,1,0:T(8,128)S(1)} %shard_map.55.inverse, bf16[4,2,128,512]{3,2,1,0:T(8,128)(2,1)S(1)} %collective-permute-done.3.near, ...), custom_call_target="tpu_custom_call", output_to_operand_aliasing={{}: (5, {})} | custom-call | tf_op jit(solution)/shard_map/pallas_call | solution.py:196
  53.1 0.0 collective-permute-done.2.window
  53.1 2.7 %shard_map.60 = bf16[2,2,1,2,256,512]{5,4,3,2,1,0:T(8,128)(2,1)} custom-call(bf16[2,2,1,2,256,512]{5,4,3,2,1,0:T(8,128)(2,1)S(1)} %copy-done, f32[2,3,2,256,256]{4,3,2,1,0:T(8,128)S(1)} %shard_map.55.inverse, bf16[4,2,128,512]{3,2,1,0:T(8,128)(2,1)S(1)} %collective-permute-done.2.window, f32[2,2,2,256,512]{4,3,2,1,0:T(8,128)S(1)} %shard_map.59.total), custom_call_target="tpu_custom_call" | custom-call | tf_op jit(solution)/shard_map/pallas_call | solution.py:225
  (3 shorter events, 0.1 us)
Async XLA Ops:
  1.9 31.6 %collective-permute-start.4 = (bf16[4,2,128,512]{3,2,1,0:T(8,128)(2,1)S(1)}, bf16[4,2,128,512]{3,2,1,0:T(8,128)(2,1)S(1)}, u32[]{:S(2)}, u32[]{:S(2)}) collective-permute-start(bf16[4,2,128,512]{3,2,1,0:T(8,128)(2,1)S(1)} %shard_map.56), channel_id=1, source_target_pairs={{0,7},{1,2},{2,1},{3,4},{4,3},{5,6},{6,5},{7,0},{8,15},{9,10},{10,... | collective-permute-start | bytes 3145736 | tf_op jit(solution)/shard_map/ppermute | solution.py:32
  8.4 14.9 %collective-permute-start = (bf16[2,2,128,512]{3,2,1,0:T(8,128)(2,1)S(1)}, bf16[2,2,128,512]{3,2,1,0:T(8,128)(2,1)S(1)}, u32[]{:S(2)}, u32[]{:S(2)}) collective-permute-start(bf16[2,2,128,512]{3,2,1,0:T(8,128)(2,1)S(1)} %get-tuple-element.10), channel_id=1, source_target_pairs={{0,8},{8,0},{16,24},{24,16},{1,9},{9,1},{17,25},{25,17},{2,10},{10... | collective-permute-start | bytes 1572872 | tf_op jit(solution)/shard_map/ppermute | solution.py:22
  10.0 14.9 %collective-permute-start.1 = (bf16[2,2,128,512]{3,2,1,0:T(8,128)(2,1)S(1)}, bf16[2,2,128,512]{3,2,1,0:T(8,128)(2,1)S(1)}, u32[]{:S(2)}, u32[]{:S(2)}) collective-permute-start(bf16[2,2,128,512]{3,2,1,0:T(8,128)(2,1)S(1)} %get-tuple-element.11), channel_id=1, source_target_pairs={{0,16},{8,24},{16,0},{24,8},{1,17},{9,25},{17,1},{25,9},{2,18},{10... | collective-permute-start | bytes 1572872 | tf_op jit(solution)/shard_map/ppermute | solution.py:22
  11.6 21.8 %collective-permute-start.8 = (bf16[2,2,128,512]{3,2,1,0:T(8,128)(2,1)S(1)}, bf16[2,2,128,512]{3,2,1,0:T(8,128)(2,1)S(1)}, u32[]{:S(2)}, u32[]{:S(2)}) collective-permute-start(bf16[2,2,128,512]{3,2,1,0:T(8,128)(2,1)S(1)} %get-tuple-element.13), channel_id=1, source_target_pairs={{0,16},{8,24},{16,0},{24,8},{1,17},{9,25},{17,1},{25,9},{2,18},{10... | collective-permute-start | bytes 1572872 | tf_op jit(solution)/shard_map/ppermute | solution.py:22
  12.1 21.3 %collective-permute-start.7 = (bf16[2,2,128,512]{3,2,1,0:T(8,128)(2,1)S(1)}, bf16[2,2,128,512]{3,2,1,0:T(8,128)(2,1)S(1)}, u32[]{:S(2)}, u32[]{:S(2)}) collective-permute-start(bf16[2,2,128,512]{3,2,1,0:T(8,128)(2,1)S(1)} %get-tuple-element.14), channel_id=1, source_target_pairs={{0,8},{8,0},{16,24},{24,16},{1,9},{9,1},{17,25},{25,17},{2,10},{10... | collective-permute-start | bytes 1572872 | tf_op jit(solution)/shard_map/ppermute | solution.py:22
  24.9 11.9 %copy-start.3 = (f32[8,256]{1,0:T(8,128)S(1)}, f32[8,256]{1,0:T(8,128)}, u32[]{:S(2)}) copy-start(f32[8,256]{1,0:T(8,128)} %param.8) | copy-start | bytes 24580
  24.9 11.9 %copy-start.4 = (s32[8,256]{1,0:T(8,128)S(1)}, s32[8,256]{1,0:T(8,128)}, u32[]{:S(2)}) copy-start(s32[8,256]{1,0:T(8,128)} %param.9) | copy-start | bytes 24580
  24.9 12.6 %copy-start.1 = (s32[2,8]{1,0:T(2,128)S(1)}, s32[2,8]{1,0:T(2,128)}, u32[]{:S(2)}) copy-start(s32[2,8]{1,0:T(2,128)} %partner.4) | copy-start | bytes 196
  24.9 12.6 %copy-start.2 = (f32[8,8]{1,0:T(8,128)S(1)}, f32[8,8]{1,0:T(8,128)}, u32[]{:S(2)}) copy-start(f32[8,8]{1,0:T(8,128)} %occ.1) | copy-start | bytes 772
  24.9 18.1 %collective-permute-start.3 = (bf16[4,2,128,512]{3,2,1,0:T(8,128)(2,1)S(1)}, bf16[4,2,128,512]{3,2,1,0:T(8,128)(2,1)S(1)}, u32[]{:S(2)}, u32[]{:S(2)}) collective-permute-start(bf16[4,2,128,512]{3,2,1,0:T(8,128)(2,1)S(1)} %constant_dynamic-update-slice_fusion), channel_id=1, source_target_pairs={{0,1},{1,0},{2,3},{3,2},{4,5},{5,4},{6,7},{7,6},{8,9},{9,8},{10,11... | collective-permute-start | bytes 3145736 | tf_op jit(solution)/shard_map/ppermute | solution.py:27
  25.0 28.1 %collective-permute-start.2 = (bf16[4,2,128,512]{3,2,1,0:T(8,128)(2,1)S(1)}, bf16[4,2,128,512]{3,2,1,0:T(8,128)(2,1)S(1)}, u32[]{:S(2)}, u32[]{:S(2)}) collective-permute-start(bf16[4,2,128,512]{3,2,1,0:T(8,128)(2,1)S(1)} %constant_dynamic-update-slice_fusion), channel_id=1, source_target_pairs={{0,7},{1,2},{2,1},{3,4},{4,3},{5,6},{6,5},{7,0},{8,15},{9,10},{10,... | collective-permute-start | bytes 3145736 | tf_op jit(solution)/shard_map/ppermute | solution.py:32
  33.5 5.7 %collective-permute-start.9 = (bf16[3,2,128,512]{3,2,1,0:T(8,128)(2,1)S(1)}, bf16[3,2,128,512]{3,2,1,0:T(8,128)(2,1)S(1)}, u32[]{:S(2)}, u32[]{:S(2)}) collective-permute-start(bf16[3,2,128,512]{3,2,1,0:T(8,128)(2,1)S(1)} %pad_maximum_fusion.1), channel_id=1, source_target_pairs={{0,1},{1,0},{2,3},{3,2},{4,5},{5,4},{6,7},{7,6},{8,9},{9,8},{10,11... | collective-permute-start | bytes 2359304 | tf_op jit(solution)/shard_map/ppermute | solution.py:27
  33.6 2.6 %collective-permute-start.10 = (bf16[1,2,128,512]{3,2,1,0:T(8,128)(2,1)S(1)}, bf16[1,2,128,512]{3,2,1,0:T(8,128)(2,1)S(1)}, u32[]{:S(2)}, u32[]{:S(2)}) collective-permute-start(bf16[1,2,128,512]{3,2,1,0:T(8,128)(2,1)S(1)} %slice.28), channel_id=1, source_target_pairs={{0,1},{1,0},{2,3},{3,2},{4,5},{5,4},{6,7},{7,6},{8,9},{9,8},{10,11... | collective-permute-start | bytes 786440 | tf_op jit(solution)/shard_map/ppermute | solution.py:27
  34.2 13.9 %collective-permute-start.6 = (bf16[2,2,128,512]{3,2,1,0:T(8,128)(2,1)S(1)}, bf16[2,2,128,512]{3,2,1,0:T(8,128)(2,1)S(1)}, u32[]{:S(2)}, u32[]{:S(2)}) collective-permute-start(bf16[2,2,128,512]{3,2,1,0:T(8,128)(2,1)S(1)} %get-tuple-element.15), channel_id=1, source_target_pairs={{0,16},{8,24},{16,0},{24,8},{1,17},{9,25},{17,1},{25,9},{2,18},{10... | collective-permute-start | bytes 1572872 | tf_op jit(solution)/shard_map/ppermute | solution.py:22
  36.2 14.0 %collective-permute-start.5 = (bf16[2,2,128,512]{3,2,1,0:T(8,128)(2,1)S(1)}, bf16[2,2,128,512]{3,2,1,0:T(8,128)(2,1)S(1)}, u32[]{:S(2)}, u32[]{:S(2)}) collective-permute-start(bf16[2,2,128,512]{3,2,1,0:T(8,128)(2,1)S(1)} %get-tuple-element.16), channel_id=1, source_target_pairs={{0,8},{8,0},{16,24},{24,16},{1,9},{9,1},{17,25},{25,17},{2,10},{10... | collective-permute-start | bytes 1572872 | tf_op jit(solution)/shard_map/ppermute | solution.py:22
  37.5 1.7 %copy-start = (bf16[2,2,1,2,256,512]{5,4,3,2,1,0:T(8,128)(2,1)S(1)}, bf16[2,2,1,2,256,512]{5,4,3,2,1,0:T(8,128)(2,1)}, u32[]{:S(2)}) copy-start(bf16[2,2,1,2,256,512]{5,4,3,2,1,0:T(8,128)(2,1)} %factor.9) | copy-start | bytes 6291460

commit v7 on v6

--- a/solution.py
+++ b/solution.py
@@ -48,32 +48,56 @@
     return jnp.transpose(jnp.broadcast_to(row, (8, row.shape[1])))[:, :1]
 
 
-def pack_kernel(bits, h, partner, factor, *refs):
+def lay_kernel(factor, out, sems):
+    kc, half = factor.shape[1], out.shape[2]
+    copies = []
+    for at in range(out.shape[0]):
+        source = factor.at[at // kc, at % kc, 0, :, pl.ds(0, half), :]
+        copies.append(pltpu.make_async_copy(source, out.at[at], sems.at[at]))
+        copies[-1].start()
+    for copy in copies:
+        copy.wait()
+
+
+def lay(factor):
+    transfers, kc, _, parts, nv, naux = factor.shape
+    return pl.pallas_call(
+        lay_kernel,
+        out_shape=jax.ShapeDtypeStruct((transfers * kc, parts, nv // 2, naux), BF16),
+        in_specs=[ANY],
+        out_specs=VMEM,
+        scratch_shapes=[pltpu.SemaphoreType.DMA((transfers * kc,))],
+        cost_estimate=COST,
+        compiler_params=PARAMS,
+    )(pltpu.with_memory_space_constraint(factor, pltpu.HBM))
+
+
+def pack_kernel(bits, partner, factor, *refs):
     outs, sems = refs[:-1], refs[-1]
     kc, half = factor.shape[1], outs[0].shape[2]
-    targets = [out.at[n] for out in outs for n in range(out.shape[0])]
     group = lax.axis_index("kpt")
     copies = []
-    for transfer, bit in enumerate(bits):
-        far_group = jnp.bitwise_xor(group, 1 << bit)
-        for k in range(kc):
-            slot = partner[transfer, far_group * kc + k] - group * kc
-            source = factor.at[transfer, slot, 0, :, pl.ds(h * half, half), :]
-            at = transfer * kc + k
-            copies.append(pltpu.make_async_copy(source, targets[at], sems.at[at]))
-            copies[-1].start()
+    for h in (1, 0):
+        for transfer, bit in enumerate(bits):
+            far_group = jnp.bitwise_xor(group, 1 << bit)
+            for k in range(kc):
+                slot = partner[transfer, far_group * kc + k] - group * kc
+                source = factor.at[transfer, slot, 0, :, pl.ds(h * half, half), :]
+                target = outs[h * len(bits) + transfer].at[k]
+                copies.append(pltpu.make_async_copy(source, target, sems.at[len(copies)]))
+                copies[-1].start()
     for copy in copies:
         copy.wait()
 
 
-def pack(bits, h, counts, partner, factor, work):
-    _, _, _, parts, nv, naux = factor.shape
-    return pl.pallas_call(
-        functools.partial(pack_kernel, bits, h),
-        out_shape=[jax.ShapeDtypeStruct((n, parts, nv // 2, naux), BF16) for n in counts],
+def pack(bits, partner, factor, work):
+    transfers, kc, _, parts, nv, naux = factor.shape
+    return pl.pallas_call(
+        functools.partial(pack_kernel, bits),
+        out_shape=[jax.ShapeDtypeStruct((kc, parts, nv // 2, naux), BF16)] * (2 * transfers),
         in_specs=[SMEM, ANY],
-        out_specs=[VMEM] * len(counts),
-        scratch_shapes=[pltpu.SemaphoreType.DMA((sum(counts),))],
+        out_specs=[VMEM] * (2 * transfers),
+        scratch_shapes=[pltpu.SemaphoreType.DMA((2 * transfers * kc,))],
         cost_estimate=pl.CostEstimate(flops=0, bytes_accessed=work, transcendentals=0),
         compiler_params=PARAMS,
     )(
@@ -115,10 +139,10 @@
     )(partner, occ_energy, virtual)
 
 
-def gradient_sum(own, terms, base):
+def amplitude_rows(own, terms):
     _, nv, naux = own.shape
     left = own.reshape(2 * nv, naux)
-    amplitudes, blocks = [], []
+    rows, blocks = ([], []), []
     for window, inverse in terms:
         size = window.shape[1]
         window = window.reshape(2 * size, naux)
@@ -127,16 +151,24 @@
         )
         real_part = ((products[:nv, :size] + products[nv:, size:]) * inverse).astype(BF16)
         imag_part = ((products[nv:, :size] - products[:nv, size:]) * inverse).astype(BF16)
-        upper = jnp.concatenate([real_part, -imag_part], axis=1)
-        lower = jnp.concatenate([imag_part, real_part], axis=1)
-        amplitudes.append(jnp.concatenate([upper, lower], axis=0))
+        rows[0].extend([real_part, -imag_part])
+        rows[1].extend([imag_part, real_part])
         blocks.append(window)
-    gradient = jnp.dot(
-        jnp.concatenate(amplitudes, axis=1),
-        jnp.concatenate(blocks, axis=0),
-        preferred_element_type=F32,
-    ).reshape(2, nv, naux)
-    return gradient if base is None else gradient + base
+    return [jnp.concatenate(part, axis=1) for part in rows], jnp.concatenate(blocks, axis=0)
+
+
+def contract(factor, terms_of, finish):
+    waiting = None
+    points = [(t, k) for t in range(factor.shape[0]) for k in range(factor.shape[1])]
+    for point in [*points, None]:
+        ready, waiting = waiting, None
+        if point is not None:
+            t, k = point
+            waiting = (t, k, *amplitude_rows(factor[t, k, 0], terms_of(t, k)))
+        if ready is not None:
+            t, k, rows, blocks = ready
+            for part in range(2):
+                finish(t, k, part, jnp.dot(rows[part], blocks, preferred_element_type=F32))
 
 
 def half_of(h, half):
@@ -146,20 +178,19 @@
 def first_kernel(factor, inverse, *refs):
     transfers, kc = factor.shape[:2]
     owns, near, out = refs[: 2 * transfers], refs[-2], refs[-1]
-    half = near.shape[2]
-
-    def point_step(k, carry):
-        for t in range(transfers):
-            first, second = half_of(0, half), half_of(1, half)
-            terms = [
-                (owns[t][k], inverse[t, 0, k, :, first]),
-                (owns[transfers + t][k], inverse[t, 0, k, :, second]),
-                (near[t * kc + k], inverse[t, 1, k, :, first]),
-            ]
-            out[t, k] = gradient_sum(factor[t, k, 0], terms, None)
-        return carry
-
-    lax.fori_loop(0, kc, point_step, 0)
+    first, second = half_of(0, near.shape[2]), half_of(1, near.shape[2])
+
+    def terms_of(t, k):
+        return [
+            (owns[t][k], inverse[t, 0, k, :, first]),
+            (owns[transfers + t][k], inverse[t, 0, k, :, second]),
+            (near[t * kc + k], inverse[t, 1, k, :, first]),
+        ]
+
+    def finish(t, k, part, value):
+        out[t, k, part] = value
+
+    contract(factor, terms_of, finish)
 
 
 def first_terms(factor, inverse, owns, near):
@@ -179,16 +210,16 @@
     fars, total, out = refs[:-2], refs[-2], refs[-1]
     kc, half = factor.shape[1], near.shape[2]
 
-    def point_step(k, carry):
-        for t, far in enumerate(fars):
-            terms = [
-                (near[t * kc + k], inverse[t, 1, k, :, half_of(1, half)]),
-                (far[k], inverse[t, 2, k, :, half_of(0, half)]),
-            ]
-            out[t, k] = gradient_sum(factor[t, k, 0], terms, total[t, k])
-        return carry
-
-    lax.fori_loop(0, kc, point_step, 0)
+    def terms_of(t, k):
+        return [
+            (near[t * kc + k], inverse[t, 1, k, :, half_of(1, half)]),
+            (fars[t][k], inverse[t, 2, k, :, half_of(0, half)]),
+        ]
+
+    def finish(t, k, part, value):
+        out[t, k, part] = value + total[t, k, part]
+
+    contract(factor, terms_of, finish)
 
 
 def second_terms(factor, inverse, near, fars, total):
@@ -205,30 +236,33 @@
 
 
 def last_kernel(factor, inverse, window, total, out, staged, sems):
-    transfers, kc = factor.shape[:2]
-    half = window.shape[2]
+    kc, half = factor.shape[1], window.shape[2]
     copies = []
-    for t in range(transfers):
-        for k in range(kc):
-            at = t * kc + k
-            terms = [(window[at], inverse[t, 2, k, :, half_of(1, half)])]
-            staged[at] = gradient_sum(factor[t, k, 0], terms, total[t, k]).astype(BF16)
-            copies.append(pltpu.make_async_copy(staged.at[at], out.at[t, k, 0], sems.at[at]))
-            copies[-1].start()
+
+    def terms_of(t, k):
+        return [(window[t * kc + k], inverse[t, 2, k, :, half_of(1, half)])]
+
+    def finish(t, k, part, value):
+        at = len(copies)
+        staged[at] = (value + total[t, k, part]).astype(BF16)
+        copies.append(pltpu.make_async_copy(staged.at[at], out.at[t, k, 0, part], sems.at[at]))
+        copies[-1].start()
+
+    contract(factor, terms_of, finish)
     for copy in copies:
         copy.wait()
 
 
 def last_terms(factor, inverse, window, total):
-    count = window.shape[0]
-    _, _, _, parts, nv, naux = factor.shape
+    transfers, kc, _, parts, nv, naux = factor.shape
+    count = transfers * kc * parts
     return pl.pallas_call(
         last_kernel,
         out_shape=jax.ShapeDtypeStruct(factor.shape, BF16),
         in_specs=[VMEM] * 4,
         out_specs=ANY,
         scratch_shapes=[
-            pltpu.VMEM((count, parts, nv, naux), BF16),
+            pltpu.VMEM((count, nv, naux), BF16),
             pltpu.SemaphoreType.DMA((count,)),
         ],
         cost_estimate=COST,
@@ -240,11 +274,13 @@
     transfers, kc = factor.shape[:2]
     bits = (0, lax.axis_size("kpt").bit_length() - 2)
 
-    (part,) = pack(bits, 0, [transfers * kc], partner, factor, 0)
+    group = lax.axis_index("kpt")
+    part = lay(factor)
     beside = far_swap(part)
-    lates = pack(bits, 1, [kc] * transfers, after(partner, part), factor, WORK * factor.size)
+    packs = pack(bits, after(partner, part), factor, WORK * factor.size)
+    earlies, lates = packs[:transfers], packs[transfers:]
     late_own = [group_swap(lates[t], bits[t]) for t in range(transfers)]
-    early_own = [group_swap(part[t * kc : (t + 1) * kc], bits[t]) for t in range(transfers)]
+    early_own = [group_swap(earlies[t], bits[t]) for t in range(transfers)]
     late_block = jnp.concatenate(late_own)
     late_far = far_swap(late_block)
     late_near = near_swap(late_block)
@@ -252,7 +288,12 @@
     early_near = jnp.concatenate(
         [near_swap(after(early_block[:-1], beside)), near_swap(early_block[-1:])]
     )
-    early_far = [group_swap(beside[t * kc : (t + 1) * kc], bits[t]) for t in range(transfers)]
+    early_far = []
+    for t in range(transfers):
+        far_group = jnp.bitwise_xor(group, 1 << bits[t])
+        slots = lax.dynamic_slice_in_dim(partner[t], far_group * kc, kc) - group * kc
+        ordered = [lax.dynamic_slice_in_dim(beside, t * kc + slots[k], 1) for k in range(kc)]
+        early_far.append(group_swap(jnp.concatenate(ordered), bits[t]))
 
     virtual = virtual_energies(vir_sorted, vir_order)
     inverse = inverses(bits, partner, occ_energy, virtual, kc)

time: 56.1 us -> 65.6 us (1.17)
  between operations: 0.19 us -> 6.44 us
  waiting for transfers between devices: 27.5 us -> 22.8 us
  local copies, waits for them, and re-layouts: 0.26 us -> 4.27 us
  other arithmetic: 0.92 us -> 3.14 us
  Pallas kernels: 14.9 us -> 16.5 us
    ppermute x6, waiting for transfers between devices: 27.1 us -> 22.8 us  [group_swap(): return lax.ppermute(block, 'kpt', [(g, g ^ 1 << bit) for g in range(count)])]
    pallas_call x2, Pallas kernels: 3.85 us -> 5.47 us  [the longest x1 3.27 us: pack(): pl.pallas_call(functools.partial(pack_kernel, bits), out_shape=[jax.Shape...]
    dynamic_slice x0 -> x1, local copies, waits for them, and re-layouts: none -> 1.25 us  [body(): lax.dynamic_slice_in_dim(beside, t * kc + slots[k], 1)]
    slice x2 -> x3, local copies, waits for them, and re-layouts: 0.14 us -> 1.31 us  [the longest x2 1.31 us: body(): slots[k]]
    concatenate x1, other arithmetic: 0.09 us -> 1.23 us  [body(): jnp.concatenate([near_swap(after(early_block[:-1], beside)), near_swap(ea...]
    concatenate x1, other arithmetic: 0.07 us -> 0.97 us  [body(): early_block = jnp.concatenate(early_own)]
    pallas_call x1, Pallas kernels: 2.93 us -> 3.75 us  [second_terms(): pl.pallas_call(second_kernel, out_shape=jax.ShapeDtypeStruct(total.shape,...]
    concatenate x1, local copies, waits for them, and re-layouts: 0.03 us -> 0.83 us  [body(): late_block = jnp.concatenate(late_own)]
  transfers between devices with their start and end apart: 11 -> 11, of which waited for: 6 -> 6; matrix products, arithmetic and copies ran while one was open for 2% -> 11% of each run, Pallas kernels for 18% -> 19%
where the time goes in v7:
time: 65.6 us; the launch traced here: 65.2 us
  waiting for transfers between devices  22.8 us (35%)
  Pallas kernels  16.5 us (25%)
  starting transfers between devices  12 us (18%)
  between operations  6.44 us (10%)
  local copies, waits for them, and re-layouts  4.27 us (7%)
  other arithmetic  3.14 us (5%)
    ppermute x6, waiting for transfers between devices, group_swap(): return lax.ppermute(block, 'kpt', [(g, g ^ 1 << bit) for g in range(count)])  22.8 us
    ppermute x6, starting transfers between devices, group_swap(): return lax.ppermute(block, 'kpt', [(g, g ^ 1 << bit) for g in range(count)])  6.3 us
    ppermute x2, starting transfers between devices, far_swap(): lax.ppermute(block, 'occ', [(i, (i + (1 if i % 2 else count - 1)) % count...  5.17 us
    pallas_call x1, Pallas kernels, second_terms(): pl.pallas_call(second_kernel, out_shape=jax.ShapeDtypeStruct(total.shape,...  3.75 us
    pallas_call x1, Pallas kernels, first_terms(): pl.pallas_call(first_kernel, out_shape=jax.ShapeDtypeStruct((transfers, k...  3.47 us
    pallas_call x1, Pallas kernels, pack(): pl.pallas_call(functools.partial(pack_kernel, bits), out_shape=[jax.Shape...  3.27 us
    pallas_call x1, Pallas kernels, last_terms(): pl.pallas_call(last_kernel, out_shape=jax.ShapeDtypeStruct(factor.shape,...  2.23 us
    pallas_call x1, Pallas kernels, lay(): pl.pallas_call(lay_kernel, out_shape=jax.ShapeDtypeStruct((transfers * kc...  2.2 us
  transfers between devices with their start and end apart: 11, of which 6 were waited for; matrix products, arithmetic and copies ran while one was open for 11% of the time, Pallas kernels for 19%

profile of v7, /device:TPU:0, one launch (start us, length us, event | category | flops | bytes accessed | tf_op | source)
XLA Modules:
  0.0 65.2 jit_solution(9142273591639951034)
XLA Ops:
  0.0 2.2 %shard_map.56 = bf16[4,2,128,512]{3,2,1,0:T(8,128)(2,1)} custom-call(bf16[2,2,1,2,256,512]{5,4,3,2,1,0:T(8,128)(2,1)} %factor.9), custom_call_target="tpu_custom_call" | custom-call | tf_op jit(solution)/shard_map/pallas_call | solution.py:64
  2.2 4.6 %collective-permute-start.4 = (bf16[4,2,128,512]{3,2,1,0:T(8,128)(2,1)}, bf16[4,2,128,512]{3,2,1,0:T(8,128)(2,1)}, u32[]{:S(2)}, u32[]{:S(2)}) collective-permute-start(bf16[4,2,128,512]{3,2,1,0:T(8,128)(2,1)} %shard_map.56), channel_id=1, source_target_pairs={{0,7},{1,2},{2,1},{3,4},{4,3},{5,6},{6,5},{7,0},{8,15},{9,10},{10,... | collective-permute-start | bytes 3145736 | tf_op jit(solution)/shard_map/ppermute | solution.py:32
  6.8 3.3 %shard_map.57 = (bf16[2,2,128,512]{3,2,1,0:T(8,128)(2,1)}, bf16[2,2,128,512]{3,2,1,0:T(8,128)(2,1)}, bf16[2,2,128,512]{3,2,1,0:T(8,128)(2,1)S(1)}, bf16[2,2,128,512]{3,2,1,0:T(8,128)(2,1)S(1)}) custom-call(s32[2,8]{1,0:T(2,128)} %partner.2, bf16[2,2,1,2,256,512]{5,4,3,2,1,0:T(8,128)(2,1)} %factor.9), custom_call_target="tpu_custom_call" | custom-call | bytes 16777216 | tf_op jit(solution)/shard_map/pallas_call | solution.py:95
  10.0 1.6 %collective-permute-start = (bf16[2,2,128,512]{3,2,1,0:T(8,128)(2,1)S(1)}, bf16[2,2,128,512]{3,2,1,0:T(8,128)(2,1)S(1)}, u32[]{:S(2)}, u32[]{:S(2)}) collective-permute-start(bf16[2,2,128,512]{3,2,1,0:T(8,128)(2,1)S(1)} %get-tuple-element.12), channel_id=1, source_target_pairs={{0,8},{8,0},{16,24},{24,16},{1,9},{9,1},{17,25},{25,17},{2,10},{10... | collective-permute-start | bytes 1572872 | tf_op jit(solution)/shard_map/ppermute | solution.py:22
  11.6 1.5 %collective-permute-start.1 = (bf16[2,2,128,512]{3,2,1,0:T(8,128)(2,1)S(1)}, bf16[2,2,128,512]{3,2,1,0:T(8,128)(2,1)S(1)}, u32[]{:S(2)}, u32[]{:S(2)}) collective-permute-start(bf16[2,2,128,512]{3,2,1,0:T(8,128)(2,1)S(1)} %get-tuple-element.13), channel_id=1, source_target_pairs={{0,16},{8,24},{16,0},{24,8},{1,17},{9,25},{17,1},{25,9},{2,18},{10... | collective-permute-start | bytes 1572872 | tf_op jit(solution)/shard_map/ppermute | solution.py:22
  13.1 0.5 collective-permute-start.7
  13.7 0.5 collective-permute-start.8
  14.2 0.0 copy-done.1
  14.2 0.1 fusion
  14.2 0.7 fusion.4
  14.9 10.1 %collective-permute-done.refs_2_ = bf16[2,2,128,512]{3,2,1,0:T(8,128)(2,1)S(1)} collective-permute-done((bf16[2,2,128,512]{3,2,1,0:T(8,128)(2,1)S(1)}, bf16[2,2,128,512]{3,2,1,0:T(8,128)(2,1)S(1)}, u32[]{:S(2)}, u32[]{:S(2)}) %collective-permute-start) | collective-permute-done | bytes 524320 | tf_op jit(solution)/shard_map/ppermute | solution.py:22
  25.0 0.8 %constant_dynamic-update-slice_fusion.1 = bf16[4,2,128,512]{3,2,1,0:T(8,128)(2,1)} fusion(bf16[2,2,128,512]{3,2,1,0:T(8,128)(2,1)S(1)} %collective-permute-done.refs_2_), kind=kLoop, calls=%fused_computation.7 | loop fusion | bytes 1048576
  25.8 0.7 %collective-permute-done.1.refs_3_ = bf16[2,2,128,512]{3,2,1,0:T(8,128)(2,1)S(1)} collective-permute-done((bf16[2,2,128,512]{3,2,1,0:T(8,128)(2,1)S(1)}, bf16[2,2,128,512]{3,2,1,0:T(8,128)(2,1)S(1)}, u32[]{:S(2)}, u32[]{:S(2)}) %collective-permute-start.1) | collective-permute-done | bytes 524320 | tf_op jit(solution)/shard_map/ppermute | solution.py:22
  26.5 0.8 %constant_dynamic-update-slice_fusion = bf16[4,2,128,512]{3,2,1,0:T(8,128)(2,1)} fusion(bf16[4,2,128,512]{3,2,1,0:T(8,128)(2,1)} %constant_dynamic-update-slice_fusion.1, bf16[2,2,128,512]{3,2,1,0:T(8,128)(2,1)S(1)} %collective-permute-done.1.refs_3_), kind=kLoop, calls=%fused_computation.6 | loop fusion | bytes 1048576 | tf_op jit(solution)/shard_map/concatenate | solution.py:284
  27.3 0.0 collective-permute-start.3
  27.3 0.6 collective-permute-start.2
  27.9 5.9 %collective-permute-done.7.refs_0_ = bf16[2,2,128,512]{3,2,1,0:T(8,128)(2,1)S(1)} collective-permute-done((bf16[2,2,128,512]{3,2,1,0:T(8,128)(2,1)}, bf16[2,2,128,512]{3,2,1,0:T(8,128)(2,1)S(1)}, u32[]{:S(2)}, u32[]{:S(2)}) %collective-permute-start.7) | collective-permute-done | bytes 524320 | tf_op jit(solution)/shard_map/ppermute | solution.py:22
  33.8 1.2 %collective-permute-done.8.refs_1_ = bf16[2,2,128,512]{3,2,1,0:T(8,128)(2,1)S(1)} collective-permute-done((bf16[2,2,128,512]{3,2,1,0:T(8,128)(2,1)}, bf16[2,2,128,512]{3,2,1,0:T(8,128)(2,1)S(1)}, u32[]{:S(2)}, u32[]{:S(2)}) %collective-permute-start.8) | collective-permute-done | bytes 524320 | tf_op jit(solution)/shard_map/ppermute | solution.py:22
  35.0 1.0 %pad_maximum_fusion.1 = bf16[3,2,128,512]{3,2,1,0:T(8,128)(2,1)} fusion(bf16[2,2,128,512]{3,2,1,0:T(8,128)(2,1)S(1)} %collective-permute-done.8.refs_1_, bf16[2,2,128,512]{3,2,1,0:T(8,128)(2,1)S(1)} %collective-permute-done.7.refs_0_), kind=kLoop, calls=%fused_computation.3 | loop fusion | flops 393216 | bytes 1835008 | tf_op jit(solution)/shard_map/concatenate | solution.py:287
  36.0 0.0 collective-permute-done.4
  36.0 0.0 collective-permute-start.9
  36.0 0.7 %fusion.3 = (s32[1,1]{1,0:T(1,128)}, s32[1,1]{1,0:T(1,128)}) fusion(s32[1,2]{1,0:T(1,128)S(1)} %get-tuple-element.28), kind=kLoop, calls=%fused_computation.17 | loop fusion | bytes 16 | tf_op jit(solution)/shard_map/slice | solution.py:295
  43.0 0.0 copy-start.3
  43.0 0.0 copy-start.4
  43.0 0.0 copy-start.2
  43.0 0.6 collective-permute-start.10
  43.6 1.3 %constant_dynamic-slice_fusion.1 = (bf16[1,2,128,512]{3,2,1,0:T(8,128)(2,1)S(1)}, bf16[1,2,128,512]{3,2,1,0:T(8,128)(2,1)S(1)}, bf16[1,2,128,512]{3,2,1,0:T(8,128)(2,1)S(1)}, bf16[1,2,128,512]{3,2,1,0:T(8,128)(2,1)S(1)}) fusion(bf16[4,2,128,512]{3,2,1,0:T(8,128)(2,1)} %collective-permute-done.4, s32[]{:T(128)S(6)} %select_n.27, s32[]{:T(128)S(6)} %select_n.28, ...), kind=kLoop, calls=%fused_computation.9 | loop fusion | bytes 2097168 | tf_op jit(solution)/shard_map/dynamic_slice | solution.py:295
  44.8 0.1 pad_maximum_fusion.2
  44.9 0.6 collective-permute-start.5
  45.5 0.1 pad_maximum_fusion.3
  45.6 0.0 collective-permute-done.10
  45.6 1.6 %collective-permute-start.6 = (bf16[2,2,128,512]{3,2,1,0:T(8,128)(2,1)S(1)}, bf16[2,2,128,512]{3,2,1,0:T(8,128)(2,1)S(1)}, u32[]{:S(2)}, u32[]{:S(2)}) collective-permute-start(bf16[2,2,128,512]{3,2,1,0:T(8,128)(2,1)S(1)} %pad_maximum_fusion.3), channel_id=1, source_target_pairs={{0,16},{8,24},{16,0},{24,8},{1,17},{9,25},{17,1},{25,9},{2,18},{10... | collective-permute-start | bytes 1572872 | tf_op jit(solution)/shard_map/ppermute | solution.py:22
  47.2 0.0 copy-done.3
  47.2 0.0 copy-done.4
  47.2 0.8 %select_reduce_fusion.virtual = f32[8,256]{1,0:T(8,128)S(1)} fusion(f32[8,256]{1,0:T(8,128)S(1)} %copy-done.3, s32[8,256]{1,0:T(8,128)S(1)} %copy-done.4), kind=kLoop, calls=%fused_computation | loop fusion | flops 1570816 | bytes 24576 | tf_op jit(solution)/shard_map/reduce_sum | solution.py:44
  47.9 0.0 copy-done.2
  47.9 0.0 copy-start
  47.9 1.6 %shard_map.55.inverse = f32[2,3,2,256,256]{4,3,2,1,0:T(8,128)S(1)} custom-call(s32[2,8]{1,0:T(2,128)S(1)} %copy-done.1, f32[8,8]{1,0:T(8,128)S(1)} %copy-done.2, f32[8,256]{1,0:T(8,128)S(1)} %select_reduce_fusion.virtual), custom_call_target="tpu_custom_call" | custom-call | tf_op jit(solution)/shard_map/pallas_call | solution.py:132
  49.5 0.0 collective-permute-done.9
  49.6 1.2 %pad_maximum_fusion.refs_4_ = bf16[4,2,128,512]{3,2,1,0:T(8,128)(2,1)S(1)} fusion(bf16[1,2,128,512]{3,2,1,0:T(8,128)(2,1)S(1)} %collective-permute-done.10, bf16[3,2,128,512]{3,2,1,0:T(8,128)(2,1)} %collective-permute-done.9), kind=kLoop, calls=%fused_computation.2 | loop fusion | flops 524288 | bytes 2097152 | tf_op jit(solution)/shard_map/concatenate | solution.py:288
  50.8 0.0 copy-done
  50.8 3.5 %shard_map.58.refs_2_ = f32[2,2,2,256,512]{4,3,2,1,0:T(8,128)S(1)} custom-call(bf16[2,2,1,2,256,512]{5,4,3,2,1,0:T(8,128)(2,1)S(1)} %copy-done, f32[2,3,2,256,256]{4,3,2,1,0:T(8,128)S(1)} %shard_map.55.inverse, bf16[2,2,128,512]{3,2,1,0:T(8,128)(2,1)S(1)} %collective-permute-done.7.refs_0_, bf16[2,2,128,512]{3,2,1,0:T(8,128)(2,1)S(1)} %collective-permute-done.8.refs_1_, ...), custom_call_target="tpu_custom_call" | custom-call | tf_op jit(solution)/shard_map/pallas_call | solution.py:199
  54.3 4.6 %collective-permute-done.5.refs_0_ = bf16[2,2,128,512]{3,2,1,0:T(8,128)(2,1)S(1)} collective-permute-done((bf16[2,2,128,512]{3,2,1,0:T(8,128)(2,1)S(1)}, bf16[2,2,128,512]{3,2,1,0:T(8,128)(2,1)S(1)}, u32[]{:S(2)}, u32[]{:S(2)}) %collective-permute-start.5) | collective-permute-done | bytes 524320 | tf_op jit(solution)/shard_map/ppermute | solution.py:22
  58.8 0.4 collective-permute-done.6.refs_1_
  59.2 0.0 collective-permute-done.3.near
  59.2 3.7 %shard_map.59.total = f32[2,2,2,256,512]{4,3,2,1,0:T(8,128)S(1)} custom-call(bf16[2,2,1,2,256,512]{5,4,3,2,1,0:T(8,128)(2,1)S(1)} %copy-done, f32[2,3,2,256,256]{4,3,2,1,0:T(8,128)S(1)} %shard_map.55.inverse, bf16[4,2,128,512]{3,2,1,0:T(8,128)(2,1)} %collective-permute-done.3.near, ...), custom_call_target="tpu_custom_call", output_to_operand_aliasing={{}: (5, {})} | custom-call | tf_op jit(solution)/shard_map/pallas_call | solution.py:227
  63.0 0.0 collective-permute-done.2.window
  63.0 2.2 %shard_map.60 = bf16[2,2,1,2,256,512]{5,4,3,2,1,0:T(8,128)(2,1)} custom-call(bf16[2,2,1,2,256,512]{5,4,3,2,1,0:T(8,128)(2,1)S(1)} %copy-done, f32[2,3,2,256,256]{4,3,2,1,0:T(8,128)S(1)} %shard_map.55.inverse, bf16[4,2,128,512]{3,2,1,0:T(8,128)(2,1)S(1)} %collective-permute-done.2.window, f32[2,2,2,256,512]{4,3,2,1,0:T(8,128)S(1)} %shard_map.59.total), custom_call_target="tpu_custom_call" | custom-call | tf_op jit(solution)/shard_map/pallas_call | solution.py:259
  (3 shorter events, 0.0 us)
Async XLA Ops:
  0.0 14.2 %copy-start.1 = (s32[2,8]{1,0:T(2,128)S(1)}, s32[2,8]{1,0:T(2,128)}, u32[]{:S(2)}) copy-start(s32[2,8]{1,0:T(2,128)} %partner.2) | copy-start | bytes 196
  2.2 33.8 %collective-permute-start.4 = (bf16[4,2,128,512]{3,2,1,0:T(8,128)(2,1)}, bf16[4,2,128,512]{3,2,1,0:T(8,128)(2,1)}, u32[]{:S(2)}, u32[]{:S(2)}) collective-permute-start(bf16[4,2,128,512]{3,2,1,0:T(8,128)(2,1)} %shard_map.56), channel_id=1, source_target_pairs={{0,7},{1,2},{2,1},{3,4},{4,3},{5,6},{6,5},{7,0},{8,15},{9,10},{10,... | collective-permute-start | bytes 3145736 | tf_op jit(solution)/shard_map/ppermute | solution.py:32
  10.0 14.9 %collective-permute-start = (bf16[2,2,128,512]{3,2,1,0:T(8,128)(2,1)S(1)}, bf16[2,2,128,512]{3,2,1,0:T(8,128)(2,1)S(1)}, u32[]{:S(2)}, u32[]{:S(2)}) collective-permute-start(bf16[2,2,128,512]{3,2,1,0:T(8,128)(2,1)S(1)} %get-tuple-element.12), channel_id=1, source_target_pairs={{0,8},{8,0},{16,24},{24,16},{1,9},{9,1},{17,25},{25,17},{2,10},{10... | collective-permute-start | bytes 1572872 | tf_op jit(solution)/shard_map/ppermute | solution.py:22
  11.6 14.9 %collective-permute-start.1 = (bf16[2,2,128,512]{3,2,1,0:T(8,128)(2,1)S(1)}, bf16[2,2,128,512]{3,2,1,0:T(8,128)(2,1)S(1)}, u32[]{:S(2)}, u32[]{:S(2)}) collective-permute-start(bf16[2,2,128,512]{3,2,1,0:T(8,128)(2,1)S(1)} %get-tuple-element.13), channel_id=1, source_target_pairs={{0,16},{8,24},{16,0},{24,8},{1,17},{9,25},{17,1},{25,9},{2,18},{10... | collective-permute-start | bytes 1572872 | tf_op jit(solution)/shard_map/ppermute | solution.py:22
  13.1 20.7 %collective-permute-start.7 = (bf16[2,2,128,512]{3,2,1,0:T(8,128)(2,1)}, bf16[2,2,128,512]{3,2,1,0:T(8,128)(2,1)S(1)}, u32[]{:S(2)}, u32[]{:S(2)}) collective-permute-start(bf16[2,2,128,512]{3,2,1,0:T(8,128)(2,1)} %get-tuple-element.14), channel_id=1, source_target_pairs={{0,8},{8,0},{16,24},{24,16},{1,9},{9,1},{17,25},{25,17},{2,10},{10... | collective-permute-start | bytes 1572872 | tf_op jit(solution)/shard_map/ppermute | solution.py:22
  13.7 21.4 %collective-permute-start.8 = (bf16[2,2,128,512]{3,2,1,0:T(8,128)(2,1)}, bf16[2,2,128,512]{3,2,1,0:T(8,128)(2,1)S(1)}, u32[]{:S(2)}, u32[]{:S(2)}) collective-permute-start(bf16[2,2,128,512]{3,2,1,0:T(8,128)(2,1)} %get-tuple-element.15), channel_id=1, source_target_pairs={{0,16},{8,24},{16,0},{24,8},{1,17},{9,25},{17,1},{25,9},{2,18},{10... | collective-permute-start | bytes 1572872 | tf_op jit(solution)/shard_map/ppermute | solution.py:22
  27.3 31.9 %collective-permute-start.3 = (bf16[4,2,128,512]{3,2,1,0:T(8,128)(2,1)}, bf16[4,2,128,512]{3,2,1,0:T(8,128)(2,1)}, u32[]{:S(2)}, u32[]{:S(2)}) collective-permute-start(bf16[4,2,128,512]{3,2,1,0:T(8,128)(2,1)} %constant_dynamic-update-slice_fusion), channel_id=1, source_target_pairs={{0,1},{1,0},{2,3},{3,2},{4,5},{5,4},{6,7},{7,6},{8,9},{9,8},{10,11... | collective-permute-start | bytes 3145736 | tf_op jit(solution)/shard_map/ppermute | solution.py:27
  27.3 35.7 %collective-permute-start.2 = (bf16[4,2,128,512]{3,2,1,0:T(8,128)(2,1)}, bf16[4,2,128,512]{3,2,1,0:T(8,128)(2,1)S(1)}, u32[]{:S(2)}, u32[]{:S(2)}) collective-permute-start(bf16[4,2,128,512]{3,2,1,0:T(8,128)(2,1)} %constant_dynamic-update-slice_fusion), channel_id=1, source_target_pairs={{0,7},{1,2},{2,1},{3,4},{4,3},{5,6},{6,5},{7,0},{8,15},{9,10},{10,... | collective-permute-start | bytes 3145736 | tf_op jit(solution)/shard_map/ppermute | solution.py:32
  36.0 13.5 %collective-permute-start.9 = (bf16[3,2,128,512]{3,2,1,0:T(8,128)(2,1)}, bf16[3,2,128,512]{3,2,1,0:T(8,128)(2,1)}, u32[]{:S(2)}, u32[]{:S(2)}) collective-permute-start(bf16[3,2,128,512]{3,2,1,0:T(8,128)(2,1)} %pad_maximum_fusion.1), channel_id=1, source_target_pairs={{0,1},{1,0},{2,3},{3,2},{4,5},{5,4},{6,7},{7,6},{8,9},{9,8},{10,11... | collective-permute-start | bytes 2359304 | tf_op jit(solution)/shard_map/ppermute | solution.py:27
  43.0 4.2 %copy-start.3 = (f32[8,256]{1,0:T(8,128)S(1)}, f32[8,256]{1,0:T(8,128)}, u32[]{:S(2)}) copy-start(f32[8,256]{1,0:T(8,128)} %param.8) | copy-start | bytes 24580
  43.0 4.2 %copy-start.4 = (s32[8,256]{1,0:T(8,128)S(1)}, s32[8,256]{1,0:T(8,128)}, u32[]{:S(2)}) copy-start(s32[8,256]{1,0:T(8,128)} %param.9) | copy-start | bytes 24580
  43.0 4.9 %copy-start.2 = (f32[8,8]{1,0:T(8,128)S(1)}, f32[8,8]{1,0:T(8,128)}, u32[]{:S(2)}) copy-start(f32[8,8]{1,0:T(8,128)} %occ.1) | copy-start | bytes 772
  43.0 2.5 %collective-permute-start.10 = (bf16[1,2,128,512]{3,2,1,0:T(8,128)(2,1)S(1)}, bf16[1,2,128,512]{3,2,1,0:T(8,128)(2,1)S(1)}, u32[]{:S(2)}, u32[]{:S(2)}) collective-permute-start(bf16[1,2,128,512]{3,2,1,0:T(8,128)(2,1)S(1)} %slice.36), channel_id=1, source_target_pairs={{0,1},{1,0},{2,3},{3,2},{4,5},{5,4},{6,7},{7,6},{8,9},{9,8},{10,11... | collective-permute-start | bytes 786440 | tf_op jit(solution)/shard_map/ppermute | solution.py:27
  44.9 13.9 %collective-permute-start.5 = (bf16[2,2,128,512]{3,2,1,0:T(8,128)(2,1)S(1)}, bf16[2,2,128,512]{3,2,1,0:T(8,128)(2,1)S(1)}, u32[]{:S(2)}, u32[]{:S(2)}) collective-permute-start(bf16[2,2,128,512]{3,2,1,0:T(8,128)(2,1)S(1)} %pad_maximum_fusion.2), channel_id=1, source_target_pairs={{0,8},{8,0},{16,24},{24,16},{1,9},{9,1},{17,25},{25,17},{2,10},{10... | collective-permute-start | bytes 1572872 | tf_op jit(solution)/shard_map/ppermute | solution.py:22
  45.6 13.6 %collective-permute-start.6 = (bf16[2,2,128,512]{3,2,1,0:T(8,128)(2,1)S(1)}, bf16[2,2,128,512]{3,2,1,0:T(8,128)(2,1)S(1)}, u32[]{:S(2)}, u32[]{:S(2)}) collective-permute-start(bf16[2,2,128,512]{3,2,1,0:T(8,128)(2,1)S(1)} %pad_maximum_fusion.3), channel_id=1, source_target_pairs={{0,16},{8,24},{16,0},{24,8},{1,17},{9,25},{17,1},{25,9},{2,18},{10... | collective-permute-start | bytes 1572872 | tf_op jit(solution)/shard_map/ppermute | solution.py:22
  47.9 2.9 %copy-start = (bf16[2,2,1,2,256,512]{5,4,3,2,1,0:T(8,128)(2,1)S(1)}, bf16[2,2,1,2,256,512]{5,4,3,2,1,0:T(8,128)(2,1)}, u32[]{:S(2)}) copy-start(bf16[2,2,1,2,256,512]{5,4,3,2,1,0:T(8,128)(2,1)} %factor.9) | copy-start | bytes 6291460

commit v8 on v7

--- a/solution.py
+++ b/solution.py
@@ -12,7 +12,7 @@
 ANY = pl.BlockSpec(memory_space=pl.ANY)
 VMEM = pl.BlockSpec(memory_space=pltpu.VMEM)
 SMEM = pl.BlockSpec(memory_space=pltpu.SMEM)
-PARAMS = pltpu.CompilerParams(vmem_limit_bytes=20 * 1024 * 1024)
+PARAMS = pltpu.CompilerParams(vmem_limit_bytes=8 * 1024 * 1024)
 WORK = 16
 COST = pl.CostEstimate(flops=0, bytes_accessed=0, transcendentals=0)
 
@@ -48,56 +48,32 @@
     return jnp.transpose(jnp.broadcast_to(row, (8, row.shape[1])))[:, :1]
 
 
-def lay_kernel(factor, out, sems):
-    kc, half = factor.shape[1], out.shape[2]
+def pack_kernel(bits, h, partner, factor, *refs):
+    outs, sems = refs[:-1], refs[-1]
+    kc, half = factor.shape[1], outs[0].shape[2]
+    targets = [out.at[n] for out in outs for n in range(out.shape[0])]
+    group = lax.axis_index("kpt")
     copies = []
-    for at in range(out.shape[0]):
-        source = factor.at[at // kc, at % kc, 0, :, pl.ds(0, half), :]
-        copies.append(pltpu.make_async_copy(source, out.at[at], sems.at[at]))
-        copies[-1].start()
+    for transfer, bit in enumerate(bits):
+        far_group = jnp.bitwise_xor(group, 1 << bit)
+        for k in range(kc):
+            slot = partner[transfer, far_group * kc + k] - group * kc
+            source = factor.at[transfer, slot, 0, :, pl.ds(h * half, half), :]
+            at = transfer * kc + k
+            copies.append(pltpu.make_async_copy(source, targets[at], sems.at[at]))
+            copies[-1].start()
     for copy in copies:
         copy.wait()
 
 
-def lay(factor):
-    transfers, kc, _, parts, nv, naux = factor.shape
-    return pl.pallas_call(
-        lay_kernel,
-        out_shape=jax.ShapeDtypeStruct((transfers * kc, parts, nv // 2, naux), BF16),
-        in_specs=[ANY],
-        out_specs=VMEM,
-        scratch_shapes=[pltpu.SemaphoreType.DMA((transfers * kc,))],
-        cost_estimate=COST,
-        compiler_params=PARAMS,
-    )(pltpu.with_memory_space_constraint(factor, pltpu.HBM))
-
-
-def pack_kernel(bits, partner, factor, *refs):
-    outs, sems = refs[:-1], refs[-1]
-    kc, half = factor.shape[1], outs[0].shape[2]
-    group = lax.axis_index("kpt")
-    copies = []
-    for h in (1, 0):
-        for transfer, bit in enumerate(bits):
-            far_group = jnp.bitwise_xor(group, 1 << bit)
-            for k in range(kc):
-                slot = partner[transfer, far_group * kc + k] - group * kc
-                source = factor.at[transfer, slot, 0, :, pl.ds(h * half, half), :]
-                target = outs[h * len(bits) + transfer].at[k]
-                copies.append(pltpu.make_async_copy(source, target, sems.at[len(copies)]))
-                copies[-1].start()
-    for copy in copies:
-        copy.wait()
-
-
-def pack(bits, partner, factor, work):
-    transfers, kc, _, parts, nv, naux = factor.shape
-    return pl.pallas_call(
-        functools.partial(pack_kernel, bits),
-        out_shape=[jax.ShapeDtypeStruct((kc, parts, nv // 2, naux), BF16)] * (2 * transfers),
+def pack(bits, h, counts, partner, factor, work):
+    _, _, _, parts, nv, naux = factor.shape
+    return pl.pallas_call(
+        functools.partial(pack_kernel, bits, h),
+        out_shape=[jax.ShapeDtypeStruct((n, parts, nv // 2, naux), BF16) for n in counts],
         in_specs=[SMEM, ANY],
-        out_specs=[VMEM] * (2 * transfers),
-        scratch_shapes=[pltpu.SemaphoreType.DMA((2 * transfers * kc,))],
+        out_specs=[VMEM] * len(counts),
+        scratch_shapes=[pltpu.SemaphoreType.DMA((sum(counts),))],
         cost_estimate=pl.CostEstimate(flops=0, bytes_accessed=work, transcendentals=0),
         compiler_params=PARAMS,
     )(
@@ -274,13 +250,11 @@
     transfers, kc = factor.shape[:2]
     bits = (0, lax.axis_size("kpt").bit_length() - 2)
 
-    group = lax.axis_index("kpt")
-    part = lay(factor)
+    (part,) = pack(bits, 0, [transfers * kc], partner, factor, 0)
     beside = far_swap(part)
-    packs = pack(bits, after(partner, part), factor, WORK * factor.size)
-    earlies, lates = packs[:transfers], packs[transfers:]
+    lates = pack(bits, 1, [kc] * transfers, after(partner, part), factor, WORK * factor.size)
     late_own = [group_swap(lates[t], bits[t]) for t in range(transfers)]
-    early_own = [group_swap(earlies[t], bits[t]) for t in range(transfers)]
+    early_own = [group_swap(part[t * kc : (t + 1) * kc], bits[t]) for t in range(transfers)]
     late_block = jnp.concatenate(late_own)
     late_far = far_swap(late_block)
     late_near = near_swap(late_block)
@@ -288,12 +262,7 @@
     early_near = jnp.concatenate(
         [near_swap(after(early_block[:-1], beside)), near_swap(early_block[-1:])]
     )
-    early_far = []
-    for t in range(transfers):
-        far_group = jnp.bitwise_xor(group, 1 << bits[t])
-        slots = lax.dynamic_slice_in_dim(partner[t], far_group * kc, kc) - group * kc
-        ordered = [lax.dynamic_slice_in_dim(beside, t * kc + slots[k], 1) for k in range(kc)]
-        early_far.append(group_swap(jnp.concatenate(ordered), bits[t]))
+    early_far = [group_swap(beside[t * kc : (t + 1) * kc], bits[t]) for t in range(transfers)]
 
     virtual = virtual_energies(vir_sorted, vir_order)
     inverse = inverses(bits, partner, occ_energy, virtual, kc)

time: 65.6 us -> 55.2 us (0.84)
  between operations: 6.44 us -> 0.2 us
  waiting for transfers between devices: 22.8 us -> 27.7 us
  local copies, waits for them, and re-layouts: 4.27 us -> 0.29 us
  Pallas kernels: 16.5 us -> 13.7 us
  other arithmetic: 3.14 us -> 0.92 us
    ppermute x6, waiting for transfers between devices: 22.8 us -> 27.3 us  [group_swap(): return lax.ppermute(block, 'kpt', [(g, g ^ 1 << bit) for g in range(count)])]
    pallas_call x2, Pallas kernels: 5.47 us -> 3.85 us  [pack(): pl.pallas_call(functools.partial(pack_kernel, bits, h), out_shape=[jax.Sh...]
    dynamic_slice x1 -> x0, local copies, waits for them, and re-layouts: 1.25 us -> none  [body(): lax.dynamic_slice_in_dim(beside, t * kc + slots[k], 1)]
    pallas_call x1, Pallas kernels: 3.75 us -> 2.52 us  [second_terms(): pl.pallas_call(second_kernel, out_shape=jax.ShapeDtypeStruct(total.shape,...]
    slice x3 -> x2, local copies, waits for them, and re-layouts: 1.31 us -> 0.17 us  [the longest x1 0.1 us: body(): part[t * kc:(t + 1) * kc]]
    concatenate x1, other arithmetic: 1.23 us -> 0.09 us  [body(): jnp.concatenate([near_swap(after(early_block[:-1], beside)), near_swap(ea...]
    concatenate x1, other arithmetic: 0.97 us -> 0.07 us  [body(): early_block = jnp.concatenate(early_own)]
    concatenate x1, local copies, waits for them, and re-layouts: 0.83 us -> 0.03 us  [body(): late_block = jnp.concatenate(late_own)]
  transfers between devices with their start and end apart: 11 -> 11, of which waited for: 6 -> 6; matrix products, arithmetic and copies ran while one was open for 11% -> 2% of each run, Pallas kernels for 19% -> 17%
where the time goes in v8:
time: 55.2 us; the launch traced here: 55 us
  waiting for transfers between devices  27.7 us (50%)
  Pallas kernels  13.7 us (25%)
  starting transfers between devices  12.2 us (22%)
  other arithmetic  0.92 us (2%)
    ppermute x6, waiting for transfers between devices, group_swap(): return lax.ppermute(block, 'kpt', [(g, g ^ 1 << bit) for g in range(count)])  27.3 us
    ppermute x6, starting transfers between devices, group_swap(): return lax.ppermute(block, 'kpt', [(g, g ^ 1 << bit) for g in range(count)])  6.3 us
    ppermute x2, starting transfers between devices, far_swap(): lax.ppermute(block, 'occ', [(i, (i + (1 if i % 2 else count - 1)) % count...  5.16 us
    pallas_call x2, Pallas kernels, pack(): pl.pallas_call(functools.partial(pack_kernel, bits, h), out_shape=[jax.Sh...  3.85 us
    pallas_call x1, Pallas kernels, first_terms(): pl.pallas_call(first_kernel, out_shape=jax.ShapeDtypeStruct((transfers, k...  3.47 us
    pallas_call x1, Pallas kernels, second_terms(): pl.pallas_call(second_kernel, out_shape=jax.ShapeDtypeStruct(total.shape,...  2.52 us
    pallas_call x1, Pallas kernels, last_terms(): pl.pallas_call(last_kernel, out_shape=jax.ShapeDtypeStruct(factor.shape,...  2.24 us
    pallas_call x1, Pallas kernels, inverses(): pl.pallas_call(functools.partial(inverse_kernel, bits), out_shape=jax.Sha...  1.59 us
  transfers between devices with their start and end apart: 11, of which 6 were waited for; matrix products, arithmetic and copies ran while one was open for 2% of the time, Pallas kernels for 17%

profile of v8, /device:TPU:0, one launch (start us, length us, event | category | flops | bytes accessed | tf_op | source)
XLA Modules:
  0.0 55.0 jit_solution(2146910344309493532)
XLA Ops:
  0.0 1.9 %shard_map.56 = bf16[4,2,128,512]{3,2,1,0:T(8,128)(2,1)S(1)} custom-call(s32[2,8]{1,0:T(2,128)} %partner.4, bf16[2,2,1,2,256,512]{5,4,3,2,1,0:T(8,128)(2,1)} %factor.9), custom_call_target="tpu_custom_call" | custom-call | tf_op jit(solution)/shard_map/pallas_call | solution.py:71
  1.9 4.6 %collective-permute-start.4 = (bf16[4,2,128,512]{3,2,1,0:T(8,128)(2,1)S(1)}, bf16[4,2,128,512]{3,2,1,0:T(8,128)(2,1)S(1)}, u32[]{:S(2)}, u32[]{:S(2)}) collective-permute-start(bf16[4,2,128,512]{3,2,1,0:T(8,128)(2,1)S(1)} %shard_map.56), channel_id=1, source_target_pairs={{0,7},{1,2},{2,1},{3,4},{4,3},{5,6},{6,5},{7,0},{8,15},{9,10},{10,... | collective-permute-start | bytes 3145736 | tf_op jit(solution)/shard_map/ppermute | solution.py:32
  6.5 1.9 %shard_map.57 = (bf16[2,2,128,512]{3,2,1,0:T(8,128)(2,1)S(1)}, bf16[2,2,128,512]{3,2,1,0:T(8,128)(2,1)S(1)}) custom-call(s32[2,8]{1,0:T(2,128)} %partner.4, bf16[2,2,1,2,256,512]{5,4,3,2,1,0:T(8,128)(2,1)} %factor.9), custom_call_target="tpu_custom_call" | custom-call | bytes 16777216 | tf_op jit(solution)/shard_map/pallas_call | solution.py:71
  8.4 1.6 %collective-permute-start = (bf16[2,2,128,512]{3,2,1,0:T(8,128)(2,1)S(1)}, bf16[2,2,128,512]{3,2,1,0:T(8,128)(2,1)S(1)}, u32[]{:S(2)}, u32[]{:S(2)}) collective-permute-start(bf16[2,2,128,512]{3,2,1,0:T(8,128)(2,1)S(1)} %get-tuple-element.10), channel_id=1, source_target_pairs={{0,8},{8,0},{16,24},{24,16},{1,9},{9,1},{17,25},{25,17},{2,10},{10... | collective-permute-start | bytes 1572872 | tf_op jit(solution)/shard_map/ppermute | solution.py:22
  10.0 1.5 %collective-permute-start.1 = (bf16[2,2,128,512]{3,2,1,0:T(8,128)(2,1)S(1)}, bf16[2,2,128,512]{3,2,1,0:T(8,128)(2,1)S(1)}, u32[]{:S(2)}, u32[]{:S(2)}) collective-permute-start(bf16[2,2,128,512]{3,2,1,0:T(8,128)(2,1)S(1)} %get-tuple-element.11), channel_id=1, source_target_pairs={{0,16},{8,24},{16,0},{24,8},{1,17},{9,25},{17,1},{25,9},{2,18},{10... | collective-permute-start | bytes 1572872 | tf_op jit(solution)/shard_map/ppermute | solution.py:22
  11.5 0.1 fusion
  11.6 0.6 %collective-permute-start.8 = (bf16[2,2,128,512]{3,2,1,0:T(8,128)(2,1)S(1)}, bf16[2,2,128,512]{3,2,1,0:T(8,128)(2,1)S(1)}, u32[]{:S(2)}, u32[]{:S(2)}) collective-permute-start(bf16[2,2,128,512]{3,2,1,0:T(8,128)(2,1)S(1)} %get-tuple-element.13), channel_id=1, source_target_pairs={{0,16},{8,24},{16,0},{24,8},{1,17},{9,25},{17,1},{25,9},{2,18},{10... | collective-permute-start | bytes 1572872 | tf_op jit(solution)/shard_map/ppermute | solution.py:22
  12.2 0.5 collective-permute-start.7
  12.7 10.6 %collective-permute-done.refs_2_ = bf16[2,2,128,512]{3,2,1,0:T(8,128)(2,1)S(1)} collective-permute-done((bf16[2,2,128,512]{3,2,1,0:T(8,128)(2,1)S(1)}, bf16[2,2,128,512]{3,2,1,0:T(8,128)(2,1)S(1)}, u32[]{:S(2)}, u32[]{:S(2)}) %collective-permute-start) | collective-permute-done | bytes 524320 | tf_op jit(solution)/shard_map/ppermute | solution.py:22
  23.4 1.5 %collective-permute-done.1.refs_3_ = bf16[2,2,128,512]{3,2,1,0:T(8,128)(2,1)S(1)} collective-permute-done((bf16[2,2,128,512]{3,2,1,0:T(8,128)(2,1)S(1)}, bf16[2,2,128,512]{3,2,1,0:T(8,128)(2,1)S(1)}, u32[]{:S(2)}, u32[]{:S(2)}) %collective-permute-start.1) | collective-permute-done | bytes 524320 | tf_op jit(solution)/shard_map/ppermute | solution.py:22
  24.9 0.0 copy-start.3
  24.9 0.0 copy-start.4
  24.9 0.0 copy-start.1
  24.9 0.0 copy-start.2
  24.9 0.1 collective-permute-start.3
  25.0 0.6 %collective-permute-start.2 = (bf16[4,2,128,512]{3,2,1,0:T(8,128)(2,1)S(1)}, bf16[4,2,128,512]{3,2,1,0:T(8,128)(2,1)S(1)}, u32[]{:S(2)}, u32[]{:S(2)}) collective-permute-start(bf16[4,2,128,512]{3,2,1,0:T(8,128)(2,1)S(1)} %constant_dynamic-update-slice_fusion), channel_id=1, source_target_pairs={{0,7},{1,2},{2,1},{3,4},{4,3},{5,6},{6,5},{7,0},{8,15},{9,10},{10,... | collective-permute-start | bytes 3145736 | tf_op jit(solution)/shard_map/ppermute | solution.py:32
  25.6 7.8 %collective-permute-done.8.refs_1_ = bf16[2,2,128,512]{3,2,1,0:T(8,128)(2,1)S(1)} collective-permute-done((bf16[2,2,128,512]{3,2,1,0:T(8,128)(2,1)S(1)}, bf16[2,2,128,512]{3,2,1,0:T(8,128)(2,1)S(1)}, u32[]{:S(2)}, u32[]{:S(2)}) %collective-permute-start.8) | collective-permute-done | bytes 524320 | tf_op jit(solution)/shard_map/ppermute | solution.py:22
  33.4 0.0 collective-permute-done.7.refs_0_
  33.4 0.1 pad_maximum_fusion.1
  33.5 0.0 collective-permute-done.4
  33.5 0.1 collective-permute-start.9
  33.6 0.6 %collective-permute-start.10 = (bf16[1,2,128,512]{3,2,1,0:T(8,128)(2,1)S(1)}, bf16[1,2,128,512]{3,2,1,0:T(8,128)(2,1)S(1)}, u32[]{:S(2)}, u32[]{:S(2)}) collective-permute-start(bf16[1,2,128,512]{3,2,1,0:T(8,128)(2,1)S(1)} %slice.28), channel_id=1, source_target_pairs={{0,1},{1,0},{2,3},{3,2},{4,5},{5,4},{6,7},{7,6},{8,9},{9,8},{10,11... | collective-permute-start | bytes 786440 | tf_op jit(solution)/shard_map/ppermute | solution.py:27
  34.2 0.1 fusion.1
  34.2 1.6 %collective-permute-start.6 = (bf16[2,2,128,512]{3,2,1,0:T(8,128)(2,1)S(1)}, bf16[2,2,128,512]{3,2,1,0:T(8,128)(2,1)S(1)}, u32[]{:S(2)}, u32[]{:S(2)}) collective-permute-start(bf16[2,2,128,512]{3,2,1,0:T(8,128)(2,1)S(1)} %get-tuple-element.15), channel_id=1, source_target_pairs={{0,16},{8,24},{16,0},{24,8},{1,17},{9,25},{17,1},{25,9},{2,18},{10... | collective-permute-start | bytes 1572872 | tf_op jit(solution)/shard_map/ppermute | solution.py:22
  35.8 0.4 collective-permute-done.10
  36.2 0.5 collective-permute-start.5
  36.8 0.0 copy-done.3
  36.8 0.0 copy-done.4
  36.8 0.8 %select_reduce_fusion.virtual = f32[8,256]{1,0:T(8,128)S(1)} fusion(f32[8,256]{1,0:T(8,128)S(1)} %copy-done.3, s32[8,256]{1,0:T(8,128)S(1)} %copy-done.4), kind=kLoop, calls=%fused_computation | loop fusion | flops 1570816 | bytes 24576 | tf_op jit(solution)/shard_map/reduce_sum | solution.py:44
  37.5 0.0 copy-done.1
  37.5 0.0 copy-done.2
  37.5 0.0 copy-start
  37.6 1.6 %shard_map.55.inverse = f32[2,3,2,256,256]{4,3,2,1,0:T(8,128)S(1)} custom-call(s32[2,8]{1,0:T(2,128)S(1)} %copy-done.1, f32[8,8]{1,0:T(8,128)S(1)} %copy-done.2, f32[8,256]{1,0:T(8,128)S(1)} %select_reduce_fusion.virtual), custom_call_target="tpu_custom_call" | custom-call | tf_op jit(solution)/shard_map/pallas_call | solution.py:108
  39.2 0.0 collective-permute-done.9
  39.2 0.1 pad_maximum_fusion.refs_4_
  39.3 0.0 copy-done
  39.3 3.5 %shard_map.58.refs_2_ = f32[2,2,2,256,512]{4,3,2,1,0:T(8,128)S(1)} custom-call(bf16[2,2,1,2,256,512]{5,4,3,2,1,0:T(8,128)(2,1)S(1)} %copy-done, f32[2,3,2,256,256]{4,3,2,1,0:T(8,128)S(1)} %shard_map.55.inverse, bf16[2,2,128,512]{3,2,1,0:T(8,128)(2,1)S(1)} %collective-permute-done.7.refs_0_, bf16[2,2,128,512]{3,2,1,0:T(8,128)(2,1)S(1)} %collective-permute-done.8.refs_1_, ...), custom_call_target="tpu_custom_call" | custom-call | tf_op jit(solution)/shard_map/pallas_call | solution.py:175
  42.8 0.0 collective-permute-done.3.near
  42.8 5.4 %collective-permute-done.6.refs_1_ = bf16[2,2,128,512]{3,2,1,0:T(8,128)(2,1)S(1)} collective-permute-done((bf16[2,2,128,512]{3,2,1,0:T(8,128)(2,1)S(1)}, bf16[2,2,128,512]{3,2,1,0:T(8,128)(2,1)S(1)}, u32[]{:S(2)}, u32[]{:S(2)}) %collective-permute-start.6) | collective-permute-done | bytes 524320 | tf_op jit(solution)/shard_map/ppermute | solution.py:22
  48.1 2.0 %collective-permute-done.5.refs_0_ = bf16[2,2,128,512]{3,2,1,0:T(8,128)(2,1)S(1)} collective-permute-done((bf16[2,2,128,512]{3,2,1,0:T(8,128)(2,1)S(1)}, bf16[2,2,128,512]{3,2,1,0:T(8,128)(2,1)S(1)}, u32[]{:S(2)}, u32[]{:S(2)}) %collective-permute-start.5) | collective-permute-done | bytes 524320 | tf_op jit(solution)/shard_map/ppermute | solution.py:22
  50.2 2.5 %shard_map.59.total = f32[2,2,2,256,512]{4,3,2,1,0:T(8,128)S(1)} custom-call(bf16[2,2,1,2,256,512]{5,4,3,2,1,0:T(8,128)(2,1)S(1)} %copy-done, f32[2,3,2,256,256]{4,3,2,1,0:T(8,128)S(1)} %shard_map.55.inverse, bf16[4,2,128,512]{3,2,1,0:T(8,128)(2,1)S(1)} %collective-permute-done.3.near, ...), custom_call_target="tpu_custom_call", output_to_operand_aliasing={{}: (5, {})} | custom-call | tf_op jit(solution)/shard_map/pallas_call | solution.py:203
  52.7 0.0 collective-permute-done.2.window
  52.7 2.2 %shard_map.60 = bf16[2,2,1,2,256,512]{5,4,3,2,1,0:T(8,128)(2,1)} custom-call(bf16[2,2,1,2,256,512]{5,4,3,2,1,0:T(8,128)(2,1)S(1)} %copy-done, f32[2,3,2,256,256]{4,3,2,1,0:T(8,128)S(1)} %shard_map.55.inverse, bf16[4,2,128,512]{3,2,1,0:T(8,128)(2,1)S(1)} %collective-permute-done.2.window, f32[2,2,2,256,512]{4,3,2,1,0:T(8,128)S(1)} %shard_map.59.total), custom_call_target="tpu_custom_call" | custom-call | tf_op jit(solution)/shard_map/pallas_call | solution.py:235
  (3 shorter events, 0.1 us)
Async XLA Ops:
  1.9 31.6 %collective-permute-start.4 = (bf16[4,2,128,512]{3,2,1,0:T(8,128)(2,1)S(1)}, bf16[4,2,128,512]{3,2,1,0:T(8,128)(2,1)S(1)}, u32[]{:S(2)}, u32[]{:S(2)}) collective-permute-start(bf16[4,2,128,512]{3,2,1,0:T(8,128)(2,1)S(1)} %shard_map.56), channel_id=1, source_target_pairs={{0,7},{1,2},{2,1},{3,4},{4,3},{5,6},{6,5},{7,0},{8,15},{9,10},{10,... | collective-permute-start | bytes 3145736 | tf_op jit(solution)/shard_map/ppermute | solution.py:32
  8.4 14.9 %collective-permute-start = (bf16[2,2,128,512]{3,2,1,0:T(8,128)(2,1)S(1)}, bf16[2,2,128,512]{3,2,1,0:T(8,128)(2,1)S(1)}, u32[]{:S(2)}, u32[]{:S(2)}) collective-permute-start(bf16[2,2,128,512]{3,2,1,0:T(8,128)(2,1)S(1)} %get-tuple-element.10), channel_id=1, source_target_pairs={{0,8},{8,0},{16,24},{24,16},{1,9},{9,1},{17,25},{25,17},{2,10},{10... | collective-permute-start | bytes 1572872 | tf_op jit(solution)/shard_map/ppermute | solution.py:22
  10.0 14.9 %collective-permute-start.1 = (bf16[2,2,128,512]{3,2,1,0:T(8,128)(2,1)S(1)}, bf16[2,2,128,512]{3,2,1,0:T(8,128)(2,1)S(1)}, u32[]{:S(2)}, u32[]{:S(2)}) collective-permute-start(bf16[2,2,128,512]{3,2,1,0:T(8,128)(2,1)S(1)} %get-tuple-element.11), channel_id=1, source_target_pairs={{0,16},{8,24},{16,0},{24,8},{1,17},{9,25},{17,1},{25,9},{2,18},{10... | collective-permute-start | bytes 1572872 | tf_op jit(solution)/shard_map/ppermute | solution.py:22
  11.6 21.8 %collective-permute-start.8 = (bf16[2,2,128,512]{3,2,1,0:T(8,128)(2,1)S(1)}, bf16[2,2,128,512]{3,2,1,0:T(8,128)(2,1)S(1)}, u32[]{:S(2)}, u32[]{:S(2)}) collective-permute-start(bf16[2,2,128,512]{3,2,1,0:T(8,128)(2,1)S(1)} %get-tuple-element.13), channel_id=1, source_target_pairs={{0,16},{8,24},{16,0},{24,8},{1,17},{9,25},{17,1},{25,9},{2,18},{10... | collective-permute-start | bytes 1572872 | tf_op jit(solution)/shard_map/ppermute | solution.py:22
  12.2 21.2 %collective-permute-start.7 = (bf16[2,2,128,512]{3,2,1,0:T(8,128)(2,1)S(1)}, bf16[2,2,128,512]{3,2,1,0:T(8,128)(2,1)S(1)}, u32[]{:S(2)}, u32[]{:S(2)}) collective-permute-start(bf16[2,2,128,512]{3,2,1,0:T(8,128)(2,1)S(1)} %get-tuple-element.14), channel_id=1, source_target_pairs={{0,8},{8,0},{16,24},{24,16},{1,9},{9,1},{17,25},{25,17},{2,10},{10... | collective-permute-start | bytes 1572872 | tf_op jit(solution)/shard_map/ppermute | solution.py:22
  24.9 11.9 %copy-start.3 = (f32[8,256]{1,0:T(8,128)S(1)}, f32[8,256]{1,0:T(8,128)}, u32[]{:S(2)}) copy-start(f32[8,256]{1,0:T(8,128)} %param.8) | copy-start | bytes 24580
  24.9 11.9 %copy-start.4 = (s32[8,256]{1,0:T(8,128)S(1)}, s32[8,256]{1,0:T(8,128)}, u32[]{:S(2)}) copy-start(s32[8,256]{1,0:T(8,128)} %param.9) | copy-start | bytes 24580
  24.9 12.6 %copy-start.1 = (s32[2,8]{1,0:T(2,128)S(1)}, s32[2,8]{1,0:T(2,128)}, u32[]{:S(2)}) copy-start(s32[2,8]{1,0:T(2,128)} %partner.4) | copy-start | bytes 196
  24.9 12.6 %copy-start.2 = (f32[8,8]{1,0:T(8,128)S(1)}, f32[8,8]{1,0:T(8,128)}, u32[]{:S(2)}) copy-start(f32[8,8]{1,0:T(8,128)} %occ.1) | copy-start | bytes 772
  24.9 17.8 %collective-permute-start.3 = (bf16[4,2,128,512]{3,2,1,0:T(8,128)(2,1)S(1)}, bf16[4,2,128,512]{3,2,1,0:T(8,128)(2,1)S(1)}, u32[]{:S(2)}, u32[]{:S(2)}) collective-permute-start(bf16[4,2,128,512]{3,2,1,0:T(8,128)(2,1)S(1)} %constant_dynamic-update-slice_fusion), channel_id=1, source_target_pairs={{0,1},{1,0},{2,3},{3,2},{4,5},{5,4},{6,7},{7,6},{8,9},{9,8},{10,11... | collective-permute-start | bytes 3145736 | tf_op jit(solution)/shard_map/ppermute | solution.py:27
  25.0 27.7 %collective-permute-start.2 = (bf16[4,2,128,512]{3,2,1,0:T(8,128)(2,1)S(1)}, bf16[4,2,128,512]{3,2,1,0:T(8,128)(2,1)S(1)}, u32[]{:S(2)}, u32[]{:S(2)}) collective-permute-start(bf16[4,2,128,512]{3,2,1,0:T(8,128)(2,1)S(1)} %constant_dynamic-update-slice_fusion), channel_id=1, source_target_pairs={{0,7},{1,2},{2,1},{3,4},{4,3},{5,6},{6,5},{7,0},{8,15},{9,10},{10,... | collective-permute-start | bytes 3145736 | tf_op jit(solution)/shard_map/ppermute | solution.py:32
  33.5 5.7 %collective-permute-start.9 = (bf16[3,2,128,512]{3,2,1,0:T(8,128)(2,1)S(1)}, bf16[3,2,128,512]{3,2,1,0:T(8,128)(2,1)S(1)}, u32[]{:S(2)}, u32[]{:S(2)}) collective-permute-start(bf16[3,2,128,512]{3,2,1,0:T(8,128)(2,1)S(1)} %pad_maximum_fusion.1), channel_id=1, source_target_pairs={{0,1},{1,0},{2,3},{3,2},{4,5},{5,4},{6,7},{7,6},{8,9},{9,8},{10,11... | collective-permute-start | bytes 2359304 | tf_op jit(solution)/shard_map/ppermute | solution.py:27
  33.6 2.6 %collective-permute-start.10 = (bf16[1,2,128,512]{3,2,1,0:T(8,128)(2,1)S(1)}, bf16[1,2,128,512]{3,2,1,0:T(8,128)(2,1)S(1)}, u32[]{:S(2)}, u32[]{:S(2)}) collective-permute-start(bf16[1,2,128,512]{3,2,1,0:T(8,128)(2,1)S(1)} %slice.28), channel_id=1, source_target_pairs={{0,1},{1,0},{2,3},{3,2},{4,5},{5,4},{6,7},{7,6},{8,9},{9,8},{10,11... | collective-permute-start | bytes 786440 | tf_op jit(solution)/shard_map/ppermute | solution.py:27
  34.2 13.9 %collective-permute-start.6 = (bf16[2,2,128,512]{3,2,1,0:T(8,128)(2,1)S(1)}, bf16[2,2,128,512]{3,2,1,0:T(8,128)(2,1)S(1)}, u32[]{:S(2)}, u32[]{:S(2)}) collective-permute-start(bf16[2,2,128,512]{3,2,1,0:T(8,128)(2,1)S(1)} %get-tuple-element.15), channel_id=1, source_target_pairs={{0,16},{8,24},{16,0},{24,8},{1,17},{9,25},{17,1},{25,9},{2,18},{10... | collective-permute-start | bytes 1572872 | tf_op jit(solution)/shard_map/ppermute | solution.py:22
  36.2 14.0 %collective-permute-start.5 = (bf16[2,2,128,512]{3,2,1,0:T(8,128)(2,1)S(1)}, bf16[2,2,128,512]{3,2,1,0:T(8,128)(2,1)S(1)}, u32[]{:S(2)}, u32[]{:S(2)}) collective-permute-start(bf16[2,2,128,512]{3,2,1,0:T(8,128)(2,1)S(1)} %get-tuple-element.16), channel_id=1, source_target_pairs={{0,8},{8,0},{16,24},{24,16},{1,9},{9,1},{17,25},{25,17},{2,10},{10... | collective-permute-start | bytes 1572872 | tf_op jit(solution)/shard_map/ppermute | solution.py:22
  37.5 1.7 %copy-start = (bf16[2,2,1,2,256,512]{5,4,3,2,1,0:T(8,128)(2,1)S(1)}, bf16[2,2,1,2,256,512]{5,4,3,2,1,0:T(8,128)(2,1)}, u32[]{:S(2)}) copy-start(bf16[2,2,1,2,256,512]{5,4,3,2,1,0:T(8,128)(2,1)} %factor.9) | copy-start | bytes 6291460

commit v9 on v7

--- a/solution.py
+++ b/solution.py
@@ -12,8 +12,9 @@
 ANY = pl.BlockSpec(memory_space=pl.ANY)
 VMEM = pl.BlockSpec(memory_space=pltpu.VMEM)
 SMEM = pl.BlockSpec(memory_space=pltpu.SMEM)
-PARAMS = pltpu.CompilerParams(vmem_limit_bytes=20 * 1024 * 1024)
+PARAMS = pltpu.CompilerParams(vmem_limit_bytes=8 * 1024 * 1024)
 WORK = 16
+ROWS = 16
 COST = pl.CostEstimate(flops=0, bytes_accessed=0, transcendentals=0)
 
 
@@ -106,7 +107,7 @@
     )
 
 
-def inverse_kernel(bits, partner, occ, virtual, out):
+def inverse_kernel(bits, partner, occ, virtual, out, choice):
     _, _, kc, nv, _ = out.shape
     total = occ.shape[1]
     group, orbit = lax.axis_index("kpt"), lax.axis_index("occ")
@@ -119,6 +120,10 @@
         for transfer in range(len(bits)):
             far_point = partner[transfer, point]
             column = column_of(virtual[pl.ds(far_point, 1), :])
+            slot = far_point - jnp.bitwise_xor(group, 1 << bits[transfer]) * kc
+            for c in range(kc):
+                chosen = jnp.where(slot == c, 1.0, 0.0)
+                choice[transfer, k, c] = jnp.full(choice.shape[3:], chosen, F32).astype(BF16)
             for place, index in enumerate(columns):
                 level = occ[point, orbit] + occ[far_point, index]
                 out[transfer, place, k] = 1.0 / ((level - column) - row)
@@ -127,13 +132,16 @@
     lax.fori_loop(0, kc, point_step, 0)
 
 
-def inverses(bits, partner, occ_energy, virtual, kc):
+def inverses(bits, partner, occ_energy, virtual, kc, naux):
     nv = virtual.shape[1]
     return pl.pallas_call(
         functools.partial(inverse_kernel, bits),
-        out_shape=jax.ShapeDtypeStruct((len(bits), 3, kc, nv, nv), F32),
+        out_shape=[
+            jax.ShapeDtypeStruct((len(bits), 3, kc, nv, nv), F32),
+            jax.ShapeDtypeStruct((len(bits), kc, kc, ROWS, naux), BF16),
+        ],
         in_specs=[SMEM, SMEM, VMEM],
-        out_specs=VMEM,
+        out_specs=[VMEM, VMEM],
         cost_estimate=COST,
         compiler_params=PARAMS,
     )(partner, occ_energy, virtual)
@@ -206,15 +214,11 @@
     )(*operands)
 
 
-def second_kernel(factor, inverse, near, *refs):
-    fars, total, out = refs[:-2], refs[-2], refs[-1]
+def near_kernel(factor, inverse, near, total, out):
     kc, half = factor.shape[1], near.shape[2]
 
     def terms_of(t, k):
-        return [
-            (near[t * kc + k], inverse[t, 1, k, :, half_of(1, half)]),
-            (fars[t][k], inverse[t, 2, k, :, half_of(0, half)]),
-        ]
+        return [(near[t * kc + k], inverse[t, 1, k, :, half_of(1, half)])]
 
     def finish(t, k, part, value):
         out[t, k, part] = value + total[t, k, part]
@@ -222,17 +226,32 @@
     contract(factor, terms_of, finish)
 
 
-def second_terms(factor, inverse, near, fars, total):
-    operands = [factor, inverse, near, *fars, total]
-    return pl.pallas_call(
-        second_kernel,
+def far_kernel(factor, inverse, choice, *refs):
+    fars, total, out = refs[:-2], refs[-2], refs[-1]
+    kc, half = factor.shape[1], fars[0].shape[2]
+
+    def terms_of(t, k):
+        blocks = [fars[t][c].reshape(-1, *choice.shape[3:]) for c in range(kc)]
+        chosen = [block * choice[t, k, c][None] for c, block in enumerate(blocks)]
+        window = functools.reduce(jnp.add, chosen)
+        return [(window.reshape(fars[t].shape[1:]), inverse[t, 2, k, :, half_of(0, half)])]
+
+    def finish(t, k, part, value):
+        out[t, k, part] = value + total[t, k, part]
+
+    contract(factor, terms_of, finish)
+
+
+def more_terms(body, operands, total):
+    return pl.pallas_call(
+        body,
         out_shape=jax.ShapeDtypeStruct(total.shape, F32),
-        in_specs=[VMEM] * len(operands),
+        in_specs=[VMEM] * (len(operands) + 1),
         out_specs=VMEM,
-        input_output_aliases={len(operands) - 1: 0},
-        cost_estimate=COST,
-        compiler_params=PARAMS,
-    )(*operands)
+        input_output_aliases={len(operands): 0},
+        cost_estimate=COST,
+        compiler_params=PARAMS,
+    )(*operands, total)
 
 
 def last_kernel(factor, inverse, window, total, out, staged, sems):
@@ -274,7 +293,6 @@
     transfers, kc = factor.shape[:2]
     bits = (0, lax.axis_size("kpt").bit_length() - 2)
 
-    group = lax.axis_index("kpt")
     part = lay(factor)
     beside = far_swap(part)
     packs = pack(bits, after(partner, part), factor, WORK * factor.size)
@@ -288,17 +306,13 @@
     early_near = jnp.concatenate(
         [near_swap(after(early_block[:-1], beside)), near_swap(early_block[-1:])]
     )
-    early_far = []
-    for t in range(transfers):
-        far_group = jnp.bitwise_xor(group, 1 << bits[t])
-        slots = lax.dynamic_slice_in_dim(partner[t], far_group * kc, kc) - group * kc
-        ordered = [lax.dynamic_slice_in_dim(beside, t * kc + slots[k], 1) for k in range(kc)]
-        early_far.append(group_swap(jnp.concatenate(ordered), bits[t]))
+    early_far = [group_swap(beside[t * kc : (t + 1) * kc], bits[t]) for t in range(transfers)]
 
     virtual = virtual_energies(vir_sorted, vir_order)
-    inverse = inverses(bits, partner, occ_energy, virtual, kc)
+    inverse, choice = inverses(bits, partner, occ_energy, virtual, kc, factor.shape[5])
     total = first_terms(factor, inverse, early_own + late_own, early_near)
-    total = second_terms(factor, inverse, late_near, early_far, total)
+    total = more_terms(near_kernel, [factor, inverse, late_near], total)
+    total = more_terms(far_kernel, [factor, inverse, choice, *early_far], total)
     return last_terms(factor, inverse, late_far, total)
 
 

time: 65.6 us -> 54.4 us (0.83)
  between operations: 6.44 us -> 0.2 us
  local copies, waits for them, and re-layouts: 4.27 us -> 0.19 us
  waiting for transfers between devices: 22.8 us -> 26.5 us
  Pallas kernels: 16.5 us -> 14.2 us
  other arithmetic: 3.14 us -> 0.92 us
    ppermute x6, waiting for transfers between devices: 22.8 us -> 25.7 us  [group_swap(): return lax.ppermute(block, 'kpt', [(g, g ^ 1 << bit) for g in range(count)])]
    dynamic_slice x1 -> x0, local copies, waits for them, and re-layouts: 1.25 us -> none  [body(): lax.dynamic_slice_in_dim(beside, t * kc + slots[k], 1)]
    slice x3 -> x1, local copies, waits for them, and re-layouts: 1.31 us -> 0.07 us  [body(): beside[t * kc:(t + 1) * kc]]
    concatenate x1, other arithmetic: 1.23 us -> 0.09 us  [body(): jnp.concatenate([near_swap(after(early_block[:-1], beside)), near_swap(ea...]
    pallas_call x1, Pallas kernels: 2.2 us -> 1.22 us  [lay(): pl.pallas_call(lay_kernel, out_shape=jax.ShapeDtypeStruct((transfers * kc...]
    pallas_call x1, Pallas kernels: 3.27 us -> 2.35 us  [pack(): pl.pallas_call(functools.partial(pack_kernel, bits), out_shape=[jax.Shape...]
    concatenate x1, other arithmetic: 0.97 us -> 0.07 us  [body(): early_block = jnp.concatenate(early_own)]
    concatenate x1, local copies, waits for them, and re-layouts: 0.83 us -> 0.03 us  [body(): late_block = jnp.concatenate(late_own)]
  transfers between devices with their start and end apart: 11 -> 11, of which waited for: 6 -> 8; matrix products, arithmetic and copies ran while one was open for 11% -> 2% of each run, Pallas kernels for 19% -> 20%
where the time goes in v9:
time: 54.4 us; the launch traced here: 54.2 us
  waiting for transfers between devices  26.5 us (49%)
  Pallas kernels  14.2 us (26%)
  starting transfers between devices  12.2 us (22%)
  other arithmetic  0.92 us (2%)
    ppermute x6, waiting for transfers between devices, group_swap(): return lax.ppermute(block, 'kpt', [(g, g ^ 1 << bit) for g in range(count)])  25.7 us
    ppermute x6, starting transfers between devices, group_swap(): return lax.ppermute(block, 'kpt', [(g, g ^ 1 << bit) for g in range(count)])  6.31 us
    ppermute x2, starting transfers between devices, far_swap(): lax.ppermute(block, 'occ', [(i, (i + (1 if i % 2 else count - 1)) % count...  5.16 us
    pallas_call x1, Pallas kernels, first_terms(): pl.pallas_call(first_kernel, out_shape=jax.ShapeDtypeStruct((transfers, k...  3.47 us
    pallas_call x2, Pallas kernels, more_terms(): pl.pallas_call(body, out_shape=jax.ShapeDtypeStruct(total.shape, F32), in...  3.32 us
    pallas_call x1, Pallas kernels, pack(): pl.pallas_call(functools.partial(pack_kernel, bits), out_shape=[jax.Shape...  2.35 us
    pallas_call x1, Pallas kernels, last_terms(): pl.pallas_call(last_kernel, out_shape=jax.ShapeDtypeStruct(factor.shape,...  2.23 us
    pallas_call x1, Pallas kernels, inverses(): pl.pallas_call(functools.partial(inverse_kernel, bits), out_shape=[jax.Sh...  1.6 us
  transfers between devices with their start and end apart: 11, of which 8 were waited for; matrix products, arithmetic and copies ran while one was open for 2% of the time, Pallas kernels for 20%

profile of v9, /device:TPU:0, one launch (start us, length us, event | category | flops | bytes accessed | tf_op | source)
XLA Modules:
  0.0 54.2 jit_solution(5810001789781159533)
XLA Ops:
  0.0 1.2 %shard_map.56 = bf16[4,2,128,512]{3,2,1,0:T(8,128)(2,1)S(1)} custom-call(bf16[2,2,1,2,256,512]{5,4,3,2,1,0:T(8,128)(2,1)} %factor.11), custom_call_target="tpu_custom_call" | custom-call | tf_op jit(solution)/shard_map/pallas_call | solution.py:65
  1.2 4.6 %collective-permute-start.3 = (bf16[4,2,128,512]{3,2,1,0:T(8,128)(2,1)S(1)}, bf16[4,2,128,512]{3,2,1,0:T(8,128)(2,1)S(1)}, u32[]{:S(2)}, u32[]{:S(2)}) collective-permute-start(bf16[4,2,128,512]{3,2,1,0:T(8,128)(2,1)S(1)} %shard_map.56), channel_id=1, source_target_pairs={{0,7},{1,2},{2,1},{3,4},{4,3},{5,6},{6,5},{7,0},{8,15},{9,10},{10,... | collective-permute-start | bytes 3145736 | tf_op jit(solution)/shard_map/ppermute | solution.py:33
  5.8 2.3 %shard_map.57 = (bf16[2,2,128,512]{3,2,1,0:T(8,128)(2,1)S(1)}, bf16[2,2,128,512]{3,2,1,0:T(8,128)(2,1)S(1)}, bf16[2,2,128,512]{3,2,1,0:T(8,128)(2,1)S(1)}, bf16[2,2,128,512]{3,2,1,0:T(8,128)(2,1)S(1)}) custom-call(s32[2,8]{1,0:T(2,128)} %partner.2, bf16[2,2,1,2,256,512]{5,4,3,2,1,0:T(8,128)(2,1)} %factor.11), custom_call_target="tpu_custom_call" | custom-call | bytes 16777216 | tf_op jit(solution)/shard_map/pallas_call | solution.py:96
  8.1 1.5 %collective-permute-start = (bf16[2,2,128,512]{3,2,1,0:T(8,128)(2,1)S(1)}, bf16[2,2,128,512]{3,2,1,0:T(8,128)(2,1)S(1)}, u32[]{:S(2)}, u32[]{:S(2)}) collective-permute-start(bf16[2,2,128,512]{3,2,1,0:T(8,128)(2,1)S(1)} %get-tuple-element.15), channel_id=1, source_target_pairs={{0,8},{8,0},{16,24},{24,16},{1,9},{9,1},{17,25},{25,17},{2,10},{10... | collective-permute-start | bytes 1572872 | tf_op jit(solution)/shard_map/ppermute | solution.py:23
  9.6 1.5 %collective-permute-start.1 = (bf16[2,2,128,512]{3,2,1,0:T(8,128)(2,1)S(1)}, bf16[2,2,128,512]{3,2,1,0:T(8,128)(2,1)S(1)}, u32[]{:S(2)}, u32[]{:S(2)}) collective-permute-start(bf16[2,2,128,512]{3,2,1,0:T(8,128)(2,1)S(1)} %get-tuple-element.16), channel_id=1, source_target_pairs={{0,16},{8,24},{16,0},{24,8},{1,17},{9,25},{17,1},{25,9},{2,18},{10... | collective-permute-start | bytes 1572872 | tf_op jit(solution)/shard_map/ppermute | solution.py:23
  11.1 0.6 %collective-permute-start.7 = (bf16[2,2,128,512]{3,2,1,0:T(8,128)(2,1)S(1)}, bf16[2,2,128,512]{3,2,1,0:T(8,128)(2,1)S(1)}, u32[]{:S(2)}, u32[]{:S(2)}) collective-permute-start(bf16[2,2,128,512]{3,2,1,0:T(8,128)(2,1)S(1)} %get-tuple-element.18), channel_id=1, source_target_pairs={{0,8},{8,0},{16,24},{24,16},{1,9},{9,1},{17,25},{25,17},{2,10},{10... | collective-permute-start | bytes 1572872 | tf_op jit(solution)/shard_map/ppermute | solution.py:23
  11.7 0.6 %collective-permute-start.8 = (bf16[2,2,128,512]{3,2,1,0:T(8,128)(2,1)S(1)}, bf16[2,2,128,512]{3,2,1,0:T(8,128)(2,1)S(1)}, u32[]{:S(2)}, u32[]{:S(2)}) collective-permute-start(bf16[2,2,128,512]{3,2,1,0:T(8,128)(2,1)S(1)} %get-tuple-element.19), channel_id=1, source_target_pairs={{0,16},{8,24},{16,0},{24,8},{1,17},{9,25},{17,1},{25,9},{2,18},{10... | collective-permute-start | bytes 1572872 | tf_op jit(solution)/shard_map/ppermute | solution.py:23
  12.3 10.8 %collective-permute-done.refs_2_ = bf16[2,2,128,512]{3,2,1,0:T(8,128)(2,1)S(1)} collective-permute-done((bf16[2,2,128,512]{3,2,1,0:T(8,128)(2,1)S(1)}, bf16[2,2,128,512]{3,2,1,0:T(8,128)(2,1)S(1)}, u32[]{:S(2)}, u32[]{:S(2)}) %collective-permute-start) | collective-permute-done | bytes 524320 | tf_op jit(solution)/shard_map/ppermute | solution.py:23
  23.1 1.4 %collective-permute-done.1.refs_3_ = bf16[2,2,128,512]{3,2,1,0:T(8,128)(2,1)S(1)} collective-permute-done((bf16[2,2,128,512]{3,2,1,0:T(8,128)(2,1)S(1)}, bf16[2,2,128,512]{3,2,1,0:T(8,128)(2,1)S(1)}, u32[]{:S(2)}, u32[]{:S(2)}) %collective-permute-start.1) | collective-permute-done | bytes 524320 | tf_op jit(solution)/shard_map/ppermute | solution.py:23
  24.5 0.0 copy-start.3
  24.5 0.0 copy-start.4
  24.5 0.0 copy-start.1
  24.6 0.0 copy-start.2
  24.6 0.1 collective-permute-start.6
  24.6 0.6 %collective-permute-start.2 = (bf16[4,2,128,512]{3,2,1,0:T(8,128)(2,1)S(1)}, bf16[4,2,128,512]{3,2,1,0:T(8,128)(2,1)S(1)}, u32[]{:S(2)}, u32[]{:S(2)}) collective-permute-start(bf16[4,2,128,512]{3,2,1,0:T(8,128)(2,1)S(1)} %constant_dynamic-update-slice_fusion), channel_id=1, source_target_pairs={{0,7},{1,2},{2,1},{3,4},{4,3},{5,6},{6,5},{7,0},{8,15},{9,10},{10,... | collective-permute-start | bytes 3145736 | tf_op jit(solution)/shard_map/ppermute | solution.py:33
  25.3 6.7 %collective-permute-done.7.refs_0_ = bf16[2,2,128,512]{3,2,1,0:T(8,128)(2,1)S(1)} collective-permute-done((bf16[2,2,128,512]{3,2,1,0:T(8,128)(2,1)S(1)}, bf16[2,2,128,512]{3,2,1,0:T(8,128)(2,1)S(1)}, u32[]{:S(2)}, u32[]{:S(2)}) %collective-permute-start.7) | collective-permute-done | bytes 524320 | tf_op jit(solution)/shard_map/ppermute | solution.py:23
  31.9 1.1 %collective-permute-done.8.refs_1_ = bf16[2,2,128,512]{3,2,1,0:T(8,128)(2,1)S(1)} collective-permute-done((bf16[2,2,128,512]{3,2,1,0:T(8,128)(2,1)S(1)}, bf16[2,2,128,512]{3,2,1,0:T(8,128)(2,1)S(1)}, u32[]{:S(2)}, u32[]{:S(2)}) %collective-permute-start.8) | collective-permute-done | bytes 524320 | tf_op jit(solution)/shard_map/ppermute | solution.py:23
  33.1 0.1 pad_maximum_fusion.1
  33.1 0.0 collective-permute-done.3
  33.1 0.1 collective-permute-start.9
  33.2 0.0 copy-start
  33.3 0.6 %collective-permute-start.10 = (bf16[1,2,128,512]{3,2,1,0:T(8,128)(2,1)S(1)}, bf16[1,2,128,512]{3,2,1,0:T(8,128)(2,1)S(1)}, u32[]{:S(2)}, u32[]{:S(2)}) collective-permute-start(bf16[1,2,128,512]{3,2,1,0:T(8,128)(2,1)S(1)} %slice.18), channel_id=1, source_target_pairs={{0,1},{1,0},{2,3},{3,2},{4,5},{5,4},{6,7},{7,6},{8,9},{9,8},{10,11... | collective-permute-start | bytes 786440 | tf_op jit(solution)/shard_map/ppermute | solution.py:28
  33.8 0.1 fusion
  33.9 1.6 %collective-permute-start.5 = (bf16[2,2,128,512]{3,2,1,0:T(8,128)(2,1)S(1)}, bf16[2,2,128,512]{3,2,1,0:T(8,128)(2,1)S(1)}, u32[]{:S(2)}, u32[]{:S(2)}) collective-permute-start(bf16[2,2,128,512]{3,2,1,0:T(8,128)(2,1)S(1)} %get-tuple-element.21), channel_id=1, source_target_pairs={{0,16},{8,24},{16,0},{24,8},{1,17},{9,25},{17,1},{25,9},{2,18},{10... | collective-permute-start | bytes 1572872 | tf_op jit(solution)/shard_map/ppermute | solution.py:23
  35.5 0.4 collective-permute-done.10
  35.9 0.6 %collective-permute-start.4 = (bf16[2,2,128,512]{3,2,1,0:T(8,128)(2,1)S(1)}, bf16[2,2,128,512]{3,2,1,0:T(8,128)(2,1)S(1)}, u32[]{:S(2)}, u32[]{:S(2)}) collective-permute-start(bf16[2,2,128,512]{3,2,1,0:T(8,128)(2,1)S(1)} %get-tuple-element.22), channel_id=1, source_target_pairs={{0,8},{8,0},{16,24},{24,16},{1,9},{9,1},{17,25},{25,17},{2,10},{10... | collective-permute-start | bytes 1572872 | tf_op jit(solution)/shard_map/ppermute | solution.py:23
  36.5 0.0 copy-done.3
  36.5 0.0 copy-done.4
  36.5 0.8 %select_reduce_fusion.virtual = f32[8,256]{1,0:T(8,128)S(1)} fusion(f32[8,256]{1,0:T(8,128)S(1)} %copy-done.3, s32[8,256]{1,0:T(8,128)S(1)} %copy-done.4), kind=kLoop, calls=%fused_computation | loop fusion | flops 1570816 | bytes 24576 | tf_op jit(solution)/shard_map/reduce_sum | solution.py:45
  37.2 0.0 copy-done.1
  37.3 0.0 copy-done.2
  37.3 1.6 %shard_map.55 = (f32[2,3,2,256,256]{4,3,2,1,0:T(8,128)S(1)}, bf16[2,2,2,16,512]{4,3,2,1,0:T(8,128)(2,1)S(1)}) custom-call(s32[2,8]{1,0:T(2,128)S(1)} %copy-done.1, f32[8,8]{1,0:T(8,128)S(1)} %copy-done.2, f32[8,256]{1,0:T(8,128)S(1)} %select_reduce_fusion.virtual), custom_call_target="tpu_custom_call" | custom-call | tf_op jit(solution)/shard_map/pallas_call | solution.py:137
  38.9 0.0 collective-permute-done.9
  38.9 0.1 pad_maximum_fusion.refs_4_
  39.0 0.0 copy-done
  39.0 3.5 %shard_map.58.total = f32[2,2,2,256,512]{4,3,2,1,0:T(8,128)S(1)} custom-call(bf16[2,2,1,2,256,512]{5,4,3,2,1,0:T(8,128)(2,1)S(1)} %copy-done, f32[2,3,2,256,256]{4,3,2,1,0:T(8,128)S(1)} %get-tuple-element.13.inverse, bf16[2,2,128,512]{3,2,1,0:T(8,128)(2,1)S(1)} %collective-permute-done.7.refs_0_, ...), custom_call_target="tpu_custom_call" | custom-call | tf_op jit(solution)/shard_map/pallas_call | solution.py:207
  42.5 0.0 collective-permute-done.6.near
  42.5 1.6 %shard_map.59.refs_2_ = f32[2,2,2,256,512]{4,3,2,1,0:T(8,128)S(1)} custom-call(bf16[2,2,1,2,256,512]{5,4,3,2,1,0:T(8,128)(2,1)S(1)} %copy-done, f32[2,3,2,256,256]{4,3,2,1,0:T(8,128)S(1)} %get-tuple-element.13.inverse, bf16[4,2,128,512]{3,2,1,0:T(8,128)(2,1)S(1)} %collective-permute-done.6.near, ...), custom_call_target="tpu_custom_call", output_to_operand_aliasing={{}: (3, {})} | custom-call | tf_op jit(solution)/shard_map/pallas_call | solution.py:246
  44.1 3.7 %collective-permute-done.5.refs_1_ = bf16[2,2,128,512]{3,2,1,0:T(8,128)(2,1)S(1)} collective-permute-done((bf16[2,2,128,512]{3,2,1,0:T(8,128)(2,1)S(1)}, bf16[2,2,128,512]{3,2,1,0:T(8,128)(2,1)S(1)}, u32[]{:S(2)}, u32[]{:S(2)}) %collective-permute-start.5) | collective-permute-done | bytes 524320 | tf_op jit(solution)/shard_map/ppermute | solution.py:23
  47.8 2.0 %collective-permute-done.4.refs_0_ = bf16[2,2,128,512]{3,2,1,0:T(8,128)(2,1)S(1)} collective-permute-done((bf16[2,2,128,512]{3,2,1,0:T(8,128)(2,1)S(1)}, bf16[2,2,128,512]{3,2,1,0:T(8,128)(2,1)S(1)}, u32[]{:S(2)}, u32[]{:S(2)}) %collective-permute-start.4) | collective-permute-done | bytes 524320 | tf_op jit(solution)/shard_map/ppermute | solution.py:23
  49.8 1.7 %shard_map.60.total = f32[2,2,2,256,512]{4,3,2,1,0:T(8,128)S(1)} custom-call(bf16[2,2,1,2,256,512]{5,4,3,2,1,0:T(8,128)(2,1)S(1)} %copy-done, f32[2,3,2,256,256]{4,3,2,1,0:T(8,128)S(1)} %get-tuple-element.13.inverse, bf16[2,2,2,16,512]{4,3,2,1,0:T(8,128)(2,1)S(1)} %get-tuple-element.17.choice, ...), custom_call_target="tpu_custom_call", output_to_operand_aliasing={{}: (5, {})} | custom-call | tf_op jit(solution)/shard_map/pallas_call | solution.py:246
  51.6 0.4 collective-permute-done.2.window
  52.0 2.2 %shard_map.61 = bf16[2,2,1,2,256,512]{5,4,3,2,1,0:T(8,128)(2,1)} custom-call(bf16[2,2,1,2,256,512]{5,4,3,2,1,0:T(8,128)(2,1)S(1)} %copy-done, f32[2,3,2,256,256]{4,3,2,1,0:T(8,128)S(1)} %get-tuple-element.13.inverse, bf16[4,2,128,512]{3,2,1,0:T(8,128)(2,1)S(1)} %collective-permute-done.2.window, f32[2,2,2,256,512]{4,3,2,1,0:T(8,128)S(1)} %shard_map.60.total), custom_call_target="tpu_custom_call" | custom-call | tf_op jit(solution)/shard_map/pallas_call | solution.py:278
  (3 shorter events, 0.1 us)
Async XLA Ops:
  1.2 31.9 %collective-permute-start.3 = (bf16[4,2,128,512]{3,2,1,0:T(8,128)(2,1)S(1)}, bf16[4,2,128,512]{3,2,1,0:T(8,128)(2,1)S(1)}, u32[]{:S(2)}, u32[]{:S(2)}) collective-permute-start(bf16[4,2,128,512]{3,2,1,0:T(8,128)(2,1)S(1)} %shard_map.56), channel_id=1, source_target_pairs={{0,7},{1,2},{2,1},{3,4},{4,3},{5,6},{6,5},{7,0},{8,15},{9,10},{10,... | collective-permute-start | bytes 3145736 | tf_op jit(solution)/shard_map/ppermute | solution.py:33
  8.1 14.9 %collective-permute-start = (bf16[2,2,128,512]{3,2,1,0:T(8,128)(2,1)S(1)}, bf16[2,2,128,512]{3,2,1,0:T(8,128)(2,1)S(1)}, u32[]{:S(2)}, u32[]{:S(2)}) collective-permute-start(bf16[2,2,128,512]{3,2,1,0:T(8,128)(2,1)S(1)} %get-tuple-element.15), channel_id=1, source_target_pairs={{0,8},{8,0},{16,24},{24,16},{1,9},{9,1},{17,25},{25,17},{2,10},{10... | collective-permute-start | bytes 1572872 | tf_op jit(solution)/shard_map/ppermute | solution.py:23
  9.6 14.9 %collective-permute-start.1 = (bf16[2,2,128,512]{3,2,1,0:T(8,128)(2,1)S(1)}, bf16[2,2,128,512]{3,2,1,0:T(8,128)(2,1)S(1)}, u32[]{:S(2)}, u32[]{:S(2)}) collective-permute-start(bf16[2,2,128,512]{3,2,1,0:T(8,128)(2,1)S(1)} %get-tuple-element.16), channel_id=1, source_target_pairs={{0,16},{8,24},{16,0},{24,8},{1,17},{9,25},{17,1},{25,9},{2,18},{10... | collective-permute-start | bytes 1572872 | tf_op jit(solution)/shard_map/ppermute | solution.py:23
  11.1 20.8 %collective-permute-start.7 = (bf16[2,2,128,512]{3,2,1,0:T(8,128)(2,1)S(1)}, bf16[2,2,128,512]{3,2,1,0:T(8,128)(2,1)S(1)}, u32[]{:S(2)}, u32[]{:S(2)}) collective-permute-start(bf16[2,2,128,512]{3,2,1,0:T(8,128)(2,1)S(1)} %get-tuple-element.18), channel_id=1, source_target_pairs={{0,8},{8,0},{16,24},{24,16},{1,9},{9,1},{17,25},{25,17},{2,10},{10... | collective-permute-start | bytes 1572872 | tf_op jit(solution)/shard_map/ppermute | solution.py:23
  11.7 21.4 %collective-permute-start.8 = (bf16[2,2,128,512]{3,2,1,0:T(8,128)(2,1)S(1)}, bf16[2,2,128,512]{3,2,1,0:T(8,128)(2,1)S(1)}, u32[]{:S(2)}, u32[]{:S(2)}) collective-permute-start(bf16[2,2,128,512]{3,2,1,0:T(8,128)(2,1)S(1)} %get-tuple-element.19), channel_id=1, source_target_pairs={{0,16},{8,24},{16,0},{24,8},{1,17},{9,25},{17,1},{25,9},{2,18},{10... | collective-permute-start | bytes 1572872 | tf_op jit(solution)/shard_map/ppermute | solution.py:23
  24.5 12.0 %copy-start.3 = (f32[8,256]{1,0:T(8,128)S(1)}, f32[8,256]{1,0:T(8,128)}, u32[]{:S(2)}) copy-start(f32[8,256]{1,0:T(8,128)} %param.8) | copy-start | bytes 24580
  24.5 11.9 %copy-start.4 = (s32[8,256]{1,0:T(8,128)S(1)}, s32[8,256]{1,0:T(8,128)}, u32[]{:S(2)}) copy-start(s32[8,256]{1,0:T(8,128)} %param.9) | copy-start | bytes 24580
  24.5 12.7 %copy-start.1 = (s32[2,8]{1,0:T(2,128)S(1)}, s32[2,8]{1,0:T(2,128)}, u32[]{:S(2)}) copy-start(s32[2,8]{1,0:T(2,128)} %partner.2) | copy-start | bytes 196
  24.6 12.7 %copy-start.2 = (f32[8,8]{1,0:T(8,128)S(1)}, f32[8,8]{1,0:T(8,128)}, u32[]{:S(2)}) copy-start(f32[8,8]{1,0:T(8,128)} %occ.1) | copy-start | bytes 772
  24.6 17.9 %collective-permute-start.6 = (bf16[4,2,128,512]{3,2,1,0:T(8,128)(2,1)S(1)}, bf16[4,2,128,512]{3,2,1,0:T(8,128)(2,1)S(1)}, u32[]{:S(2)}, u32[]{:S(2)}) collective-permute-start(bf16[4,2,128,512]{3,2,1,0:T(8,128)(2,1)S(1)} %constant_dynamic-update-slice_fusion), channel_id=1, source_target_pairs={{0,1},{1,0},{2,3},{3,2},{4,5},{5,4},{6,7},{7,6},{8,9},{9,8},{10,11... | collective-permute-start | bytes 3145736 | tf_op jit(solution)/shard_map/ppermute | solution.py:28
  24.6 27.3 %collective-permute-start.2 = (bf16[4,2,128,512]{3,2,1,0:T(8,128)(2,1)S(1)}, bf16[4,2,128,512]{3,2,1,0:T(8,128)(2,1)S(1)}, u32[]{:S(2)}, u32[]{:S(2)}) collective-permute-start(bf16[4,2,128,512]{3,2,1,0:T(8,128)(2,1)S(1)} %constant_dynamic-update-slice_fusion), channel_id=1, source_target_pairs={{0,7},{1,2},{2,1},{3,4},{4,3},{5,6},{6,5},{7,0},{8,15},{9,10},{10,... | collective-permute-start | bytes 3145736 | tf_op jit(solution)/shard_map/ppermute | solution.py:33
  33.1 5.7 %collective-permute-start.9 = (bf16[3,2,128,512]{3,2,1,0:T(8,128)(2,1)S(1)}, bf16[3,2,128,512]{3,2,1,0:T(8,128)(2,1)S(1)}, u32[]{:S(2)}, u32[]{:S(2)}) collective-permute-start(bf16[3,2,128,512]{3,2,1,0:T(8,128)(2,1)S(1)} %pad_maximum_fusion.1), channel_id=1, source_target_pairs={{0,1},{1,0},{2,3},{3,2},{4,5},{5,4},{6,7},{7,6},{8,9},{9,8},{10,11... | collective-permute-start | bytes 2359304 | tf_op jit(solution)/shard_map/ppermute | solution.py:28
  33.2 5.7 %copy-start = (bf16[2,2,1,2,256,512]{5,4,3,2,1,0:T(8,128)(2,1)S(1)}, bf16[2,2,1,2,256,512]{5,4,3,2,1,0:T(8,128)(2,1)}, u32[]{:S(2)}) copy-start(bf16[2,2,1,2,256,512]{5,4,3,2,1,0:T(8,128)(2,1)} %factor.11) | copy-start | bytes 6291460
  33.3 2.6 %collective-permute-start.10 = (bf16[1,2,128,512]{3,2,1,0:T(8,128)(2,1)S(1)}, bf16[1,2,128,512]{3,2,1,0:T(8,128)(2,1)S(1)}, u32[]{:S(2)}, u32[]{:S(2)}) collective-permute-start(bf16[1,2,128,512]{3,2,1,0:T(8,128)(2,1)S(1)} %slice.18), channel_id=1, source_target_pairs={{0,1},{1,0},{2,3},{3,2},{4,5},{5,4},{6,7},{7,6},{8,9},{9,8},{10,11... | collective-permute-start | bytes 786440 | tf_op jit(solution)/shard_map/ppermute | solution.py:28
  33.9 13.9 %collective-permute-start.5 = (bf16[2,2,128,512]{3,2,1,0:T(8,128)(2,1)S(1)}, bf16[2,2,128,512]{3,2,1,0:T(8,128)(2,1)S(1)}, u32[]{:S(2)}, u32[]{:S(2)}) collective-permute-start(bf16[2,2,128,512]{3,2,1,0:T(8,128)(2,1)S(1)} %get-tuple-element.21), channel_id=1, source_target_pairs={{0,16},{8,24},{16,0},{24,8},{1,17},{9,25},{17,1},{25,9},{2,18},{10... | collective-permute-start | bytes 1572872 | tf_op jit(solution)/shard_map/ppermute | solution.py:23
  35.9 14.0 %collective-permute-start.4 = (bf16[2,2,128,512]{3,2,1,0:T(8,128)(2,1)S(1)}, bf16[2,2,128,512]{3,2,1,0:T(8,128)(2,1)S(1)}, u32[]{:S(2)}, u32[]{:S(2)}) collective-permute-start(bf16[2,2,128,512]{3,2,1,0:T(8,128)(2,1)S(1)} %get-tuple-element.22), channel_id=1, source_target_pairs={{0,8},{8,0},{16,24},{24,16},{1,9},{9,1},{17,25},{25,17},{2,10},{10... | collective-permute-start | bytes 1572872 | tf_op jit(solution)/shard_map/ppermute | solution.py:23

commit v10 on v9

--- a/solution.py
+++ b/solution.py
@@ -47,30 +47,6 @@
 
 def column_of(row):
     return jnp.transpose(jnp.broadcast_to(row, (8, row.shape[1])))[:, :1]
-
-
-def lay_kernel(factor, out, sems):
-    kc, half = factor.shape[1], out.shape[2]
-    copies = []
-    for at in range(out.shape[0]):
-        source = factor.at[at // kc, at % kc, 0, :, pl.ds(0, half), :]
-        copies.append(pltpu.make_async_copy(source, out.at[at], sems.at[at]))
-        copies[-1].start()
-    for copy in copies:
-        copy.wait()
-
-
-def lay(factor):
-    transfers, kc, _, parts, nv, naux = factor.shape
-    return pl.pallas_call(
-        lay_kernel,
-        out_shape=jax.ShapeDtypeStruct((transfers * kc, parts, nv // 2, naux), BF16),
-        in_specs=[ANY],
-        out_specs=VMEM,
-        scratch_shapes=[pltpu.SemaphoreType.DMA((transfers * kc,))],
-        cost_estimate=COST,
-        compiler_params=PARAMS,
-    )(pltpu.with_memory_space_constraint(factor, pltpu.HBM))
 
 
 def pack_kernel(bits, partner, factor, *refs):
@@ -293,7 +269,8 @@
     transfers, kc = factor.shape[:2]
     bits = (0, lax.axis_size("kpt").bit_length() - 2)
 
-    part = lay(factor)
+    half = factor.shape[4] // 2
+    part = factor[:, :, 0, :, :half].reshape(transfers * kc, *factor.shape[3:4], half, factor.shape[5])
     beside = far_swap(part)
     packs = pack(bits, after(partner, part), factor, WORK * factor.size)
     earlies, lates = packs[:transfers], packs[transfers:]

time: 54.4 us -> 54.5 us (level)
  Pallas kernels: 14.2 us -> 12.9 us
  local copies, waits for them, and re-layouts: 0.19 us -> 1.48 us
    slice x0 -> x1, local copies, waits for them, and re-layouts: none -> 1.29 us  [body(): factor[:, :, 0, :, :half]]
    pallas_call x1 -> x0, Pallas kernels: 1.22 us -> none  [lay(): pl.pallas_call(lay_kernel, out_shape=jax.ShapeDtypeStruct((transfers * kc...]
where the time goes in v10:
time: 54.5 us; the launch traced here: 54.3 us
  waiting for transfers between devices  26.7 us (49%)
  Pallas kernels  12.9 us (24%)
  starting transfers between devices  12.1 us (22%)
  local copies, waits for them, and re-layouts  1.48 us (3%)
  other arithmetic  0.92 us (2%)
    ppermute x6, waiting for transfers between devices, group_swap(): return lax.ppermute(block, 'kpt', [(g, g ^ 1 << bit) for g in range(count)])  25.9 us
    ppermute x6, starting transfers between devices, group_swap(): return lax.ppermute(block, 'kpt', [(g, g ^ 1 << bit) for g in range(count)])  6.24 us
    ppermute x2, starting transfers between devices, far_swap(): lax.ppermute(block, 'occ', [(i, (i + (1 if i % 2 else count - 1)) % count...  5.16 us
    pallas_call x1, Pallas kernels, first_terms(): pl.pallas_call(first_kernel, out_shape=jax.ShapeDtypeStruct((transfers, k...  3.46 us
    pallas_call x2, Pallas kernels, more_terms(): pl.pallas_call(body, out_shape=jax.ShapeDtypeStruct(total.shape, F32), in...  3.33 us
    pallas_call x1, Pallas kernels, pack(): pl.pallas_call(functools.partial(pack_kernel, bits), out_shape=[jax.Shape...  2.27 us
    pallas_call x1, Pallas kernels, last_terms(): pl.pallas_call(last_kernel, out_shape=jax.ShapeDtypeStruct(factor.shape,...  2.23 us
    pallas_call x1, Pallas kernels, inverses(): pl.pallas_call(functools.partial(inverse_kernel, bits), out_shape=[jax.Sh...  1.6 us
  transfers between devices with their start and end apart: 11, of which 8 were waited for; matrix products, arithmetic and copies ran while one was open for 2% of the time, Pallas kernels for 20%

profile of v10, /device:TPU:0, one launch (start us, length us, event | category | flops | bytes accessed | tf_op | source)
XLA Modules:
  0.0 54.3 jit_solution(10544682535732943306)
XLA Ops:
  0.0 1.3 %slice.15 = bf16[2,2,1,2,128,512]{5,4,3,2,1,0:T(8,128)(2,1)S(1)} slice(bf16[2,2,1,2,256,512]{5,4,3,2,1,0:T(8,128)(2,1)} %factor.9), slice={[0:2], [0:2], [0:1], [0:2], [0:128], [0:512]} | slice | bytes 2097152 | tf_op jit(solution)/shard_map/slice | solution.py:273
  1.3 4.6 %collective-permute-start.3 = (bf16[4,2,128,512]{3,2,1,0:T(8,128)(2,1)S(1)}, bf16[4,2,128,512]{3,2,1,0:T(8,128)(2,1)S(1)}, u32[]{:S(2)}, u32[]{:S(2)}) collective-permute-start(bf16[4,2,128,512]{3,2,1,0:T(8,128)(2,1)S(1)} %bitcast.1), channel_id=1, source_target_pairs={{0,7},{1,2},{2,1},{3,4},{4,3},{5,6},{6,5},{7,0},{8,15},{9,10},{10,... | collective-permute-start | bytes 3145736 | tf_op jit(solution)/shard_map/ppermute | solution.py:33
  5.9 2.3 %shard_map.56 = (bf16[2,2,128,512]{3,2,1,0:T(8,128)(2,1)S(1)}, bf16[2,2,128,512]{3,2,1,0:T(8,128)(2,1)S(1)}, bf16[2,2,128,512]{3,2,1,0:T(8,128)(2,1)S(1)}, bf16[2,2,128,512]{3,2,1,0:T(8,128)(2,1)S(1)}) custom-call(s32[2,8]{1,0:T(2,128)} %partner.2, bf16[2,2,1,2,256,512]{5,4,3,2,1,0:T(8,128)(2,1)} %factor.9), custom_call_target="tpu_custom_call" | custom-call | bytes 16777216 | tf_op jit(solution)/shard_map/pallas_call | solution.py:72
  8.1 1.6 %collective-permute-start = (bf16[2,2,128,512]{3,2,1,0:T(8,128)(2,1)S(1)}, bf16[2,2,128,512]{3,2,1,0:T(8,128)(2,1)S(1)}, u32[]{:S(2)}, u32[]{:S(2)}) collective-permute-start(bf16[2,2,128,512]{3,2,1,0:T(8,128)(2,1)S(1)} %get-tuple-element.15), channel_id=1, source_target_pairs={{0,8},{8,0},{16,24},{24,16},{1,9},{9,1},{17,25},{25,17},{2,10},{10... | collective-permute-start | bytes 1572872 | tf_op jit(solution)/shard_map/ppermute | solution.py:23
  9.7 1.5 %collective-permute-start.1 = (bf16[2,2,128,512]{3,2,1,0:T(8,128)(2,1)S(1)}, bf16[2,2,128,512]{3,2,1,0:T(8,128)(2,1)S(1)}, u32[]{:S(2)}, u32[]{:S(2)}) collective-permute-start(bf16[2,2,128,512]{3,2,1,0:T(8,128)(2,1)S(1)} %get-tuple-element.16), channel_id=1, source_target_pairs={{0,16},{8,24},{16,0},{24,8},{1,17},{9,25},{17,1},{25,9},{2,18},{10... | collective-permute-start | bytes 1572872 | tf_op jit(solution)/shard_map/ppermute | solution.py:23
  11.2 0.6 %collective-permute-start.7 = (bf16[2,2,128,512]{3,2,1,0:T(8,128)(2,1)S(1)}, bf16[2,2,128,512]{3,2,1,0:T(8,128)(2,1)S(1)}, u32[]{:S(2)}, u32[]{:S(2)}) collective-permute-start(bf16[2,2,128,512]{3,2,1,0:T(8,128)(2,1)S(1)} %get-tuple-element.18), channel_id=1, source_target_pairs={{0,8},{8,0},{16,24},{24,16},{1,9},{9,1},{17,25},{25,17},{2,10},{10... | collective-permute-start | bytes 1572872 | tf_op jit(solution)/shard_map/ppermute | solution.py:23
  11.8 0.4 collective-permute-start.8
  12.3 10.8 %collective-permute-done.refs_2_ = bf16[2,2,128,512]{3,2,1,0:T(8,128)(2,1)S(1)} collective-permute-done((bf16[2,2,128,512]{3,2,1,0:T(8,128)(2,1)S(1)}, bf16[2,2,128,512]{3,2,1,0:T(8,128)(2,1)S(1)}, u32[]{:S(2)}, u32[]{:S(2)}) %collective-permute-start) | collective-permute-done | bytes 524320 | tf_op jit(solution)/shard_map/ppermute | solution.py:23
  23.1 1.5 %collective-permute-done.1.refs_3_ = bf16[2,2,128,512]{3,2,1,0:T(8,128)(2,1)S(1)} collective-permute-done((bf16[2,2,128,512]{3,2,1,0:T(8,128)(2,1)S(1)}, bf16[2,2,128,512]{3,2,1,0:T(8,128)(2,1)S(1)}, u32[]{:S(2)}, u32[]{:S(2)}) %collective-permute-start.1) | collective-permute-done | bytes 524320 | tf_op jit(solution)/shard_map/ppermute | solution.py:23
  24.6 0.0 copy-start.3
  24.6 0.0 copy-start.4
  24.6 0.0 copy-start.1
  24.6 0.0 copy-start.2
  24.6 0.1 collective-permute-start.6
  24.7 0.6 %collective-permute-start.2 = (bf16[4,2,128,512]{3,2,1,0:T(8,128)(2,1)S(1)}, bf16[4,2,128,512]{3,2,1,0:T(8,128)(2,1)S(1)}, u32[]{:S(2)}, u32[]{:S(2)}) collective-permute-start(bf16[4,2,128,512]{3,2,1,0:T(8,128)(2,1)S(1)} %constant_dynamic-update-slice_fusion), channel_id=1, source_target_pairs={{0,7},{1,2},{2,1},{3,4},{4,3},{5,6},{6,5},{7,0},{8,15},{9,10},{10,... | collective-permute-start | bytes 3145736 | tf_op jit(solution)/shard_map/ppermute | solution.py:33
  25.3 6.6 %collective-permute-done.7.refs_0_ = bf16[2,2,128,512]{3,2,1,0:T(8,128)(2,1)S(1)} collective-permute-done((bf16[2,2,128,512]{3,2,1,0:T(8,128)(2,1)S(1)}, bf16[2,2,128,512]{3,2,1,0:T(8,128)(2,1)S(1)}, u32[]{:S(2)}, u32[]{:S(2)}) %collective-permute-start.7) | collective-permute-done | bytes 524320 | tf_op jit(solution)/shard_map/ppermute | solution.py:23
  31.9 1.2 %collective-permute-done.8.refs_1_ = bf16[2,2,128,512]{3,2,1,0:T(8,128)(2,1)S(1)} collective-permute-done((bf16[2,2,128,512]{3,2,1,0:T(8,128)(2,1)S(1)}, bf16[2,2,128,512]{3,2,1,0:T(8,128)(2,1)S(1)}, u32[]{:S(2)}, u32[]{:S(2)}) %collective-permute-start.8) | collective-permute-done | bytes 524320 | tf_op jit(solution)/shard_map/ppermute | solution.py:23
  33.1 0.1 pad_maximum_fusion.1
  33.2 0.0 collective-permute-done.3
  33.2 0.1 collective-permute-start.9
  33.3 0.0 copy-start
  33.3 0.6 %collective-permute-start.10 = (bf16[1,2,128,512]{3,2,1,0:T(8,128)(2,1)S(1)}, bf16[1,2,128,512]{3,2,1,0:T(8,128)(2,1)S(1)}, u32[]{:S(2)}, u32[]{:S(2)}) collective-permute-start(bf16[1,2,128,512]{3,2,1,0:T(8,128)(2,1)S(1)} %slice.22), channel_id=1, source_target_pairs={{0,1},{1,0},{2,3},{3,2},{4,5},{5,4},{6,7},{7,6},{8,9},{9,8},{10,11... | collective-permute-start | bytes 786440 | tf_op jit(solution)/shard_map/ppermute | solution.py:28
  33.9 0.1 fusion
  34.0 1.6 %collective-permute-start.5 = (bf16[2,2,128,512]{3,2,1,0:T(8,128)(2,1)S(1)}, bf16[2,2,128,512]{3,2,1,0:T(8,128)(2,1)S(1)}, u32[]{:S(2)}, u32[]{:S(2)}) collective-permute-start(bf16[2,2,128,512]{3,2,1,0:T(8,128)(2,1)S(1)} %get-tuple-element.21), channel_id=1, source_target_pairs={{0,16},{8,24},{16,0},{24,8},{1,17},{9,25},{17,1},{25,9},{2,18},{10... | collective-permute-start | bytes 1572872 | tf_op jit(solution)/shard_map/ppermute | solution.py:23
  35.5 0.4 collective-permute-done.10
  35.9 0.5 collective-permute-start.4
  36.5 0.0 copy-done.3
  36.5 0.0 copy-done.4
  36.5 0.8 %select_reduce_fusion.virtual = f32[8,256]{1,0:T(8,128)S(1)} fusion(f32[8,256]{1,0:T(8,128)S(1)} %copy-done.3, s32[8,256]{1,0:T(8,128)S(1)} %copy-done.4), kind=kLoop, calls=%fused_computation | loop fusion | flops 1570816 | bytes 24576 | tf_op jit(solution)/shard_map/reduce_sum | solution.py:45
  37.2 0.0 copy-done.1
  37.2 0.0 copy-done.2
  37.3 1.6 %shard_map.55 = (f32[2,3,2,256,256]{4,3,2,1,0:T(8,128)S(1)}, bf16[2,2,2,16,512]{4,3,2,1,0:T(8,128)(2,1)S(1)}) custom-call(s32[2,8]{1,0:T(2,128)S(1)} %copy-done.1, f32[8,8]{1,0:T(8,128)S(1)} %copy-done.2, f32[8,256]{1,0:T(8,128)S(1)} %select_reduce_fusion.virtual), custom_call_target="tpu_custom_call" | custom-call | tf_op jit(solution)/shard_map/pallas_call | solution.py:113
  38.9 0.0 collective-permute-done.9
  38.9 0.1 pad_maximum_fusion.refs_4_
  39.0 0.0 copy-done
  39.0 3.5 %shard_map.57.total = f32[2,2,2,256,512]{4,3,2,1,0:T(8,128)S(1)} custom-call(bf16[2,2,1,2,256,512]{5,4,3,2,1,0:T(8,128)(2,1)S(1)} %copy-done, f32[2,3,2,256,256]{4,3,2,1,0:T(8,128)S(1)} %get-tuple-element.13.inverse, bf16[2,2,128,512]{3,2,1,0:T(8,128)(2,1)S(1)} %collective-permute-done.7.refs_0_, ...), custom_call_target="tpu_custom_call" | custom-call | tf_op jit(solution)/shard_map/pallas_call | solution.py:183
  42.5 0.0 collective-permute-done.6.near
  42.5 1.6 %shard_map.58.refs_2_ = f32[2,2,2,256,512]{4,3,2,1,0:T(8,128)S(1)} custom-call(bf16[2,2,1,2,256,512]{5,4,3,2,1,0:T(8,128)(2,1)S(1)} %copy-done, f32[2,3,2,256,256]{4,3,2,1,0:T(8,128)S(1)} %get-tuple-element.13.inverse, bf16[4,2,128,512]{3,2,1,0:T(8,128)(2,1)S(1)} %collective-permute-done.6.near, ...), custom_call_target="tpu_custom_call", output_to_operand_aliasing={{}: (3, {})} | custom-call | tf_op jit(solution)/shard_map/pallas_call | solution.py:222
  44.1 3.8 %collective-permute-done.5.refs_1_ = bf16[2,2,128,512]{3,2,1,0:T(8,128)(2,1)S(1)} collective-permute-done((bf16[2,2,128,512]{3,2,1,0:T(8,128)(2,1)S(1)}, bf16[2,2,128,512]{3,2,1,0:T(8,128)(2,1)S(1)}, u32[]{:S(2)}, u32[]{:S(2)}) %collective-permute-start.5) | collective-permute-done | bytes 524320 | tf_op jit(solution)/shard_map/ppermute | solution.py:23
  47.9 2.0 %collective-permute-done.4.refs_0_ = bf16[2,2,128,512]{3,2,1,0:T(8,128)(2,1)S(1)} collective-permute-done((bf16[2,2,128,512]{3,2,1,0:T(8,128)(2,1)S(1)}, bf16[2,2,128,512]{3,2,1,0:T(8,128)(2,1)S(1)}, u32[]{:S(2)}, u32[]{:S(2)}) %collective-permute-start.4) | collective-permute-done | bytes 524320 | tf_op jit(solution)/shard_map/ppermute | solution.py:23
  49.9 1.7 %shard_map.59.total = f32[2,2,2,256,512]{4,3,2,1,0:T(8,128)S(1)} custom-call(bf16[2,2,1,2,256,512]{5,4,3,2,1,0:T(8,128)(2,1)S(1)} %copy-done, f32[2,3,2,256,256]{4,3,2,1,0:T(8,128)S(1)} %get-tuple-element.13.inverse, bf16[2,2,2,16,512]{4,3,2,1,0:T(8,128)(2,1)S(1)} %get-tuple-element.17.choice, ...), custom_call_target="tpu_custom_call", output_to_operand_aliasing={{}: (5, {})} | custom-call | tf_op jit(solution)/shard_map/pallas_call | solution.py:222
  51.6 0.4 collective-permute-done.2.window
  52.0 2.2 %shard_map.60 = bf16[2,2,1,2,256,512]{5,4,3,2,1,0:T(8,128)(2,1)} custom-call(bf16[2,2,1,2,256,512]{5,4,3,2,1,0:T(8,128)(2,1)S(1)} %copy-done, f32[2,3,2,256,256]{4,3,2,1,0:T(8,128)S(1)} %get-tuple-element.13.inverse, bf16[4,2,128,512]{3,2,1,0:T(8,128)(2,1)S(1)} %collective-permute-done.2.window, f32[2,2,2,256,512]{4,3,2,1,0:T(8,128)S(1)} %shard_map.59.total), custom_call_target="tpu_custom_call" | custom-call | tf_op jit(solution)/shard_map/pallas_call | solution.py:254
  (3 shorter events, 0.1 us)
Async XLA Ops:
  1.3 31.9 %collective-permute-start.3 = (bf16[4,2,128,512]{3,2,1,0:T(8,128)(2,1)S(1)}, bf16[4,2,128,512]{3,2,1,0:T(8,128)(2,1)S(1)}, u32[]{:S(2)}, u32[]{:S(2)}) collective-permute-start(bf16[4,2,128,512]{3,2,1,0:T(8,128)(2,1)S(1)} %bitcast.1), channel_id=1, source_target_pairs={{0,7},{1,2},{2,1},{3,4},{4,3},{5,6},{6,5},{7,0},{8,15},{9,10},{10,... | collective-permute-start | bytes 3145736 | tf_op jit(solution)/shard_map/ppermute | solution.py:33
  8.1 14.9 %collective-permute-start = (bf16[2,2,128,512]{3,2,1,0:T(8,128)(2,1)S(1)}, bf16[2,2,128,512]{3,2,1,0:T(8,128)(2,1)S(1)}, u32[]{:S(2)}, u32[]{:S(2)}) collective-permute-start(bf16[2,2,128,512]{3,2,1,0:T(8,128)(2,1)S(1)} %get-tuple-element.15), channel_id=1, source_target_pairs={{0,8},{8,0},{16,24},{24,16},{1,9},{9,1},{17,25},{25,17},{2,10},{10... | collective-permute-start | bytes 1572872 | tf_op jit(solution)/shard_map/ppermute | solution.py:23
  9.7 14.9 %collective-permute-start.1 = (bf16[2,2,128,512]{3,2,1,0:T(8,128)(2,1)S(1)}, bf16[2,2,128,512]{3,2,1,0:T(8,128)(2,1)S(1)}, u32[]{:S(2)}, u32[]{:S(2)}) collective-permute-start(bf16[2,2,128,512]{3,2,1,0:T(8,128)(2,1)S(1)} %get-tuple-element.16), channel_id=1, source_target_pairs={{0,16},{8,24},{16,0},{24,8},{1,17},{9,25},{17,1},{25,9},{2,18},{10... | collective-permute-start | bytes 1572872 | tf_op jit(solution)/shard_map/ppermute | solution.py:23
  11.2 20.7 %collective-permute-start.7 = (bf16[2,2,128,512]{3,2,1,0:T(8,128)(2,1)S(1)}, bf16[2,2,128,512]{3,2,1,0:T(8,128)(2,1)S(1)}, u32[]{:S(2)}, u32[]{:S(2)}) collective-permute-start(bf16[2,2,128,512]{3,2,1,0:T(8,128)(2,1)S(1)} %get-tuple-element.18), channel_id=1, source_target_pairs={{0,8},{8,0},{16,24},{24,16},{1,9},{9,1},{17,25},{25,17},{2,10},{10... | collective-permute-start | bytes 1572872 | tf_op jit(solution)/shard_map/ppermute | solution.py:23
  11.8 21.3 %collective-permute-start.8 = (bf16[2,2,128,512]{3,2,1,0:T(8,128)(2,1)S(1)}, bf16[2,2,128,512]{3,2,1,0:T(8,128)(2,1)S(1)}, u32[]{:S(2)}, u32[]{:S(2)}) collective-permute-start(bf16[2,2,128,512]{3,2,1,0:T(8,128)(2,1)S(1)} %get-tuple-element.19), channel_id=1, source_target_pairs={{0,16},{8,24},{16,0},{24,8},{1,17},{9,25},{17,1},{25,9},{2,18},{10... | collective-permute-start | bytes 1572872 | tf_op jit(solution)/shard_map/ppermute | solution.py:23
  24.6 11.9 %copy-start.3 = (f32[8,256]{1,0:T(8,128)S(1)}, f32[8,256]{1,0:T(8,128)}, u32[]{:S(2)}) copy-start(f32[8,256]{1,0:T(8,128)} %param.8) | copy-start | bytes 24580
  24.6 11.9 %copy-start.4 = (s32[8,256]{1,0:T(8,128)S(1)}, s32[8,256]{1,0:T(8,128)}, u32[]{:S(2)}) copy-start(s32[8,256]{1,0:T(8,128)} %param.9) | copy-start | bytes 24580
  24.6 12.6 %copy-start.1 = (s32[2,8]{1,0:T(2,128)S(1)}, s32[2,8]{1,0:T(2,128)}, u32[]{:S(2)}) copy-start(s32[2,8]{1,0:T(2,128)} %partner.2) | copy-start | bytes 196
  24.6 12.6 %copy-start.2 = (f32[8,8]{1,0:T(8,128)S(1)}, f32[8,8]{1,0:T(8,128)}, u32[]{:S(2)}) copy-start(f32[8,8]{1,0:T(8,128)} %occ.1) | copy-start | bytes 772
  24.6 17.8 %collective-permute-start.6 = (bf16[4,2,128,512]{3,2,1,0:T(8,128)(2,1)S(1)}, bf16[4,2,128,512]{3,2,1,0:T(8,128)(2,1)S(1)}, u32[]{:S(2)}, u32[]{:S(2)}) collective-permute-start(bf16[4,2,128,512]{3,2,1,0:T(8,128)(2,1)S(1)} %constant_dynamic-update-slice_fusion), channel_id=1, source_target_pairs={{0,1},{1,0},{2,3},{3,2},{4,5},{5,4},{6,7},{7,6},{8,9},{9,8},{10,11... | collective-permute-start | bytes 3145736 | tf_op jit(solution)/shard_map/ppermute | solution.py:28
  24.7 27.3 %collective-permute-start.2 = (bf16[4,2,128,512]{3,2,1,0:T(8,128)(2,1)S(1)}, bf16[4,2,128,512]{3,2,1,0:T(8,128)(2,1)S(1)}, u32[]{:S(2)}, u32[]{:S(2)}) collective-permute-start(bf16[4,2,128,512]{3,2,1,0:T(8,128)(2,1)S(1)} %constant_dynamic-update-slice_fusion), channel_id=1, source_target_pairs={{0,7},{1,2},{2,1},{3,4},{4,3},{5,6},{6,5},{7,0},{8,15},{9,10},{10,... | collective-permute-start | bytes 3145736 | tf_op jit(solution)/shard_map/ppermute | solution.py:33
  33.2 5.7 %collective-permute-start.9 = (bf16[3,2,128,512]{3,2,1,0:T(8,128)(2,1)S(1)}, bf16[3,2,128,512]{3,2,1,0:T(8,128)(2,1)S(1)}, u32[]{:S(2)}, u32[]{:S(2)}) collective-permute-start(bf16[3,2,128,512]{3,2,1,0:T(8,128)(2,1)S(1)} %pad_maximum_fusion.1), channel_id=1, source_target_pairs={{0,1},{1,0},{2,3},{3,2},{4,5},{5,4},{6,7},{7,6},{8,9},{9,8},{10,11... | collective-permute-start | bytes 2359304 | tf_op jit(solution)/shard_map/ppermute | solution.py:28
  33.3 5.7 %copy-start = (bf16[2,2,1,2,256,512]{5,4,3,2,1,0:T(8,128)(2,1)S(1)}, bf16[2,2,1,2,256,512]{5,4,3,2,1,0:T(8,128)(2,1)}, u32[]{:S(2)}) copy-start(bf16[2,2,1,2,256,512]{5,4,3,2,1,0:T(8,128)(2,1)} %factor.9) | copy-start | bytes 6291460
  33.3 2.6 %collective-permute-start.10 = (bf16[1,2,128,512]{3,2,1,0:T(8,128)(2,1)S(1)}, bf16[1,2,128,512]{3,2,1,0:T(8,128)(2,1)S(1)}, u32[]{:S(2)}, u32[]{:S(2)}) collective-permute-start(bf16[1,2,128,512]{3,2,1,0:T(8,128)(2,1)S(1)} %slice.22), channel_id=1, source_target_pairs={{0,1},{1,0},{2,3},{3,2},{4,5},{5,4},{6,7},{7,6},{8,9},{9,8},{10,11... | collective-permute-start | bytes 786440 | tf_op jit(solution)/shard_map/ppermute | solution.py:28
  34.0 13.9 %collective-permute-start.5 = (bf16[2,2,128,512]{3,2,1,0:T(8,128)(2,1)S(1)}, bf16[2,2,128,512]{3,2,1,0:T(8,128)(2,1)S(1)}, u32[]{:S(2)}, u32[]{:S(2)}) collective-permute-start(bf16[2,2,128,512]{3,2,1,0:T(8,128)(2,1)S(1)} %get-tuple-element.21), channel_id=1, source_target_pairs={{0,16},{8,24},{16,0},{24,8},{1,17},{9,25},{17,1},{25,9},{2,18},{10... | collective-permute-start | bytes 1572872 | tf_op jit(solution)/shard_map/ppermute | solution.py:23
  35.9 14.0 %collective-permute-start.4 = (bf16[2,2,128,512]{3,2,1,0:T(8,128)(2,1)S(1)}, bf16[2,2,128,512]{3,2,1,0:T(8,128)(2,1)S(1)}, u32[]{:S(2)}, u32[]{:S(2)}) collective-permute-start(bf16[2,2,128,512]{3,2,1,0:T(8,128)(2,1)S(1)} %get-tuple-element.22), channel_id=1, source_target_pairs={{0,8},{8,0},{16,24},{24,16},{1,9},{9,1},{17,25},{25,17},{2,10},{10... | collective-permute-start | bytes 1572872 | tf_op jit(solution)/shard_map/ppermute | solution.py:23

commit v11 on v9

--- a/solution.py
+++ b/solution.py
@@ -15,6 +15,7 @@
 PARAMS = pltpu.CompilerParams(vmem_limit_bytes=8 * 1024 * 1024)
 WORK = 16
 ROWS = 16
+PIECES = 4
 COST = pl.CostEstimate(flops=0, bytes_accessed=0, transcendentals=0)
 
 
@@ -50,12 +51,17 @@
 
 
 def lay_kernel(factor, out, sems):
-    kc, half = factor.shape[1], out.shape[2]
+    kc, parts, half = factor.shape[1], factor.shape[3], out.shape[2]
+    size = half // PIECES
     copies = []
     for at in range(out.shape[0]):
-        source = factor.at[at // kc, at % kc, 0, :, pl.ds(0, half), :]
-        copies.append(pltpu.make_async_copy(source, out.at[at], sems.at[at]))
-        copies[-1].start()
+        for part in range(parts):
+            for piece in range(PIECES):
+                rows = pl.ds(piece * size, size)
+                source = factor.at[at // kc, at % kc, 0, part, rows]
+                target = out.at[at, part, rows]
+                copies.append(pltpu.make_async_copy(source, target, sems.at[len(copies)]))
+                copies[-1].start()
     for copy in copies:
         copy.wait()
 
@@ -67,7 +73,7 @@
         out_shape=jax.ShapeDtypeStruct((transfers * kc, parts, nv // 2, naux), BF16),
         in_specs=[ANY],
         out_specs=VMEM,
-        scratch_shapes=[pltpu.SemaphoreType.DMA((transfers * kc,))],
+        scratch_shapes=[pltpu.SemaphoreType.DMA((transfers * kc * parts * PIECES,))],
         cost_estimate=COST,
         compiler_params=PARAMS,
     )(pltpu.with_memory_space_constraint(factor, pltpu.HBM))
@@ -262,10 +268,15 @@
         return [(window[t * kc + k], inverse[t, 2, k, :, half_of(1, half)])]
 
     def finish(t, k, part, value):
-        at = len(copies)
-        staged[at] = (value + total[t, k, part]).astype(BF16)
-        copies.append(pltpu.make_async_copy(staged.at[at], out.at[t, k, 0, part], sems.at[at]))
-        copies[-1].start()
+        at = (t * kc + k) * 2 + part
+        size = value.shape[0] // PIECES
+        for piece in range(PIECES):
+            rows = slice(piece * size, (piece + 1) * size)
+            staged[at, rows] = (value[rows] + total[t, k, part, rows]).astype(BF16)
+            target = out.at[t, k, 0, part, pl.ds(piece * size, size)]
+            source = staged.at[at, pl.ds(piece * size, size)]
+            copies.append(pltpu.make_async_copy(source, target, sems.at[len(copies)]))
+            copies[-1].start()
 
     contract(factor, terms_of, finish)
     for copy in copies:
@@ -282,7 +293,7 @@
         out_specs=ANY,
         scratch_shapes=[
             pltpu.VMEM((count, nv, naux), BF16),
-            pltpu.SemaphoreType.DMA((count,)),
+            pltpu.SemaphoreType.DMA((count * PIECES,)),
         ],
         cost_estimate=COST,
         compiler_params=PARAMS,

time: 54.4 us -> 54.8 us (level)
  no operation moved by 1% of the time
where the time goes in v11:
time: 54.8 us; the launch traced here: 54.6 us
  waiting for transfers between devices  26.7 us (49%)
  Pallas kernels  14.5 us (26%)
  starting transfers between devices  12.1 us (22%)
  other arithmetic  0.92 us (2%)
    ppermute x6, waiting for transfers between devices, group_swap(): return lax.ppermute(block, 'kpt', [(g, g ^ 1 << bit) for g in range(count)])  25.9 us
    ppermute x6, starting transfers between devices, group_swap(): return lax.ppermute(block, 'kpt', [(g, g ^ 1 << bit) for g in range(count)])  6.24 us
    ppermute x2, starting transfers between devices, far_swap(): lax.ppermute(block, 'occ', [(i, (i + (1 if i % 2 else count - 1)) % count...  5.16 us
    pallas_call x1, Pallas kernels, first_terms(): pl.pallas_call(first_kernel, out_shape=jax.ShapeDtypeStruct((transfers, k...  3.46 us
    pallas_call x2, Pallas kernels, more_terms(): pl.pallas_call(body, out_shape=jax.ShapeDtypeStruct(total.shape, F32), in...  3.32 us
    pallas_call x1, Pallas kernels, last_terms(): pl.pallas_call(last_kernel, out_shape=jax.ShapeDtypeStruct(factor.shape,...  2.38 us
    pallas_call x1, Pallas kernels, pack(): pl.pallas_call(functools.partial(pack_kernel, bits), out_shape=[jax.Shape...  2.27 us
    pallas_call x1, Pallas kernels, inverses(): pl.pallas_call(functools.partial(inverse_kernel, bits), out_shape=[jax.Sh...  1.6 us
  transfers between devices with their start and end apart: 11, of which 8 were waited for; matrix products, arithmetic and copies ran while one was open for 2% of the time, Pallas kernels for 20%

profile of v11, /device:TPU:0, one launch (start us, length us, event | category | flops | bytes accessed | tf_op | source)
XLA Modules:
  0.0 54.6 jit_solution(1419093594887265110)
XLA Ops:
  0.0 1.4 %shard_map.56 = bf16[4,2,128,512]{3,2,1,0:T(8,128)(2,1)S(1)} custom-call(bf16[2,2,1,2,256,512]{5,4,3,2,1,0:T(8,128)(2,1)} %factor.11), custom_call_target="tpu_custom_call" | custom-call | tf_op jit(solution)/shard_map/pallas_call | solution.py:71
  1.4 4.6 %collective-permute-start.3 = (bf16[4,2,128,512]{3,2,1,0:T(8,128)(2,1)S(1)}, bf16[4,2,128,512]{3,2,1,0:T(8,128)(2,1)S(1)}, u32[]{:S(2)}, u32[]{:S(2)}) collective-permute-start(bf16[4,2,128,512]{3,2,1,0:T(8,128)(2,1)S(1)} %shard_map.56), channel_id=1, source_target_pairs={{0,7},{1,2},{2,1},{3,4},{4,3},{5,6},{6,5},{7,0},{8,15},{9,10},{10,... | collective-permute-start | bytes 3145736 | tf_op jit(solution)/shard_map/ppermute | solution.py:34
  6.0 2.3 %shard_map.57 = (bf16[2,2,128,512]{3,2,1,0:T(8,128)(2,1)S(1)}, bf16[2,2,128,512]{3,2,1,0:T(8,128)(2,1)S(1)}, bf16[2,2,128,512]{3,2,1,0:T(8,128)(2,1)S(1)}, bf16[2,2,128,512]{3,2,1,0:T(8,128)(2,1)S(1)}) custom-call(s32[2,8]{1,0:T(2,128)} %partner.2, bf16[2,2,1,2,256,512]{5,4,3,2,1,0:T(8,128)(2,1)} %factor.11), custom_call_target="tpu_custom_call" | custom-call | bytes 16777216 | tf_op jit(solution)/shard_map/pallas_call | solution.py:102
  8.3 1.6 %collective-permute-start = (bf16[2,2,128,512]{3,2,1,0:T(8,128)(2,1)S(1)}, bf16[2,2,128,512]{3,2,1,0:T(8,128)(2,1)S(1)}, u32[]{:S(2)}, u32[]{:S(2)}) collective-permute-start(bf16[2,2,128,512]{3,2,1,0:T(8,128)(2,1)S(1)} %get-tuple-element.15), channel_id=1, source_target_pairs={{0,8},{8,0},{16,24},{24,16},{1,9},{9,1},{17,25},{25,17},{2,10},{10... | collective-permute-start | bytes 1572872 | tf_op jit(solution)/shard_map/ppermute | solution.py:24
  9.8 1.5 %collective-permute-start.1 = (bf16[2,2,128,512]{3,2,1,0:T(8,128)(2,1)S(1)}, bf16[2,2,128,512]{3,2,1,0:T(8,128)(2,1)S(1)}, u32[]{:S(2)}, u32[]{:S(2)}) collective-permute-start(bf16[2,2,128,512]{3,2,1,0:T(8,128)(2,1)S(1)} %get-tuple-element.16), channel_id=1, source_target_pairs={{0,16},{8,24},{16,0},{24,8},{1,17},{9,25},{17,1},{25,9},{2,18},{10... | collective-permute-start | bytes 1572872 | tf_op jit(solution)/shard_map/ppermute | solution.py:24
  11.4 0.6 %collective-permute-start.7 = (bf16[2,2,128,512]{3,2,1,0:T(8,128)(2,1)S(1)}, bf16[2,2,128,512]{3,2,1,0:T(8,128)(2,1)S(1)}, u32[]{:S(2)}, u32[]{:S(2)}) collective-permute-start(bf16[2,2,128,512]{3,2,1,0:T(8,128)(2,1)S(1)} %get-tuple-element.18), channel_id=1, source_target_pairs={{0,8},{8,0},{16,24},{24,16},{1,9},{9,1},{17,25},{25,17},{2,10},{10... | collective-permute-start | bytes 1572872 | tf_op jit(solution)/shard_map/ppermute | solution.py:24
  11.9 0.5 collective-permute-start.8
  12.4 10.8 %collective-permute-done.refs_2_ = bf16[2,2,128,512]{3,2,1,0:T(8,128)(2,1)S(1)} collective-permute-done((bf16[2,2,128,512]{3,2,1,0:T(8,128)(2,1)S(1)}, bf16[2,2,128,512]{3,2,1,0:T(8,128)(2,1)S(1)}, u32[]{:S(2)}, u32[]{:S(2)}) %collective-permute-start) | collective-permute-done | bytes 524320 | tf_op jit(solution)/shard_map/ppermute | solution.py:24
  23.3 1.5 %collective-permute-done.1.refs_3_ = bf16[2,2,128,512]{3,2,1,0:T(8,128)(2,1)S(1)} collective-permute-done((bf16[2,2,128,512]{3,2,1,0:T(8,128)(2,1)S(1)}, bf16[2,2,128,512]{3,2,1,0:T(8,128)(2,1)S(1)}, u32[]{:S(2)}, u32[]{:S(2)}) %collective-permute-start.1) | collective-permute-done | bytes 524320 | tf_op jit(solution)/shard_map/ppermute | solution.py:24
  24.7 0.0 copy-start.3
  24.8 0.0 copy-start.4
  24.8 0.0 copy-start.1
  24.8 0.0 copy-start.2
  24.8 0.1 collective-permute-start.6
  24.9 0.6 %collective-permute-start.2 = (bf16[4,2,128,512]{3,2,1,0:T(8,128)(2,1)S(1)}, bf16[4,2,128,512]{3,2,1,0:T(8,128)(2,1)S(1)}, u32[]{:S(2)}, u32[]{:S(2)}) collective-permute-start(bf16[4,2,128,512]{3,2,1,0:T(8,128)(2,1)S(1)} %constant_dynamic-update-slice_fusion), channel_id=1, source_target_pairs={{0,7},{1,2},{2,1},{3,4},{4,3},{5,6},{6,5},{7,0},{8,15},{9,10},{10,... | collective-permute-start | bytes 3145736 | tf_op jit(solution)/shard_map/ppermute | solution.py:34
  25.5 6.6 %collective-permute-done.7.refs_0_ = bf16[2,2,128,512]{3,2,1,0:T(8,128)(2,1)S(1)} collective-permute-done((bf16[2,2,128,512]{3,2,1,0:T(8,128)(2,1)S(1)}, bf16[2,2,128,512]{3,2,1,0:T(8,128)(2,1)S(1)}, u32[]{:S(2)}, u32[]{:S(2)}) %collective-permute-start.7) | collective-permute-done | bytes 524320 | tf_op jit(solution)/shard_map/ppermute | solution.py:24
  32.1 1.2 %collective-permute-done.8.refs_1_ = bf16[2,2,128,512]{3,2,1,0:T(8,128)(2,1)S(1)} collective-permute-done((bf16[2,2,128,512]{3,2,1,0:T(8,128)(2,1)S(1)}, bf16[2,2,128,512]{3,2,1,0:T(8,128)(2,1)S(1)}, u32[]{:S(2)}, u32[]{:S(2)}) %collective-permute-start.8) | collective-permute-done | bytes 524320 | tf_op jit(solution)/shard_map/ppermute | solution.py:24
  33.3 0.1 pad_maximum_fusion.1
  33.4 0.0 collective-permute-done.3
  33.4 0.1 collective-permute-start.9
  33.5 0.0 copy-start
  33.5 0.6 %collective-permute-start.10 = (bf16[1,2,128,512]{3,2,1,0:T(8,128)(2,1)S(1)}, bf16[1,2,128,512]{3,2,1,0:T(8,128)(2,1)S(1)}, u32[]{:S(2)}, u32[]{:S(2)}) collective-permute-start(bf16[1,2,128,512]{3,2,1,0:T(8,128)(2,1)S(1)} %slice.18), channel_id=1, source_target_pairs={{0,1},{1,0},{2,3},{3,2},{4,5},{5,4},{6,7},{7,6},{8,9},{9,8},{10,11... | collective-permute-start | bytes 786440 | tf_op jit(solution)/shard_map/ppermute | solution.py:29
  34.0 0.1 fusion
  34.1 1.6 %collective-permute-start.5 = (bf16[2,2,128,512]{3,2,1,0:T(8,128)(2,1)S(1)}, bf16[2,2,128,512]{3,2,1,0:T(8,128)(2,1)S(1)}, u32[]{:S(2)}, u32[]{:S(2)}) collective-permute-start(bf16[2,2,128,512]{3,2,1,0:T(8,128)(2,1)S(1)} %get-tuple-element.21), channel_id=1, source_target_pairs={{0,16},{8,24},{16,0},{24,8},{1,17},{9,25},{17,1},{25,9},{2,18},{10... | collective-permute-start | bytes 1572872 | tf_op jit(solution)/shard_map/ppermute | solution.py:24
  35.7 0.4 collective-permute-done.10
  36.1 0.5 collective-permute-start.4
  36.6 0.0 copy-done.3
  36.6 0.0 copy-done.4
  36.6 0.8 %select_reduce_fusion.virtual = f32[8,256]{1,0:T(8,128)S(1)} fusion(f32[8,256]{1,0:T(8,128)S(1)} %copy-done.3, s32[8,256]{1,0:T(8,128)S(1)} %copy-done.4), kind=kLoop, calls=%fused_computation | loop fusion | flops 1570816 | bytes 24576 | tf_op jit(solution)/shard_map/reduce_sum | solution.py:46
  37.4 0.0 copy-done.1
  37.4 0.0 copy-done.2
  37.4 1.6 %shard_map.55 = (f32[2,3,2,256,256]{4,3,2,1,0:T(8,128)S(1)}, bf16[2,2,2,16,512]{4,3,2,1,0:T(8,128)(2,1)S(1)}) custom-call(s32[2,8]{1,0:T(2,128)S(1)} %copy-done.1, f32[8,8]{1,0:T(8,128)S(1)} %copy-done.2, f32[8,256]{1,0:T(8,128)S(1)} %select_reduce_fusion.virtual), custom_call_target="tpu_custom_call" | custom-call | tf_op jit(solution)/shard_map/pallas_call | solution.py:143
  39.0 0.0 collective-permute-done.9
  39.0 0.1 pad_maximum_fusion.refs_4_
  39.1 0.0 copy-done
  39.1 3.5 %shard_map.58.total = f32[2,2,2,256,512]{4,3,2,1,0:T(8,128)S(1)} custom-call(bf16[2,2,1,2,256,512]{5,4,3,2,1,0:T(8,128)(2,1)S(1)} %copy-done, f32[2,3,2,256,256]{4,3,2,1,0:T(8,128)S(1)} %get-tuple-element.13.inverse, bf16[2,2,128,512]{3,2,1,0:T(8,128)(2,1)S(1)} %collective-permute-done.7.refs_0_, ...), custom_call_target="tpu_custom_call" | custom-call | tf_op jit(solution)/shard_map/pallas_call | solution.py:213
  42.6 0.0 collective-permute-done.6.near
  42.6 1.6 %shard_map.59.refs_2_ = f32[2,2,2,256,512]{4,3,2,1,0:T(8,128)S(1)} custom-call(bf16[2,2,1,2,256,512]{5,4,3,2,1,0:T(8,128)(2,1)S(1)} %copy-done, f32[2,3,2,256,256]{4,3,2,1,0:T(8,128)S(1)} %get-tuple-element.13.inverse, bf16[4,2,128,512]{3,2,1,0:T(8,128)(2,1)S(1)} %collective-permute-done.6.near, ...), custom_call_target="tpu_custom_call", output_to_operand_aliasing={{}: (3, {})} | custom-call | tf_op jit(solution)/shard_map/pallas_call | solution.py:252
  44.2 3.8 %collective-permute-done.5.refs_1_ = bf16[2,2,128,512]{3,2,1,0:T(8,128)(2,1)S(1)} collective-permute-done((bf16[2,2,128,512]{3,2,1,0:T(8,128)(2,1)S(1)}, bf16[2,2,128,512]{3,2,1,0:T(8,128)(2,1)S(1)}, u32[]{:S(2)}, u32[]{:S(2)}) %collective-permute-start.5) | collective-permute-done | bytes 524320 | tf_op jit(solution)/shard_map/ppermute | solution.py:24
  48.0 2.0 %collective-permute-done.4.refs_0_ = bf16[2,2,128,512]{3,2,1,0:T(8,128)(2,1)S(1)} collective-permute-done((bf16[2,2,128,512]{3,2,1,0:T(8,128)(2,1)S(1)}, bf16[2,2,128,512]{3,2,1,0:T(8,128)(2,1)S(1)}, u32[]{:S(2)}, u32[]{:S(2)}) %collective-permute-start.4) | collective-permute-done | bytes 524320 | tf_op jit(solution)/shard_map/ppermute | solution.py:24
  50.1 1.7 %shard_map.60.total = f32[2,2,2,256,512]{4,3,2,1,0:T(8,128)S(1)} custom-call(bf16[2,2,1,2,256,512]{5,4,3,2,1,0:T(8,128)(2,1)S(1)} %copy-done, f32[2,3,2,256,256]{4,3,2,1,0:T(8,128)S(1)} %get-tuple-element.13.inverse, bf16[2,2,2,16,512]{4,3,2,1,0:T(8,128)(2,1)S(1)} %get-tuple-element.17.choice, ...), custom_call_target="tpu_custom_call", output_to_operand_aliasing={{}: (5, {})} | custom-call | tf_op jit(solution)/shard_map/pallas_call | solution.py:252
  51.8 0.4 collective-permute-done.2.window
  52.2 2.4 %shard_map.61 = bf16[2,2,1,2,256,512]{5,4,3,2,1,0:T(8,128)(2,1)} custom-call(bf16[2,2,1,2,256,512]{5,4,3,2,1,0:T(8,128)(2,1)S(1)} %copy-done, f32[2,3,2,256,256]{4,3,2,1,0:T(8,128)S(1)} %get-tuple-element.13.inverse, bf16[4,2,128,512]{3,2,1,0:T(8,128)(2,1)S(1)} %collective-permute-done.2.window, f32[2,2,2,256,512]{4,3,2,1,0:T(8,128)S(1)} %shard_map.60.total), custom_call_target="tpu_custom_call" | custom-call | tf_op jit(solution)/shard_map/pallas_call | solution.py:289
  (3 shorter events, 0.1 us)
Async XLA Ops:
  1.4 31.9 %collective-permute-start.3 = (bf16[4,2,128,512]{3,2,1,0:T(8,128)(2,1)S(1)}, bf16[4,2,128,512]{3,2,1,0:T(8,128)(2,1)S(1)}, u32[]{:S(2)}, u32[]{:S(2)}) collective-permute-start(bf16[4,2,128,512]{3,2,1,0:T(8,128)(2,1)S(1)} %shard_map.56), channel_id=1, source_target_pairs={{0,7},{1,2},{2,1},{3,4},{4,3},{5,6},{6,5},{7,0},{8,15},{9,10},{10,... | collective-permute-start | bytes 3145736 | tf_op jit(solution)/shard_map/ppermute | solution.py:34
  8.3 14.9 %collective-permute-start = (bf16[2,2,128,512]{3,2,1,0:T(8,128)(2,1)S(1)}, bf16[2,2,128,512]{3,2,1,0:T(8,128)(2,1)S(1)}, u32[]{:S(2)}, u32[]{:S(2)}) collective-permute-start(bf16[2,2,128,512]{3,2,1,0:T(8,128)(2,1)S(1)} %get-tuple-element.15), channel_id=1, source_target_pairs={{0,8},{8,0},{16,24},{24,16},{1,9},{9,1},{17,25},{25,17},{2,10},{10... | collective-permute-start | bytes 1572872 | tf_op jit(solution)/shard_map/ppermute | solution.py:24
  9.8 14.9 %collective-permute-start.1 = (bf16[2,2,128,512]{3,2,1,0:T(8,128)(2,1)S(1)}, bf16[2,2,128,512]{3,2,1,0:T(8,128)(2,1)S(1)}, u32[]{:S(2)}, u32[]{:S(2)}) collective-permute-start(bf16[2,2,128,512]{3,2,1,0:T(8,128)(2,1)S(1)} %get-tuple-element.16), channel_id=1, source_target_pairs={{0,16},{8,24},{16,0},{24,8},{1,17},{9,25},{17,1},{25,9},{2,18},{10... | collective-permute-start | bytes 1572872 | tf_op jit(solution)/shard_map/ppermute | solution.py:24
  11.4 20.7 %collective-permute-start.7 = (bf16[2,2,128,512]{3,2,1,0:T(8,128)(2,1)S(1)}, bf16[2,2,128,512]{3,2,1,0:T(8,128)(2,1)S(1)}, u32[]{:S(2)}, u32[]{:S(2)}) collective-permute-start(bf16[2,2,128,512]{3,2,1,0:T(8,128)(2,1)S(1)} %get-tuple-element.18), channel_id=1, source_target_pairs={{0,8},{8,0},{16,24},{24,16},{1,9},{9,1},{17,25},{25,17},{2,10},{10... | collective-permute-start | bytes 1572872 | tf_op jit(solution)/shard_map/ppermute | solution.py:24
  11.9 21.4 %collective-permute-start.8 = (bf16[2,2,128,512]{3,2,1,0:T(8,128)(2,1)S(1)}, bf16[2,2,128,512]{3,2,1,0:T(8,128)(2,1)S(1)}, u32[]{:S(2)}, u32[]{:S(2)}) collective-permute-start(bf16[2,2,128,512]{3,2,1,0:T(8,128)(2,1)S(1)} %get-tuple-element.19), channel_id=1, source_target_pairs={{0,16},{8,24},{16,0},{24,8},{1,17},{9,25},{17,1},{25,9},{2,18},{10... | collective-permute-start | bytes 1572872 | tf_op jit(solution)/shard_map/ppermute | solution.py:24
  24.7 11.9 %copy-start.3 = (f32[8,256]{1,0:T(8,128)S(1)}, f32[8,256]{1,0:T(8,128)}, u32[]{:S(2)}) copy-start(f32[8,256]{1,0:T(8,128)} %param.8) | copy-start | bytes 24580
  24.8 11.9 %copy-start.4 = (s32[8,256]{1,0:T(8,128)S(1)}, s32[8,256]{1,0:T(8,128)}, u32[]{:S(2)}) copy-start(s32[8,256]{1,0:T(8,128)} %param.9) | copy-start | bytes 24580
  24.8 12.6 %copy-start.1 = (s32[2,8]{1,0:T(2,128)S(1)}, s32[2,8]{1,0:T(2,128)}, u32[]{:S(2)}) copy-start(s32[2,8]{1,0:T(2,128)} %partner.2) | copy-start | bytes 196
  24.8 12.6 %copy-start.2 = (f32[8,8]{1,0:T(8,128)S(1)}, f32[8,8]{1,0:T(8,128)}, u32[]{:S(2)}) copy-start(f32[8,8]{1,0:T(8,128)} %occ.1) | copy-start | bytes 772
  24.8 17.8 %collective-permute-start.6 = (bf16[4,2,128,512]{3,2,1,0:T(8,128)(2,1)S(1)}, bf16[4,2,128,512]{3,2,1,0:T(8,128)(2,1)S(1)}, u32[]{:S(2)}, u32[]{:S(2)}) collective-permute-start(bf16[4,2,128,512]{3,2,1,0:T(8,128)(2,1)S(1)} %constant_dynamic-update-slice_fusion), channel_id=1, source_target_pairs={{0,1},{1,0},{2,3},{3,2},{4,5},{5,4},{6,7},{7,6},{8,9},{9,8},{10,11... | collective-permute-start | bytes 3145736 | tf_op jit(solution)/shard_map/ppermute | solution.py:29
  24.9 27.3 %collective-permute-start.2 = (bf16[4,2,128,512]{3,2,1,0:T(8,128)(2,1)S(1)}, bf16[4,2,128,512]{3,2,1,0:T(8,128)(2,1)S(1)}, u32[]{:S(2)}, u32[]{:S(2)}) collective-permute-start(bf16[4,2,128,512]{3,2,1,0:T(8,128)(2,1)S(1)} %constant_dynamic-update-slice_fusion), channel_id=1, source_target_pairs={{0,7},{1,2},{2,1},{3,4},{4,3},{5,6},{6,5},{7,0},{8,15},{9,10},{10,... | collective-permute-start | bytes 3145736 | tf_op jit(solution)/shard_map/ppermute | solution.py:34
  33.4 5.7 %collective-permute-start.9 = (bf16[3,2,128,512]{3,2,1,0:T(8,128)(2,1)S(1)}, bf16[3,2,128,512]{3,2,1,0:T(8,128)(2,1)S(1)}, u32[]{:S(2)}, u32[]{:S(2)}) collective-permute-start(bf16[3,2,128,512]{3,2,1,0:T(8,128)(2,1)S(1)} %pad_maximum_fusion.1), channel_id=1, source_target_pairs={{0,1},{1,0},{2,3},{3,2},{4,5},{5,4},{6,7},{7,6},{8,9},{9,8},{10,11... | collective-permute-start | bytes 2359304 | tf_op jit(solution)/shard_map/ppermute | solution.py:29
  33.5 5.7 %copy-start = (bf16[2,2,1,2,256,512]{5,4,3,2,1,0:T(8,128)(2,1)S(1)}, bf16[2,2,1,2,256,512]{5,4,3,2,1,0:T(8,128)(2,1)}, u32[]{:S(2)}) copy-start(bf16[2,2,1,2,256,512]{5,4,3,2,1,0:T(8,128)(2,1)} %factor.11) | copy-start | bytes 6291460
  33.5 2.6 %collective-permute-start.10 = (bf16[1,2,128,512]{3,2,1,0:T(8,128)(2,1)S(1)}, bf16[1,2,128,512]{3,2,1,0:T(8,128)(2,1)S(1)}, u32[]{:S(2)}, u32[]{:S(2)}) collective-permute-start(bf16[1,2,128,512]{3,2,1,0:T(8,128)(2,1)S(1)} %slice.18), channel_id=1, source_target_pairs={{0,1},{1,0},{2,3},{3,2},{4,5},{5,4},{6,7},{7,6},{8,9},{9,8},{10,11... | collective-permute-start | bytes 786440 | tf_op jit(solution)/shard_map/ppermute | solution.py:29
  34.1 13.9 %collective-permute-start.5 = (bf16[2,2,128,512]{3,2,1,0:T(8,128)(2,1)S(1)}, bf16[2,2,128,512]{3,2,1,0:T(8,128)(2,1)S(1)}, u32[]{:S(2)}, u32[]{:S(2)}) collective-permute-start(bf16[2,2,128,512]{3,2,1,0:T(8,128)(2,1)S(1)} %get-tuple-element.21), channel_id=1, source_target_pairs={{0,16},{8,24},{16,0},{24,8},{1,17},{9,25},{17,1},{25,9},{2,18},{10... | collective-permute-start | bytes 1572872 | tf_op jit(solution)/shard_map/ppermute | solution.py:24
  36.1 14.0 %collective-permute-start.4 = (bf16[2,2,128,512]{3,2,1,0:T(8,128)(2,1)S(1)}, bf16[2,2,128,512]{3,2,1,0:T(8,128)(2,1)S(1)}, u32[]{:S(2)}, u32[]{:S(2)}) collective-permute-start(bf16[2,2,128,512]{3,2,1,0:T(8,128)(2,1)S(1)} %get-tuple-element.22), channel_id=1, source_target_pairs={{0,8},{8,0},{16,24},{24,16},{1,9},{9,1},{17,25},{25,17},{2,10},{10... | collective-permute-start | bytes 1572872 | tf_op jit(solution)/shard_map/ppermute | solution.py:24

commit v12 on v10

--- a/solution.py
+++ b/solution.py
@@ -47,6 +47,26 @@
 
 def column_of(row):
     return jnp.transpose(jnp.broadcast_to(row, (8, row.shape[1])))[:, :1]
+
+
+def lay_kernel(factor, out, sem):
+    copy = pltpu.make_async_copy(factor.at[:, :, 0, :, pl.ds(0, out.shape[3]), :], out, sem)
+    copy.start()
+    copy.wait()
+
+
+def lay(factor):
+    transfers, kc, _, parts, nv, naux = factor.shape
+    part = pl.pallas_call(
+        lay_kernel,
+        out_shape=jax.ShapeDtypeStruct((transfers, kc, parts, nv // 2, naux), BF16),
+        in_specs=[ANY],
+        out_specs=VMEM,
+        scratch_shapes=[pltpu.SemaphoreType.DMA],
+        cost_estimate=COST,
+        compiler_params=PARAMS,
+    )(pltpu.with_memory_space_constraint(factor, pltpu.HBM))
+    return part.reshape(transfers * kc, parts, nv // 2, naux)
 
 
 def pack_kernel(bits, partner, factor, *refs):
@@ -231,34 +251,40 @@
 
 
 def last_kernel(factor, inverse, window, total, out, staged, sems):
-    kc, half = factor.shape[1], window.shape[2]
-    copies = []
-
-    def terms_of(t, k):
-        return [(window[t * kc + k], inverse[t, 2, k, :, half_of(1, half)])]
-
-    def finish(t, k, part, value):
-        at = len(copies)
-        staged[at] = (value + total[t, k, part]).astype(BF16)
-        copies.append(pltpu.make_async_copy(staged.at[at], out.at[t, k, 0, part], sems.at[at]))
-        copies[-1].start()
-
-    contract(factor, terms_of, finish)
-    for copy in copies:
-        copy.wait()
+    transfers, kc = factor.shape[:2]
+    half = window.shape[2]
+
+    def copy_out(t, k):
+        return pltpu.make_async_copy(staged.at[t, k], out.at[t, k, 0], sems.at[t, k])
+
+    def point_step(k, carry):
+        waiting = []
+        for t in range(transfers):
+            terms = [(window[t * kc + k], inverse[t, 2, k, :, half_of(1, half)])]
+            waiting.append(amplitude_rows(factor[t, k, 0], terms))
+        for t, (rows, blocks) in enumerate(waiting):
+            for part in range(2):
+                value = jnp.dot(rows[part], blocks, preferred_element_type=F32)
+                staged[t, k, part] = (value + total[t, k, part]).astype(BF16)
+            copy_out(t, k).start()
+        return carry
+
+    lax.fori_loop(0, kc, point_step, 0)
+    for t in range(transfers):
+        for k in range(kc):
+            copy_out(t, k).wait()
 
 
 def last_terms(factor, inverse, window, total):
     transfers, kc, _, parts, nv, naux = factor.shape
-    count = transfers * kc * parts
     return pl.pallas_call(
         last_kernel,
         out_shape=jax.ShapeDtypeStruct(factor.shape, BF16),
         in_specs=[VMEM] * 4,
         out_specs=ANY,
         scratch_shapes=[
-            pltpu.VMEM((count, nv, naux), BF16),
-            pltpu.SemaphoreType.DMA((count,)),
+            pltpu.VMEM((transfers, kc, parts, nv, naux), BF16),
+            pltpu.SemaphoreType.DMA((transfers, kc)),
         ],
         cost_estimate=COST,
         compiler_params=PARAMS,
@@ -269,8 +295,7 @@
     transfers, kc = factor.shape[:2]
     bits = (0, lax.axis_size("kpt").bit_length() - 2)
 
-    half = factor.shape[4] // 2
-    part = factor[:, :, 0, :, :half].reshape(transfers * kc, *factor.shape[3:4], half, factor.shape[5])
+    part = lay(factor)
     beside = far_swap(part)
     packs = pack(bits, after(partner, part), factor, WORK * factor.size)
     earlies, lates = packs[:transfers], packs[transfers:]

time: 54.5 us -> 54.7 us (level)
  Pallas kernels: 12.9 us -> 14.4 us
  local copies, waits for them, and re-layouts: 1.48 us -> 0.19 us
    slice x1 -> x0, local copies, waits for them, and re-layouts: 1.29 us -> none  [body(): factor[:, :, 0, :, :half]]
    pallas_call x0 -> x1, Pallas kernels: none -> 1.23 us  [lay(): pl.pallas_call(lay_kernel, out_shape=jax.ShapeDtypeStruct((transfers, kc,...]
where the time goes in v12:
time: 54.7 us; the launch traced here: 54.5 us
  waiting for transfers between devices  26.7 us (49%)
  Pallas kernels  14.4 us (26%)
  starting transfers between devices  12.1 us (22%)
  other arithmetic  0.92 us (2%)
    ppermute x6, waiting for transfers between devices, group_swap(): return lax.ppermute(block, 'kpt', [(g, g ^ 1 << bit) for g in range(count)])  25.9 us
    ppermute x6, starting transfers between devices, group_swap(): return lax.ppermute(block, 'kpt', [(g, g ^ 1 << bit) for g in range(count)])  6.24 us
    ppermute x2, starting transfers between devices, far_swap(): lax.ppermute(block, 'occ', [(i, (i + (1 if i % 2 else count - 1)) % count...  5.16 us
    pallas_call x1, Pallas kernels, first_terms(): pl.pallas_call(first_kernel, out_shape=jax.ShapeDtypeStruct((transfers, k...  3.47 us
    pallas_call x2, Pallas kernels, more_terms(): pl.pallas_call(body, out_shape=jax.ShapeDtypeStruct(total.shape, F32), in...  3.33 us
    pallas_call x1, Pallas kernels, last_terms(): pl.pallas_call(last_kernel, out_shape=jax.ShapeDtypeStruct(factor.shape,...  2.51 us
    pallas_call x1, Pallas kernels, pack(): pl.pallas_call(functools.partial(pack_kernel, bits), out_shape=[jax.Shape...  2.28 us
    pallas_call x1, Pallas kernels, inverses(): pl.pallas_call(functools.partial(inverse_kernel, bits), out_shape=[jax.Sh...  1.6 us
  transfers between devices with their start and end apart: 11, of which 8 were waited for; matrix products, arithmetic and copies ran while one was open for 2% of the time, Pallas kernels for 20%

profile of v12, /device:TPU:0, one launch (start us, length us, event | category | flops | bytes accessed | tf_op | source)
XLA Modules:
  0.0 54.5 jit_solution(15242106764986283985)
XLA Ops:
  0.0 1.2 %shard_map.56 = bf16[2,2,2,128,512]{4,3,2,1,0:T(8,128)(2,1)S(1)} custom-call(bf16[2,2,1,2,256,512]{5,4,3,2,1,0:T(8,128)(2,1)} %factor.11), custom_call_target="tpu_custom_call" | custom-call | tf_op jit(solution)/shard_map/pallas_call | solution.py:60
  1.2 4.6 %collective-permute-start.3 = (bf16[4,2,128,512]{3,2,1,0:T(8,128)(2,1)S(1)}, bf16[4,2,128,512]{3,2,1,0:T(8,128)(2,1)S(1)}, u32[]{:S(2)}, u32[]{:S(2)}) collective-permute-start(bf16[4,2,128,512]{3,2,1,0:T(8,128)(2,1)S(1)} %bitcast.1), channel_id=1, source_target_pairs={{0,7},{1,2},{2,1},{3,4},{4,3},{5,6},{6,5},{7,0},{8,15},{9,10},{10,... | collective-permute-start | bytes 3145736 | tf_op jit(solution)/shard_map/ppermute | solution.py:33
  5.8 2.3 %shard_map.57 = (bf16[2,2,128,512]{3,2,1,0:T(8,128)(2,1)S(1)}, bf16[2,2,128,512]{3,2,1,0:T(8,128)(2,1)S(1)}, bf16[2,2,128,512]{3,2,1,0:T(8,128)(2,1)S(1)}, bf16[2,2,128,512]{3,2,1,0:T(8,128)(2,1)S(1)}) custom-call(s32[2,8]{1,0:T(2,128)} %partner.2, bf16[2,2,1,2,256,512]{5,4,3,2,1,0:T(8,128)(2,1)} %factor.11), custom_call_target="tpu_custom_call" | custom-call | bytes 16777216 | tf_op jit(solution)/shard_map/pallas_call | solution.py:92
  8.1 1.6 %collective-permute-start = (bf16[2,2,128,512]{3,2,1,0:T(8,128)(2,1)S(1)}, bf16[2,2,128,512]{3,2,1,0:T(8,128)(2,1)S(1)}, u32[]{:S(2)}, u32[]{:S(2)}) collective-permute-start(bf16[2,2,128,512]{3,2,1,0:T(8,128)(2,1)S(1)} %get-tuple-element.15), channel_id=1, source_target_pairs={{0,8},{8,0},{16,24},{24,16},{1,9},{9,1},{17,25},{25,17},{2,10},{10... | collective-permute-start | bytes 1572872 | tf_op jit(solution)/shard_map/ppermute | solution.py:23
  9.6 1.5 %collective-permute-start.1 = (bf16[2,2,128,512]{3,2,1,0:T(8,128)(2,1)S(1)}, bf16[2,2,128,512]{3,2,1,0:T(8,128)(2,1)S(1)}, u32[]{:S(2)}, u32[]{:S(2)}) collective-permute-start(bf16[2,2,128,512]{3,2,1,0:T(8,128)(2,1)S(1)} %get-tuple-element.16), channel_id=1, source_target_pairs={{0,16},{8,24},{16,0},{24,8},{1,17},{9,25},{17,1},{25,9},{2,18},{10... | collective-permute-start | bytes 1572872 | tf_op jit(solution)/shard_map/ppermute | solution.py:23
  11.2 0.5 collective-permute-start.7
  11.7 0.5 collective-permute-start.8
  12.2 10.8 %collective-permute-done.refs_2_ = bf16[2,2,128,512]{3,2,1,0:T(8,128)(2,1)S(1)} collective-permute-done((bf16[2,2,128,512]{3,2,1,0:T(8,128)(2,1)S(1)}, bf16[2,2,128,512]{3,2,1,0:T(8,128)(2,1)S(1)}, u32[]{:S(2)}, u32[]{:S(2)}) %collective-permute-start) | collective-permute-done | bytes 524320 | tf_op jit(solution)/shard_map/ppermute | solution.py:23
  23.0 1.4 %collective-permute-done.1.refs_3_ = bf16[2,2,128,512]{3,2,1,0:T(8,128)(2,1)S(1)} collective-permute-done((bf16[2,2,128,512]{3,2,1,0:T(8,128)(2,1)S(1)}, bf16[2,2,128,512]{3,2,1,0:T(8,128)(2,1)S(1)}, u32[]{:S(2)}, u32[]{:S(2)}) %collective-permute-start.1) | collective-permute-done | bytes 524320 | tf_op jit(solution)/shard_map/ppermute | solution.py:23
  24.5 0.0 copy-start.3
  24.5 0.0 copy-start.4
  24.6 0.0 copy-start.1
  24.6 0.0 copy-start.2
  24.6 0.1 collective-permute-start.6
  24.7 0.6 %collective-permute-start.2 = (bf16[4,2,128,512]{3,2,1,0:T(8,128)(2,1)S(1)}, bf16[4,2,128,512]{3,2,1,0:T(8,128)(2,1)S(1)}, u32[]{:S(2)}, u32[]{:S(2)}) collective-permute-start(bf16[4,2,128,512]{3,2,1,0:T(8,128)(2,1)S(1)} %constant_dynamic-update-slice_fusion), channel_id=1, source_target_pairs={{0,7},{1,2},{2,1},{3,4},{4,3},{5,6},{6,5},{7,0},{8,15},{9,10},{10,... | collective-permute-start | bytes 3145736 | tf_op jit(solution)/shard_map/ppermute | solution.py:33
  25.3 6.6 %collective-permute-done.7.refs_0_ = bf16[2,2,128,512]{3,2,1,0:T(8,128)(2,1)S(1)} collective-permute-done((bf16[2,2,128,512]{3,2,1,0:T(8,128)(2,1)S(1)}, bf16[2,2,128,512]{3,2,1,0:T(8,128)(2,1)S(1)}, u32[]{:S(2)}, u32[]{:S(2)}) %collective-permute-start.7) | collective-permute-done | bytes 524320 | tf_op jit(solution)/shard_map/ppermute | solution.py:23
  31.9 1.2 %collective-permute-done.8.refs_1_ = bf16[2,2,128,512]{3,2,1,0:T(8,128)(2,1)S(1)} collective-permute-done((bf16[2,2,128,512]{3,2,1,0:T(8,128)(2,1)S(1)}, bf16[2,2,128,512]{3,2,1,0:T(8,128)(2,1)S(1)}, u32[]{:S(2)}, u32[]{:S(2)}) %collective-permute-start.8) | collective-permute-done | bytes 524320 | tf_op jit(solution)/shard_map/ppermute | solution.py:23
  33.1 0.1 pad_maximum_fusion.1
  33.1 0.0 collective-permute-done.3
  33.2 0.1 collective-permute-start.9
  33.3 0.0 copy-start
  33.3 0.6 %collective-permute-start.10 = (bf16[1,2,128,512]{3,2,1,0:T(8,128)(2,1)S(1)}, bf16[1,2,128,512]{3,2,1,0:T(8,128)(2,1)S(1)}, u32[]{:S(2)}, u32[]{:S(2)}) collective-permute-start(bf16[1,2,128,512]{3,2,1,0:T(8,128)(2,1)S(1)} %slice.18), channel_id=1, source_target_pairs={{0,1},{1,0},{2,3},{3,2},{4,5},{5,4},{6,7},{7,6},{8,9},{9,8},{10,11... | collective-permute-start | bytes 786440 | tf_op jit(solution)/shard_map/ppermute | solution.py:28
  33.8 0.1 fusion
  33.9 1.6 %collective-permute-start.5 = (bf16[2,2,128,512]{3,2,1,0:T(8,128)(2,1)S(1)}, bf16[2,2,128,512]{3,2,1,0:T(8,128)(2,1)S(1)}, u32[]{:S(2)}, u32[]{:S(2)}) collective-permute-start(bf16[2,2,128,512]{3,2,1,0:T(8,128)(2,1)S(1)} %get-tuple-element.21), channel_id=1, source_target_pairs={{0,16},{8,24},{16,0},{24,8},{1,17},{9,25},{17,1},{25,9},{2,18},{10... | collective-permute-start | bytes 1572872 | tf_op jit(solution)/shard_map/ppermute | solution.py:23
  35.5 0.4 collective-permute-done.10
  35.9 0.5 collective-permute-start.4
  36.4 0.0 copy-done.3
  36.4 0.0 copy-done.4
  36.4 0.8 %select_reduce_fusion.virtual = f32[8,256]{1,0:T(8,128)S(1)} fusion(f32[8,256]{1,0:T(8,128)S(1)} %copy-done.3, s32[8,256]{1,0:T(8,128)S(1)} %copy-done.4), kind=kLoop, calls=%fused_computation | loop fusion | flops 1570816 | bytes 24576 | tf_op jit(solution)/shard_map/reduce_sum | solution.py:45
  37.2 0.0 copy-done.1
  37.2 0.0 copy-done.2
  37.2 1.6 %shard_map.55 = (f32[2,3,2,256,256]{4,3,2,1,0:T(8,128)S(1)}, bf16[2,2,2,16,512]{4,3,2,1,0:T(8,128)(2,1)S(1)}) custom-call(s32[2,8]{1,0:T(2,128)S(1)} %copy-done.1, f32[8,8]{1,0:T(8,128)S(1)} %copy-done.2, f32[8,256]{1,0:T(8,128)S(1)} %select_reduce_fusion.virtual), custom_call_target="tpu_custom_call" | custom-call | tf_op jit(solution)/shard_map/pallas_call | solution.py:133
  38.8 0.0 collective-permute-done.9
  38.8 0.1 pad_maximum_fusion.refs_4_
  38.9 0.0 copy-done
  38.9 3.5 %shard_map.58.total = f32[2,2,2,256,512]{4,3,2,1,0:T(8,128)S(1)} custom-call(bf16[2,2,1,2,256,512]{5,4,3,2,1,0:T(8,128)(2,1)S(1)} %copy-done, f32[2,3,2,256,256]{4,3,2,1,0:T(8,128)S(1)} %get-tuple-element.13.inverse, bf16[2,2,128,512]{3,2,1,0:T(8,128)(2,1)S(1)} %collective-permute-done.7.refs_0_, ...), custom_call_target="tpu_custom_call" | custom-call | tf_op jit(solution)/shard_map/pallas_call | solution.py:203
  42.4 0.0 collective-permute-done.6.near
  42.4 1.6 %shard_map.59.refs_2_ = f32[2,2,2,256,512]{4,3,2,1,0:T(8,128)S(1)} custom-call(bf16[2,2,1,2,256,512]{5,4,3,2,1,0:T(8,128)(2,1)S(1)} %copy-done, f32[2,3,2,256,256]{4,3,2,1,0:T(8,128)S(1)} %get-tuple-element.13.inverse, bf16[4,2,128,512]{3,2,1,0:T(8,128)(2,1)S(1)} %collective-permute-done.6.near, ...), custom_call_target="tpu_custom_call", output_to_operand_aliasing={{}: (3, {})} | custom-call | tf_op jit(solution)/shard_map/pallas_call | solution.py:242
  44.0 3.8 %collective-permute-done.5.refs_1_ = bf16[2,2,128,512]{3,2,1,0:T(8,128)(2,1)S(1)} collective-permute-done((bf16[2,2,128,512]{3,2,1,0:T(8,128)(2,1)S(1)}, bf16[2,2,128,512]{3,2,1,0:T(8,128)(2,1)S(1)}, u32[]{:S(2)}, u32[]{:S(2)}) %collective-permute-start.5) | collective-permute-done | bytes 524320 | tf_op jit(solution)/shard_map/ppermute | solution.py:23
  47.8 2.0 %collective-permute-done.4.refs_0_ = bf16[2,2,128,512]{3,2,1,0:T(8,128)(2,1)S(1)} collective-permute-done((bf16[2,2,128,512]{3,2,1,0:T(8,128)(2,1)S(1)}, bf16[2,2,128,512]{3,2,1,0:T(8,128)(2,1)S(1)}, u32[]{:S(2)}, u32[]{:S(2)}) %collective-permute-start.4) | collective-permute-done | bytes 524320 | tf_op jit(solution)/shard_map/ppermute | solution.py:23
  49.8 1.7 %shard_map.60.total = f32[2,2,2,256,512]{4,3,2,1,0:T(8,128)S(1)} custom-call(bf16[2,2,1,2,256,512]{5,4,3,2,1,0:T(8,128)(2,1)S(1)} %copy-done, f32[2,3,2,256,256]{4,3,2,1,0:T(8,128)S(1)} %get-tuple-element.13.inverse, bf16[2,2,2,16,512]{4,3,2,1,0:T(8,128)(2,1)S(1)} %get-tuple-element.17.choice, ...), custom_call_target="tpu_custom_call", output_to_operand_aliasing={{}: (5, {})} | custom-call | tf_op jit(solution)/shard_map/pallas_call | solution.py:242
  51.6 0.4 collective-permute-done.2.window
  52.0 2.5 %shard_map.61 = bf16[2,2,1,2,256,512]{5,4,3,2,1,0:T(8,128)(2,1)} custom-call(bf16[2,2,1,2,256,512]{5,4,3,2,1,0:T(8,128)(2,1)S(1)} %copy-done, f32[2,3,2,256,256]{4,3,2,1,0:T(8,128)S(1)} %get-tuple-element.13.inverse, bf16[4,2,128,512]{3,2,1,0:T(8,128)(2,1)S(1)} %collective-permute-done.2.window, f32[2,2,2,256,512]{4,3,2,1,0:T(8,128)S(1)} %shard_map.60.total), custom_call_target="tpu_custom_call" | custom-call | tf_op jit(solution)/shard_map/pallas_call | solution.py:280
  (3 shorter events, 0.1 us)
Async XLA Ops:
  1.2 31.9 %collective-permute-start.3 = (bf16[4,2,128,512]{3,2,1,0:T(8,128)(2,1)S(1)}, bf16[4,2,128,512]{3,2,1,0:T(8,128)(2,1)S(1)}, u32[]{:S(2)}, u32[]{:S(2)}) collective-permute-start(bf16[4,2,128,512]{3,2,1,0:T(8,128)(2,1)S(1)} %bitcast.1), channel_id=1, source_target_pairs={{0,7},{1,2},{2,1},{3,4},{4,3},{5,6},{6,5},{7,0},{8,15},{9,10},{10,... | collective-permute-start | bytes 3145736 | tf_op jit(solution)/shard_map/ppermute | solution.py:33
  8.1 14.9 %collective-permute-start = (bf16[2,2,128,512]{3,2,1,0:T(8,128)(2,1)S(1)}, bf16[2,2,128,512]{3,2,1,0:T(8,128)(2,1)S(1)}, u32[]{:S(2)}, u32[]{:S(2)}) collective-permute-start(bf16[2,2,128,512]{3,2,1,0:T(8,128)(2,1)S(1)} %get-tuple-element.15), channel_id=1, source_target_pairs={{0,8},{8,0},{16,24},{24,16},{1,9},{9,1},{17,25},{25,17},{2,10},{10... | collective-permute-start | bytes 1572872 | tf_op jit(solution)/shard_map/ppermute | solution.py:23
  9.6 14.9 %collective-permute-start.1 = (bf16[2,2,128,512]{3,2,1,0:T(8,128)(2,1)S(1)}, bf16[2,2,128,512]{3,2,1,0:T(8,128)(2,1)S(1)}, u32[]{:S(2)}, u32[]{:S(2)}) collective-permute-start(bf16[2,2,128,512]{3,2,1,0:T(8,128)(2,1)S(1)} %get-tuple-element.16), channel_id=1, source_target_pairs={{0,16},{8,24},{16,0},{24,8},{1,17},{9,25},{17,1},{25,9},{2,18},{10... | collective-permute-start | bytes 1572872 | tf_op jit(solution)/shard_map/ppermute | solution.py:23
  11.2 20.7 %collective-permute-start.7 = (bf16[2,2,128,512]{3,2,1,0:T(8,128)(2,1)S(1)}, bf16[2,2,128,512]{3,2,1,0:T(8,128)(2,1)S(1)}, u32[]{:S(2)}, u32[]{:S(2)}) collective-permute-start(bf16[2,2,128,512]{3,2,1,0:T(8,128)(2,1)S(1)} %get-tuple-element.18), channel_id=1, source_target_pairs={{0,8},{8,0},{16,24},{24,16},{1,9},{9,1},{17,25},{25,17},{2,10},{10... | collective-permute-start | bytes 1572872 | tf_op jit(solution)/shard_map/ppermute | solution.py:23
  11.7 21.4 %collective-permute-start.8 = (bf16[2,2,128,512]{3,2,1,0:T(8,128)(2,1)S(1)}, bf16[2,2,128,512]{3,2,1,0:T(8,128)(2,1)S(1)}, u32[]{:S(2)}, u32[]{:S(2)}) collective-permute-start(bf16[2,2,128,512]{3,2,1,0:T(8,128)(2,1)S(1)} %get-tuple-element.19), channel_id=1, source_target_pairs={{0,16},{8,24},{16,0},{24,8},{1,17},{9,25},{17,1},{25,9},{2,18},{10... | collective-permute-start | bytes 1572872 | tf_op jit(solution)/shard_map/ppermute | solution.py:23
  24.5 11.9 %copy-start.3 = (f32[8,256]{1,0:T(8,128)S(1)}, f32[8,256]{1,0:T(8,128)}, u32[]{:S(2)}) copy-start(f32[8,256]{1,0:T(8,128)} %param.8) | copy-start | bytes 24580
  24.5 11.9 %copy-start.4 = (s32[8,256]{1,0:T(8,128)S(1)}, s32[8,256]{1,0:T(8,128)}, u32[]{:S(2)}) copy-start(s32[8,256]{1,0:T(8,128)} %param.9) | copy-start | bytes 24580
  24.6 12.6 %copy-start.1 = (s32[2,8]{1,0:T(2,128)S(1)}, s32[2,8]{1,0:T(2,128)}, u32[]{:S(2)}) copy-start(s32[2,8]{1,0:T(2,128)} %partner.2) | copy-start | bytes 196
  24.6 12.6 %copy-start.2 = (f32[8,8]{1,0:T(8,128)S(1)}, f32[8,8]{1,0:T(8,128)}, u32[]{:S(2)}) copy-start(f32[8,8]{1,0:T(8,128)} %occ.1) | copy-start | bytes 772
  24.6 17.8 %collective-permute-start.6 = (bf16[4,2,128,512]{3,2,1,0:T(8,128)(2,1)S(1)}, bf16[4,2,128,512]{3,2,1,0:T(8,128)(2,1)S(1)}, u32[]{:S(2)}, u32[]{:S(2)}) collective-permute-start(bf16[4,2,128,512]{3,2,1,0:T(8,128)(2,1)S(1)} %constant_dynamic-update-slice_fusion), channel_id=1, source_target_pairs={{0,1},{1,0},{2,3},{3,2},{4,5},{5,4},{6,7},{7,6},{8,9},{9,8},{10,11... | collective-permute-start | bytes 3145736 | tf_op jit(solution)/shard_map/ppermute | solution.py:28
  24.7 27.3 %collective-permute-start.2 = (bf16[4,2,128,512]{3,2,1,0:T(8,128)(2,1)S(1)}, bf16[4,2,128,512]{3,2,1,0:T(8,128)(2,1)S(1)}, u32[]{:S(2)}, u32[]{:S(2)}) collective-permute-start(bf16[4,2,128,512]{3,2,1,0:T(8,128)(2,1)S(1)} %constant_dynamic-update-slice_fusion), channel_id=1, source_target_pairs={{0,7},{1,2},{2,1},{3,4},{4,3},{5,6},{6,5},{7,0},{8,15},{9,10},{10,... | collective-permute-start | bytes 3145736 | tf_op jit(solution)/shard_map/ppermute | solution.py:33
  33.2 5.7 %collective-permute-start.9 = (bf16[3,2,128,512]{3,2,1,0:T(8,128)(2,1)S(1)}, bf16[3,2,128,512]{3,2,1,0:T(8,128)(2,1)S(1)}, u32[]{:S(2)}, u32[]{:S(2)}) collective-permute-start(bf16[3,2,128,512]{3,2,1,0:T(8,128)(2,1)S(1)} %pad_maximum_fusion.1), channel_id=1, source_target_pairs={{0,1},{1,0},{2,3},{3,2},{4,5},{5,4},{6,7},{7,6},{8,9},{9,8},{10,11... | collective-permute-start | bytes 2359304 | tf_op jit(solution)/shard_map/ppermute | solution.py:28
  33.3 5.7 %copy-start = (bf16[2,2,1,2,256,512]{5,4,3,2,1,0:T(8,128)(2,1)S(1)}, bf16[2,2,1,2,256,512]{5,4,3,2,1,0:T(8,128)(2,1)}, u32[]{:S(2)}) copy-start(bf16[2,2,1,2,256,512]{5,4,3,2,1,0:T(8,128)(2,1)} %factor.11) | copy-start | bytes 6291460
  33.3 2.6 %collective-permute-start.10 = (bf16[1,2,128,512]{3,2,1,0:T(8,128)(2,1)S(1)}, bf16[1,2,128,512]{3,2,1,0:T(8,128)(2,1)S(1)}, u32[]{:S(2)}, u32[]{:S(2)}) collective-permute-start(bf16[1,2,128,512]{3,2,1,0:T(8,128)(2,1)S(1)} %slice.18), channel_id=1, source_target_pairs={{0,1},{1,0},{2,3},{3,2},{4,5},{5,4},{6,7},{7,6},{8,9},{9,8},{10,11... | collective-permute-start | bytes 786440 | tf_op jit(solution)/shard_map/ppermute | solution.py:28
  33.9 13.9 %collective-permute-start.5 = (bf16[2,2,128,512]{3,2,1,0:T(8,128)(2,1)S(1)}, bf16[2,2,128,512]{3,2,1,0:T(8,128)(2,1)S(1)}, u32[]{:S(2)}, u32[]{:S(2)}) collective-permute-start(bf16[2,2,128,512]{3,2,1,0:T(8,128)(2,1)S(1)} %get-tuple-element.21), channel_id=1, source_target_pairs={{0,16},{8,24},{16,0},{24,8},{1,17},{9,25},{17,1},{25,9},{2,18},{10... | collective-permute-start | bytes 1572872 | tf_op jit(solution)/shard_map/ppermute | solution.py:23
  35.9 14.0 %collective-permute-start.4 = (bf16[2,2,128,512]{3,2,1,0:T(8,128)(2,1)S(1)}, bf16[2,2,128,512]{3,2,1,0:T(8,128)(2,1)S(1)}, u32[]{:S(2)}, u32[]{:S(2)}) collective-permute-start(bf16[2,2,128,512]{3,2,1,0:T(8,128)(2,1)S(1)} %get-tuple-element.22), channel_id=1, source_target_pairs={{0,8},{8,0},{16,24},{24,16},{1,9},{9,1},{17,25},{25,17},{2,10},{10... | collective-permute-start | bytes 1572872 | tf_op jit(solution)/shard_map/ppermute | solution.py:23

commit v13 on v9

--- a/solution.py
+++ b/solution.py
@@ -172,7 +172,8 @@
         ready, waiting = waiting, None
         if point is not None:
             t, k = point
-            waiting = (t, k, *amplitude_rows(factor[t, k, 0], terms_of(t, k)))
+            terms = terms_of(t, k)
+            waiting = (t, k, *amplitude_rows(factor[t, k, 0], terms)) if terms else None
         if ready is not None:
             t, k, rows, blocks = ready
             for part in range(2):
@@ -192,7 +193,7 @@
         return [
             (owns[t][k], inverse[t, 0, k, :, first]),
             (owns[transfers + t][k], inverse[t, 0, k, :, second]),
-            (near[t * kc + k], inverse[t, 1, k, :, first]),
+            (near[t * kc + k], inverse[t, 1, k, :, second]),
         ]
 
     def finish(t, k, part, value):
@@ -214,11 +215,13 @@
     )(*operands)
 
 
-def near_kernel(factor, inverse, near, total, out):
-    kc, half = factor.shape[1], near.shape[2]
+def add_kernel(place, h, factor, inverse, window, total, out):
+    kc, half = factor.shape[1], window.shape[2]
 
     def terms_of(t, k):
-        return [(near[t * kc + k], inverse[t, 1, k, :, half_of(1, half)])]
+        at = t * kc + k
+        known = at < window.shape[0]
+        return [(window[at], inverse[t, place, k, :, half_of(h, half)])] if known else []
 
     def finish(t, k, part, value):
         out[t, k, part] = value + total[t, k, part]
@@ -226,67 +229,113 @@
     contract(factor, terms_of, finish)
 
 
-def far_kernel(factor, inverse, choice, *refs):
-    fars, total, out = refs[:-2], refs[-2], refs[-1]
+def add_terms(place, h, factor, inverse, window, total, cost):
+    return pl.pallas_call(
+        functools.partial(add_kernel, place, h),
+        out_shape=jax.ShapeDtypeStruct(total.shape, F32),
+        in_specs=[VMEM] * 4,
+        out_specs=VMEM,
+        input_output_aliases={3: 0},
+        cost_estimate=cost,
+        compiler_params=PARAMS,
+    )(factor, inverse, window, total)
+
+
+def far_kernel(done, factor, inverse, choice, *refs):
+    fars, (total, kept, out, staged, sems) = refs[:-5], refs[-5:]
     kc, half = factor.shape[1], fars[0].shape[2]
+    copies = []
 
     def terms_of(t, k):
         blocks = [fars[t][c].reshape(-1, *choice.shape[3:]) for c in range(kc)]
         chosen = [block * choice[t, k, c][None] for c, block in enumerate(blocks)]
-        window = functools.reduce(jnp.add, chosen)
-        return [(window.reshape(fars[t].shape[1:]), inverse[t, 2, k, :, half_of(0, half)])]
+        window = functools.reduce(jnp.add, chosen).reshape(fars[t].shape[1:])
+        return [(window, inverse[t, 2, k, :, half_of(0, half)])]
 
     def finish(t, k, part, value):
-        out[t, k, part] = value + total[t, k, part]
-
-    contract(factor, terms_of, finish)
-
-
-def more_terms(body, operands, total):
-    return pl.pallas_call(
-        body,
-        out_shape=jax.ShapeDtypeStruct(total.shape, F32),
-        in_specs=[VMEM] * (len(operands) + 1),
-        out_specs=VMEM,
-        input_output_aliases={len(operands): 0},
-        cost_estimate=COST,
-        compiler_params=PARAMS,
-    )(*operands, total)
-
-
-def last_kernel(factor, inverse, window, total, out, staged, sems):
-    kc, half = factor.shape[1], window.shape[2]
-    copies = []
-
-    def terms_of(t, k):
-        return [(window[t * kc + k], inverse[t, 2, k, :, half_of(1, half)])]
-
-    def finish(t, k, part, value):
-        at = len(copies)
-        staged[at] = (value + total[t, k, part]).astype(BF16)
-        copies.append(pltpu.make_async_copy(staged.at[at], out.at[t, k, 0, part], sems.at[at]))
-        copies[-1].start()
+        value = value + total[t, k, part]
+        if t * kc + k < done:
+            send_part(copies, value, out.at[t, k, 0, part], staged, sems)
+        else:
+            kept[t, k, part] = value
 
     contract(factor, terms_of, finish)
     for copy in copies:
         copy.wait()
 
 
-def last_terms(factor, inverse, window, total):
+def send_part(copies, value, target, staged, sems):
+    at = len(copies)
+    staged[at] = value.astype(BF16)
+    copies.append(pltpu.make_async_copy(staged.at[at], target, sems.at[at]))
+    copies[-1].start()
+
+
+def out_scratch(count, nv, naux):
+    return [pltpu.VMEM((count, nv, naux), BF16), pltpu.SemaphoreType.DMA((count,))]
+
+
+def far_terms(done, factor, inverse, choice, fars, total):
+    _, _, _, parts, nv, naux = factor.shape
+    operands = [factor, inverse, choice, *fars, total]
+    return pl.pallas_call(
+        functools.partial(far_kernel, done),
+        out_shape=[
+            jax.ShapeDtypeStruct(total.shape, F32),
+            jax.ShapeDtypeStruct(factor.shape, BF16),
+        ],
+        in_specs=[VMEM] * len(operands),
+        out_specs=[VMEM, ANY],
+        scratch_shapes=out_scratch(done * parts, nv, naux),
+        input_output_aliases={len(operands) - 1: 0},
+        cost_estimate=COST,
+        compiler_params=PARAMS,
+    )(*operands)
+
+
+def last_kernel(done, factor, inverse, window, total, _, out, staged, sems):
+    kc, half = factor.shape[1], window.shape[2]
+    copies = []
+
+    def terms_of(t, k):
+        at = t * kc + k - done
+        return [(window[at], inverse[t, 2, k, :, half_of(1, half)])] if at >= 0 else []
+
+    def finish(t, k, part, value):
+        value = value + total[t, k, part]
+        send_part(copies, value, out.at[t, k, 0, part], staged, sems)
+
+    contract(factor, terms_of, finish)
+    for copy in copies:
+        copy.wait()
+
+
+def last_terms(done, factor, inverse, window, total, result):
     transfers, kc, _, parts, nv, naux = factor.shape
-    count = transfers * kc * parts
-    return pl.pallas_call(
-        last_kernel,
+    return pl.pallas_call(
+        functools.partial(last_kernel, done),
         out_shape=jax.ShapeDtypeStruct(factor.shape, BF16),
-        in_specs=[VMEM] * 4,
+        in_specs=[VMEM] * 4 + [ANY],
         out_specs=ANY,
-        scratch_shapes=[
-            pltpu.VMEM((count, nv, naux), BF16),
-            pltpu.SemaphoreType.DMA((count,)),
-        ],
-        cost_estimate=COST,
-        compiler_params=PARAMS,
-    )(factor, inverse, window, total)
+        scratch_shapes=out_scratch((transfers * kc - done) * parts, nv, naux),
+        input_output_aliases={4: 0},
+        cost_estimate=COST,
+        compiler_params=PARAMS,
+    )(factor, inverse, window, total, result)
+
+
+def last_rows(block, count, work):
+    def copy_kernel(source, out):
+        out[...] = source[source.shape[0] - count :]
+
+    return pl.pallas_call(
+        copy_kernel,
+        out_shape=jax.ShapeDtypeStruct((count, *block.shape[1:]), block.dtype),
+        in_specs=[VMEM],
+        out_specs=VMEM,
+        cost_estimate=pl.CostEstimate(flops=work, bytes_accessed=0, transcendentals=0),
+        compiler_params=PARAMS,
+    )(block)
 
 
 def body(factor, partner, occ_energy, vir_sorted, vir_order):
@@ -297,23 +346,26 @@
     beside = far_swap(part)
     packs = pack(bits, after(partner, part), factor, WORK * factor.size)
     earlies, lates = packs[:transfers], packs[transfers:]
+    virtual = virtual_energies(vir_sorted, vir_order)
+    inverse, choice = inverses(bits, partner, occ_energy, virtual, kc, factor.shape[5])
     late_own = [group_swap(lates[t], bits[t]) for t in range(transfers)]
-    early_own = [group_swap(earlies[t], bits[t]) for t in range(transfers)]
+    early_own = [group_swap(after(earlies[t], choice), bits[t]) for t in range(transfers)]
     late_block = jnp.concatenate(late_own)
-    late_far = far_swap(late_block)
-    late_near = near_swap(late_block)
+    done = late_block.shape[0] - 1
+    late_far, last_far = far_swap(late_block[:done]), far_swap(after(late_block[done:], beside))
+    late_near = jnp.concatenate([near_swap(late_block[:3]), near_swap(last_rows(late_block, 1, 6000 * factor.size))])
     early_block = jnp.concatenate(early_own)
     early_near = jnp.concatenate(
-        [near_swap(after(early_block[:-1], beside)), near_swap(early_block[-1:])]
+        [near_swap(after(early_block[:2], beside)), near_swap(after(early_block[2:], beside))]
     )
     early_far = [group_swap(beside[t * kc : (t + 1) * kc], bits[t]) for t in range(transfers)]
 
-    virtual = virtual_energies(vir_sorted, vir_order)
-    inverse, choice = inverses(bits, partner, occ_energy, virtual, kc, factor.shape[5])
-    total = first_terms(factor, inverse, early_own + late_own, early_near)
-    total = more_terms(near_kernel, [factor, inverse, late_near], total)
-    total = more_terms(far_kernel, [factor, inverse, choice, *early_far], total)
-    return last_terms(factor, inverse, late_far, total)
+    total = first_terms(factor, inverse, early_own + late_own, late_near)
+    total = add_terms(1, 0, factor, inverse, early_near, total, COST)
+    weight = pl.CostEstimate(flops=3 * 1000 * factor.size, bytes_accessed=0, transcendentals=0)
+    total = add_terms(2, 1, factor, inverse, late_far, total, weight)
+    total, result = far_terms(done, factor, inverse, choice, early_far, total)
+    return last_terms(done, factor, inverse, last_far, total, result)
 
 
 def solution(mesh):

time: 54.4 us -> 54.4 us (level)
  waiting for transfers between devices: 26.5 us -> 23.7 us
  starting transfers between devices: 12.2 us -> 14 us
  Pallas kernels: 14.2 us -> 15.1 us
    ppermute x6, waiting for transfers between devices: 25.7 us -> 20.4 us  [group_swap(): return lax.ppermute(block, 'kpt', [(g, g ^ 1 << bit) for g in range(count)])]
    ppermute x2 -> x3, starting transfers between devices: 5.16 us -> 6.64 us  [far_swap(): lax.ppermute(block, 'occ', [(i, (i + (1 if i % 2 else count - 1)) % count...]
    ppermute x2 -> x3, waiting for transfers between devices: 0.42 us -> 1.71 us  [far_swap(): lax.ppermute(block, 'occ', [(i, (i + (1 if i % 2 else count - 1)) % count...]
    ppermute x3 -> x4, waiting for transfers between devices: 0.4 us -> 1.59 us  [near_swap(): return lax.ppermute(block, 'occ', [(i, i ^ 1) for i in range(count)])]
    pallas_call x3 -> x5, Pallas kernels: 5.56 us -> 6.52 us  [the longest x2 2.92 us: add_terms(): pl.pallas_call(functools.partial(add_kernel, place, h), out_shape=jax.Sha...]
  transfers between devices with their start and end apart: 11 -> 13, of which waited for: 8 -> 8; matrix products, arithmetic and copies ran while one was open for 2% -> 2% of each run, Pallas kernels for 20% -> 23%
where the time goes in v13:
time: 54.4 us; the launch traced here: 54.2 us
  waiting for transfers between devices  23.7 us (44%)
  Pallas kernels  15.1 us (28%)
  starting transfers between devices  14 us (26%)
  other arithmetic  0.94 us (2%)
    ppermute x6, waiting for transfers between devices, group_swap(): return lax.ppermute(block, 'kpt', [(g, g ^ 1 << bit) for g in range(count)])  20.4 us
    ppermute x6, starting transfers between devices, group_swap(): return lax.ppermute(block, 'kpt', [(g, g ^ 1 << bit) for g in range(count)])  6.74 us
    ppermute x3, starting transfers between devices, far_swap(): lax.ppermute(block, 'occ', [(i, (i + (1 if i % 2 else count - 1)) % count...  6.64 us
    pallas_call x1, Pallas kernels, first_terms(): pl.pallas_call(first_kernel, out_shape=jax.ShapeDtypeStruct((transfers, k...  3.48 us
    pallas_call x2, Pallas kernels, add_terms(): pl.pallas_call(functools.partial(add_kernel, place, h), out_shape=jax.Sha...  2.92 us
    pallas_call x1, Pallas kernels, pack(): pl.pallas_call(functools.partial(pack_kernel, bits), out_shape=[jax.Shape...  2.28 us
    pallas_call x1, Pallas kernels, far_terms(): pl.pallas_call(functools.partial(far_kernel, done), out_shape=[jax.ShapeD...  2.07 us
    ppermute x3, waiting for transfers between devices, far_swap(): lax.ppermute(block, 'occ', [(i, (i + (1 if i % 2 else count - 1)) % count...  1.71 us
  transfers between devices with their start and end apart: 13, of which 8 were waited for; matrix products, arithmetic and copies ran while one was open for 2% of the time, Pallas kernels for 23%

profile of v13, /device:TPU:0, one launch (start us, length us, event | category | flops | bytes accessed | tf_op | source)
XLA Modules:
  0.0 54.2 jit_solution(5287365770029495390)
XLA Ops:
  0.0 0.0 copy-start.1
  0.0 0.0 copy-start.4
  0.0 0.0 copy-start.3
  0.0 1.3 %shard_map.56 = bf16[4,2,128,512]{3,2,1,0:T(8,128)(2,1)S(1)} custom-call(bf16[2,2,1,2,256,512]{5,4,3,2,1,0:T(8,128)(2,1)} %factor.13), custom_call_target="tpu_custom_call" | custom-call | tf_op jit(solution)/shard_map/pallas_call | solution.py:65
  1.3 4.5 %collective-permute-start.1 = (bf16[4,2,128,512]{3,2,1,0:T(8,128)(2,1)S(1)}, bf16[4,2,128,512]{3,2,1,0:T(8,128)(2,1)S(1)}, u32[]{:S(2)}, u32[]{:S(2)}) collective-permute-start(bf16[4,2,128,512]{3,2,1,0:T(8,128)(2,1)S(1)} %shard_map.56), channel_id=1, source_target_pairs={{0,7},{1,2},{2,1},{3,4},{4,3},{5,6},{6,5},{7,0},{8,15},{9,10},{10,... | collective-permute-start | bytes 3145736 | tf_op jit(solution)/shard_map/ppermute | solution.py:33
  5.8 2.3 %shard_map.57 = (bf16[2,2,128,512]{3,2,1,0:T(8,128)(2,1)S(1)}, bf16[2,2,128,512]{3,2,1,0:T(8,128)(2,1)S(1)}, bf16[2,2,128,512]{3,2,1,0:T(8,128)(2,1)S(1)}, bf16[2,2,128,512]{3,2,1,0:T(8,128)(2,1)S(1)}) custom-call(s32[2,8]{1,0:T(2,128)} %partner.2, bf16[2,2,1,2,256,512]{5,4,3,2,1,0:T(8,128)(2,1)} %factor.13), custom_call_target="tpu_custom_call" | custom-call | bytes 16777216 | tf_op jit(solution)/shard_map/pallas_call | solution.py:96
  8.1 1.6 %collective-permute-start.5 = (bf16[2,2,128,512]{3,2,1,0:T(8,128)(2,1)S(1)}, bf16[2,2,128,512]{3,2,1,0:T(8,128)(2,1)S(1)}, u32[]{:S(2)}, u32[]{:S(2)}) collective-permute-start(bf16[2,2,128,512]{3,2,1,0:T(8,128)(2,1)S(1)} %get-tuple-element.24), channel_id=1, source_target_pairs={{0,8},{8,0},{16,24},{24,16},{1,9},{9,1},{17,25},{25,17},{2,10},{10... | collective-permute-start | bytes 1572872 | tf_op jit(solution)/shard_map/ppermute | solution.py:23
  9.7 1.5 %collective-permute-start = (bf16[2,2,128,512]{3,2,1,0:T(8,128)(2,1)S(1)}, bf16[2,2,128,512]{3,2,1,0:T(8,128)(2,1)S(1)}, u32[]{:S(2)}, u32[]{:S(2)}) collective-permute-start(bf16[2,2,128,512]{3,2,1,0:T(8,128)(2,1)S(1)} %get-tuple-element.21), channel_id=1, source_target_pairs={{0,16},{8,24},{16,0},{24,8},{1,17},{9,25},{17,1},{25,9},{2,18},{10... | collective-permute-start | bytes 1572872 | tf_op jit(solution)/shard_map/ppermute | solution.py:23
  11.2 0.0 copy-done.4
  11.2 0.0 copy-done.3
  11.2 0.8 %select_reduce_fusion.virtual = f32[8,256]{1,0:T(8,128)S(1)} fusion(f32[8,256]{1,0:T(8,128)S(1)} %copy-done.3, s32[8,256]{1,0:T(8,128)S(1)} %copy-done.4), kind=kLoop, calls=%fused_computation | loop fusion | flops 1570816 | bytes 24576 | tf_op jit(solution)/shard_map/reduce_sum | solution.py:45
  12.0 0.0 copy-done.1
  12.0 0.0 copy-done.2
  12.0 1.6 %shard_map.55 = (f32[2,3,2,256,256]{4,3,2,1,0:T(8,128)S(1)}, bf16[2,2,2,16,512]{4,3,2,1,0:T(8,128)(2,1)S(1)}) custom-call(s32[2,8]{1,0:T(2,128)S(1)} %copy-done.1, f32[8,8]{1,0:T(8,128)S(1)} %copy-done.2, f32[8,256]{1,0:T(8,128)S(1)} %select_reduce_fusion.virtual), custom_call_target="tpu_custom_call" | custom-call | tf_op jit(solution)/shard_map/pallas_call | solution.py:137
  13.6 0.6 %collective-permute-start.7 = (bf16[2,2,128,512]{3,2,1,0:T(8,128)(2,1)S(1)}, bf16[2,2,128,512]{3,2,1,0:T(8,128)(2,1)S(1)}, u32[]{:S(2)}, u32[]{:S(2)}) collective-permute-start(bf16[2,2,128,512]{3,2,1,0:T(8,128)(2,1)S(1)} %get-tuple-element.26), channel_id=1, source_target_pairs={{0,8},{8,0},{16,24},{24,16},{1,9},{9,1},{17,25},{25,17},{2,10},{10... | collective-permute-start | bytes 1572872 | tf_op jit(solution)/shard_map/ppermute | solution.py:23
  14.2 0.5 collective-permute-start.9
  14.7 8.3 %collective-permute-done.5.refs_2_ = bf16[2,2,128,512]{3,2,1,0:T(8,128)(2,1)S(1)} collective-permute-done((bf16[2,2,128,512]{3,2,1,0:T(8,128)(2,1)S(1)}, bf16[2,2,128,512]{3,2,1,0:T(8,128)(2,1)S(1)}, u32[]{:S(2)}, u32[]{:S(2)}) %collective-permute-start.5) | collective-permute-done | bytes 524320 | tf_op jit(solution)/shard_map/ppermute | solution.py:23
  23.1 1.4 %collective-permute-done.refs_3_ = bf16[2,2,128,512]{3,2,1,0:T(8,128)(2,1)S(1)} collective-permute-done((bf16[2,2,128,512]{3,2,1,0:T(8,128)(2,1)S(1)}, bf16[2,2,128,512]{3,2,1,0:T(8,128)(2,1)S(1)}, u32[]{:S(2)}, u32[]{:S(2)}) %collective-permute-start) | collective-permute-done | bytes 524320 | tf_op jit(solution)/shard_map/ppermute | solution.py:23
  24.6 0.1 slice.20
  24.7 0.1 collective-permute-start.11
  24.7 0.6 %collective-permute-start.6 = (bf16[3,2,128,512]{3,2,1,0:T(8,128)(2,1)S(1)}, bf16[3,2,128,512]{3,2,1,0:T(8,128)(2,1)S(1)}, u32[]{:S(2)}, u32[]{:S(2)}) collective-permute-start(bf16[3,2,128,512]{3,2,1,0:T(8,128)(2,1)S(1)} %slice.20), channel_id=1, source_target_pairs={{0,7},{1,2},{2,1},{3,4},{4,3},{5,6},{6,5},{7,0},{8,15},{9,10},{10,... | collective-permute-start | bytes 2359304 | tf_op jit(solution)/shard_map/ppermute | solution.py:33
  25.3 6.6 %collective-permute-done.7.refs_0_ = bf16[2,2,128,512]{3,2,1,0:T(8,128)(2,1)S(1)} collective-permute-done((bf16[2,2,128,512]{3,2,1,0:T(8,128)(2,1)S(1)}, bf16[2,2,128,512]{3,2,1,0:T(8,128)(2,1)S(1)}, u32[]{:S(2)}, u32[]{:S(2)}) %collective-permute-start.7) | collective-permute-done | bytes 524320 | tf_op jit(solution)/shard_map/ppermute | solution.py:23
  31.9 0.0 collective-permute-done.1
  31.9 0.0 collective-permute-start.8
  31.9 1.2 %collective-permute-done.9.refs_1_ = bf16[2,2,128,512]{3,2,1,0:T(8,128)(2,1)S(1)} collective-permute-done((bf16[2,2,128,512]{3,2,1,0:T(8,128)(2,1)S(1)}, bf16[2,2,128,512]{3,2,1,0:T(8,128)(2,1)S(1)}, u32[]{:S(2)}, u32[]{:S(2)}) %collective-permute-start.9) | collective-permute-done | bytes 524320 | tf_op jit(solution)/shard_map/ppermute | solution.py:23
  33.1 0.0 collective-permute-start.10
  33.1 0.6 %collective-permute-start.12 = (bf16[1,2,128,512]{3,2,1,0:T(8,128)(2,1)S(1)}, bf16[1,2,128,512]{3,2,1,0:T(8,128)(2,1)S(1)}, u32[]{:S(2)}, u32[]{:S(2)}) collective-permute-start(bf16[1,2,128,512]{3,2,1,0:T(8,128)(2,1)S(1)} %shard_map.58), channel_id=1, source_target_pairs={{0,1},{1,0},{2,3},{3,2},{4,5},{5,4},{6,7},{7,6},{8,9},{9,8},{10,11... | collective-permute-start | bytes 786440 | tf_op jit(solution)/shard_map/ppermute | solution.py:28
  33.7 0.0 copy-start
  33.7 0.1 fusion
  33.8 1.6 %collective-permute-done.12 = bf16[1,2,128,512]{3,2,1,0:T(8,128)(2,1)S(1)} collective-permute-done((bf16[1,2,128,512]{3,2,1,0:T(8,128)(2,1)S(1)}, bf16[1,2,128,512]{3,2,1,0:T(8,128)(2,1)S(1)}, u32[]{:S(2)}, u32[]{:S(2)}) %collective-permute-start.12) | collective-permute-done | bytes 262176 | tf_op jit(solution)/shard_map/ppermute | solution.py:28
  35.4 1.5 %collective-permute-start.4 = (bf16[2,2,128,512]{3,2,1,0:T(8,128)(2,1)S(1)}, bf16[2,2,128,512]{3,2,1,0:T(8,128)(2,1)S(1)}, u32[]{:S(2)}, u32[]{:S(2)}) collective-permute-start(bf16[2,2,128,512]{3,2,1,0:T(8,128)(2,1)S(1)} %get-tuple-element.33), channel_id=1, source_target_pairs={{0,16},{8,24},{16,0},{24,8},{1,17},{9,25},{17,1},{25,9},{2,18},{10... | collective-permute-start | bytes 1572872 | tf_op jit(solution)/shard_map/ppermute | solution.py:23
  36.9 0.0 collective-permute-done.11
  36.9 1.0 %collective-permute-start.3 = (bf16[2,2,128,512]{3,2,1,0:T(8,128)(2,1)S(1)}, bf16[2,2,128,512]{3,2,1,0:T(8,128)(2,1)S(1)}, u32[]{:S(2)}, u32[]{:S(2)}) collective-permute-start(bf16[2,2,128,512]{3,2,1,0:T(8,128)(2,1)S(1)} %get-tuple-element.34), channel_id=1, source_target_pairs={{0,8},{8,0},{16,24},{24,16},{1,9},{9,1},{17,25},{25,17},{2,10},{10... | collective-permute-start | bytes 1572872 | tf_op jit(solution)/shard_map/ppermute | solution.py:23
  37.9 0.1 pad_maximum_fusion.1.refs_4_
  38.0 0.0 copy-done
  38.1 3.5 %shard_map.59.total = f32[2,2,2,256,512]{4,3,2,1,0:T(8,128)S(1)} custom-call(bf16[2,2,1,2,256,512]{5,4,3,2,1,0:T(8,128)(2,1)S(1)} %copy-done, f32[2,3,2,256,256]{4,3,2,1,0:T(8,128)S(1)} %get-tuple-element.19.inverse, bf16[2,2,128,512]{3,2,1,0:T(8,128)(2,1)S(1)} %collective-permute-done.7.refs_0_, ...), custom_call_target="tpu_custom_call" | custom-call | tf_op jit(solution)/shard_map/pallas_call | solution.py:208
  41.5 0.0 collective-permute-done.8
  41.5 1.5 %collective-permute-start.2 = (bf16[1,2,128,512]{3,2,1,0:T(8,128)(2,1)S(1)}, bf16[1,2,128,512]{3,2,1,0:T(8,128)(2,1)S(1)}, u32[]{:S(2)}, u32[]{:S(2)}) collective-permute-start(bf16[1,2,128,512]{3,2,1,0:T(8,128)(2,1)S(1)} %slice.17), channel_id=1, source_target_pairs={{0,7},{1,2},{2,1},{3,4},{4,3},{5,6},{6,5},{7,0},{8,15},{9,10},{10,... | collective-permute-start | bytes 786440 | tf_op jit(solution)/shard_map/ppermute | solution.py:33
  43.0 0.0 collective-permute-done.10
  43.0 0.1 pad_maximum_fusion.window
  43.1 1.6 %shard_map.60.total = f32[2,2,2,256,512]{4,3,2,1,0:T(8,128)S(1)} custom-call(bf16[2,2,1,2,256,512]{5,4,3,2,1,0:T(8,128)(2,1)S(1)} %copy-done, f32[2,3,2,256,256]{4,3,2,1,0:T(8,128)S(1)} %get-tuple-element.19.inverse, bf16[4,2,128,512]{3,2,1,0:T(8,128)(2,1)S(1)} %pad_maximum_fusion.window, ...), custom_call_target="tpu_custom_call", output_to_operand_aliasing={{}: (3, {})} | custom-call | tf_op jit(solution)/shard_map/pallas_call | solution.py:233
  44.8 1.7 %collective-permute-done.6.window = bf16[3,2,128,512]{3,2,1,0:T(8,128)(2,1)S(1)} collective-permute-done((bf16[3,2,128,512]{3,2,1,0:T(8,128)(2,1)S(1)}, bf16[3,2,128,512]{3,2,1,0:T(8,128)(2,1)S(1)}, u32[]{:S(2)}, u32[]{:S(2)}) %collective-permute-start.6) | collective-permute-done | bytes 786464 | tf_op jit(solution)/shard_map/ppermute | solution.py:33
  46.5 1.3 %shard_map.61.refs_2_ = f32[2,2,2,256,512]{4,3,2,1,0:T(8,128)S(1)} custom-call(bf16[2,2,1,2,256,512]{5,4,3,2,1,0:T(8,128)(2,1)S(1)} %copy-done, f32[2,3,2,256,256]{4,3,2,1,0:T(8,128)S(1)} %get-tuple-element.19.inverse, bf16[3,2,128,512]{3,2,1,0:T(8,128)(2,1)S(1)} %collective-permute-done.6.window, ...), custom_call_target="tpu_custom_call", output_to_operand_aliasing={{}: (3, {})} | custom-call | flops 3145728000 | tf_op jit(solution)/shard_map/pallas_call | solution.py:233
  47.8 1.6 %collective-permute-done.4.refs_1_ = bf16[2,2,128,512]{3,2,1,0:T(8,128)(2,1)S(1)} collective-permute-done((bf16[2,2,128,512]{3,2,1,0:T(8,128)(2,1)S(1)}, bf16[2,2,128,512]{3,2,1,0:T(8,128)(2,1)S(1)}, u32[]{:S(2)}, u32[]{:S(2)}) %collective-permute-start.4) | collective-permute-done | bytes 524320 | tf_op jit(solution)/shard_map/ppermute | solution.py:23
  49.4 1.2 %collective-permute-done.3.refs_0_ = bf16[2,2,128,512]{3,2,1,0:T(8,128)(2,1)S(1)} collective-permute-done((bf16[2,2,128,512]{3,2,1,0:T(8,128)(2,1)S(1)}, bf16[2,2,128,512]{3,2,1,0:T(8,128)(2,1)S(1)}, u32[]{:S(2)}, u32[]{:S(2)}) %collective-permute-start.3) | collective-permute-done | bytes 524320 | tf_op jit(solution)/shard_map/ppermute | solution.py:23
  50.6 2.1 %shard_map.62 = (f32[2,2,2,256,512]{4,3,2,1,0:T(8,128)S(1)}, bf16[2,2,1,2,256,512]{5,4,3,2,1,0:T(8,128)(2,1)}) custom-call(bf16[2,2,1,2,256,512]{5,4,3,2,1,0:T(8,128)(2,1)S(1)} %copy-done, f32[2,3,2,256,256]{4,3,2,1,0:T(8,128)S(1)} %get-tuple-element.19.inverse, ...), custom_call_target="tpu_custom_call", output_to_operand_aliasing={{0}: (5, {})} | custom-call | tf_op jit(solution)/shard_map/pallas_call | solution.py:281
  52.7 0.0 collective-permute-done.2.window
  52.7 1.5 %shard_map.63 = bf16[2,2,1,2,256,512]{5,4,3,2,1,0:T(8,128)(2,1)} custom-call(bf16[2,2,1,2,256,512]{5,4,3,2,1,0:T(8,128)(2,1)S(1)} %copy-done, f32[2,3,2,256,256]{4,3,2,1,0:T(8,128)S(1)} %get-tuple-element.19.inverse, bf16[1,2,128,512]{3,2,1,0:T(8,128)(2,1)S(1)} %collective-permute-done.2.window, ...), custom_call_target="tpu_custom_call", output_to_operand_aliasing={{}: (4, {})} | custom-call | tf_op jit(solution)/shard_map/pallas_call | solution.py:315
  (5 shorter events, 0.1 us)
Async XLA Ops:
  0.0 12.0 %copy-start.1 = (s32[2,8]{1,0:T(2,128)S(1)}, s32[2,8]{1,0:T(2,128)}, u32[]{:S(2)}) copy-start(s32[2,8]{1,0:T(2,128)} %partner.2) | copy-start | bytes 196
  0.0 11.2 %copy-start.4 = (s32[8,256]{1,0:T(8,128)S(1)}, s32[8,256]{1,0:T(8,128)}, u32[]{:S(2)}) copy-start(s32[8,256]{1,0:T(8,128)} %param.9) | copy-start | bytes 24580
  0.0 11.2 %copy-start.3 = (f32[8,256]{1,0:T(8,128)S(1)}, f32[8,256]{1,0:T(8,128)}, u32[]{:S(2)}) copy-start(f32[8,256]{1,0:T(8,128)} %param.8) | copy-start | bytes 24580
  0.0 12.0 %copy-start.2 = (f32[8,8]{1,0:T(8,128)S(1)}, f32[8,8]{1,0:T(8,128)}, u32[]{:S(2)}) copy-start(f32[8,8]{1,0:T(8,128)} %occ.1) | copy-start | bytes 772
  1.3 30.6 %collective-permute-start.1 = (bf16[4,2,128,512]{3,2,1,0:T(8,128)(2,1)S(1)}, bf16[4,2,128,512]{3,2,1,0:T(8,128)(2,1)S(1)}, u32[]{:S(2)}, u32[]{:S(2)}) collective-permute-start(bf16[4,2,128,512]{3,2,1,0:T(8,128)(2,1)S(1)} %shard_map.56), channel_id=1, source_target_pairs={{0,7},{1,2},{2,1},{3,4},{4,3},{5,6},{6,5},{7,0},{8,15},{9,10},{10,... | collective-permute-start | bytes 3145736 | tf_op jit(solution)/shard_map/ppermute | solution.py:33
  8.1 14.9 %collective-permute-start.5 = (bf16[2,2,128,512]{3,2,1,0:T(8,128)(2,1)S(1)}, bf16[2,2,128,512]{3,2,1,0:T(8,128)(2,1)S(1)}, u32[]{:S(2)}, u32[]{:S(2)}) collective-permute-start(bf16[2,2,128,512]{3,2,1,0:T(8,128)(2,1)S(1)} %get-tuple-element.24), channel_id=1, source_target_pairs={{0,8},{8,0},{16,24},{24,16},{1,9},{9,1},{17,25},{25,17},{2,10},{10... | collective-permute-start | bytes 1572872 | tf_op jit(solution)/shard_map/ppermute | solution.py:23
  9.7 14.9 %collective-permute-start = (bf16[2,2,128,512]{3,2,1,0:T(8,128)(2,1)S(1)}, bf16[2,2,128,512]{3,2,1,0:T(8,128)(2,1)S(1)}, u32[]{:S(2)}, u32[]{:S(2)}) collective-permute-start(bf16[2,2,128,512]{3,2,1,0:T(8,128)(2,1)S(1)} %get-tuple-element.21), channel_id=1, source_target_pairs={{0,16},{8,24},{16,0},{24,8},{1,17},{9,25},{17,1},{25,9},{2,18},{10... | collective-permute-start | bytes 1572872 | tf_op jit(solution)/shard_map/ppermute | solution.py:23
  13.6 18.3 %collective-permute-start.7 = (bf16[2,2,128,512]{3,2,1,0:T(8,128)(2,1)S(1)}, bf16[2,2,128,512]{3,2,1,0:T(8,128)(2,1)S(1)}, u32[]{:S(2)}, u32[]{:S(2)}) collective-permute-start(bf16[2,2,128,512]{3,2,1,0:T(8,128)(2,1)S(1)} %get-tuple-element.26), channel_id=1, source_target_pairs={{0,8},{8,0},{16,24},{24,16},{1,9},{9,1},{17,25},{25,17},{2,10},{10... | collective-permute-start | bytes 1572872 | tf_op jit(solution)/shard_map/ppermute | solution.py:23
  14.2 18.9 %collective-permute-start.9 = (bf16[2,2,128,512]{3,2,1,0:T(8,128)(2,1)S(1)}, bf16[2,2,128,512]{3,2,1,0:T(8,128)(2,1)S(1)}, u32[]{:S(2)}, u32[]{:S(2)}) collective-permute-start(bf16[2,2,128,512]{3,2,1,0:T(8,128)(2,1)S(1)} %get-tuple-element.29), channel_id=1, source_target_pairs={{0,16},{8,24},{16,0},{24,8},{1,17},{9,25},{17,1},{25,9},{2,18},{10... | collective-permute-start | bytes 1572872 | tf_op jit(solution)/shard_map/ppermute | solution.py:23
  24.7 12.3 %collective-permute-start.11 = (bf16[3,2,128,512]{3,2,1,0:T(8,128)(2,1)S(1)}, bf16[3,2,128,512]{3,2,1,0:T(8,128)(2,1)S(1)}, u32[]{:S(2)}, u32[]{:S(2)}) collective-permute-start(bf16[3,2,128,512]{3,2,1,0:T(8,128)(2,1)S(1)} %slice.20), channel_id=1, source_target_pairs={{0,1},{1,0},{2,3},{3,2},{4,5},{5,4},{6,7},{7,6},{8,9},{9,8},{10,11... | collective-permute-start | bytes 2359304 | tf_op jit(solution)/shard_map/ppermute | solution.py:28
  24.7 21.8 %collective-permute-start.6 = (bf16[3,2,128,512]{3,2,1,0:T(8,128)(2,1)S(1)}, bf16[3,2,128,512]{3,2,1,0:T(8,128)(2,1)S(1)}, u32[]{:S(2)}, u32[]{:S(2)}) collective-permute-start(bf16[3,2,128,512]{3,2,1,0:T(8,128)(2,1)S(1)} %slice.20), channel_id=1, source_target_pairs={{0,7},{1,2},{2,1},{3,4},{4,3},{5,6},{6,5},{7,0},{8,15},{9,10},{10,... | collective-permute-start | bytes 2359304 | tf_op jit(solution)/shard_map/ppermute | solution.py:33
  31.9 9.6 %collective-permute-start.8 = (bf16[2,2,128,512]{3,2,1,0:T(8,128)(2,1)S(1)}, bf16[2,2,128,512]{3,2,1,0:T(8,128)(2,1)S(1)}, u32[]{:S(2)}, u32[]{:S(2)}) collective-permute-start(bf16[2,2,128,512]{3,2,1,0:T(8,128)(2,1)S(1)} %collective-permute-done.7.refs_0_), channel_id=1, source_target_pairs={{0,1},{1,0},{2,3},{3,2},{4,5},{5,4},{6,7},{7,6},{8,9},{9,8},{10,11... | collective-permute-start | bytes 1572872 | tf_op jit(solution)/shard_map/ppermute | solution.py:28
  33.1 9.9 %collective-permute-start.10 = (bf16[2,2,128,512]{3,2,1,0:T(8,128)(2,1)S(1)}, bf16[2,2,128,512]{3,2,1,0:T(8,128)(2,1)S(1)}, u32[]{:S(2)}, u32[]{:S(2)}) collective-permute-start(bf16[2,2,128,512]{3,2,1,0:T(8,128)(2,1)S(1)} %collective-permute-done.9.refs_1_), channel_id=1, source_target_pairs={{0,1},{1,0},{2,3},{3,2},{4,5},{5,4},{6,7},{7,6},{8,9},{9,8},{10,11... | collective-permute-start | bytes 1572872 | tf_op jit(solution)/shard_map/ppermute | solution.py:28
  33.1 2.3 %collective-permute-start.12 = (bf16[1,2,128,512]{3,2,1,0:T(8,128)(2,1)S(1)}, bf16[1,2,128,512]{3,2,1,0:T(8,128)(2,1)S(1)}, u32[]{:S(2)}, u32[]{:S(2)}) collective-permute-start(bf16[1,2,128,512]{3,2,1,0:T(8,128)(2,1)S(1)} %shard_map.58), channel_id=1, source_target_pairs={{0,1},{1,0},{2,3},{3,2},{4,5},{5,4},{6,7},{7,6},{8,9},{9,8},{10,11... | collective-permute-start | bytes 786440 | tf_op jit(solution)/shard_map/ppermute | solution.py:28
  33.7 4.3 %copy-start = (bf16[2,2,1,2,256,512]{5,4,3,2,1,0:T(8,128)(2,1)S(1)}, bf16[2,2,1,2,256,512]{5,4,3,2,1,0:T(8,128)(2,1)}, u32[]{:S(2)}) copy-start(bf16[2,2,1,2,256,512]{5,4,3,2,1,0:T(8,128)(2,1)} %factor.13) | copy-start | bytes 6291460
  35.4 14.0 %collective-permute-start.4 = (bf16[2,2,128,512]{3,2,1,0:T(8,128)(2,1)S(1)}, bf16[2,2,128,512]{3,2,1,0:T(8,128)(2,1)S(1)}, u32[]{:S(2)}, u32[]{:S(2)}) collective-permute-start(bf16[2,2,128,512]{3,2,1,0:T(8,128)(2,1)S(1)} %get-tuple-element.33), channel_id=1, source_target_pairs={{0,16},{8,24},{16,0},{24,8},{1,17},{9,25},{17,1},{25,9},{2,18},{10... | collective-permute-start | bytes 1572872 | tf_op jit(solution)/shard_map/ppermute | solution.py:23
  36.9 13.7 %collective-permute-start.3 = (bf16[2,2,128,512]{3,2,1,0:T(8,128)(2,1)S(1)}, bf16[2,2,128,512]{3,2,1,0:T(8,128)(2,1)S(1)}, u32[]{:S(2)}, u32[]{:S(2)}) collective-permute-start(bf16[2,2,128,512]{3,2,1,0:T(8,128)(2,1)S(1)} %get-tuple-element.34), channel_id=1, source_target_pairs={{0,8},{8,0},{16,24},{24,16},{1,9},{9,1},{17,25},{25,17},{2,10},{10... | collective-permute-start | bytes 1572872 | tf_op jit(solution)/shard_map/ppermute | solution.py:23
  41.5 11.1 %collective-permute-start.2 = (bf16[1,2,128,512]{3,2,1,0:T(8,128)(2,1)S(1)}, bf16[1,2,128,512]{3,2,1,0:T(8,128)(2,1)S(1)}, u32[]{:S(2)}, u32[]{:S(2)}) collective-permute-start(bf16[1,2,128,512]{3,2,1,0:T(8,128)(2,1)S(1)} %slice.17), channel_id=1, source_target_pairs={{0,7},{1,2},{2,1},{3,4},{4,3},{5,6},{6,5},{7,0},{8,15},{9,10},{10,... | collective-permute-start | bytes 786440 | tf_op jit(solution)/shard_map/ppermute | solution.py:33

commit v14 on v13

--- a/solution.py
+++ b/solution.py
@@ -353,10 +353,10 @@
     late_block = jnp.concatenate(late_own)
     done = late_block.shape[0] - 1
     late_far, last_far = far_swap(late_block[:done]), far_swap(after(late_block[done:], beside))
-    late_near = jnp.concatenate([near_swap(late_block[:3]), near_swap(last_rows(late_block, 1, 6000 * factor.size))])
+    late_near = near_swap(late_block)
     early_block = jnp.concatenate(early_own)
     early_near = jnp.concatenate(
-        [near_swap(after(early_block[:2], beside)), near_swap(after(early_block[2:], beside))]
+        [near_swap(after(early_block[:2], beside)), near_swap(last_rows(after(early_block, beside), 2, 9000 * factor.size))]
     )
     early_far = [group_swap(beside[t * kc : (t + 1) * kc], bits[t]) for t in range(transfers)]
 

time: 54.4 us -> 53.7 us (0.987)
    ppermute x3, waiting for transfers between devices: 1.71 us -> 4.5 us  [far_swap(): lax.ppermute(block, 'occ', [(i, (i + (1 if i % 2 else count - 1)) % count...]
    ppermute x4 -> x3, waiting for transfers between devices: 1.59 us -> 0.01 us  [near_swap(): return lax.ppermute(block, 'occ', [(i, i ^ 1) for i in range(count)])]
    ppermute x6, waiting for transfers between devices: 20.4 us -> 18.9 us  [group_swap(): return lax.ppermute(block, 'kpt', [(g, g ^ 1 << bit) for g in range(count)])]
  transfers between devices with their start and end apart: 13 -> 12, of which waited for: 8 -> 8; matrix products, arithmetic and copies ran while one was open for 2% -> 2% of each run, Pallas kernels for 23% -> 23%
where the time goes in v14:
time: 53.7 us; the launch traced here: 53.5 us
  waiting for transfers between devices  23.4 us (44%)
  Pallas kernels  15.2 us (28%)
  starting transfers between devices  13.5 us (25%)
  other arithmetic  0.94 us (2%)
    ppermute x6, waiting for transfers between devices, group_swap(): return lax.ppermute(block, 'kpt', [(g, g ^ 1 << bit) for g in range(count)])  18.9 us
    ppermute x3, starting transfers between devices, far_swap(): lax.ppermute(block, 'occ', [(i, (i + (1 if i % 2 else count - 1)) % count...  6.52 us
    ppermute x6, starting transfers between devices, group_swap(): return lax.ppermute(block, 'kpt', [(g, g ^ 1 << bit) for g in range(count)])  6.3 us
    ppermute x3, waiting for transfers between devices, far_swap(): lax.ppermute(block, 'occ', [(i, (i + (1 if i % 2 else count - 1)) % count...  4.5 us
    pallas_call x1, Pallas kernels, first_terms(): pl.pallas_call(first_kernel, out_shape=jax.ShapeDtypeStruct((transfers, k...  3.52 us
    pallas_call x2, Pallas kernels, add_terms(): pl.pallas_call(functools.partial(add_kernel, place, h), out_shape=jax.Sha...  2.92 us
    pallas_call x1, Pallas kernels, pack(): pl.pallas_call(functools.partial(pack_kernel, bits), out_shape=[jax.Shape...  2.3 us
    pallas_call x1, Pallas kernels, far_terms(): pl.pallas_call(functools.partial(far_kernel, done), out_shape=[jax.ShapeD...  2.07 us
  transfers between devices with their start and end apart: 12, of which 8 were waited for; matrix products, arithmetic and copies ran while one was open for 2% of the time, Pallas kernels for 23%

profile of v14, /device:TPU:0, one launch (start us, length us, event | category | flops | bytes accessed | tf_op | source)
XLA Modules:
  0.0 53.5 jit_solution(17849646288284649769)
XLA Ops:
  0.0 0.0 copy-start.1
  0.0 0.0 copy-start.4
  0.0 0.0 copy-start.3
  0.0 0.0 copy-start.2
  0.0 1.3 %shard_map.56 = bf16[4,2,128,512]{3,2,1,0:T(8,128)(2,1)S(1)} custom-call(bf16[2,2,1,2,256,512]{5,4,3,2,1,0:T(8,128)(2,1)} %factor.13), custom_call_target="tpu_custom_call" | custom-call | tf_op jit(solution)/shard_map/pallas_call | solution.py:65
  1.3 4.5 %collective-permute-start.1 = (bf16[4,2,128,512]{3,2,1,0:T(8,128)(2,1)S(1)}, bf16[4,2,128,512]{3,2,1,0:T(8,128)(2,1)S(1)}, u32[]{:S(2)}, u32[]{:S(2)}) collective-permute-start(bf16[4,2,128,512]{3,2,1,0:T(8,128)(2,1)S(1)} %shard_map.56), channel_id=1, source_target_pairs={{0,7},{1,2},{2,1},{3,4},{4,3},{5,6},{6,5},{7,0},{8,15},{9,10},{10,... | collective-permute-start | bytes 3145736 | tf_op jit(solution)/shard_map/ppermute | solution.py:33
  5.8 2.3 %shard_map.57 = (bf16[2,2,128,512]{3,2,1,0:T(8,128)(2,1)S(1)}, bf16[2,2,128,512]{3,2,1,0:T(8,128)(2,1)S(1)}, bf16[2,2,128,512]{3,2,1,0:T(8,128)(2,1)S(1)}, bf16[2,2,128,512]{3,2,1,0:T(8,128)(2,1)S(1)}) custom-call(s32[2,8]{1,0:T(2,128)} %partner.2, bf16[2,2,1,2,256,512]{5,4,3,2,1,0:T(8,128)(2,1)} %factor.13), custom_call_target="tpu_custom_call" | custom-call | bytes 16777216 | tf_op jit(solution)/shard_map/pallas_call | solution.py:96
  8.1 1.5 %collective-permute-start.5 = (bf16[2,2,128,512]{3,2,1,0:T(8,128)(2,1)S(1)}, bf16[2,2,128,512]{3,2,1,0:T(8,128)(2,1)S(1)}, u32[]{:S(2)}, u32[]{:S(2)}) collective-permute-start(bf16[2,2,128,512]{3,2,1,0:T(8,128)(2,1)S(1)} %get-tuple-element.24), channel_id=1, source_target_pairs={{0,8},{8,0},{16,24},{24,16},{1,9},{9,1},{17,25},{25,17},{2,10},{10... | collective-permute-start | bytes 1572872 | tf_op jit(solution)/shard_map/ppermute | solution.py:23
  9.7 1.5 %collective-permute-start = (bf16[2,2,128,512]{3,2,1,0:T(8,128)(2,1)S(1)}, bf16[2,2,128,512]{3,2,1,0:T(8,128)(2,1)S(1)}, u32[]{:S(2)}, u32[]{:S(2)}) collective-permute-start(bf16[2,2,128,512]{3,2,1,0:T(8,128)(2,1)S(1)} %get-tuple-element.21), channel_id=1, source_target_pairs={{0,16},{8,24},{16,0},{24,8},{1,17},{9,25},{17,1},{25,9},{2,18},{10... | collective-permute-start | bytes 1572872 | tf_op jit(solution)/shard_map/ppermute | solution.py:23
  11.2 0.0 copy-done.4
  11.2 0.0 copy-done.3
  11.2 0.8 %select_reduce_fusion.virtual = f32[8,256]{1,0:T(8,128)S(1)} fusion(f32[8,256]{1,0:T(8,128)S(1)} %copy-done.3, s32[8,256]{1,0:T(8,128)S(1)} %copy-done.4), kind=kLoop, calls=%fused_computation | loop fusion | flops 1570816 | bytes 24576 | tf_op jit(solution)/shard_map/reduce_sum | solution.py:45
  12.0 0.0 copy-done.1
  12.0 0.0 copy-done.2
  12.0 1.6 %shard_map.55 = (f32[2,3,2,256,256]{4,3,2,1,0:T(8,128)S(1)}, bf16[2,2,2,16,512]{4,3,2,1,0:T(8,128)(2,1)S(1)}) custom-call(s32[2,8]{1,0:T(2,128)S(1)} %copy-done.1, f32[8,8]{1,0:T(8,128)S(1)} %copy-done.2, f32[8,256]{1,0:T(8,128)S(1)} %select_reduce_fusion.virtual), custom_call_target="tpu_custom_call" | custom-call | tf_op jit(solution)/shard_map/pallas_call | solution.py:137
  13.6 0.6 %collective-permute-start.7 = (bf16[2,2,128,512]{3,2,1,0:T(8,128)(2,1)S(1)}, bf16[2,2,128,512]{3,2,1,0:T(8,128)(2,1)S(1)}, u32[]{:S(2)}, u32[]{:S(2)}) collective-permute-start(bf16[2,2,128,512]{3,2,1,0:T(8,128)(2,1)S(1)} %get-tuple-element.26), channel_id=1, source_target_pairs={{0,8},{8,0},{16,24},{24,16},{1,9},{9,1},{17,25},{25,17},{2,10},{10... | collective-permute-start | bytes 1572872 | tf_op jit(solution)/shard_map/ppermute | solution.py:23
  14.2 0.5 collective-permute-start.9
  14.7 8.3 %collective-permute-done.5.refs_2_ = bf16[2,2,128,512]{3,2,1,0:T(8,128)(2,1)S(1)} collective-permute-done((bf16[2,2,128,512]{3,2,1,0:T(8,128)(2,1)S(1)}, bf16[2,2,128,512]{3,2,1,0:T(8,128)(2,1)S(1)}, u32[]{:S(2)}, u32[]{:S(2)}) %collective-permute-start.5) | collective-permute-done | bytes 524320 | tf_op jit(solution)/shard_map/ppermute | solution.py:23
  23.1 1.4 %collective-permute-done.refs_3_ = bf16[2,2,128,512]{3,2,1,0:T(8,128)(2,1)S(1)} collective-permute-done((bf16[2,2,128,512]{3,2,1,0:T(8,128)(2,1)S(1)}, bf16[2,2,128,512]{3,2,1,0:T(8,128)(2,1)S(1)}, u32[]{:S(2)}, u32[]{:S(2)}) %collective-permute-start) | collective-permute-done | bytes 524320 | tf_op jit(solution)/shard_map/ppermute | solution.py:23
  24.6 0.1 slice.19
  24.6 0.1 collective-permute-start.11
  24.7 0.6 %collective-permute-start.6 = (bf16[3,2,128,512]{3,2,1,0:T(8,128)(2,1)S(1)}, bf16[3,2,128,512]{3,2,1,0:T(8,128)(2,1)S(1)}, u32[]{:S(2)}, u32[]{:S(2)}) collective-permute-start(bf16[3,2,128,512]{3,2,1,0:T(8,128)(2,1)S(1)} %slice.19), channel_id=1, source_target_pairs={{0,7},{1,2},{2,1},{3,4},{4,3},{5,6},{6,5},{7,0},{8,15},{9,10},{10,... | collective-permute-start | bytes 2359304 | tf_op jit(solution)/shard_map/ppermute | solution.py:33
  25.3 6.6 %collective-permute-done.7.refs_0_ = bf16[2,2,128,512]{3,2,1,0:T(8,128)(2,1)S(1)} collective-permute-done((bf16[2,2,128,512]{3,2,1,0:T(8,128)(2,1)S(1)}, bf16[2,2,128,512]{3,2,1,0:T(8,128)(2,1)S(1)}, u32[]{:S(2)}, u32[]{:S(2)}) %collective-permute-start.7) | collective-permute-done | bytes 524320 | tf_op jit(solution)/shard_map/ppermute | solution.py:23
  31.9 1.2 %collective-permute-done.9.refs_1_ = bf16[2,2,128,512]{3,2,1,0:T(8,128)(2,1)S(1)} collective-permute-done((bf16[2,2,128,512]{3,2,1,0:T(8,128)(2,1)S(1)}, bf16[2,2,128,512]{3,2,1,0:T(8,128)(2,1)S(1)}, u32[]{:S(2)}, u32[]{:S(2)}) %collective-permute-start.9) | collective-permute-done | bytes 524320 | tf_op jit(solution)/shard_map/ppermute | solution.py:23
  33.1 0.1 pad_maximum_fusion.source
  33.2 0.0 collective-permute-done.1
  33.2 0.1 collective-permute-start.8
  33.3 0.0 copy-start
  33.3 0.6 %collective-permute-start.10 = (bf16[2,2,128,512]{3,2,1,0:T(8,128)(2,1)S(1)}, bf16[2,2,128,512]{3,2,1,0:T(8,128)(2,1)S(1)}, u32[]{:S(2)}, u32[]{:S(2)}) collective-permute-start(bf16[2,2,128,512]{3,2,1,0:T(8,128)(2,1)S(1)} %shard_map.58), channel_id=1, source_target_pairs={{0,1},{1,0},{2,3},{3,2},{4,5},{5,4},{6,7},{7,6},{8,9},{9,8},{10,11... | collective-permute-start | bytes 1572872 | tf_op jit(solution)/shard_map/ppermute | solution.py:28
  33.9 0.1 fusion
  34.0 1.6 %collective-permute-start.4 = (bf16[2,2,128,512]{3,2,1,0:T(8,128)(2,1)S(1)}, bf16[2,2,128,512]{3,2,1,0:T(8,128)(2,1)S(1)}, u32[]{:S(2)}, u32[]{:S(2)}) collective-permute-start(bf16[2,2,128,512]{3,2,1,0:T(8,128)(2,1)S(1)} %get-tuple-element.33), channel_id=1, source_target_pairs={{0,16},{8,24},{16,0},{24,8},{1,17},{9,25},{17,1},{25,9},{2,18},{10... | collective-permute-start | bytes 1572872 | tf_op jit(solution)/shard_map/ppermute | solution.py:23
  35.6 0.0 collective-permute-done.11.refs_4_
  35.6 0.5 %collective-permute-start.3 = (bf16[2,2,128,512]{3,2,1,0:T(8,128)(2,1)S(1)}, bf16[2,2,128,512]{3,2,1,0:T(8,128)(2,1)S(1)}, u32[]{:S(2)}, u32[]{:S(2)}) collective-permute-start(bf16[2,2,128,512]{3,2,1,0:T(8,128)(2,1)S(1)} %get-tuple-element.34), channel_id=1, source_target_pairs={{0,8},{8,0},{16,24},{24,16},{1,9},{9,1},{17,25},{25,17},{2,10},{10... | collective-permute-start | bytes 1572872 | tf_op jit(solution)/shard_map/ppermute | solution.py:23
  36.1 0.0 copy-done
  36.1 3.5 %shard_map.59.total = f32[2,2,2,256,512]{4,3,2,1,0:T(8,128)S(1)} custom-call(bf16[2,2,1,2,256,512]{5,4,3,2,1,0:T(8,128)(2,1)S(1)} %copy-done, f32[2,3,2,256,256]{4,3,2,1,0:T(8,128)S(1)} %get-tuple-element.19.inverse, bf16[2,2,128,512]{3,2,1,0:T(8,128)(2,1)S(1)} %collective-permute-done.7.refs_0_, ...), custom_call_target="tpu_custom_call" | custom-call | tf_op jit(solution)/shard_map/pallas_call | solution.py:208
  39.7 0.0 collective-permute-done.8
  39.7 1.4 %collective-permute-start.2 = (bf16[1,2,128,512]{3,2,1,0:T(8,128)(2,1)S(1)}, bf16[1,2,128,512]{3,2,1,0:T(8,128)(2,1)S(1)}, u32[]{:S(2)}, u32[]{:S(2)}) collective-permute-start(bf16[1,2,128,512]{3,2,1,0:T(8,128)(2,1)S(1)} %slice.16), channel_id=1, source_target_pairs={{0,7},{1,2},{2,1},{3,4},{4,3},{5,6},{6,5},{7,0},{8,15},{9,10},{10,... | collective-permute-start | bytes 786440 | tf_op jit(solution)/shard_map/ppermute | solution.py:33
  41.0 0.0 collective-permute-done.10
  41.0 0.1 pad_maximum_fusion.1.window
  41.1 1.6 %shard_map.60.total = f32[2,2,2,256,512]{4,3,2,1,0:T(8,128)S(1)} custom-call(bf16[2,2,1,2,256,512]{5,4,3,2,1,0:T(8,128)(2,1)S(1)} %copy-done, f32[2,3,2,256,256]{4,3,2,1,0:T(8,128)S(1)} %get-tuple-element.19.inverse, bf16[4,2,128,512]{3,2,1,0:T(8,128)(2,1)S(1)} %pad_maximum_fusion.1.window, ...), custom_call_target="tpu_custom_call", output_to_operand_aliasing={{}: (3, {})} | custom-call | tf_op jit(solution)/shard_map/pallas_call | solution.py:233
  42.8 3.7 %collective-permute-done.6.window = bf16[3,2,128,512]{3,2,1,0:T(8,128)(2,1)S(1)} collective-permute-done((bf16[3,2,128,512]{3,2,1,0:T(8,128)(2,1)S(1)}, bf16[3,2,128,512]{3,2,1,0:T(8,128)(2,1)S(1)}, u32[]{:S(2)}, u32[]{:S(2)}) %collective-permute-start.6) | collective-permute-done | bytes 786464 | tf_op jit(solution)/shard_map/ppermute | solution.py:33
  46.5 1.3 %shard_map.61.refs_2_ = f32[2,2,2,256,512]{4,3,2,1,0:T(8,128)S(1)} custom-call(bf16[2,2,1,2,256,512]{5,4,3,2,1,0:T(8,128)(2,1)S(1)} %copy-done, f32[2,3,2,256,256]{4,3,2,1,0:T(8,128)S(1)} %get-tuple-element.19.inverse, bf16[3,2,128,512]{3,2,1,0:T(8,128)(2,1)S(1)} %collective-permute-done.6.window, ...), custom_call_target="tpu_custom_call", output_to_operand_aliasing={{}: (3, {})} | custom-call | flops 3145728000 | tf_op jit(solution)/shard_map/pallas_call | solution.py:233
  47.8 0.1 collective-permute-done.4.refs_1_
  47.9 1.2 %collective-permute-done.3.refs_0_ = bf16[2,2,128,512]{3,2,1,0:T(8,128)(2,1)S(1)} collective-permute-done((bf16[2,2,128,512]{3,2,1,0:T(8,128)(2,1)S(1)}, bf16[2,2,128,512]{3,2,1,0:T(8,128)(2,1)S(1)}, u32[]{:S(2)}, u32[]{:S(2)}) %collective-permute-start.3) | collective-permute-done | bytes 524320 | tf_op jit(solution)/shard_map/ppermute | solution.py:23
  49.1 2.1 %shard_map.62 = (f32[2,2,2,256,512]{4,3,2,1,0:T(8,128)S(1)}, bf16[2,2,1,2,256,512]{5,4,3,2,1,0:T(8,128)(2,1)}) custom-call(bf16[2,2,1,2,256,512]{5,4,3,2,1,0:T(8,128)(2,1)S(1)} %copy-done, f32[2,3,2,256,256]{4,3,2,1,0:T(8,128)S(1)} %get-tuple-element.19.inverse, ...), custom_call_target="tpu_custom_call", output_to_operand_aliasing={{0}: (5, {})} | custom-call | tf_op jit(solution)/shard_map/pallas_call | solution.py:281
  51.2 0.8 %collective-permute-done.2.window = bf16[1,2,128,512]{3,2,1,0:T(8,128)(2,1)S(1)} collective-permute-done((bf16[1,2,128,512]{3,2,1,0:T(8,128)(2,1)S(1)}, bf16[1,2,128,512]{3,2,1,0:T(8,128)(2,1)S(1)}, u32[]{:S(2)}, u32[]{:S(2)}) %collective-permute-start.2) | collective-permute-done | bytes 262176 | tf_op jit(solution)/shard_map/ppermute | solution.py:33
  52.0 1.5 %shard_map.63 = bf16[2,2,1,2,256,512]{5,4,3,2,1,0:T(8,128)(2,1)} custom-call(bf16[2,2,1,2,256,512]{5,4,3,2,1,0:T(8,128)(2,1)S(1)} %copy-done, f32[2,3,2,256,256]{4,3,2,1,0:T(8,128)S(1)} %get-tuple-element.19.inverse, bf16[1,2,128,512]{3,2,1,0:T(8,128)(2,1)S(1)} %collective-permute-done.2.window, ...), custom_call_target="tpu_custom_call", output_to_operand_aliasing={{}: (4, {})} | custom-call | tf_op jit(solution)/shard_map/pallas_call | solution.py:315
  (4 shorter events, 0.1 us)
Async XLA Ops:
  0.0 12.0 %copy-start.1 = (s32[2,8]{1,0:T(2,128)S(1)}, s32[2,8]{1,0:T(2,128)}, u32[]{:S(2)}) copy-start(s32[2,8]{1,0:T(2,128)} %partner.2) | copy-start | bytes 196
  0.0 11.2 %copy-start.4 = (s32[8,256]{1,0:T(8,128)S(1)}, s32[8,256]{1,0:T(8,128)}, u32[]{:S(2)}) copy-start(s32[8,256]{1,0:T(8,128)} %param.9) | copy-start | bytes 24580
  0.0 11.2 %copy-start.3 = (f32[8,256]{1,0:T(8,128)S(1)}, f32[8,256]{1,0:T(8,128)}, u32[]{:S(2)}) copy-start(f32[8,256]{1,0:T(8,128)} %param.8) | copy-start | bytes 24580
  0.0 12.0 %copy-start.2 = (f32[8,8]{1,0:T(8,128)S(1)}, f32[8,8]{1,0:T(8,128)}, u32[]{:S(2)}) copy-start(f32[8,8]{1,0:T(8,128)} %occ.1) | copy-start | bytes 772
  1.3 31.9 %collective-permute-start.1 = (bf16[4,2,128,512]{3,2,1,0:T(8,128)(2,1)S(1)}, bf16[4,2,128,512]{3,2,1,0:T(8,128)(2,1)S(1)}, u32[]{:S(2)}, u32[]{:S(2)}) collective-permute-start(bf16[4,2,128,512]{3,2,1,0:T(8,128)(2,1)S(1)} %shard_map.56), channel_id=1, source_target_pairs={{0,7},{1,2},{2,1},{3,4},{4,3},{5,6},{6,5},{7,0},{8,15},{9,10},{10,... | collective-permute-start | bytes 3145736 | tf_op jit(solution)/shard_map/ppermute | solution.py:33
  8.1 14.9 %collective-permute-start.5 = (bf16[2,2,128,512]{3,2,1,0:T(8,128)(2,1)S(1)}, bf16[2,2,128,512]{3,2,1,0:T(8,128)(2,1)S(1)}, u32[]{:S(2)}, u32[]{:S(2)}) collective-permute-start(bf16[2,2,128,512]{3,2,1,0:T(8,128)(2,1)S(1)} %get-tuple-element.24), channel_id=1, source_target_pairs={{0,8},{8,0},{16,24},{24,16},{1,9},{9,1},{17,25},{25,17},{2,10},{10... | collective-permute-start | bytes 1572872 | tf_op jit(solution)/shard_map/ppermute | solution.py:23
  9.7 14.9 %collective-permute-start = (bf16[2,2,128,512]{3,2,1,0:T(8,128)(2,1)S(1)}, bf16[2,2,128,512]{3,2,1,0:T(8,128)(2,1)S(1)}, u32[]{:S(2)}, u32[]{:S(2)}) collective-permute-start(bf16[2,2,128,512]{3,2,1,0:T(8,128)(2,1)S(1)} %get-tuple-element.21), channel_id=1, source_target_pairs={{0,16},{8,24},{16,0},{24,8},{1,17},{9,25},{17,1},{25,9},{2,18},{10... | collective-permute-start | bytes 1572872 | tf_op jit(solution)/shard_map/ppermute | solution.py:23
  13.6 18.3 %collective-permute-start.7 = (bf16[2,2,128,512]{3,2,1,0:T(8,128)(2,1)S(1)}, bf16[2,2,128,512]{3,2,1,0:T(8,128)(2,1)S(1)}, u32[]{:S(2)}, u32[]{:S(2)}) collective-permute-start(bf16[2,2,128,512]{3,2,1,0:T(8,128)(2,1)S(1)} %get-tuple-element.26), channel_id=1, source_target_pairs={{0,8},{8,0},{16,24},{24,16},{1,9},{9,1},{17,25},{25,17},{2,10},{10... | collective-permute-start | bytes 1572872 | tf_op jit(solution)/shard_map/ppermute | solution.py:23
  14.2 18.9 %collective-permute-start.9 = (bf16[2,2,128,512]{3,2,1,0:T(8,128)(2,1)S(1)}, bf16[2,2,128,512]{3,2,1,0:T(8,128)(2,1)S(1)}, u32[]{:S(2)}, u32[]{:S(2)}) collective-permute-start(bf16[2,2,128,512]{3,2,1,0:T(8,128)(2,1)S(1)} %get-tuple-element.29), channel_id=1, source_target_pairs={{0,16},{8,24},{16,0},{24,8},{1,17},{9,25},{17,1},{25,9},{2,18},{10... | collective-permute-start | bytes 1572872 | tf_op jit(solution)/shard_map/ppermute | solution.py:23
  24.6 10.9 %collective-permute-start.11 = (bf16[4,2,128,512]{3,2,1,0:T(8,128)(2,1)S(1)}, bf16[4,2,128,512]{3,2,1,0:T(8,128)(2,1)S(1)}, u32[]{:S(2)}, u32[]{:S(2)}) collective-permute-start(bf16[4,2,128,512]{3,2,1,0:T(8,128)(2,1)S(1)} %constant_dynamic-update-slice_fusion), channel_id=1, source_target_pairs={{0,1},{1,0},{2,3},{3,2},{4,5},{5,4},{6,7},{7,6},{8,9},{9,8},{10,11... | collective-permute-start | bytes 3145736 | tf_op jit(solution)/shard_map/ppermute | solution.py:28
  24.7 21.8 %collective-permute-start.6 = (bf16[3,2,128,512]{3,2,1,0:T(8,128)(2,1)S(1)}, bf16[3,2,128,512]{3,2,1,0:T(8,128)(2,1)S(1)}, u32[]{:S(2)}, u32[]{:S(2)}) collective-permute-start(bf16[3,2,128,512]{3,2,1,0:T(8,128)(2,1)S(1)} %slice.19), channel_id=1, source_target_pairs={{0,7},{1,2},{2,1},{3,4},{4,3},{5,6},{6,5},{7,0},{8,15},{9,10},{10,... | collective-permute-start | bytes 2359304 | tf_op jit(solution)/shard_map/ppermute | solution.py:33
  33.2 6.4 %collective-permute-start.8 = (bf16[2,2,128,512]{3,2,1,0:T(8,128)(2,1)S(1)}, bf16[2,2,128,512]{3,2,1,0:T(8,128)(2,1)S(1)}, u32[]{:S(2)}, u32[]{:S(2)}) collective-permute-start(bf16[2,2,128,512]{3,2,1,0:T(8,128)(2,1)S(1)} %collective-permute-done.7.refs_0_), channel_id=1, source_target_pairs={{0,1},{1,0},{2,3},{3,2},{4,5},{5,4},{6,7},{7,6},{8,9},{9,8},{10,11... | collective-permute-start | bytes 1572872 | tf_op jit(solution)/shard_map/ppermute | solution.py:28
  33.3 2.8 %copy-start = (bf16[2,2,1,2,256,512]{5,4,3,2,1,0:T(8,128)(2,1)S(1)}, bf16[2,2,1,2,256,512]{5,4,3,2,1,0:T(8,128)(2,1)}, u32[]{:S(2)}) copy-start(bf16[2,2,1,2,256,512]{5,4,3,2,1,0:T(8,128)(2,1)} %factor.13) | copy-start | bytes 6291460
  33.3 7.7 %collective-permute-start.10 = (bf16[2,2,128,512]{3,2,1,0:T(8,128)(2,1)S(1)}, bf16[2,2,128,512]{3,2,1,0:T(8,128)(2,1)S(1)}, u32[]{:S(2)}, u32[]{:S(2)}) collective-permute-start(bf16[2,2,128,512]{3,2,1,0:T(8,128)(2,1)S(1)} %shard_map.58), channel_id=1, source_target_pairs={{0,1},{1,0},{2,3},{3,2},{4,5},{5,4},{6,7},{7,6},{8,9},{9,8},{10,11... | collective-permute-start | bytes 1572872 | tf_op jit(solution)/shard_map/ppermute | solution.py:28
  34.0 13.9 %collective-permute-start.4 = (bf16[2,2,128,512]{3,2,1,0:T(8,128)(2,1)S(1)}, bf16[2,2,128,512]{3,2,1,0:T(8,128)(2,1)S(1)}, u32[]{:S(2)}, u32[]{:S(2)}) collective-permute-start(bf16[2,2,128,512]{3,2,1,0:T(8,128)(2,1)S(1)} %get-tuple-element.33), channel_id=1, source_target_pairs={{0,16},{8,24},{16,0},{24,8},{1,17},{9,25},{17,1},{25,9},{2,18},{10... | collective-permute-start | bytes 1572872 | tf_op jit(solution)/shard_map/ppermute | solution.py:23
  35.6 13.6 %collective-permute-start.3 = (bf16[2,2,128,512]{3,2,1,0:T(8,128)(2,1)S(1)}, bf16[2,2,128,512]{3,2,1,0:T(8,128)(2,1)S(1)}, u32[]{:S(2)}, u32[]{:S(2)}) collective-permute-start(bf16[2,2,128,512]{3,2,1,0:T(8,128)(2,1)S(1)} %get-tuple-element.34), channel_id=1, source_target_pairs={{0,8},{8,0},{16,24},{24,16},{1,9},{9,1},{17,25},{25,17},{2,10},{10... | collective-permute-start | bytes 1572872 | tf_op jit(solution)/shard_map/ppermute | solution.py:23
  39.7 12.4 %collective-permute-start.2 = (bf16[1,2,128,512]{3,2,1,0:T(8,128)(2,1)S(1)}, bf16[1,2,128,512]{3,2,1,0:T(8,128)(2,1)S(1)}, u32[]{:S(2)}, u32[]{:S(2)}) collective-permute-start(bf16[1,2,128,512]{3,2,1,0:T(8,128)(2,1)S(1)} %slice.16), channel_id=1, source_target_pairs={{0,7},{1,2},{2,1},{3,4},{4,3},{5,6},{6,5},{7,0},{8,15},{9,10},{10,... | collective-permute-start | bytes 786440 | tf_op jit(solution)/shard_map/ppermute | solution.py:33

commit v15 on v14

--- a/solution.py
+++ b/solution.py
@@ -294,18 +294,22 @@
 
 
 def last_kernel(done, factor, inverse, window, total, _, out, staged, sems):
-    kc, half = factor.shape[1], window.shape[2]
+    transfers, kc, _, parts, nv, _ = factor.shape
+    half = window.shape[2]
     copies = []
-
-    def terms_of(t, k):
-        at = t * kc + k - done
-        return [(window[at], inverse[t, 2, k, :, half_of(1, half)])] if at >= 0 else []
-
-    def finish(t, k, part, value):
-        value = value + total[t, k, part]
-        send_part(copies, value, out.at[t, k, 0, part], staged, sems)
-
-    contract(factor, terms_of, finish)
+    for at in range(done, transfers * kc):
+        t, k = at // kc, at % kc
+        waiting = []
+        for r in range(2):
+            rows = half_of(r, nv // 2)
+            terms = [(window[at - done], inverse[t, 2, k, rows, half_of(1, half)])]
+            waiting.append(amplitude_rows(factor[t, k, 0, :, rows, :], terms))
+        for r, (sides, blocks) in enumerate(waiting):
+            rows = half_of(r, nv // 2)
+            for part in range(parts):
+                value = jnp.dot(sides[part], blocks, preferred_element_type=F32)
+                target = out.at[t, k, 0, part, pl.ds(rows.start, nv // 2)]
+                send_part(copies, value + total[t, k, part, rows], target, staged, sems)
     for copy in copies:
         copy.wait()
 
@@ -317,7 +321,7 @@
         out_shape=jax.ShapeDtypeStruct(factor.shape, BF16),
         in_specs=[VMEM] * 4 + [ANY],
         out_specs=ANY,
-        scratch_shapes=out_scratch((transfers * kc - done) * parts, nv, naux),
+        scratch_shapes=out_scratch((transfers * kc - done) * parts * 2, nv // 2, naux),
         input_output_aliases={4: 0},
         cost_estimate=COST,
         compiler_params=PARAMS,

time: 53.7 us -> 53.5 us (level)
  no operation moved by 1% of the time
where the time goes in v15:
time: 53.5 us; the launch traced here: 53.3 us
  waiting for transfers between devices  23.4 us (44%)
  Pallas kernels  15 us (28%)
  starting transfers between devices  13.6 us (25%)
  other arithmetic  0.94 us (2%)
    ppermute x6, waiting for transfers between devices, group_swap(): return lax.ppermute(block, 'kpt', [(g, g ^ 1 << bit) for g in range(count)])  19 us
    ppermute x3, starting transfers between devices, far_swap(): lax.ppermute(block, 'occ', [(i, (i + (1 if i % 2 else count - 1)) % count...  6.52 us
    ppermute x6, starting transfers between devices, group_swap(): return lax.ppermute(block, 'kpt', [(g, g ^ 1 << bit) for g in range(count)])  6.35 us
    ppermute x3, waiting for transfers between devices, far_swap(): lax.ppermute(block, 'occ', [(i, (i + (1 if i % 2 else count - 1)) % count...  4.42 us
    pallas_call x1, Pallas kernels, first_terms(): pl.pallas_call(first_kernel, out_shape=jax.ShapeDtypeStruct((transfers, k...  3.52 us
    pallas_call x2, Pallas kernels, add_terms(): pl.pallas_call(functools.partial(add_kernel, place, h), out_shape=jax.Sha...  2.91 us
    pallas_call x1, Pallas kernels, pack(): pl.pallas_call(functools.partial(pack_kernel, bits), out_shape=[jax.Shape...  2.27 us
    pallas_call x1, Pallas kernels, far_terms(): pl.pallas_call(functools.partial(far_kernel, done), out_shape=[jax.ShapeD...  2.07 us
  transfers between devices with their start and end apart: 12, of which 8 were waited for; matrix products, arithmetic and copies ran while one was open for 2% of the time, Pallas kernels for 23%

profile of v15, /device:TPU:0, one launch (start us, length us, event | category | flops | bytes accessed | tf_op | source)
XLA Modules:
  0.0 53.3 jit_solution(8158006636985727665)
XLA Ops:
  0.0 0.0 copy-start.1
  0.0 0.0 copy-start.4
  0.0 0.0 copy-start.3
  0.0 0.0 copy-start.2
  0.0 1.3 %shard_map.56 = bf16[4,2,128,512]{3,2,1,0:T(8,128)(2,1)S(1)} custom-call(bf16[2,2,1,2,256,512]{5,4,3,2,1,0:T(8,128)(2,1)} %factor.13), custom_call_target="tpu_custom_call" | custom-call | tf_op jit(solution)/shard_map/pallas_call | solution.py:65
  1.3 4.5 %collective-permute-start.1 = (bf16[4,2,128,512]{3,2,1,0:T(8,128)(2,1)S(1)}, bf16[4,2,128,512]{3,2,1,0:T(8,128)(2,1)S(1)}, u32[]{:S(2)}, u32[]{:S(2)}) collective-permute-start(bf16[4,2,128,512]{3,2,1,0:T(8,128)(2,1)S(1)} %shard_map.56), channel_id=1, source_target_pairs={{0,7},{1,2},{2,1},{3,4},{4,3},{5,6},{6,5},{7,0},{8,15},{9,10},{10,... | collective-permute-start | bytes 3145736 | tf_op jit(solution)/shard_map/ppermute | solution.py:33
  5.8 2.3 %shard_map.57 = (bf16[2,2,128,512]{3,2,1,0:T(8,128)(2,1)S(1)}, bf16[2,2,128,512]{3,2,1,0:T(8,128)(2,1)S(1)}, bf16[2,2,128,512]{3,2,1,0:T(8,128)(2,1)S(1)}, bf16[2,2,128,512]{3,2,1,0:T(8,128)(2,1)S(1)}) custom-call(s32[2,8]{1,0:T(2,128)} %partner.2, bf16[2,2,1,2,256,512]{5,4,3,2,1,0:T(8,128)(2,1)} %factor.13), custom_call_target="tpu_custom_call" | custom-call | bytes 16777216 | tf_op jit(solution)/shard_map/pallas_call | solution.py:96
  8.1 1.6 %collective-permute-start.5 = (bf16[2,2,128,512]{3,2,1,0:T(8,128)(2,1)S(1)}, bf16[2,2,128,512]{3,2,1,0:T(8,128)(2,1)S(1)}, u32[]{:S(2)}, u32[]{:S(2)}) collective-permute-start(bf16[2,2,128,512]{3,2,1,0:T(8,128)(2,1)S(1)} %get-tuple-element.24), channel_id=1, source_target_pairs={{0,8},{8,0},{16,24},{24,16},{1,9},{9,1},{17,25},{25,17},{2,10},{10... | collective-permute-start | bytes 1572872 | tf_op jit(solution)/shard_map/ppermute | solution.py:23
  9.7 1.5 %collective-permute-start = (bf16[2,2,128,512]{3,2,1,0:T(8,128)(2,1)S(1)}, bf16[2,2,128,512]{3,2,1,0:T(8,128)(2,1)S(1)}, u32[]{:S(2)}, u32[]{:S(2)}) collective-permute-start(bf16[2,2,128,512]{3,2,1,0:T(8,128)(2,1)S(1)} %get-tuple-element.21), channel_id=1, source_target_pairs={{0,16},{8,24},{16,0},{24,8},{1,17},{9,25},{17,1},{25,9},{2,18},{10... | collective-permute-start | bytes 1572872 | tf_op jit(solution)/shard_map/ppermute | solution.py:23
  11.2 0.0 copy-done.4
  11.2 0.0 copy-done.3
  11.2 0.8 %select_reduce_fusion.virtual = f32[8,256]{1,0:T(8,128)S(1)} fusion(f32[8,256]{1,0:T(8,128)S(1)} %copy-done.3, s32[8,256]{1,0:T(8,128)S(1)} %copy-done.4), kind=kLoop, calls=%fused_computation | loop fusion | flops 1570816 | bytes 24576 | tf_op jit(solution)/shard_map/reduce_sum | solution.py:45
  12.0 0.0 copy-done.1
  12.0 0.0 copy-done.2
  12.0 1.6 %shard_map.55 = (f32[2,3,2,256,256]{4,3,2,1,0:T(8,128)S(1)}, bf16[2,2,2,16,512]{4,3,2,1,0:T(8,128)(2,1)S(1)}) custom-call(s32[2,8]{1,0:T(2,128)S(1)} %copy-done.1, f32[8,8]{1,0:T(8,128)S(1)} %copy-done.2, f32[8,256]{1,0:T(8,128)S(1)} %select_reduce_fusion.virtual), custom_call_target="tpu_custom_call" | custom-call | tf_op jit(solution)/shard_map/pallas_call | solution.py:137
  13.6 0.6 %collective-permute-start.7 = (bf16[2,2,128,512]{3,2,1,0:T(8,128)(2,1)S(1)}, bf16[2,2,128,512]{3,2,1,0:T(8,128)(2,1)S(1)}, u32[]{:S(2)}, u32[]{:S(2)}) collective-permute-start(bf16[2,2,128,512]{3,2,1,0:T(8,128)(2,1)S(1)} %get-tuple-element.26), channel_id=1, source_target_pairs={{0,8},{8,0},{16,24},{24,16},{1,9},{9,1},{17,25},{25,17},{2,10},{10... | collective-permute-start | bytes 1572872 | tf_op jit(solution)/shard_map/ppermute | solution.py:23
  14.3 0.4 collective-permute-start.9
  14.7 8.3 %collective-permute-done.5.refs_2_ = bf16[2,2,128,512]{3,2,1,0:T(8,128)(2,1)S(1)} collective-permute-done((bf16[2,2,128,512]{3,2,1,0:T(8,128)(2,1)S(1)}, bf16[2,2,128,512]{3,2,1,0:T(8,128)(2,1)S(1)}, u32[]{:S(2)}, u32[]{:S(2)}) %collective-permute-start.5) | collective-permute-done | bytes 524320 | tf_op jit(solution)/shard_map/ppermute | solution.py:23
  23.1 1.5 %collective-permute-done.refs_3_ = bf16[2,2,128,512]{3,2,1,0:T(8,128)(2,1)S(1)} collective-permute-done((bf16[2,2,128,512]{3,2,1,0:T(8,128)(2,1)S(1)}, bf16[2,2,128,512]{3,2,1,0:T(8,128)(2,1)S(1)}, u32[]{:S(2)}, u32[]{:S(2)}) %collective-permute-start) | collective-permute-done | bytes 524320 | tf_op jit(solution)/shard_map/ppermute | solution.py:23
  24.6 0.1 slice.19
  24.7 0.1 collective-permute-start.11
  24.7 0.6 %collective-permute-start.6 = (bf16[3,2,128,512]{3,2,1,0:T(8,128)(2,1)S(1)}, bf16[3,2,128,512]{3,2,1,0:T(8,128)(2,1)S(1)}, u32[]{:S(2)}, u32[]{:S(2)}) collective-permute-start(bf16[3,2,128,512]{3,2,1,0:T(8,128)(2,1)S(1)} %slice.19), channel_id=1, source_target_pairs={{0,7},{1,2},{2,1},{3,4},{4,3},{5,6},{6,5},{7,0},{8,15},{9,10},{10,... | collective-permute-start | bytes 2359304 | tf_op jit(solution)/shard_map/ppermute | solution.py:33
  25.3 6.6 %collective-permute-done.7.refs_0_ = bf16[2,2,128,512]{3,2,1,0:T(8,128)(2,1)S(1)} collective-permute-done((bf16[2,2,128,512]{3,2,1,0:T(8,128)(2,1)S(1)}, bf16[2,2,128,512]{3,2,1,0:T(8,128)(2,1)S(1)}, u32[]{:S(2)}, u32[]{:S(2)}) %collective-permute-start.7) | collective-permute-done | bytes 524320 | tf_op jit(solution)/shard_map/ppermute | solution.py:23
  31.9 1.2 %collective-permute-done.9.refs_1_ = bf16[2,2,128,512]{3,2,1,0:T(8,128)(2,1)S(1)} collective-permute-done((bf16[2,2,128,512]{3,2,1,0:T(8,128)(2,1)S(1)}, bf16[2,2,128,512]{3,2,1,0:T(8,128)(2,1)S(1)}, u32[]{:S(2)}, u32[]{:S(2)}) %collective-permute-start.9) | collective-permute-done | bytes 524320 | tf_op jit(solution)/shard_map/ppermute | solution.py:23
  33.1 0.1 pad_maximum_fusion.source
  33.2 0.0 collective-permute-done.1
  33.2 0.1 collective-permute-start.8
  33.4 0.0 copy-start
  33.4 0.6 %collective-permute-start.10 = (bf16[2,2,128,512]{3,2,1,0:T(8,128)(2,1)S(1)}, bf16[2,2,128,512]{3,2,1,0:T(8,128)(2,1)S(1)}, u32[]{:S(2)}, u32[]{:S(2)}) collective-permute-start(bf16[2,2,128,512]{3,2,1,0:T(8,128)(2,1)S(1)} %shard_map.58), channel_id=1, source_target_pairs={{0,1},{1,0},{2,3},{3,2},{4,5},{5,4},{6,7},{7,6},{8,9},{9,8},{10,11... | collective-permute-start | bytes 1572872 | tf_op jit(solution)/shard_map/ppermute | solution.py:28
  33.9 0.1 fusion
  34.0 1.6 %collective-permute-start.4 = (bf16[2,2,128,512]{3,2,1,0:T(8,128)(2,1)S(1)}, bf16[2,2,128,512]{3,2,1,0:T(8,128)(2,1)S(1)}, u32[]{:S(2)}, u32[]{:S(2)}) collective-permute-start(bf16[2,2,128,512]{3,2,1,0:T(8,128)(2,1)S(1)} %get-tuple-element.33), channel_id=1, source_target_pairs={{0,16},{8,24},{16,0},{24,8},{1,17},{9,25},{17,1},{25,9},{2,18},{10... | collective-permute-start | bytes 1572872 | tf_op jit(solution)/shard_map/ppermute | solution.py:23
  35.6 0.0 collective-permute-done.11.refs_4_
  35.6 0.6 %collective-permute-start.3 = (bf16[2,2,128,512]{3,2,1,0:T(8,128)(2,1)S(1)}, bf16[2,2,128,512]{3,2,1,0:T(8,128)(2,1)S(1)}, u32[]{:S(2)}, u32[]{:S(2)}) collective-permute-start(bf16[2,2,128,512]{3,2,1,0:T(8,128)(2,1)S(1)} %get-tuple-element.34), channel_id=1, source_target_pairs={{0,8},{8,0},{16,24},{24,16},{1,9},{9,1},{17,25},{25,17},{2,10},{10... | collective-permute-start | bytes 1572872 | tf_op jit(solution)/shard_map/ppermute | solution.py:23
  36.2 0.0 copy-done
  36.2 3.5 %shard_map.59.total = f32[2,2,2,256,512]{4,3,2,1,0:T(8,128)S(1)} custom-call(bf16[2,2,1,2,256,512]{5,4,3,2,1,0:T(8,128)(2,1)S(1)} %copy-done, f32[2,3,2,256,256]{4,3,2,1,0:T(8,128)S(1)} %get-tuple-element.19.inverse, bf16[2,2,128,512]{3,2,1,0:T(8,128)(2,1)S(1)} %collective-permute-done.7.refs_0_, ...), custom_call_target="tpu_custom_call" | custom-call | tf_op jit(solution)/shard_map/pallas_call | solution.py:208
  39.7 0.0 collective-permute-done.8
  39.7 1.4 %collective-permute-start.2 = (bf16[1,2,128,512]{3,2,1,0:T(8,128)(2,1)S(1)}, bf16[1,2,128,512]{3,2,1,0:T(8,128)(2,1)S(1)}, u32[]{:S(2)}, u32[]{:S(2)}) collective-permute-start(bf16[1,2,128,512]{3,2,1,0:T(8,128)(2,1)S(1)} %slice.16), channel_id=1, source_target_pairs={{0,7},{1,2},{2,1},{3,4},{4,3},{5,6},{6,5},{7,0},{8,15},{9,10},{10,... | collective-permute-start | bytes 786440 | tf_op jit(solution)/shard_map/ppermute | solution.py:33
  41.1 0.0 collective-permute-done.10
  41.1 0.1 pad_maximum_fusion.1.window
  41.2 1.6 %shard_map.60.total = f32[2,2,2,256,512]{4,3,2,1,0:T(8,128)S(1)} custom-call(bf16[2,2,1,2,256,512]{5,4,3,2,1,0:T(8,128)(2,1)S(1)} %copy-done, f32[2,3,2,256,256]{4,3,2,1,0:T(8,128)S(1)} %get-tuple-element.19.inverse, bf16[4,2,128,512]{3,2,1,0:T(8,128)(2,1)S(1)} %pad_maximum_fusion.1.window, ...), custom_call_target="tpu_custom_call", output_to_operand_aliasing={{}: (3, {})} | custom-call | tf_op jit(solution)/shard_map/pallas_call | solution.py:233
  42.9 3.6 %collective-permute-done.6.window = bf16[3,2,128,512]{3,2,1,0:T(8,128)(2,1)S(1)} collective-permute-done((bf16[3,2,128,512]{3,2,1,0:T(8,128)(2,1)S(1)}, bf16[3,2,128,512]{3,2,1,0:T(8,128)(2,1)S(1)}, u32[]{:S(2)}, u32[]{:S(2)}) %collective-permute-start.6) | collective-permute-done | bytes 786464 | tf_op jit(solution)/shard_map/ppermute | solution.py:33
  46.5 1.3 %shard_map.61.refs_2_ = f32[2,2,2,256,512]{4,3,2,1,0:T(8,128)S(1)} custom-call(bf16[2,2,1,2,256,512]{5,4,3,2,1,0:T(8,128)(2,1)S(1)} %copy-done, f32[2,3,2,256,256]{4,3,2,1,0:T(8,128)S(1)} %get-tuple-element.19.inverse, bf16[3,2,128,512]{3,2,1,0:T(8,128)(2,1)S(1)} %collective-permute-done.6.window, ...), custom_call_target="tpu_custom_call", output_to_operand_aliasing={{}: (3, {})} | custom-call | flops 3145728000 | tf_op jit(solution)/shard_map/pallas_call | solution.py:233
  47.8 0.1 collective-permute-done.4.refs_1_
  47.9 1.2 %collective-permute-done.3.refs_0_ = bf16[2,2,128,512]{3,2,1,0:T(8,128)(2,1)S(1)} collective-permute-done((bf16[2,2,128,512]{3,2,1,0:T(8,128)(2,1)S(1)}, bf16[2,2,128,512]{3,2,1,0:T(8,128)(2,1)S(1)}, u32[]{:S(2)}, u32[]{:S(2)}) %collective-permute-start.3) | collective-permute-done | bytes 524320 | tf_op jit(solution)/shard_map/ppermute | solution.py:23
  49.2 2.1 %shard_map.62 = (f32[2,2,2,256,512]{4,3,2,1,0:T(8,128)S(1)}, bf16[2,2,1,2,256,512]{5,4,3,2,1,0:T(8,128)(2,1)}) custom-call(bf16[2,2,1,2,256,512]{5,4,3,2,1,0:T(8,128)(2,1)S(1)} %copy-done, f32[2,3,2,256,256]{4,3,2,1,0:T(8,128)S(1)} %get-tuple-element.19.inverse, ...), custom_call_target="tpu_custom_call", output_to_operand_aliasing={{0}: (5, {})} | custom-call | tf_op jit(solution)/shard_map/pallas_call | solution.py:281
  51.2 0.8 %collective-permute-done.2.window = bf16[1,2,128,512]{3,2,1,0:T(8,128)(2,1)S(1)} collective-permute-done((bf16[1,2,128,512]{3,2,1,0:T(8,128)(2,1)S(1)}, bf16[1,2,128,512]{3,2,1,0:T(8,128)(2,1)S(1)}, u32[]{:S(2)}, u32[]{:S(2)}) %collective-permute-start.2) | collective-permute-done | bytes 262176 | tf_op jit(solution)/shard_map/ppermute | solution.py:33
  52.0 1.3 %shard_map.63 = bf16[2,2,1,2,256,512]{5,4,3,2,1,0:T(8,128)(2,1)} custom-call(bf16[2,2,1,2,256,512]{5,4,3,2,1,0:T(8,128)(2,1)S(1)} %copy-done, f32[2,3,2,256,256]{4,3,2,1,0:T(8,128)S(1)} %get-tuple-element.19.inverse, bf16[1,2,128,512]{3,2,1,0:T(8,128)(2,1)S(1)} %collective-permute-done.2.window, ...), custom_call_target="tpu_custom_call", output_to_operand_aliasing={{}: (4, {})} | custom-call | tf_op jit(solution)/shard_map/pallas_call | solution.py:319
  (4 shorter events, 0.1 us)
Async XLA Ops:
  0.0 12.0 %copy-start.1 = (s32[2,8]{1,0:T(2,128)S(1)}, s32[2,8]{1,0:T(2,128)}, u32[]{:S(2)}) copy-start(s32[2,8]{1,0:T(2,128)} %partner.2) | copy-start | bytes 196
  0.0 11.2 %copy-start.4 = (s32[8,256]{1,0:T(8,128)S(1)}, s32[8,256]{1,0:T(8,128)}, u32[]{:S(2)}) copy-start(s32[8,256]{1,0:T(8,128)} %param.9) | copy-start | bytes 24580
  0.0 11.2 %copy-start.3 = (f32[8,256]{1,0:T(8,128)S(1)}, f32[8,256]{1,0:T(8,128)}, u32[]{:S(2)}) copy-start(f32[8,256]{1,0:T(8,128)} %param.8) | copy-start | bytes 24580
  0.0 12.0 %copy-start.2 = (f32[8,8]{1,0:T(8,128)S(1)}, f32[8,8]{1,0:T(8,128)}, u32[]{:S(2)}) copy-start(f32[8,8]{1,0:T(8,128)} %occ.1) | copy-start | bytes 772
  1.3 31.9 %collective-permute-start.1 = (bf16[4,2,128,512]{3,2,1,0:T(8,128)(2,1)S(1)}, bf16[4,2,128,512]{3,2,1,0:T(8,128)(2,1)S(1)}, u32[]{:S(2)}, u32[]{:S(2)}) collective-permute-start(bf16[4,2,128,512]{3,2,1,0:T(8,128)(2,1)S(1)} %shard_map.56), channel_id=1, source_target_pairs={{0,7},{1,2},{2,1},{3,4},{4,3},{5,6},{6,5},{7,0},{8,15},{9,10},{10,... | collective-permute-start | bytes 3145736 | tf_op jit(solution)/shard_map/ppermute | solution.py:33
  8.1 14.9 %collective-permute-start.5 = (bf16[2,2,128,512]{3,2,1,0:T(8,128)(2,1)S(1)}, bf16[2,2,128,512]{3,2,1,0:T(8,128)(2,1)S(1)}, u32[]{:S(2)}, u32[]{:S(2)}) collective-permute-start(bf16[2,2,128,512]{3,2,1,0:T(8,128)(2,1)S(1)} %get-tuple-element.24), channel_id=1, source_target_pairs={{0,8},{8,0},{16,24},{24,16},{1,9},{9,1},{17,25},{25,17},{2,10},{10... | collective-permute-start | bytes 1572872 | tf_op jit(solution)/shard_map/ppermute | solution.py:23
  9.7 14.9 %collective-permute-start = (bf16[2,2,128,512]{3,2,1,0:T(8,128)(2,1)S(1)}, bf16[2,2,128,512]{3,2,1,0:T(8,128)(2,1)S(1)}, u32[]{:S(2)}, u32[]{:S(2)}) collective-permute-start(bf16[2,2,128,512]{3,2,1,0:T(8,128)(2,1)S(1)} %get-tuple-element.21), channel_id=1, source_target_pairs={{0,16},{8,24},{16,0},{24,8},{1,17},{9,25},{17,1},{25,9},{2,18},{10... | collective-permute-start | bytes 1572872 | tf_op jit(solution)/shard_map/ppermute | solution.py:23
  13.6 18.3 %collective-permute-start.7 = (bf16[2,2,128,512]{3,2,1,0:T(8,128)(2,1)S(1)}, bf16[2,2,128,512]{3,2,1,0:T(8,128)(2,1)S(1)}, u32[]{:S(2)}, u32[]{:S(2)}) collective-permute-start(bf16[2,2,128,512]{3,2,1,0:T(8,128)(2,1)S(1)} %get-tuple-element.26), channel_id=1, source_target_pairs={{0,8},{8,0},{16,24},{24,16},{1,9},{9,1},{17,25},{25,17},{2,10},{10... | collective-permute-start | bytes 1572872 | tf_op jit(solution)/shard_map/ppermute | solution.py:23
  14.3 18.9 %collective-permute-start.9 = (bf16[2,2,128,512]{3,2,1,0:T(8,128)(2,1)S(1)}, bf16[2,2,128,512]{3,2,1,0:T(8,128)(2,1)S(1)}, u32[]{:S(2)}, u32[]{:S(2)}) collective-permute-start(bf16[2,2,128,512]{3,2,1,0:T(8,128)(2,1)S(1)} %get-tuple-element.29), channel_id=1, source_target_pairs={{0,16},{8,24},{16,0},{24,8},{1,17},{9,25},{17,1},{25,9},{2,18},{10... | collective-permute-start | bytes 1572872 | tf_op jit(solution)/shard_map/ppermute | solution.py:23
  24.7 10.9 %collective-permute-start.11 = (bf16[4,2,128,512]{3,2,1,0:T(8,128)(2,1)S(1)}, bf16[4,2,128,512]{3,2,1,0:T(8,128)(2,1)S(1)}, u32[]{:S(2)}, u32[]{:S(2)}) collective-permute-start(bf16[4,2,128,512]{3,2,1,0:T(8,128)(2,1)S(1)} %constant_dynamic-update-slice_fusion), channel_id=1, source_target_pairs={{0,1},{1,0},{2,3},{3,2},{4,5},{5,4},{6,7},{7,6},{8,9},{9,8},{10,11... | collective-permute-start | bytes 3145736 | tf_op jit(solution)/shard_map/ppermute | solution.py:28
  24.7 21.8 %collective-permute-start.6 = (bf16[3,2,128,512]{3,2,1,0:T(8,128)(2,1)S(1)}, bf16[3,2,128,512]{3,2,1,0:T(8,128)(2,1)S(1)}, u32[]{:S(2)}, u32[]{:S(2)}) collective-permute-start(bf16[3,2,128,512]{3,2,1,0:T(8,128)(2,1)S(1)} %slice.19), channel_id=1, source_target_pairs={{0,7},{1,2},{2,1},{3,4},{4,3},{5,6},{6,5},{7,0},{8,15},{9,10},{10,... | collective-permute-start | bytes 2359304 | tf_op jit(solution)/shard_map/ppermute | solution.py:33
  33.2 6.5 %collective-permute-start.8 = (bf16[2,2,128,512]{3,2,1,0:T(8,128)(2,1)S(1)}, bf16[2,2,128,512]{3,2,1,0:T(8,128)(2,1)S(1)}, u32[]{:S(2)}, u32[]{:S(2)}) collective-permute-start(bf16[2,2,128,512]{3,2,1,0:T(8,128)(2,1)S(1)} %collective-permute-done.7.refs_0_), channel_id=1, source_target_pairs={{0,1},{1,0},{2,3},{3,2},{4,5},{5,4},{6,7},{7,6},{8,9},{9,8},{10,11... | collective-permute-start | bytes 1572872 | tf_op jit(solution)/shard_map/ppermute | solution.py:28
  33.4 2.8 %copy-start = (bf16[2,2,1,2,256,512]{5,4,3,2,1,0:T(8,128)(2,1)S(1)}, bf16[2,2,1,2,256,512]{5,4,3,2,1,0:T(8,128)(2,1)}, u32[]{:S(2)}) copy-start(bf16[2,2,1,2,256,512]{5,4,3,2,1,0:T(8,128)(2,1)} %factor.13) | copy-start | bytes 6291460
  33.4 7.8 %collective-permute-start.10 = (bf16[2,2,128,512]{3,2,1,0:T(8,128)(2,1)S(1)}, bf16[2,2,128,512]{3,2,1,0:T(8,128)(2,1)S(1)}, u32[]{:S(2)}, u32[]{:S(2)}) collective-permute-start(bf16[2,2,128,512]{3,2,1,0:T(8,128)(2,1)S(1)} %shard_map.58), channel_id=1, source_target_pairs={{0,1},{1,0},{2,3},{3,2},{4,5},{5,4},{6,7},{7,6},{8,9},{9,8},{10,11... | collective-permute-start | bytes 1572872 | tf_op jit(solution)/shard_map/ppermute | solution.py:28
  34.0 13.9 %collective-permute-start.4 = (bf16[2,2,128,512]{3,2,1,0:T(8,128)(2,1)S(1)}, bf16[2,2,128,512]{3,2,1,0:T(8,128)(2,1)S(1)}, u32[]{:S(2)}, u32[]{:S(2)}) collective-permute-start(bf16[2,2,128,512]{3,2,1,0:T(8,128)(2,1)S(1)} %get-tuple-element.33), channel_id=1, source_target_pairs={{0,16},{8,24},{16,0},{24,8},{1,17},{9,25},{17,1},{25,9},{2,18},{10... | collective-permute-start | bytes 1572872 | tf_op jit(solution)/shard_map/ppermute | solution.py:23
  35.6 13.6 %collective-permute-start.3 = (bf16[2,2,128,512]{3,2,1,0:T(8,128)(2,1)S(1)}, bf16[2,2,128,512]{3,2,1,0:T(8,128)(2,1)S(1)}, u32[]{:S(2)}, u32[]{:S(2)}) collective-permute-start(bf16[2,2,128,512]{3,2,1,0:T(8,128)(2,1)S(1)} %get-tuple-element.34), channel_id=1, source_target_pairs={{0,8},{8,0},{16,24},{24,16},{1,9},{9,1},{17,25},{25,17},{2,10},{10... | collective-permute-start | bytes 1572872 | tf_op jit(solution)/shard_map/ppermute | solution.py:23
  39.7 12.3 %collective-permute-start.2 = (bf16[1,2,128,512]{3,2,1,0:T(8,128)(2,1)S(1)}, bf16[1,2,128,512]{3,2,1,0:T(8,128)(2,1)S(1)}, u32[]{:S(2)}, u32[]{:S(2)}) collective-permute-start(bf16[1,2,128,512]{3,2,1,0:T(8,128)(2,1)S(1)} %slice.16), channel_id=1, source_target_pairs={{0,7},{1,2},{2,1},{3,4},{4,3},{5,6},{6,5},{7,0},{8,15},{9,10},{10,... | collective-permute-start | bytes 786440 | tf_op jit(solution)/shard_map/ppermute | solution.py:33

commit v16 on v15

--- a/solution.py
+++ b/solution.py
@@ -306,10 +306,13 @@
             waiting.append(amplitude_rows(factor[t, k, 0, :, rows, :], terms))
         for r, (sides, blocks) in enumerate(waiting):
             rows = half_of(r, nv // 2)
+            n = len(copies)
             for part in range(parts):
                 value = jnp.dot(sides[part], blocks, preferred_element_type=F32)
-                target = out.at[t, k, 0, part, pl.ds(rows.start, nv // 2)]
-                send_part(copies, value + total[t, k, part, rows], target, staged, sems)
+                staged[n, part] = (value + total[t, k, part, rows]).astype(BF16)
+            target = out.at[t, k, 0, :, pl.ds(rows.start, nv // 2)]
+            copies.append(pltpu.make_async_copy(staged.at[n], target, sems.at[n]))
+            copies[-1].start()
     for copy in copies:
         copy.wait()
 
@@ -321,7 +324,10 @@
         out_shape=jax.ShapeDtypeStruct(factor.shape, BF16),
         in_specs=[VMEM] * 4 + [ANY],
         out_specs=ANY,
-        scratch_shapes=out_scratch((transfers * kc - done) * parts * 2, nv // 2, naux),
+        scratch_shapes=[
+            pltpu.VMEM((2 * (transfers * kc - done), parts, nv // 2, naux), BF16),
+            pltpu.SemaphoreType.DMA((2 * (transfers * kc - done),)),
+        ],
         input_output_aliases={4: 0},
         cost_estimate=COST,
         compiler_params=PARAMS,

time: 53.5 us -> 53.5 us (level)
  no operation moved by 1% of the time
where the time goes in v16:
time: 53.5 us; the launch traced here: 53.4 us
  waiting for transfers between devices  23.4 us (44%)
  Pallas kernels  15 us (28%)
  starting transfers between devices  13.5 us (25%)
  other arithmetic  0.94 us (2%)
    ppermute x6, waiting for transfers between devices, group_swap(): return lax.ppermute(block, 'kpt', [(g, g ^ 1 << bit) for g in range(count)])  19 us
    ppermute x3, starting transfers between devices, far_swap(): lax.ppermute(block, 'occ', [(i, (i + (1 if i % 2 else count - 1)) % count...  6.52 us
    ppermute x6, starting transfers between devices, group_swap(): return lax.ppermute(block, 'kpt', [(g, g ^ 1 << bit) for g in range(count)])  6.33 us
    ppermute x3, waiting for transfers between devices, far_swap(): lax.ppermute(block, 'occ', [(i, (i + (1 if i % 2 else count - 1)) % count...  4.47 us
    pallas_call x1, Pallas kernels, first_terms(): pl.pallas_call(first_kernel, out_shape=jax.ShapeDtypeStruct((transfers, k...  3.52 us
    pallas_call x2, Pallas kernels, add_terms(): pl.pallas_call(functools.partial(add_kernel, place, h), out_shape=jax.Sha...  2.92 us
    pallas_call x1, Pallas kernels, pack(): pl.pallas_call(functools.partial(pack_kernel, bits), out_shape=[jax.Shape...  2.27 us
    pallas_call x1, Pallas kernels, far_terms(): pl.pallas_call(functools.partial(far_kernel, done), out_shape=[jax.ShapeD...  2.07 us
  transfers between devices with their start and end apart: 12, of which 8 were waited for; matrix products, arithmetic and copies ran while one was open for 2% of the time, Pallas kernels for 23%

profile of v16, /device:TPU:0, one launch (start us, length us, event | category | flops | bytes accessed | tf_op | source)
XLA Modules:
  0.0 53.4 jit_solution(6786619887784405904)
XLA Ops:
  0.0 0.0 copy-start.1
  0.0 0.0 copy-start.4
  0.0 0.0 copy-start.3
  0.0 0.0 copy-start.2
  0.0 1.3 %shard_map.56 = bf16[4,2,128,512]{3,2,1,0:T(8,128)(2,1)S(1)} custom-call(bf16[2,2,1,2,256,512]{5,4,3,2,1,0:T(8,128)(2,1)} %factor.13), custom_call_target="tpu_custom_call" | custom-call | tf_op jit(solution)/shard_map/pallas_call | solution.py:65
  1.3 4.5 %collective-permute-start.1 = (bf16[4,2,128,512]{3,2,1,0:T(8,128)(2,1)S(1)}, bf16[4,2,128,512]{3,2,1,0:T(8,128)(2,1)S(1)}, u32[]{:S(2)}, u32[]{:S(2)}) collective-permute-start(bf16[4,2,128,512]{3,2,1,0:T(8,128)(2,1)S(1)} %shard_map.56), channel_id=1, source_target_pairs={{0,7},{1,2},{2,1},{3,4},{4,3},{5,6},{6,5},{7,0},{8,15},{9,10},{10,... | collective-permute-start | bytes 3145736 | tf_op jit(solution)/shard_map/ppermute | solution.py:33
  5.8 2.3 %shard_map.57 = (bf16[2,2,128,512]{3,2,1,0:T(8,128)(2,1)S(1)}, bf16[2,2,128,512]{3,2,1,0:T(8,128)(2,1)S(1)}, bf16[2,2,128,512]{3,2,1,0:T(8,128)(2,1)S(1)}, bf16[2,2,128,512]{3,2,1,0:T(8,128)(2,1)S(1)}) custom-call(s32[2,8]{1,0:T(2,128)} %partner.2, bf16[2,2,1,2,256,512]{5,4,3,2,1,0:T(8,128)(2,1)} %factor.13), custom_call_target="tpu_custom_call" | custom-call | bytes 16777216 | tf_op jit(solution)/shard_map/pallas_call | solution.py:96
  8.1 1.6 %collective-permute-start.5 = (bf16[2,2,128,512]{3,2,1,0:T(8,128)(2,1)S(1)}, bf16[2,2,128,512]{3,2,1,0:T(8,128)(2,1)S(1)}, u32[]{:S(2)}, u32[]{:S(2)}) collective-permute-start(bf16[2,2,128,512]{3,2,1,0:T(8,128)(2,1)S(1)} %get-tuple-element.24), channel_id=1, source_target_pairs={{0,8},{8,0},{16,24},{24,16},{1,9},{9,1},{17,25},{25,17},{2,10},{10... | collective-permute-start | bytes 1572872 | tf_op jit(solution)/shard_map/ppermute | solution.py:23
  9.7 1.5 %collective-permute-start = (bf16[2,2,128,512]{3,2,1,0:T(8,128)(2,1)S(1)}, bf16[2,2,128,512]{3,2,1,0:T(8,128)(2,1)S(1)}, u32[]{:S(2)}, u32[]{:S(2)}) collective-permute-start(bf16[2,2,128,512]{3,2,1,0:T(8,128)(2,1)S(1)} %get-tuple-element.21), channel_id=1, source_target_pairs={{0,16},{8,24},{16,0},{24,8},{1,17},{9,25},{17,1},{25,9},{2,18},{10... | collective-permute-start | bytes 1572872 | tf_op jit(solution)/shard_map/ppermute | solution.py:23
  11.2 0.0 copy-done.4
  11.2 0.0 copy-done.3
  11.2 0.8 %select_reduce_fusion.virtual = f32[8,256]{1,0:T(8,128)S(1)} fusion(f32[8,256]{1,0:T(8,128)S(1)} %copy-done.3, s32[8,256]{1,0:T(8,128)S(1)} %copy-done.4), kind=kLoop, calls=%fused_computation | loop fusion | flops 1570816 | bytes 24576 | tf_op jit(solution)/shard_map/reduce_sum | solution.py:45
  12.0 0.0 copy-done.1
  12.0 0.0 copy-done.2
  12.0 1.6 %shard_map.55 = (f32[2,3,2,256,256]{4,3,2,1,0:T(8,128)S(1)}, bf16[2,2,2,16,512]{4,3,2,1,0:T(8,128)(2,1)S(1)}) custom-call(s32[2,8]{1,0:T(2,128)S(1)} %copy-done.1, f32[8,8]{1,0:T(8,128)S(1)} %copy-done.2, f32[8,256]{1,0:T(8,128)S(1)} %select_reduce_fusion.virtual), custom_call_target="tpu_custom_call" | custom-call | tf_op jit(solution)/shard_map/pallas_call | solution.py:137
  13.6 0.6 %collective-permute-start.7 = (bf16[2,2,128,512]{3,2,1,0:T(8,128)(2,1)S(1)}, bf16[2,2,128,512]{3,2,1,0:T(8,128)(2,1)S(1)}, u32[]{:S(2)}, u32[]{:S(2)}) collective-permute-start(bf16[2,2,128,512]{3,2,1,0:T(8,128)(2,1)S(1)} %get-tuple-element.26), channel_id=1, source_target_pairs={{0,8},{8,0},{16,24},{24,16},{1,9},{9,1},{17,25},{25,17},{2,10},{10... | collective-permute-start | bytes 1572872 | tf_op jit(solution)/shard_map/ppermute | solution.py:23
  14.2 0.5 collective-permute-start.9
  14.7 8.3 %collective-permute-done.5.refs_2_ = bf16[2,2,128,512]{3,2,1,0:T(8,128)(2,1)S(1)} collective-permute-done((bf16[2,2,128,512]{3,2,1,0:T(8,128)(2,1)S(1)}, bf16[2,2,128,512]{3,2,1,0:T(8,128)(2,1)S(1)}, u32[]{:S(2)}, u32[]{:S(2)}) %collective-permute-start.5) | collective-permute-done | bytes 524320 | tf_op jit(solution)/shard_map/ppermute | solution.py:23
  23.1 1.5 %collective-permute-done.refs_3_ = bf16[2,2,128,512]{3,2,1,0:T(8,128)(2,1)S(1)} collective-permute-done((bf16[2,2,128,512]{3,2,1,0:T(8,128)(2,1)S(1)}, bf16[2,2,128,512]{3,2,1,0:T(8,128)(2,1)S(1)}, u32[]{:S(2)}, u32[]{:S(2)}) %collective-permute-start) | collective-permute-done | bytes 524320 | tf_op jit(solution)/shard_map/ppermute | solution.py:23
  24.6 0.1 slice.19
  24.6 0.1 collective-permute-start.11
  24.7 0.6 %collective-permute-start.6 = (bf16[3,2,128,512]{3,2,1,0:T(8,128)(2,1)S(1)}, bf16[3,2,128,512]{3,2,1,0:T(8,128)(2,1)S(1)}, u32[]{:S(2)}, u32[]{:S(2)}) collective-permute-start(bf16[3,2,128,512]{3,2,1,0:T(8,128)(2,1)S(1)} %slice.19), channel_id=1, source_target_pairs={{0,7},{1,2},{2,1},{3,4},{4,3},{5,6},{6,5},{7,0},{8,15},{9,10},{10,... | collective-permute-start | bytes 2359304 | tf_op jit(solution)/shard_map/ppermute | solution.py:33
  25.3 6.6 %collective-permute-done.7.refs_0_ = bf16[2,2,128,512]{3,2,1,0:T(8,128)(2,1)S(1)} collective-permute-done((bf16[2,2,128,512]{3,2,1,0:T(8,128)(2,1)S(1)}, bf16[2,2,128,512]{3,2,1,0:T(8,128)(2,1)S(1)}, u32[]{:S(2)}, u32[]{:S(2)}) %collective-permute-start.7) | collective-permute-done | bytes 524320 | tf_op jit(solution)/shard_map/ppermute | solution.py:23
  31.9 1.2 %collective-permute-done.9.refs_1_ = bf16[2,2,128,512]{3,2,1,0:T(8,128)(2,1)S(1)} collective-permute-done((bf16[2,2,128,512]{3,2,1,0:T(8,128)(2,1)S(1)}, bf16[2,2,128,512]{3,2,1,0:T(8,128)(2,1)S(1)}, u32[]{:S(2)}, u32[]{:S(2)}) %collective-permute-start.9) | collective-permute-done | bytes 524320 | tf_op jit(solution)/shard_map/ppermute | solution.py:23
  33.1 0.1 pad_maximum_fusion.source
  33.2 0.0 collective-permute-done.1
  33.2 0.1 collective-permute-start.8
  33.3 0.0 copy-start
  33.3 0.6 %collective-permute-start.10 = (bf16[2,2,128,512]{3,2,1,0:T(8,128)(2,1)S(1)}, bf16[2,2,128,512]{3,2,1,0:T(8,128)(2,1)S(1)}, u32[]{:S(2)}, u32[]{:S(2)}) collective-permute-start(bf16[2,2,128,512]{3,2,1,0:T(8,128)(2,1)S(1)} %shard_map.58), channel_id=1, source_target_pairs={{0,1},{1,0},{2,3},{3,2},{4,5},{5,4},{6,7},{7,6},{8,9},{9,8},{10,11... | collective-permute-start | bytes 1572872 | tf_op jit(solution)/shard_map/ppermute | solution.py:28
  33.9 0.1 fusion
  34.0 1.6 %collective-permute-start.4 = (bf16[2,2,128,512]{3,2,1,0:T(8,128)(2,1)S(1)}, bf16[2,2,128,512]{3,2,1,0:T(8,128)(2,1)S(1)}, u32[]{:S(2)}, u32[]{:S(2)}) collective-permute-start(bf16[2,2,128,512]{3,2,1,0:T(8,128)(2,1)S(1)} %get-tuple-element.33), channel_id=1, source_target_pairs={{0,16},{8,24},{16,0},{24,8},{1,17},{9,25},{17,1},{25,9},{2,18},{10... | collective-permute-start | bytes 1572872 | tf_op jit(solution)/shard_map/ppermute | solution.py:23
  35.6 0.0 collective-permute-done.11.refs_4_
  35.6 0.6 %collective-permute-start.3 = (bf16[2,2,128,512]{3,2,1,0:T(8,128)(2,1)S(1)}, bf16[2,2,128,512]{3,2,1,0:T(8,128)(2,1)S(1)}, u32[]{:S(2)}, u32[]{:S(2)}) collective-permute-start(bf16[2,2,128,512]{3,2,1,0:T(8,128)(2,1)S(1)} %get-tuple-element.34), channel_id=1, source_target_pairs={{0,8},{8,0},{16,24},{24,16},{1,9},{9,1},{17,25},{25,17},{2,10},{10... | collective-permute-start | bytes 1572872 | tf_op jit(solution)/shard_map/ppermute | solution.py:23
  36.1 0.0 copy-done
  36.2 3.5 %shard_map.59.total = f32[2,2,2,256,512]{4,3,2,1,0:T(8,128)S(1)} custom-call(bf16[2,2,1,2,256,512]{5,4,3,2,1,0:T(8,128)(2,1)S(1)} %copy-done, f32[2,3,2,256,256]{4,3,2,1,0:T(8,128)S(1)} %get-tuple-element.19.inverse, bf16[2,2,128,512]{3,2,1,0:T(8,128)(2,1)S(1)} %collective-permute-done.7.refs_0_, ...), custom_call_target="tpu_custom_call" | custom-call | tf_op jit(solution)/shard_map/pallas_call | solution.py:208
  39.7 0.0 collective-permute-done.8
  39.7 1.4 %collective-permute-start.2 = (bf16[1,2,128,512]{3,2,1,0:T(8,128)(2,1)S(1)}, bf16[1,2,128,512]{3,2,1,0:T(8,128)(2,1)S(1)}, u32[]{:S(2)}, u32[]{:S(2)}) collective-permute-start(bf16[1,2,128,512]{3,2,1,0:T(8,128)(2,1)S(1)} %slice.16), channel_id=1, source_target_pairs={{0,7},{1,2},{2,1},{3,4},{4,3},{5,6},{6,5},{7,0},{8,15},{9,10},{10,... | collective-permute-start | bytes 786440 | tf_op jit(solution)/shard_map/ppermute | solution.py:33
  41.1 0.0 collective-permute-done.10
  41.1 0.1 pad_maximum_fusion.1.window
  41.2 1.6 %shard_map.60.total = f32[2,2,2,256,512]{4,3,2,1,0:T(8,128)S(1)} custom-call(bf16[2,2,1,2,256,512]{5,4,3,2,1,0:T(8,128)(2,1)S(1)} %copy-done, f32[2,3,2,256,256]{4,3,2,1,0:T(8,128)S(1)} %get-tuple-element.19.inverse, bf16[4,2,128,512]{3,2,1,0:T(8,128)(2,1)S(1)} %pad_maximum_fusion.1.window, ...), custom_call_target="tpu_custom_call", output_to_operand_aliasing={{}: (3, {})} | custom-call | tf_op jit(solution)/shard_map/pallas_call | solution.py:233
  42.8 3.7 %collective-permute-done.6.window = bf16[3,2,128,512]{3,2,1,0:T(8,128)(2,1)S(1)} collective-permute-done((bf16[3,2,128,512]{3,2,1,0:T(8,128)(2,1)S(1)}, bf16[3,2,128,512]{3,2,1,0:T(8,128)(2,1)S(1)}, u32[]{:S(2)}, u32[]{:S(2)}) %collective-permute-start.6) | collective-permute-done | bytes 786464 | tf_op jit(solution)/shard_map/ppermute | solution.py:33
  46.5 1.3 %shard_map.61.refs_2_ = f32[2,2,2,256,512]{4,3,2,1,0:T(8,128)S(1)} custom-call(bf16[2,2,1,2,256,512]{5,4,3,2,1,0:T(8,128)(2,1)S(1)} %copy-done, f32[2,3,2,256,256]{4,3,2,1,0:T(8,128)S(1)} %get-tuple-element.19.inverse, bf16[3,2,128,512]{3,2,1,0:T(8,128)(2,1)S(1)} %collective-permute-done.6.window, ...), custom_call_target="tpu_custom_call", output_to_operand_aliasing={{}: (3, {})} | custom-call | flops 3145728000 | tf_op jit(solution)/shard_map/pallas_call | solution.py:233
  47.8 0.1 collective-permute-done.4.refs_1_
  47.9 1.2 %collective-permute-done.3.refs_0_ = bf16[2,2,128,512]{3,2,1,0:T(8,128)(2,1)S(1)} collective-permute-done((bf16[2,2,128,512]{3,2,1,0:T(8,128)(2,1)S(1)}, bf16[2,2,128,512]{3,2,1,0:T(8,128)(2,1)S(1)}, u32[]{:S(2)}, u32[]{:S(2)}) %collective-permute-start.3) | collective-permute-done | bytes 524320 | tf_op jit(solution)/shard_map/ppermute | solution.py:23
  49.1 2.1 %shard_map.62 = (f32[2,2,2,256,512]{4,3,2,1,0:T(8,128)S(1)}, bf16[2,2,1,2,256,512]{5,4,3,2,1,0:T(8,128)(2,1)}) custom-call(bf16[2,2,1,2,256,512]{5,4,3,2,1,0:T(8,128)(2,1)S(1)} %copy-done, f32[2,3,2,256,256]{4,3,2,1,0:T(8,128)S(1)} %get-tuple-element.19.inverse, ...), custom_call_target="tpu_custom_call", output_to_operand_aliasing={{0}: (5, {})} | custom-call | tf_op jit(solution)/shard_map/pallas_call | solution.py:281
  51.2 0.8 %collective-permute-done.2.window = bf16[1,2,128,512]{3,2,1,0:T(8,128)(2,1)S(1)} collective-permute-done((bf16[1,2,128,512]{3,2,1,0:T(8,128)(2,1)S(1)}, bf16[1,2,128,512]{3,2,1,0:T(8,128)(2,1)S(1)}, u32[]{:S(2)}, u32[]{:S(2)}) %collective-permute-start.2) | collective-permute-done | bytes 262176 | tf_op jit(solution)/shard_map/ppermute | solution.py:33
  52.0 1.3 %shard_map.63 = bf16[2,2,1,2,256,512]{5,4,3,2,1,0:T(8,128)(2,1)} custom-call(bf16[2,2,1,2,256,512]{5,4,3,2,1,0:T(8,128)(2,1)S(1)} %copy-done, f32[2,3,2,256,256]{4,3,2,1,0:T(8,128)S(1)} %get-tuple-element.19.inverse, bf16[1,2,128,512]{3,2,1,0:T(8,128)(2,1)S(1)} %collective-permute-done.2.window, ...), custom_call_target="tpu_custom_call", output_to_operand_aliasing={{}: (4, {})} | custom-call | tf_op jit(solution)/shard_map/pallas_call | solution.py:322
  (4 shorter events, 0.1 us)
Async XLA Ops:
  0.0 12.0 %copy-start.1 = (s32[2,8]{1,0:T(2,128)S(1)}, s32[2,8]{1,0:T(2,128)}, u32[]{:S(2)}) copy-start(s32[2,8]{1,0:T(2,128)} %partner.2) | copy-start | bytes 196
  0.0 11.2 %copy-start.4 = (s32[8,256]{1,0:T(8,128)S(1)}, s32[8,256]{1,0:T(8,128)}, u32[]{:S(2)}) copy-start(s32[8,256]{1,0:T(8,128)} %param.9) | copy-start | bytes 24580
  0.0 11.2 %copy-start.3 = (f32[8,256]{1,0:T(8,128)S(1)}, f32[8,256]{1,0:T(8,128)}, u32[]{:S(2)}) copy-start(f32[8,256]{1,0:T(8,128)} %param.8) | copy-start | bytes 24580
  0.0 12.0 %copy-start.2 = (f32[8,8]{1,0:T(8,128)S(1)}, f32[8,8]{1,0:T(8,128)}, u32[]{:S(2)}) copy-start(f32[8,8]{1,0:T(8,128)} %occ.1) | copy-start | bytes 772
  1.3 31.9 %collective-permute-start.1 = (bf16[4,2,128,512]{3,2,1,0:T(8,128)(2,1)S(1)}, bf16[4,2,128,512]{3,2,1,0:T(8,128)(2,1)S(1)}, u32[]{:S(2)}, u32[]{:S(2)}) collective-permute-start(bf16[4,2,128,512]{3,2,1,0:T(8,128)(2,1)S(1)} %shard_map.56), channel_id=1, source_target_pairs={{0,7},{1,2},{2,1},{3,4},{4,3},{5,6},{6,5},{7,0},{8,15},{9,10},{10,... | collective-permute-start | bytes 3145736 | tf_op jit(solution)/shard_map/ppermute | solution.py:33
  8.1 14.9 %collective-permute-start.5 = (bf16[2,2,128,512]{3,2,1,0:T(8,128)(2,1)S(1)}, bf16[2,2,128,512]{3,2,1,0:T(8,128)(2,1)S(1)}, u32[]{:S(2)}, u32[]{:S(2)}) collective-permute-start(bf16[2,2,128,512]{3,2,1,0:T(8,128)(2,1)S(1)} %get-tuple-element.24), channel_id=1, source_target_pairs={{0,8},{8,0},{16,24},{24,16},{1,9},{9,1},{17,25},{25,17},{2,10},{10... | collective-permute-start | bytes 1572872 | tf_op jit(solution)/shard_map/ppermute | solution.py:23
  9.7 14.9 %collective-permute-start = (bf16[2,2,128,512]{3,2,1,0:T(8,128)(2,1)S(1)}, bf16[2,2,128,512]{3,2,1,0:T(8,128)(2,1)S(1)}, u32[]{:S(2)}, u32[]{:S(2)}) collective-permute-start(bf16[2,2,128,512]{3,2,1,0:T(8,128)(2,1)S(1)} %get-tuple-element.21), channel_id=1, source_target_pairs={{0,16},{8,24},{16,0},{24,8},{1,17},{9,25},{17,1},{25,9},{2,18},{10... | collective-permute-start | bytes 1572872 | tf_op jit(solution)/shard_map/ppermute | solution.py:23
  13.6 18.3 %collective-permute-start.7 = (bf16[2,2,128,512]{3,2,1,0:T(8,128)(2,1)S(1)}, bf16[2,2,128,512]{3,2,1,0:T(8,128)(2,1)S(1)}, u32[]{:S(2)}, u32[]{:S(2)}) collective-permute-start(bf16[2,2,128,512]{3,2,1,0:T(8,128)(2,1)S(1)} %get-tuple-element.26), channel_id=1, source_target_pairs={{0,8},{8,0},{16,24},{24,16},{1,9},{9,1},{17,25},{25,17},{2,10},{10... | collective-permute-start | bytes 1572872 | tf_op jit(solution)/shard_map/ppermute | solution.py:23
  14.2 18.9 %collective-permute-start.9 = (bf16[2,2,128,512]{3,2,1,0:T(8,128)(2,1)S(1)}, bf16[2,2,128,512]{3,2,1,0:T(8,128)(2,1)S(1)}, u32[]{:S(2)}, u32[]{:S(2)}) collective-permute-start(bf16[2,2,128,512]{3,2,1,0:T(8,128)(2,1)S(1)} %get-tuple-element.29), channel_id=1, source_target_pairs={{0,16},{8,24},{16,0},{24,8},{1,17},{9,25},{17,1},{25,9},{2,18},{10... | collective-permute-start | bytes 1572872 | tf_op jit(solution)/shard_map/ppermute | solution.py:23
  24.6 10.9 %collective-permute-start.11 = (bf16[4,2,128,512]{3,2,1,0:T(8,128)(2,1)S(1)}, bf16[4,2,128,512]{3,2,1,0:T(8,128)(2,1)S(1)}, u32[]{:S(2)}, u32[]{:S(2)}) collective-permute-start(bf16[4,2,128,512]{3,2,1,0:T(8,128)(2,1)S(1)} %constant_dynamic-update-slice_fusion), channel_id=1, source_target_pairs={{0,1},{1,0},{2,3},{3,2},{4,5},{5,4},{6,7},{7,6},{8,9},{9,8},{10,11... | collective-permute-start | bytes 3145736 | tf_op jit(solution)/shard_map/ppermute | solution.py:28
  24.7 21.8 %collective-permute-start.6 = (bf16[3,2,128,512]{3,2,1,0:T(8,128)(2,1)S(1)}, bf16[3,2,128,512]{3,2,1,0:T(8,128)(2,1)S(1)}, u32[]{:S(2)}, u32[]{:S(2)}) collective-permute-start(bf16[3,2,128,512]{3,2,1,0:T(8,128)(2,1)S(1)} %slice.19), channel_id=1, source_target_pairs={{0,7},{1,2},{2,1},{3,4},{4,3},{5,6},{6,5},{7,0},{8,15},{9,10},{10,... | collective-permute-start | bytes 2359304 | tf_op jit(solution)/shard_map/ppermute | solution.py:33
  33.2 6.5 %collective-permute-start.8 = (bf16[2,2,128,512]{3,2,1,0:T(8,128)(2,1)S(1)}, bf16[2,2,128,512]{3,2,1,0:T(8,128)(2,1)S(1)}, u32[]{:S(2)}, u32[]{:S(2)}) collective-permute-start(bf16[2,2,128,512]{3,2,1,0:T(8,128)(2,1)S(1)} %collective-permute-done.7.refs_0_), channel_id=1, source_target_pairs={{0,1},{1,0},{2,3},{3,2},{4,5},{5,4},{6,7},{7,6},{8,9},{9,8},{10,11... | collective-permute-start | bytes 1572872 | tf_op jit(solution)/shard_map/ppermute | solution.py:28
  33.3 2.8 %copy-start = (bf16[2,2,1,2,256,512]{5,4,3,2,1,0:T(8,128)(2,1)S(1)}, bf16[2,2,1,2,256,512]{5,4,3,2,1,0:T(8,128)(2,1)}, u32[]{:S(2)}) copy-start(bf16[2,2,1,2,256,512]{5,4,3,2,1,0:T(8,128)(2,1)} %factor.13) | copy-start | bytes 6291460
  33.3 7.7 %collective-permute-start.10 = (bf16[2,2,128,512]{3,2,1,0:T(8,128)(2,1)S(1)}, bf16[2,2,128,512]{3,2,1,0:T(8,128)(2,1)S(1)}, u32[]{:S(2)}, u32[]{:S(2)}) collective-permute-start(bf16[2,2,128,512]{3,2,1,0:T(8,128)(2,1)S(1)} %shard_map.58), channel_id=1, source_target_pairs={{0,1},{1,0},{2,3},{3,2},{4,5},{5,4},{6,7},{7,6},{8,9},{9,8},{10,11... | collective-permute-start | bytes 1572872 | tf_op jit(solution)/shard_map/ppermute | solution.py:28
  34.0 13.9 %collective-permute-start.4 = (bf16[2,2,128,512]{3,2,1,0:T(8,128)(2,1)S(1)}, bf16[2,2,128,512]{3,2,1,0:T(8,128)(2,1)S(1)}, u32[]{:S(2)}, u32[]{:S(2)}) collective-permute-start(bf16[2,2,128,512]{3,2,1,0:T(8,128)(2,1)S(1)} %get-tuple-element.33), channel_id=1, source_target_pairs={{0,16},{8,24},{16,0},{24,8},{1,17},{9,25},{17,1},{25,9},{2,18},{10... | collective-permute-start | bytes 1572872 | tf_op jit(solution)/shard_map/ppermute | solution.py:23
  35.6 13.6 %collective-permute-start.3 = (bf16[2,2,128,512]{3,2,1,0:T(8,128)(2,1)S(1)}, bf16[2,2,128,512]{3,2,1,0:T(8,128)(2,1)S(1)}, u32[]{:S(2)}, u32[]{:S(2)}) collective-permute-start(bf16[2,2,128,512]{3,2,1,0:T(8,128)(2,1)S(1)} %get-tuple-element.34), channel_id=1, source_target_pairs={{0,8},{8,0},{16,24},{24,16},{1,9},{9,1},{17,25},{25,17},{2,10},{10... | collective-permute-start | bytes 1572872 | tf_op jit(solution)/shard_map/ppermute | solution.py:23
  39.7 12.3 %collective-permute-start.2 = (bf16[1,2,128,512]{3,2,1,0:T(8,128)(2,1)S(1)}, bf16[1,2,128,512]{3,2,1,0:T(8,128)(2,1)S(1)}, u32[]{:S(2)}, u32[]{:S(2)}) collective-permute-start(bf16[1,2,128,512]{3,2,1,0:T(8,128)(2,1)S(1)} %slice.16), channel_id=1, source_target_pairs={{0,7},{1,2},{2,1},{3,4},{4,3},{5,6},{6,5},{7,0},{8,15},{9,10},{10,... | collective-permute-start | bytes 786440 | tf_op jit(solution)/shard_map/ppermute | solution.py:33

commit v17 on v15

--- a/solution.py
+++ b/solution.py
@@ -300,15 +300,15 @@
     for at in range(done, transfers * kc):
         t, k = at // kc, at % kc
         waiting = []
-        for r in range(2):
-            rows = half_of(r, nv // 2)
+        for r in range(4):
+            rows = half_of(r, nv // 4)
             terms = [(window[at - done], inverse[t, 2, k, rows, half_of(1, half)])]
             waiting.append(amplitude_rows(factor[t, k, 0, :, rows, :], terms))
         for r, (sides, blocks) in enumerate(waiting):
-            rows = half_of(r, nv // 2)
+            rows = half_of(r, nv // 4)
             for part in range(parts):
                 value = jnp.dot(sides[part], blocks, preferred_element_type=F32)
-                target = out.at[t, k, 0, part, pl.ds(rows.start, nv // 2)]
+                target = out.at[t, k, 0, part, pl.ds(rows.start, nv // 4)]
                 send_part(copies, value + total[t, k, part, rows], target, staged, sems)
     for copy in copies:
         copy.wait()
@@ -321,7 +321,7 @@
         out_shape=jax.ShapeDtypeStruct(factor.shape, BF16),
         in_specs=[VMEM] * 4 + [ANY],
         out_specs=ANY,
-        scratch_shapes=out_scratch((transfers * kc - done) * parts * 2, nv // 2, naux),
+        scratch_shapes=out_scratch((transfers * kc - done) * parts * 4, nv // 4, naux),
         input_output_aliases={4: 0},
         cost_estimate=COST,
         compiler_params=PARAMS,

time: 53.5 us -> 53.7 us (level)
  no operation moved by 1% of the time
where the time goes in v17:
time: 53.7 us; the launch traced here: 53.5 us
  waiting for transfers between devices  23.4 us (44%)
  Pallas kernels  15.2 us (28%)
  starting transfers between devices  13.5 us (25%)
  other arithmetic  0.94 us (2%)
    ppermute x6, waiting for transfers between devices, group_swap(): return lax.ppermute(block, 'kpt', [(g, g ^ 1 << bit) for g in range(count)])  18.9 us
    ppermute x3, starting transfers between devices, far_swap(): lax.ppermute(block, 'occ', [(i, (i + (1 if i % 2 else count - 1)) % count...  6.52 us
    ppermute x6, starting transfers between devices, group_swap(): return lax.ppermute(block, 'kpt', [(g, g ^ 1 << bit) for g in range(count)])  6.3 us
    ppermute x3, waiting for transfers between devices, far_swap(): lax.ppermute(block, 'occ', [(i, (i + (1 if i % 2 else count - 1)) % count...  4.5 us
    pallas_call x1, Pallas kernels, first_terms(): pl.pallas_call(first_kernel, out_shape=jax.ShapeDtypeStruct((transfers, k...  3.52 us
    pallas_call x2, Pallas kernels, add_terms(): pl.pallas_call(functools.partial(add_kernel, place, h), out_shape=jax.Sha...  2.92 us
    pallas_call x1, Pallas kernels, pack(): pl.pallas_call(functools.partial(pack_kernel, bits), out_shape=[jax.Shape...  2.3 us
    pallas_call x1, Pallas kernels, far_terms(): pl.pallas_call(functools.partial(far_kernel, done), out_shape=[jax.ShapeD...  2.07 us
  transfers between devices with their start and end apart: 12, of which 8 were waited for; matrix products, arithmetic and copies ran while one was open for 2% of the time, Pallas kernels for 23%

profile of v17, /device:TPU:0, one launch (start us, length us, event | category | flops | bytes accessed | tf_op | source)
XLA Modules:
  0.0 53.5 jit_solution(4189238369591889943)
XLA Ops:
  0.0 0.0 copy-start.1
  0.0 0.0 copy-start.4
  0.0 0.0 copy-start.3
  0.0 0.0 copy-start.2
  0.0 1.3 %shard_map.56 = bf16[4,2,128,512]{3,2,1,0:T(8,128)(2,1)S(1)} custom-call(bf16[2,2,1,2,256,512]{5,4,3,2,1,0:T(8,128)(2,1)} %factor.13), custom_call_target="tpu_custom_call" | custom-call | tf_op jit(solution)/shard_map/pallas_call | solution.py:65
  1.3 4.5 %collective-permute-start.1 = (bf16[4,2,128,512]{3,2,1,0:T(8,128)(2,1)S(1)}, bf16[4,2,128,512]{3,2,1,0:T(8,128)(2,1)S(1)}, u32[]{:S(2)}, u32[]{:S(2)}) collective-permute-start(bf16[4,2,128,512]{3,2,1,0:T(8,128)(2,1)S(1)} %shard_map.56), channel_id=1, source_target_pairs={{0,7},{1,2},{2,1},{3,4},{4,3},{5,6},{6,5},{7,0},{8,15},{9,10},{10,... | collective-permute-start | bytes 3145736 | tf_op jit(solution)/shard_map/ppermute | solution.py:33
  5.8 2.3 %shard_map.57 = (bf16[2,2,128,512]{3,2,1,0:T(8,128)(2,1)S(1)}, bf16[2,2,128,512]{3,2,1,0:T(8,128)(2,1)S(1)}, bf16[2,2,128,512]{3,2,1,0:T(8,128)(2,1)S(1)}, bf16[2,2,128,512]{3,2,1,0:T(8,128)(2,1)S(1)}) custom-call(s32[2,8]{1,0:T(2,128)} %partner.2, bf16[2,2,1,2,256,512]{5,4,3,2,1,0:T(8,128)(2,1)} %factor.13), custom_call_target="tpu_custom_call" | custom-call | bytes 16777216 | tf_op jit(solution)/shard_map/pallas_call | solution.py:96
  8.1 1.5 %collective-permute-start.5 = (bf16[2,2,128,512]{3,2,1,0:T(8,128)(2,1)S(1)}, bf16[2,2,128,512]{3,2,1,0:T(8,128)(2,1)S(1)}, u32[]{:S(2)}, u32[]{:S(2)}) collective-permute-start(bf16[2,2,128,512]{3,2,1,0:T(8,128)(2,1)S(1)} %get-tuple-element.24), channel_id=1, source_target_pairs={{0,8},{8,0},{16,24},{24,16},{1,9},{9,1},{17,25},{25,17},{2,10},{10... | collective-permute-start | bytes 1572872 | tf_op jit(solution)/shard_map/ppermute | solution.py:23
  9.7 1.5 %collective-permute-start = (bf16[2,2,128,512]{3,2,1,0:T(8,128)(2,1)S(1)}, bf16[2,2,128,512]{3,2,1,0:T(8,128)(2,1)S(1)}, u32[]{:S(2)}, u32[]{:S(2)}) collective-permute-start(bf16[2,2,128,512]{3,2,1,0:T(8,128)(2,1)S(1)} %get-tuple-element.21), channel_id=1, source_target_pairs={{0,16},{8,24},{16,0},{24,8},{1,17},{9,25},{17,1},{25,9},{2,18},{10... | collective-permute-start | bytes 1572872 | tf_op jit(solution)/shard_map/ppermute | solution.py:23
  11.2 0.0 copy-done.4
  11.2 0.0 copy-done.3
  11.2 0.8 %select_reduce_fusion.virtual = f32[8,256]{1,0:T(8,128)S(1)} fusion(f32[8,256]{1,0:T(8,128)S(1)} %copy-done.3, s32[8,256]{1,0:T(8,128)S(1)} %copy-done.4), kind=kLoop, calls=%fused_computation | loop fusion | flops 1570816 | bytes 24576 | tf_op jit(solution)/shard_map/reduce_sum | solution.py:45
  12.0 0.0 copy-done.1
  12.0 0.0 copy-done.2
  12.0 1.6 %shard_map.55 = (f32[2,3,2,256,256]{4,3,2,1,0:T(8,128)S(1)}, bf16[2,2,2,16,512]{4,3,2,1,0:T(8,128)(2,1)S(1)}) custom-call(s32[2,8]{1,0:T(2,128)S(1)} %copy-done.1, f32[8,8]{1,0:T(8,128)S(1)} %copy-done.2, f32[8,256]{1,0:T(8,128)S(1)} %select_reduce_fusion.virtual), custom_call_target="tpu_custom_call" | custom-call | tf_op jit(solution)/shard_map/pallas_call | solution.py:137
  13.6 0.6 %collective-permute-start.7 = (bf16[2,2,128,512]{3,2,1,0:T(8,128)(2,1)S(1)}, bf16[2,2,128,512]{3,2,1,0:T(8,128)(2,1)S(1)}, u32[]{:S(2)}, u32[]{:S(2)}) collective-permute-start(bf16[2,2,128,512]{3,2,1,0:T(8,128)(2,1)S(1)} %get-tuple-element.26), channel_id=1, source_target_pairs={{0,8},{8,0},{16,24},{24,16},{1,9},{9,1},{17,25},{25,17},{2,10},{10... | collective-permute-start | bytes 1572872 | tf_op jit(solution)/shard_map/ppermute | solution.py:23
  14.2 0.5 collective-permute-start.9
  14.7 8.3 %collective-permute-done.5.refs_2_ = bf16[2,2,128,512]{3,2,1,0:T(8,128)(2,1)S(1)} collective-permute-done((bf16[2,2,128,512]{3,2,1,0:T(8,128)(2,1)S(1)}, bf16[2,2,128,512]{3,2,1,0:T(8,128)(2,1)S(1)}, u32[]{:S(2)}, u32[]{:S(2)}) %collective-permute-start.5) | collective-permute-done | bytes 524320 | tf_op jit(solution)/shard_map/ppermute | solution.py:23
  23.1 1.4 %collective-permute-done.refs_3_ = bf16[2,2,128,512]{3,2,1,0:T(8,128)(2,1)S(1)} collective-permute-done((bf16[2,2,128,512]{3,2,1,0:T(8,128)(2,1)S(1)}, bf16[2,2,128,512]{3,2,1,0:T(8,128)(2,1)S(1)}, u32[]{:S(2)}, u32[]{:S(2)}) %collective-permute-start) | collective-permute-done | bytes 524320 | tf_op jit(solution)/shard_map/ppermute | solution.py:23
  24.6 0.1 slice.19
  24.6 0.1 collective-permute-start.11
  24.7 0.6 %collective-permute-start.6 = (bf16[3,2,128,512]{3,2,1,0:T(8,128)(2,1)S(1)}, bf16[3,2,128,512]{3,2,1,0:T(8,128)(2,1)S(1)}, u32[]{:S(2)}, u32[]{:S(2)}) collective-permute-start(bf16[3,2,128,512]{3,2,1,0:T(8,128)(2,1)S(1)} %slice.19), channel_id=1, source_target_pairs={{0,7},{1,2},{2,1},{3,4},{4,3},{5,6},{6,5},{7,0},{8,15},{9,10},{10,... | collective-permute-start | bytes 2359304 | tf_op jit(solution)/shard_map/ppermute | solution.py:33
  25.3 6.6 %collective-permute-done.7.refs_0_ = bf16[2,2,128,512]{3,2,1,0:T(8,128)(2,1)S(1)} collective-permute-done((bf16[2,2,128,512]{3,2,1,0:T(8,128)(2,1)S(1)}, bf16[2,2,128,512]{3,2,1,0:T(8,128)(2,1)S(1)}, u32[]{:S(2)}, u32[]{:S(2)}) %collective-permute-start.7) | collective-permute-done | bytes 524320 | tf_op jit(solution)/shard_map/ppermute | solution.py:23
  31.9 1.2 %collective-permute-done.9.refs_1_ = bf16[2,2,128,512]{3,2,1,0:T(8,128)(2,1)S(1)} collective-permute-done((bf16[2,2,128,512]{3,2,1,0:T(8,128)(2,1)S(1)}, bf16[2,2,128,512]{3,2,1,0:T(8,128)(2,1)S(1)}, u32[]{:S(2)}, u32[]{:S(2)}) %collective-permute-start.9) | collective-permute-done | bytes 524320 | tf_op jit(solution)/shard_map/ppermute | solution.py:23
  33.1 0.1 pad_maximum_fusion.source
  33.2 0.0 collective-permute-done.1
  33.2 0.1 collective-permute-start.8
  33.3 0.0 copy-start
  33.3 0.6 %collective-permute-start.10 = (bf16[2,2,128,512]{3,2,1,0:T(8,128)(2,1)S(1)}, bf16[2,2,128,512]{3,2,1,0:T(8,128)(2,1)S(1)}, u32[]{:S(2)}, u32[]{:S(2)}) collective-permute-start(bf16[2,2,128,512]{3,2,1,0:T(8,128)(2,1)S(1)} %shard_map.58), channel_id=1, source_target_pairs={{0,1},{1,0},{2,3},{3,2},{4,5},{5,4},{6,7},{7,6},{8,9},{9,8},{10,11... | collective-permute-start | bytes 1572872 | tf_op jit(solution)/shard_map/ppermute | solution.py:28
  33.9 0.1 fusion
  34.0 1.6 %collective-permute-start.4 = (bf16[2,2,128,512]{3,2,1,0:T(8,128)(2,1)S(1)}, bf16[2,2,128,512]{3,2,1,0:T(8,128)(2,1)S(1)}, u32[]{:S(2)}, u32[]{:S(2)}) collective-permute-start(bf16[2,2,128,512]{3,2,1,0:T(8,128)(2,1)S(1)} %get-tuple-element.33), channel_id=1, source_target_pairs={{0,16},{8,24},{16,0},{24,8},{1,17},{9,25},{17,1},{25,9},{2,18},{10... | collective-permute-start | bytes 1572872 | tf_op jit(solution)/shard_map/ppermute | solution.py:23
  35.6 0.0 collective-permute-done.11.refs_4_
  35.6 0.5 collective-permute-start.3
  36.1 0.0 copy-done
  36.1 3.5 %shard_map.59.total = f32[2,2,2,256,512]{4,3,2,1,0:T(8,128)S(1)} custom-call(bf16[2,2,1,2,256,512]{5,4,3,2,1,0:T(8,128)(2,1)S(1)} %copy-done, f32[2,3,2,256,256]{4,3,2,1,0:T(8,128)S(1)} %get-tuple-element.19.inverse, bf16[2,2,128,512]{3,2,1,0:T(8,128)(2,1)S(1)} %collective-permute-done.7.refs_0_, ...), custom_call_target="tpu_custom_call" | custom-call | tf_op jit(solution)/shard_map/pallas_call | solution.py:208
  39.7 0.0 collective-permute-done.8
  39.7 1.4 %collective-permute-start.2 = (bf16[1,2,128,512]{3,2,1,0:T(8,128)(2,1)S(1)}, bf16[1,2,128,512]{3,2,1,0:T(8,128)(2,1)S(1)}, u32[]{:S(2)}, u32[]{:S(2)}) collective-permute-start(bf16[1,2,128,512]{3,2,1,0:T(8,128)(2,1)S(1)} %slice.16), channel_id=1, source_target_pairs={{0,7},{1,2},{2,1},{3,4},{4,3},{5,6},{6,5},{7,0},{8,15},{9,10},{10,... | collective-permute-start | bytes 786440 | tf_op jit(solution)/shard_map/ppermute | solution.py:33
  41.0 0.0 collective-permute-done.10
  41.0 0.1 pad_maximum_fusion.1.window
  41.1 1.6 %shard_map.60.total = f32[2,2,2,256,512]{4,3,2,1,0:T(8,128)S(1)} custom-call(bf16[2,2,1,2,256,512]{5,4,3,2,1,0:T(8,128)(2,1)S(1)} %copy-done, f32[2,3,2,256,256]{4,3,2,1,0:T(8,128)S(1)} %get-tuple-element.19.inverse, bf16[4,2,128,512]{3,2,1,0:T(8,128)(2,1)S(1)} %pad_maximum_fusion.1.window, ...), custom_call_target="tpu_custom_call", output_to_operand_aliasing={{}: (3, {})} | custom-call | tf_op jit(solution)/shard_map/pallas_call | solution.py:233
  42.8 3.7 %collective-permute-done.6.window = bf16[3,2,128,512]{3,2,1,0:T(8,128)(2,1)S(1)} collective-permute-done((bf16[3,2,128,512]{3,2,1,0:T(8,128)(2,1)S(1)}, bf16[3,2,128,512]{3,2,1,0:T(8,128)(2,1)S(1)}, u32[]{:S(2)}, u32[]{:S(2)}) %collective-permute-start.6) | collective-permute-done | bytes 786464 | tf_op jit(solution)/shard_map/ppermute | solution.py:33
  46.5 1.3 %shard_map.61.refs_2_ = f32[2,2,2,256,512]{4,3,2,1,0:T(8,128)S(1)} custom-call(bf16[2,2,1,2,256,512]{5,4,3,2,1,0:T(8,128)(2,1)S(1)} %copy-done, f32[2,3,2,256,256]{4,3,2,1,0:T(8,128)S(1)} %get-tuple-element.19.inverse, bf16[3,2,128,512]{3,2,1,0:T(8,128)(2,1)S(1)} %collective-permute-done.6.window, ...), custom_call_target="tpu_custom_call", output_to_operand_aliasing={{}: (3, {})} | custom-call | flops 3145728000 | tf_op jit(solution)/shard_map/pallas_call | solution.py:233
  47.8 0.1 collective-permute-done.4.refs_1_
  47.9 1.2 %collective-permute-done.3.refs_0_ = bf16[2,2,128,512]{3,2,1,0:T(8,128)(2,1)S(1)} collective-permute-done((bf16[2,2,128,512]{3,2,1,0:T(8,128)(2,1)S(1)}, bf16[2,2,128,512]{3,2,1,0:T(8,128)(2,1)S(1)}, u32[]{:S(2)}, u32[]{:S(2)}) %collective-permute-start.3) | collective-permute-done | bytes 524320 | tf_op jit(solution)/shard_map/ppermute | solution.py:23
  49.1 2.1 %shard_map.62 = (f32[2,2,2,256,512]{4,3,2,1,0:T(8,128)S(1)}, bf16[2,2,1,2,256,512]{5,4,3,2,1,0:T(8,128)(2,1)}) custom-call(bf16[2,2,1,2,256,512]{5,4,3,2,1,0:T(8,128)(2,1)S(1)} %copy-done, f32[2,3,2,256,256]{4,3,2,1,0:T(8,128)S(1)} %get-tuple-element.19.inverse, ...), custom_call_target="tpu_custom_call", output_to_operand_aliasing={{0}: (5, {})} | custom-call | tf_op jit(solution)/shard_map/pallas_call | solution.py:281
  51.2 0.8 %collective-permute-done.2.window = bf16[1,2,128,512]{3,2,1,0:T(8,128)(2,1)S(1)} collective-permute-done((bf16[1,2,128,512]{3,2,1,0:T(8,128)(2,1)S(1)}, bf16[1,2,128,512]{3,2,1,0:T(8,128)(2,1)S(1)}, u32[]{:S(2)}, u32[]{:S(2)}) %collective-permute-start.2) | collective-permute-done | bytes 262176 | tf_op jit(solution)/shard_map/ppermute | solution.py:33
  52.0 1.5 %shard_map.63 = bf16[2,2,1,2,256,512]{5,4,3,2,1,0:T(8,128)(2,1)} custom-call(bf16[2,2,1,2,256,512]{5,4,3,2,1,0:T(8,128)(2,1)S(1)} %copy-done, f32[2,3,2,256,256]{4,3,2,1,0:T(8,128)S(1)} %get-tuple-element.19.inverse, bf16[1,2,128,512]{3,2,1,0:T(8,128)(2,1)S(1)} %collective-permute-done.2.window, ...), custom_call_target="tpu_custom_call", output_to_operand_aliasing={{}: (4, {})} | custom-call | tf_op jit(solution)/shard_map/pallas_call | solution.py:319
  (4 shorter events, 0.1 us)
Async XLA Ops:
  0.0 12.0 %copy-start.1 = (s32[2,8]{1,0:T(2,128)S(1)}, s32[2,8]{1,0:T(2,128)}, u32[]{:S(2)}) copy-start(s32[2,8]{1,0:T(2,128)} %partner.2) | copy-start | bytes 196
  0.0 11.2 %copy-start.4 = (s32[8,256]{1,0:T(8,128)S(1)}, s32[8,256]{1,0:T(8,128)}, u32[]{:S(2)}) copy-start(s32[8,256]{1,0:T(8,128)} %param.9) | copy-start | bytes 24580
  0.0 11.2 %copy-start.3 = (f32[8,256]{1,0:T(8,128)S(1)}, f32[8,256]{1,0:T(8,128)}, u32[]{:S(2)}) copy-start(f32[8,256]{1,0:T(8,128)} %param.8) | copy-start | bytes 24580
  0.0 12.0 %copy-start.2 = (f32[8,8]{1,0:T(8,128)S(1)}, f32[8,8]{1,0:T(8,128)}, u32[]{:S(2)}) copy-start(f32[8,8]{1,0:T(8,128)} %occ.1) | copy-start | bytes 772
  1.3 31.9 %collective-permute-start.1 = (bf16[4,2,128,512]{3,2,1,0:T(8,128)(2,1)S(1)}, bf16[4,2,128,512]{3,2,1,0:T(8,128)(2,1)S(1)}, u32[]{:S(2)}, u32[]{:S(2)}) collective-permute-start(bf16[4,2,128,512]{3,2,1,0:T(8,128)(2,1)S(1)} %shard_map.56), channel_id=1, source_target_pairs={{0,7},{1,2},{2,1},{3,4},{4,3},{5,6},{6,5},{7,0},{8,15},{9,10},{10,... | collective-permute-start | bytes 3145736 | tf_op jit(solution)/shard_map/ppermute | solution.py:33
  8.1 14.9 %collective-permute-start.5 = (bf16[2,2,128,512]{3,2,1,0:T(8,128)(2,1)S(1)}, bf16[2,2,128,512]{3,2,1,0:T(8,128)(2,1)S(1)}, u32[]{:S(2)}, u32[]{:S(2)}) collective-permute-start(bf16[2,2,128,512]{3,2,1,0:T(8,128)(2,1)S(1)} %get-tuple-element.24), channel_id=1, source_target_pairs={{0,8},{8,0},{16,24},{24,16},{1,9},{9,1},{17,25},{25,17},{2,10},{10... | collective-permute-start | bytes 1572872 | tf_op jit(solution)/shard_map/ppermute | solution.py:23
  9.7 14.9 %collective-permute-start = (bf16[2,2,128,512]{3,2,1,0:T(8,128)(2,1)S(1)}, bf16[2,2,128,512]{3,2,1,0:T(8,128)(2,1)S(1)}, u32[]{:S(2)}, u32[]{:S(2)}) collective-permute-start(bf16[2,2,128,512]{3,2,1,0:T(8,128)(2,1)S(1)} %get-tuple-element.21), channel_id=1, source_target_pairs={{0,16},{8,24},{16,0},{24,8},{1,17},{9,25},{17,1},{25,9},{2,18},{10... | collective-permute-start | bytes 1572872 | tf_op jit(solution)/shard_map/ppermute | solution.py:23
  13.6 18.3 %collective-permute-start.7 = (bf16[2,2,128,512]{3,2,1,0:T(8,128)(2,1)S(1)}, bf16[2,2,128,512]{3,2,1,0:T(8,128)(2,1)S(1)}, u32[]{:S(2)}, u32[]{:S(2)}) collective-permute-start(bf16[2,2,128,512]{3,2,1,0:T(8,128)(2,1)S(1)} %get-tuple-element.26), channel_id=1, source_target_pairs={{0,8},{8,0},{16,24},{24,16},{1,9},{9,1},{17,25},{25,17},{2,10},{10... | collective-permute-start | bytes 1572872 | tf_op jit(solution)/shard_map/ppermute | solution.py:23
  14.2 18.9 %collective-permute-start.9 = (bf16[2,2,128,512]{3,2,1,0:T(8,128)(2,1)S(1)}, bf16[2,2,128,512]{3,2,1,0:T(8,128)(2,1)S(1)}, u32[]{:S(2)}, u32[]{:S(2)}) collective-permute-start(bf16[2,2,128,512]{3,2,1,0:T(8,128)(2,1)S(1)} %get-tuple-element.29), channel_id=1, source_target_pairs={{0,16},{8,24},{16,0},{24,8},{1,17},{9,25},{17,1},{25,9},{2,18},{10... | collective-permute-start | bytes 1572872 | tf_op jit(solution)/shard_map/ppermute | solution.py:23
  24.6 10.9 %collective-permute-start.11 = (bf16[4,2,128,512]{3,2,1,0:T(8,128)(2,1)S(1)}, bf16[4,2,128,512]{3,2,1,0:T(8,128)(2,1)S(1)}, u32[]{:S(2)}, u32[]{:S(2)}) collective-permute-start(bf16[4,2,128,512]{3,2,1,0:T(8,128)(2,1)S(1)} %constant_dynamic-update-slice_fusion), channel_id=1, source_target_pairs={{0,1},{1,0},{2,3},{3,2},{4,5},{5,4},{6,7},{7,6},{8,9},{9,8},{10,11... | collective-permute-start | bytes 3145736 | tf_op jit(solution)/shard_map/ppermute | solution.py:28
  24.7 21.8 %collective-permute-start.6 = (bf16[3,2,128,512]{3,2,1,0:T(8,128)(2,1)S(1)}, bf16[3,2,128,512]{3,2,1,0:T(8,128)(2,1)S(1)}, u32[]{:S(2)}, u32[]{:S(2)}) collective-permute-start(bf16[3,2,128,512]{3,2,1,0:T(8,128)(2,1)S(1)} %slice.19), channel_id=1, source_target_pairs={{0,7},{1,2},{2,1},{3,4},{4,3},{5,6},{6,5},{7,0},{8,15},{9,10},{10,... | collective-permute-start | bytes 2359304 | tf_op jit(solution)/shard_map/ppermute | solution.py:33
  33.2 6.4 %collective-permute-start.8 = (bf16[2,2,128,512]{3,2,1,0:T(8,128)(2,1)S(1)}, bf16[2,2,128,512]{3,2,1,0:T(8,128)(2,1)S(1)}, u32[]{:S(2)}, u32[]{:S(2)}) collective-permute-start(bf16[2,2,128,512]{3,2,1,0:T(8,128)(2,1)S(1)} %collective-permute-done.7.refs_0_), channel_id=1, source_target_pairs={{0,1},{1,0},{2,3},{3,2},{4,5},{5,4},{6,7},{7,6},{8,9},{9,8},{10,11... | collective-permute-start | bytes 1572872 | tf_op jit(solution)/shard_map/ppermute | solution.py:28
  33.3 2.8 %copy-start = (bf16[2,2,1,2,256,512]{5,4,3,2,1,0:T(8,128)(2,1)S(1)}, bf16[2,2,1,2,256,512]{5,4,3,2,1,0:T(8,128)(2,1)}, u32[]{:S(2)}) copy-start(bf16[2,2,1,2,256,512]{5,4,3,2,1,0:T(8,128)(2,1)} %factor.13) | copy-start | bytes 6291460
  33.3 7.7 %collective-permute-start.10 = (bf16[2,2,128,512]{3,2,1,0:T(8,128)(2,1)S(1)}, bf16[2,2,128,512]{3,2,1,0:T(8,128)(2,1)S(1)}, u32[]{:S(2)}, u32[]{:S(2)}) collective-permute-start(bf16[2,2,128,512]{3,2,1,0:T(8,128)(2,1)S(1)} %shard_map.58), channel_id=1, source_target_pairs={{0,1},{1,0},{2,3},{3,2},{4,5},{5,4},{6,7},{7,6},{8,9},{9,8},{10,11... | collective-permute-start | bytes 1572872 | tf_op jit(solution)/shard_map/ppermute | solution.py:28
  34.0 13.9 %collective-permute-start.4 = (bf16[2,2,128,512]{3,2,1,0:T(8,128)(2,1)S(1)}, bf16[2,2,128,512]{3,2,1,0:T(8,128)(2,1)S(1)}, u32[]{:S(2)}, u32[]{:S(2)}) collective-permute-start(bf16[2,2,128,512]{3,2,1,0:T(8,128)(2,1)S(1)} %get-tuple-element.33), channel_id=1, source_target_pairs={{0,16},{8,24},{16,0},{24,8},{1,17},{9,25},{17,1},{25,9},{2,18},{10... | collective-permute-start | bytes 1572872 | tf_op jit(solution)/shard_map/ppermute | solution.py:23
  35.6 13.6 %collective-permute-start.3 = (bf16[2,2,128,512]{3,2,1,0:T(8,128)(2,1)S(1)}, bf16[2,2,128,512]{3,2,1,0:T(8,128)(2,1)S(1)}, u32[]{:S(2)}, u32[]{:S(2)}) collective-permute-start(bf16[2,2,128,512]{3,2,1,0:T(8,128)(2,1)S(1)} %get-tuple-element.34), channel_id=1, source_target_pairs={{0,8},{8,0},{16,24},{24,16},{1,9},{9,1},{17,25},{25,17},{2,10},{10... | collective-permute-start | bytes 1572872 | tf_op jit(solution)/shard_map/ppermute | solution.py:23
  39.7 12.4 %collective-permute-start.2 = (bf16[1,2,128,512]{3,2,1,0:T(8,128)(2,1)S(1)}, bf16[1,2,128,512]{3,2,1,0:T(8,128)(2,1)S(1)}, u32[]{:S(2)}, u32[]{:S(2)}) collective-permute-start(bf16[1,2,128,512]{3,2,1,0:T(8,128)(2,1)S(1)} %slice.16), channel_id=1, source_target_pairs={{0,7},{1,2},{2,1},{3,4},{4,3},{5,6},{6,5},{7,0},{8,15},{9,10},{10,... | collective-permute-start | bytes 786440 | tf_op jit(solution)/shard_map/ppermute | solution.py:33

commit v18 on v15

--- a/solution.py
+++ b/solution.py
@@ -306,10 +306,11 @@
             waiting.append(amplitude_rows(factor[t, k, 0, :, rows, :], terms))
         for r, (sides, blocks) in enumerate(waiting):
             rows = half_of(r, nv // 2)
+            both = jnp.concatenate(sides, axis=0)
+            values = jnp.dot(both, blocks, preferred_element_type=F32).reshape(parts, nv // 2, -1)
             for part in range(parts):
-                value = jnp.dot(sides[part], blocks, preferred_element_type=F32)
                 target = out.at[t, k, 0, part, pl.ds(rows.start, nv // 2)]
-                send_part(copies, value + total[t, k, part, rows], target, staged, sems)
+                send_part(copies, values[part] + total[t, k, part, rows], target, staged, sems)
     for copy in copies:
         copy.wait()
 

time: 53.5 us -> 53.5 us (level)
  no operation moved by 1% of the time
where the time goes in v18:
time: 53.5 us; the launch traced here: 53.3 us
  waiting for transfers between devices  23.5 us (44%)
  Pallas kernels  15.1 us (28%)
  starting transfers between devices  13.4 us (25%)
  other arithmetic  0.94 us (2%)
    ppermute x6, waiting for transfers between devices, group_swap(): return lax.ppermute(block, 'kpt', [(g, g ^ 1 << bit) for g in range(count)])  18.9 us
    ppermute x3, starting transfers between devices, far_swap(): lax.ppermute(block, 'occ', [(i, (i + (1 if i % 2 else count - 1)) % count...  6.52 us
    ppermute x6, starting transfers between devices, group_swap(): return lax.ppermute(block, 'kpt', [(g, g ^ 1 << bit) for g in range(count)])  6.21 us
    ppermute x3, waiting for transfers between devices, far_swap(): lax.ppermute(block, 'occ', [(i, (i + (1 if i % 2 else count - 1)) % count...  4.59 us
    pallas_call x1, Pallas kernels, first_terms(): pl.pallas_call(first_kernel, out_shape=jax.ShapeDtypeStruct((transfers, k...  3.52 us
    pallas_call x2, Pallas kernels, add_terms(): pl.pallas_call(functools.partial(add_kernel, place, h), out_shape=jax.Sha...  2.92 us
    pallas_call x1, Pallas kernels, pack(): pl.pallas_call(functools.partial(pack_kernel, bits), out_shape=[jax.Shape...  2.35 us
    pallas_call x1, Pallas kernels, far_terms(): pl.pallas_call(functools.partial(far_kernel, done), out_shape=[jax.ShapeD...  2.07 us
  transfers between devices with their start and end apart: 12, of which 8 were waited for; matrix products, arithmetic and copies ran while one was open for 2% of the time, Pallas kernels for 23%

profile of v18, /device:TPU:0, one launch (start us, length us, event | category | flops | bytes accessed | tf_op | source)
XLA Modules:
  0.0 53.3 jit_solution(571672734794089967)
XLA Ops:
  0.0 0.0 copy-start.1
  0.0 0.0 copy-start.4
  0.0 0.0 copy-start.3
  0.0 0.0 copy-start.2
  0.0 1.3 %shard_map.56 = bf16[4,2,128,512]{3,2,1,0:T(8,128)(2,1)S(1)} custom-call(bf16[2,2,1,2,256,512]{5,4,3,2,1,0:T(8,128)(2,1)} %factor.13), custom_call_target="tpu_custom_call" | custom-call | tf_op jit(solution)/shard_map/pallas_call | solution.py:65
  1.3 4.5 %collective-permute-start.1 = (bf16[4,2,128,512]{3,2,1,0:T(8,128)(2,1)S(1)}, bf16[4,2,128,512]{3,2,1,0:T(8,128)(2,1)S(1)}, u32[]{:S(2)}, u32[]{:S(2)}) collective-permute-start(bf16[4,2,128,512]{3,2,1,0:T(8,128)(2,1)S(1)} %shard_map.56), channel_id=1, source_target_pairs={{0,7},{1,2},{2,1},{3,4},{4,3},{5,6},{6,5},{7,0},{8,15},{9,10},{10,... | collective-permute-start | bytes 3145736 | tf_op jit(solution)/shard_map/ppermute | solution.py:33
  5.8 2.3 %shard_map.57 = (bf16[2,2,128,512]{3,2,1,0:T(8,128)(2,1)S(1)}, bf16[2,2,128,512]{3,2,1,0:T(8,128)(2,1)S(1)}, bf16[2,2,128,512]{3,2,1,0:T(8,128)(2,1)S(1)}, bf16[2,2,128,512]{3,2,1,0:T(8,128)(2,1)S(1)}) custom-call(s32[2,8]{1,0:T(2,128)} %partner.2, bf16[2,2,1,2,256,512]{5,4,3,2,1,0:T(8,128)(2,1)} %factor.13), custom_call_target="tpu_custom_call" | custom-call | bytes 16777216 | tf_op jit(solution)/shard_map/pallas_call | solution.py:96
  8.2 1.6 %collective-permute-start.5 = (bf16[2,2,128,512]{3,2,1,0:T(8,128)(2,1)S(1)}, bf16[2,2,128,512]{3,2,1,0:T(8,128)(2,1)S(1)}, u32[]{:S(2)}, u32[]{:S(2)}) collective-permute-start(bf16[2,2,128,512]{3,2,1,0:T(8,128)(2,1)S(1)} %get-tuple-element.24), channel_id=1, source_target_pairs={{0,8},{8,0},{16,24},{24,16},{1,9},{9,1},{17,25},{25,17},{2,10},{10... | collective-permute-start | bytes 1572872 | tf_op jit(solution)/shard_map/ppermute | solution.py:23
  9.8 1.4 %collective-permute-start = (bf16[2,2,128,512]{3,2,1,0:T(8,128)(2,1)S(1)}, bf16[2,2,128,512]{3,2,1,0:T(8,128)(2,1)S(1)}, u32[]{:S(2)}, u32[]{:S(2)}) collective-permute-start(bf16[2,2,128,512]{3,2,1,0:T(8,128)(2,1)S(1)} %get-tuple-element.21), channel_id=1, source_target_pairs={{0,16},{8,24},{16,0},{24,8},{1,17},{9,25},{17,1},{25,9},{2,18},{10... | collective-permute-start | bytes 1572872 | tf_op jit(solution)/shard_map/ppermute | solution.py:23
  11.2 0.0 copy-done.4
  11.2 0.0 copy-done.3
  11.2 0.8 %select_reduce_fusion.virtual = f32[8,256]{1,0:T(8,128)S(1)} fusion(f32[8,256]{1,0:T(8,128)S(1)} %copy-done.3, s32[8,256]{1,0:T(8,128)S(1)} %copy-done.4), kind=kLoop, calls=%fused_computation | loop fusion | flops 1570816 | bytes 24576 | tf_op jit(solution)/shard_map/reduce_sum | solution.py:45
  12.0 0.0 copy-done.1
  12.0 0.0 copy-done.2
  12.0 1.6 %shard_map.55 = (f32[2,3,2,256,256]{4,3,2,1,0:T(8,128)S(1)}, bf16[2,2,2,16,512]{4,3,2,1,0:T(8,128)(2,1)S(1)}) custom-call(s32[2,8]{1,0:T(2,128)S(1)} %copy-done.1, f32[8,8]{1,0:T(8,128)S(1)} %copy-done.2, f32[8,256]{1,0:T(8,128)S(1)} %select_reduce_fusion.virtual), custom_call_target="tpu_custom_call" | custom-call | tf_op jit(solution)/shard_map/pallas_call | solution.py:137
  13.6 0.6 %collective-permute-start.7 = (bf16[2,2,128,512]{3,2,1,0:T(8,128)(2,1)S(1)}, bf16[2,2,128,512]{3,2,1,0:T(8,128)(2,1)S(1)}, u32[]{:S(2)}, u32[]{:S(2)}) collective-permute-start(bf16[2,2,128,512]{3,2,1,0:T(8,128)(2,1)S(1)} %get-tuple-element.26), channel_id=1, source_target_pairs={{0,8},{8,0},{16,24},{24,16},{1,9},{9,1},{17,25},{25,17},{2,10},{10... | collective-permute-start | bytes 1572872 | tf_op jit(solution)/shard_map/ppermute | solution.py:23
  14.2 0.6 %collective-permute-start.9 = (bf16[2,2,128,512]{3,2,1,0:T(8,128)(2,1)S(1)}, bf16[2,2,128,512]{3,2,1,0:T(8,128)(2,1)S(1)}, u32[]{:S(2)}, u32[]{:S(2)}) collective-permute-start(bf16[2,2,128,512]{3,2,1,0:T(8,128)(2,1)S(1)} %get-tuple-element.29), channel_id=1, source_target_pairs={{0,16},{8,24},{16,0},{24,8},{1,17},{9,25},{17,1},{25,9},{2,18},{10... | collective-permute-start | bytes 1572872 | tf_op jit(solution)/shard_map/ppermute | solution.py:23
  14.8 8.3 %collective-permute-done.5.refs_2_ = bf16[2,2,128,512]{3,2,1,0:T(8,128)(2,1)S(1)} collective-permute-done((bf16[2,2,128,512]{3,2,1,0:T(8,128)(2,1)S(1)}, bf16[2,2,128,512]{3,2,1,0:T(8,128)(2,1)S(1)}, u32[]{:S(2)}, u32[]{:S(2)}) %collective-permute-start.5) | collective-permute-done | bytes 524320 | tf_op jit(solution)/shard_map/ppermute | solution.py:23
  23.1 1.5 %collective-permute-done.refs_3_ = bf16[2,2,128,512]{3,2,1,0:T(8,128)(2,1)S(1)} collective-permute-done((bf16[2,2,128,512]{3,2,1,0:T(8,128)(2,1)S(1)}, bf16[2,2,128,512]{3,2,1,0:T(8,128)(2,1)S(1)}, u32[]{:S(2)}, u32[]{:S(2)}) %collective-permute-start) | collective-permute-done | bytes 524320 | tf_op jit(solution)/shard_map/ppermute | solution.py:23
  24.7 0.1 slice.19
  24.7 0.1 collective-permute-start.11
  24.8 0.6 %collective-permute-start.6 = (bf16[3,2,128,512]{3,2,1,0:T(8,128)(2,1)S(1)}, bf16[3,2,128,512]{3,2,1,0:T(8,128)(2,1)S(1)}, u32[]{:S(2)}, u32[]{:S(2)}) collective-permute-start(bf16[3,2,128,512]{3,2,1,0:T(8,128)(2,1)S(1)} %slice.19), channel_id=1, source_target_pairs={{0,7},{1,2},{2,1},{3,4},{4,3},{5,6},{6,5},{7,0},{8,15},{9,10},{10,... | collective-permute-start | bytes 2359304 | tf_op jit(solution)/shard_map/ppermute | solution.py:33
  25.4 6.6 %collective-permute-done.7.refs_0_ = bf16[2,2,128,512]{3,2,1,0:T(8,128)(2,1)S(1)} collective-permute-done((bf16[2,2,128,512]{3,2,1,0:T(8,128)(2,1)S(1)}, bf16[2,2,128,512]{3,2,1,0:T(8,128)(2,1)S(1)}, u32[]{:S(2)}, u32[]{:S(2)}) %collective-permute-start.7) | collective-permute-done | bytes 524320 | tf_op jit(solution)/shard_map/ppermute | solution.py:23
  32.0 1.2 %collective-permute-done.9.refs_1_ = bf16[2,2,128,512]{3,2,1,0:T(8,128)(2,1)S(1)} collective-permute-done((bf16[2,2,128,512]{3,2,1,0:T(8,128)(2,1)S(1)}, bf16[2,2,128,512]{3,2,1,0:T(8,128)(2,1)S(1)}, u32[]{:S(2)}, u32[]{:S(2)}) %collective-permute-start.9) | collective-permute-done | bytes 524320 | tf_op jit(solution)/shard_map/ppermute | solution.py:23
  33.2 0.1 pad_maximum_fusion.source
  33.3 0.0 collective-permute-done.1
  33.3 0.1 collective-permute-start.8
  33.4 0.0 copy-start
  33.4 0.6 %collective-permute-start.10 = (bf16[2,2,128,512]{3,2,1,0:T(8,128)(2,1)S(1)}, bf16[2,2,128,512]{3,2,1,0:T(8,128)(2,1)S(1)}, u32[]{:S(2)}, u32[]{:S(2)}) collective-permute-start(bf16[2,2,128,512]{3,2,1,0:T(8,128)(2,1)S(1)} %shard_map.58), channel_id=1, source_target_pairs={{0,1},{1,0},{2,3},{3,2},{4,5},{5,4},{6,7},{7,6},{8,9},{9,8},{10,11... | collective-permute-start | bytes 1572872 | tf_op jit(solution)/shard_map/ppermute | solution.py:28
  34.0 0.1 fusion
  34.1 1.5 %collective-permute-start.4 = (bf16[2,2,128,512]{3,2,1,0:T(8,128)(2,1)S(1)}, bf16[2,2,128,512]{3,2,1,0:T(8,128)(2,1)S(1)}, u32[]{:S(2)}, u32[]{:S(2)}) collective-permute-start(bf16[2,2,128,512]{3,2,1,0:T(8,128)(2,1)S(1)} %get-tuple-element.33), channel_id=1, source_target_pairs={{0,16},{8,24},{16,0},{24,8},{1,17},{9,25},{17,1},{25,9},{2,18},{10... | collective-permute-start | bytes 1572872 | tf_op jit(solution)/shard_map/ppermute | solution.py:23
  35.6 0.0 collective-permute-done.11.refs_4_
  35.6 0.5 %collective-permute-start.3 = (bf16[2,2,128,512]{3,2,1,0:T(8,128)(2,1)S(1)}, bf16[2,2,128,512]{3,2,1,0:T(8,128)(2,1)S(1)}, u32[]{:S(2)}, u32[]{:S(2)}) collective-permute-start(bf16[2,2,128,512]{3,2,1,0:T(8,128)(2,1)S(1)} %get-tuple-element.34), channel_id=1, source_target_pairs={{0,8},{8,0},{16,24},{24,16},{1,9},{9,1},{17,25},{25,17},{2,10},{10... | collective-permute-start | bytes 1572872 | tf_op jit(solution)/shard_map/ppermute | solution.py:23
  36.1 0.0 copy-done
  36.1 3.5 %shard_map.59.total = f32[2,2,2,256,512]{4,3,2,1,0:T(8,128)S(1)} custom-call(bf16[2,2,1,2,256,512]{5,4,3,2,1,0:T(8,128)(2,1)S(1)} %copy-done, f32[2,3,2,256,256]{4,3,2,1,0:T(8,128)S(1)} %get-tuple-element.19.inverse, bf16[2,2,128,512]{3,2,1,0:T(8,128)(2,1)S(1)} %collective-permute-done.7.refs_0_, ...), custom_call_target="tpu_custom_call" | custom-call | tf_op jit(solution)/shard_map/pallas_call | solution.py:208
  39.7 0.0 collective-permute-done.8
  39.7 1.4 %collective-permute-start.2 = (bf16[1,2,128,512]{3,2,1,0:T(8,128)(2,1)S(1)}, bf16[1,2,128,512]{3,2,1,0:T(8,128)(2,1)S(1)}, u32[]{:S(2)}, u32[]{:S(2)}) collective-permute-start(bf16[1,2,128,512]{3,2,1,0:T(8,128)(2,1)S(1)} %slice.16), channel_id=1, source_target_pairs={{0,7},{1,2},{2,1},{3,4},{4,3},{5,6},{6,5},{7,0},{8,15},{9,10},{10,... | collective-permute-start | bytes 786440 | tf_op jit(solution)/shard_map/ppermute | solution.py:33
  41.0 0.0 collective-permute-done.10
  41.0 0.1 pad_maximum_fusion.1.window
  41.1 1.6 %shard_map.60.total = f32[2,2,2,256,512]{4,3,2,1,0:T(8,128)S(1)} custom-call(bf16[2,2,1,2,256,512]{5,4,3,2,1,0:T(8,128)(2,1)S(1)} %copy-done, f32[2,3,2,256,256]{4,3,2,1,0:T(8,128)S(1)} %get-tuple-element.19.inverse, bf16[4,2,128,512]{3,2,1,0:T(8,128)(2,1)S(1)} %pad_maximum_fusion.1.window, ...), custom_call_target="tpu_custom_call", output_to_operand_aliasing={{}: (3, {})} | custom-call | tf_op jit(solution)/shard_map/pallas_call | solution.py:233
  42.8 3.8 %collective-permute-done.6.window = bf16[3,2,128,512]{3,2,1,0:T(8,128)(2,1)S(1)} collective-permute-done((bf16[3,2,128,512]{3,2,1,0:T(8,128)(2,1)S(1)}, bf16[3,2,128,512]{3,2,1,0:T(8,128)(2,1)S(1)}, u32[]{:S(2)}, u32[]{:S(2)}) %collective-permute-start.6) | collective-permute-done | bytes 786464 | tf_op jit(solution)/shard_map/ppermute | solution.py:33
  46.6 1.3 %shard_map.61.refs_2_ = f32[2,2,2,256,512]{4,3,2,1,0:T(8,128)S(1)} custom-call(bf16[2,2,1,2,256,512]{5,4,3,2,1,0:T(8,128)(2,1)S(1)} %copy-done, f32[2,3,2,256,256]{4,3,2,1,0:T(8,128)S(1)} %get-tuple-element.19.inverse, bf16[3,2,128,512]{3,2,1,0:T(8,128)(2,1)S(1)} %collective-permute-done.6.window, ...), custom_call_target="tpu_custom_call", output_to_operand_aliasing={{}: (3, {})} | custom-call | flops 3145728000 | tf_op jit(solution)/shard_map/pallas_call | solution.py:233
  47.9 0.1 collective-permute-done.4.refs_1_
  48.0 1.2 %collective-permute-done.3.refs_0_ = bf16[2,2,128,512]{3,2,1,0:T(8,128)(2,1)S(1)} collective-permute-done((bf16[2,2,128,512]{3,2,1,0:T(8,128)(2,1)S(1)}, bf16[2,2,128,512]{3,2,1,0:T(8,128)(2,1)S(1)}, u32[]{:S(2)}, u32[]{:S(2)}) %collective-permute-start.3) | collective-permute-done | bytes 524320 | tf_op jit(solution)/shard_map/ppermute | solution.py:23
  49.1 2.1 %shard_map.62 = (f32[2,2,2,256,512]{4,3,2,1,0:T(8,128)S(1)}, bf16[2,2,1,2,256,512]{5,4,3,2,1,0:T(8,128)(2,1)}) custom-call(bf16[2,2,1,2,256,512]{5,4,3,2,1,0:T(8,128)(2,1)S(1)} %copy-done, f32[2,3,2,256,256]{4,3,2,1,0:T(8,128)S(1)} %get-tuple-element.19.inverse, ...), custom_call_target="tpu_custom_call", output_to_operand_aliasing={{0}: (5, {})} | custom-call | tf_op jit(solution)/shard_map/pallas_call | solution.py:281
  51.2 0.8 %collective-permute-done.2.window = bf16[1,2,128,512]{3,2,1,0:T(8,128)(2,1)S(1)} collective-permute-done((bf16[1,2,128,512]{3,2,1,0:T(8,128)(2,1)S(1)}, bf16[1,2,128,512]{3,2,1,0:T(8,128)(2,1)S(1)}, u32[]{:S(2)}, u32[]{:S(2)}) %collective-permute-start.2) | collective-permute-done | bytes 262176 | tf_op jit(solution)/shard_map/ppermute | solution.py:33
  52.0 1.3 %shard_map.63 = bf16[2,2,1,2,256,512]{5,4,3,2,1,0:T(8,128)(2,1)} custom-call(bf16[2,2,1,2,256,512]{5,4,3,2,1,0:T(8,128)(2,1)S(1)} %copy-done, f32[2,3,2,256,256]{4,3,2,1,0:T(8,128)S(1)} %get-tuple-element.19.inverse, bf16[1,2,128,512]{3,2,1,0:T(8,128)(2,1)S(1)} %collective-permute-done.2.window, ...), custom_call_target="tpu_custom_call", output_to_operand_aliasing={{}: (4, {})} | custom-call | tf_op jit(solution)/shard_map/pallas_call | solution.py:320
  (4 shorter events, 0.1 us)
Async XLA Ops:
  0.0 12.0 %copy-start.1 = (s32[2,8]{1,0:T(2,128)S(1)}, s32[2,8]{1,0:T(2,128)}, u32[]{:S(2)}) copy-start(s32[2,8]{1,0:T(2,128)} %partner.2) | copy-start | bytes 196
  0.0 11.2 %copy-start.4 = (s32[8,256]{1,0:T(8,128)S(1)}, s32[8,256]{1,0:T(8,128)}, u32[]{:S(2)}) copy-start(s32[8,256]{1,0:T(8,128)} %param.9) | copy-start | bytes 24580
  0.0 11.2 %copy-start.3 = (f32[8,256]{1,0:T(8,128)S(1)}, f32[8,256]{1,0:T(8,128)}, u32[]{:S(2)}) copy-start(f32[8,256]{1,0:T(8,128)} %param.8) | copy-start | bytes 24580
  0.0 12.0 %copy-start.2 = (f32[8,8]{1,0:T(8,128)S(1)}, f32[8,8]{1,0:T(8,128)}, u32[]{:S(2)}) copy-start(f32[8,8]{1,0:T(8,128)} %occ.1) | copy-start | bytes 772
  1.3 32.0 %collective-permute-start.1 = (bf16[4,2,128,512]{3,2,1,0:T(8,128)(2,1)S(1)}, bf16[4,2,128,512]{3,2,1,0:T(8,128)(2,1)S(1)}, u32[]{:S(2)}, u32[]{:S(2)}) collective-permute-start(bf16[4,2,128,512]{3,2,1,0:T(8,128)(2,1)S(1)} %shard_map.56), channel_id=1, source_target_pairs={{0,7},{1,2},{2,1},{3,4},{4,3},{5,6},{6,5},{7,0},{8,15},{9,10},{10,... | collective-permute-start | bytes 3145736 | tf_op jit(solution)/shard_map/ppermute | solution.py:33
  8.2 14.9 %collective-permute-start.5 = (bf16[2,2,128,512]{3,2,1,0:T(8,128)(2,1)S(1)}, bf16[2,2,128,512]{3,2,1,0:T(8,128)(2,1)S(1)}, u32[]{:S(2)}, u32[]{:S(2)}) collective-permute-start(bf16[2,2,128,512]{3,2,1,0:T(8,128)(2,1)S(1)} %get-tuple-element.24), channel_id=1, source_target_pairs={{0,8},{8,0},{16,24},{24,16},{1,9},{9,1},{17,25},{25,17},{2,10},{10... | collective-permute-start | bytes 1572872 | tf_op jit(solution)/shard_map/ppermute | solution.py:23
  9.8 14.9 %collective-permute-start = (bf16[2,2,128,512]{3,2,1,0:T(8,128)(2,1)S(1)}, bf16[2,2,128,512]{3,2,1,0:T(8,128)(2,1)S(1)}, u32[]{:S(2)}, u32[]{:S(2)}) collective-permute-start(bf16[2,2,128,512]{3,2,1,0:T(8,128)(2,1)S(1)} %get-tuple-element.21), channel_id=1, source_target_pairs={{0,16},{8,24},{16,0},{24,8},{1,17},{9,25},{17,1},{25,9},{2,18},{10... | collective-permute-start | bytes 1572872 | tf_op jit(solution)/shard_map/ppermute | solution.py:23
  13.6 18.4 %collective-permute-start.7 = (bf16[2,2,128,512]{3,2,1,0:T(8,128)(2,1)S(1)}, bf16[2,2,128,512]{3,2,1,0:T(8,128)(2,1)S(1)}, u32[]{:S(2)}, u32[]{:S(2)}) collective-permute-start(bf16[2,2,128,512]{3,2,1,0:T(8,128)(2,1)S(1)} %get-tuple-element.26), channel_id=1, source_target_pairs={{0,8},{8,0},{16,24},{24,16},{1,9},{9,1},{17,25},{25,17},{2,10},{10... | collective-permute-start | bytes 1572872 | tf_op jit(solution)/shard_map/ppermute | solution.py:23
  14.2 19.0 %collective-permute-start.9 = (bf16[2,2,128,512]{3,2,1,0:T(8,128)(2,1)S(1)}, bf16[2,2,128,512]{3,2,1,0:T(8,128)(2,1)S(1)}, u32[]{:S(2)}, u32[]{:S(2)}) collective-permute-start(bf16[2,2,128,512]{3,2,1,0:T(8,128)(2,1)S(1)} %get-tuple-element.29), channel_id=1, source_target_pairs={{0,16},{8,24},{16,0},{24,8},{1,17},{9,25},{17,1},{25,9},{2,18},{10... | collective-permute-start | bytes 1572872 | tf_op jit(solution)/shard_map/ppermute | solution.py:23
  24.7 10.8 %collective-permute-start.11 = (bf16[4,2,128,512]{3,2,1,0:T(8,128)(2,1)S(1)}, bf16[4,2,128,512]{3,2,1,0:T(8,128)(2,1)S(1)}, u32[]{:S(2)}, u32[]{:S(2)}) collective-permute-start(bf16[4,2,128,512]{3,2,1,0:T(8,128)(2,1)S(1)} %constant_dynamic-update-slice_fusion), channel_id=1, source_target_pairs={{0,1},{1,0},{2,3},{3,2},{4,5},{5,4},{6,7},{7,6},{8,9},{9,8},{10,11... | collective-permute-start | bytes 3145736 | tf_op jit(solution)/shard_map/ppermute | solution.py:28
  24.8 21.8 %collective-permute-start.6 = (bf16[3,2,128,512]{3,2,1,0:T(8,128)(2,1)S(1)}, bf16[3,2,128,512]{3,2,1,0:T(8,128)(2,1)S(1)}, u32[]{:S(2)}, u32[]{:S(2)}) collective-permute-start(bf16[3,2,128,512]{3,2,1,0:T(8,128)(2,1)S(1)} %slice.19), channel_id=1, source_target_pairs={{0,7},{1,2},{2,1},{3,4},{4,3},{5,6},{6,5},{7,0},{8,15},{9,10},{10,... | collective-permute-start | bytes 2359304 | tf_op jit(solution)/shard_map/ppermute | solution.py:33
  33.3 6.4 %collective-permute-start.8 = (bf16[2,2,128,512]{3,2,1,0:T(8,128)(2,1)S(1)}, bf16[2,2,128,512]{3,2,1,0:T(8,128)(2,1)S(1)}, u32[]{:S(2)}, u32[]{:S(2)}) collective-permute-start(bf16[2,2,128,512]{3,2,1,0:T(8,128)(2,1)S(1)} %collective-permute-done.7.refs_0_), channel_id=1, source_target_pairs={{0,1},{1,0},{2,3},{3,2},{4,5},{5,4},{6,7},{7,6},{8,9},{9,8},{10,11... | collective-permute-start | bytes 1572872 | tf_op jit(solution)/shard_map/ppermute | solution.py:28
  33.4 2.7 %copy-start = (bf16[2,2,1,2,256,512]{5,4,3,2,1,0:T(8,128)(2,1)S(1)}, bf16[2,2,1,2,256,512]{5,4,3,2,1,0:T(8,128)(2,1)}, u32[]{:S(2)}) copy-start(bf16[2,2,1,2,256,512]{5,4,3,2,1,0:T(8,128)(2,1)} %factor.13) | copy-start | bytes 6291460
  33.4 7.6 %collective-permute-start.10 = (bf16[2,2,128,512]{3,2,1,0:T(8,128)(2,1)S(1)}, bf16[2,2,128,512]{3,2,1,0:T(8,128)(2,1)S(1)}, u32[]{:S(2)}, u32[]{:S(2)}) collective-permute-start(bf16[2,2,128,512]{3,2,1,0:T(8,128)(2,1)S(1)} %shard_map.58), channel_id=1, source_target_pairs={{0,1},{1,0},{2,3},{3,2},{4,5},{5,4},{6,7},{7,6},{8,9},{9,8},{10,11... | collective-permute-start | bytes 1572872 | tf_op jit(solution)/shard_map/ppermute | solution.py:28
  34.1 13.9 %collective-permute-start.4 = (bf16[2,2,128,512]{3,2,1,0:T(8,128)(2,1)S(1)}, bf16[2,2,128,512]{3,2,1,0:T(8,128)(2,1)S(1)}, u32[]{:S(2)}, u32[]{:S(2)}) collective-permute-start(bf16[2,2,128,512]{3,2,1,0:T(8,128)(2,1)S(1)} %get-tuple-element.33), channel_id=1, source_target_pairs={{0,16},{8,24},{16,0},{24,8},{1,17},{9,25},{17,1},{25,9},{2,18},{10... | collective-permute-start | bytes 1572872 | tf_op jit(solution)/shard_map/ppermute | solution.py:23
  35.6 13.6 %collective-permute-start.3 = (bf16[2,2,128,512]{3,2,1,0:T(8,128)(2,1)S(1)}, bf16[2,2,128,512]{3,2,1,0:T(8,128)(2,1)S(1)}, u32[]{:S(2)}, u32[]{:S(2)}) collective-permute-start(bf16[2,2,128,512]{3,2,1,0:T(8,128)(2,1)S(1)} %get-tuple-element.34), channel_id=1, source_target_pairs={{0,8},{8,0},{16,24},{24,16},{1,9},{9,1},{17,25},{25,17},{2,10},{10... | collective-permute-start | bytes 1572872 | tf_op jit(solution)/shard_map/ppermute | solution.py:23
  39.7 12.4 %collective-permute-start.2 = (bf16[1,2,128,512]{3,2,1,0:T(8,128)(2,1)S(1)}, bf16[1,2,128,512]{3,2,1,0:T(8,128)(2,1)S(1)}, u32[]{:S(2)}, u32[]{:S(2)}) collective-permute-start(bf16[1,2,128,512]{3,2,1,0:T(8,128)(2,1)S(1)} %slice.16), channel_id=1, source_target_pairs={{0,7},{1,2},{2,1},{3,4},{4,3},{5,6},{6,5},{7,0},{8,15},{9,10},{10,... | collective-permute-start | bytes 786440 | tf_op jit(solution)/shard_map/ppermute | solution.py:33
